TPU v7x, 32 devices: a whole 2x2x4 slice. The times are simulated.
32 devices in a mesh: member: 2 (over x), lateral: 8 (over z, y), radial: 2 (over core).
Axes of the slice: x: 2, y: 2, z: 4, core: 2. Of those that a mesh axis runs over, the one named last changes fastest.
Arguments:
- initial_displacement: float32 [6, 8, 256, 2048], P('member', 'radial', 'lateral'), parts along dimension 0, may hold values from -6 to 6
- force: float32 [6, 8, 256, 2048], P('member', 'radial', 'lateral'), parts along dimension 0, may hold values from -12 to 12
- viscosity: float32 [32], P('member'), parts along dimension 0, may hold values from 0.1 to 10
- layer_index: int32 [8, 256, 2048], P('radial', 'lateral'), may hold values from 0 to 15
- response: float32 [512, 1024], P(None, 'lateral'), may hold values from 0.2 to 2
- ocean_mask: int32 [256, 2048], P('lateral'), may hold values 0 or 1
Outputs:
- displacement: float32 [6, 8, 256, 2048], P('member', 'radial', 'lateral'), parts along dimension 0
- coefficients: float32 [1024, 1024], P('member', ('lateral', 'radial')), parts along dimension 0
- sea_load: float32 [256, 4096], P('lateral', 'member'), parts along dimension 1
There are 2 independent parts, one for each index of `member`. A program takes and returns all parts, laid end to end along the dimension named above; an argument that names none is the same for every part. Nothing has to cross between parts.
All inputs are finite; a program needn't handle non-finite values. No bound on the sum of `ocean_mask` on one device may be relied on, other than what follows from the above.
Results may differ from a plain program's by a relative error of at most 0.000073.
Values sent between devices are 32-bit elements; how exact they have to be, the bound alone decides.
No kernel may reach another device: no remote copies, remote signals or barrier semaphores. Data moves between devices by JAX's collectives and lax.ppermute only.
A program may use at most 128 MiB of HBM per device.

v0:
```python
import functools
import math

import jax
import jax.numpy as jnp
import ml_dtypes
import numpy as np
from jax import lax
from jax.experimental import pallas as pl
from jax.experimental.pallas import tpu as pltpu
from jax.sharding import PartitionSpec as P

MODES = 512
RELAXATION = 0.8
TILE = 8
MIB = 1 << 20
ANY = pl.BlockSpec(memory_space=pl.ANY)
SMEM = pl.BlockSpec(memory_space=pltpu.SMEM)
VMEM = pl.BlockSpec(memory_space=pltpu.VMEM)


def params(mib):
    return pltpu.CompilerParams(vmem_limit_bytes=mib * MIB)


def halves(table):
    high = table.astype(ml_dtypes.bfloat16)
    low = (table - high.astype(np.float64)).astype(ml_dtypes.bfloat16)
    return high, low


@functools.lru_cache
def longitude_tables(count, modes):
    points = np.arange(count // 2, dtype=np.int64)[:, None]
    orders = np.arange(modes, dtype=np.int64)[None, :]
    angle = (2.0 * math.pi / count) * (points * orders % count)
    table = np.concatenate([np.cos(angle), np.sin(angle)], axis=1) * math.sqrt(2.0 / count)
    return halves(table)


@functools.lru_cache
def colatitude_tables(count, modes):
    points = np.arange(count, dtype=np.int64)[:, None]
    waves = np.arange(modes, dtype=np.int64)[None, :]
    phase = waves * (2 * points + 1) % (4 * count)
    return halves(np.cos(math.pi / (2 * count) * phase) * math.sqrt(2.0 / count))


def split(values):
    high = values.astype(jnp.bfloat16)
    return high, (values - high.astype(jnp.float32)).astype(jnp.bfloat16)


def dot(a, b):
    return jnp.dot(a, b, preferred_element_type=jnp.float32)


def half_viscosity(index, viscosity_ref):
    values = [0.5 * viscosity_ref[k] for k in range(viscosity_ref.shape[0])]
    bit = 1
    while len(values) > 1:
        odd = (index & bit) != 0
        if len(values) % 2:
            values.append(values[-1])
        values = [jnp.where(odd, b, a) for a, b in zip(values[::2], values[1::2])]
        bit *= 2
    return values[0]


def row_number(shape):
    return lax.broadcasted_iota(jnp.int32, shape, 0)


def north_of(above, middle):
    return pltpu.roll(jnp.where(row_number(middle.shape) == TILE - 1, above, middle), 1, 0)


def south_of(below, middle):
    return pltpu.roll(jnp.where(row_number(middle.shape) == 0, below, middle), TILE - 1, 0)


def east_of(values):
    return pltpu.roll(values, values.shape[-1] - 1, values.ndim - 1)


def west_of(values):
    return pltpu.roll(values, 1, values.ndim - 1)


def relax_weights(middle, others):
    weights = [middle + other for other in others]
    diagonal = 1.0 + functools.reduce(jnp.add, weights)
    return weights, RELAXATION / diagonal


def relax(weights, factor, middle, others, force):
    total = force
    for weight, other in zip(weights, others):
        total = total + weight * other
    return (1.0 - RELAXATION) * middle + factor * total


def around(ref, lead, shell, start):
    rows = lambda first: pl.ds(pl.multiple_of(first, TILE), TILE)
    middle = ref[(*lead, shell, rows(start))]
    return middle, [
        ref[(*lead, shell + 1, rows(start))],
        ref[(*lead, shell - 1, rows(start))],
        south_of(ref[(*lead, shell, rows(start + TILE))], middle),
        north_of(ref[(*lead, shell, rows(start - TILE))], middle),
        west_of(middle),
        east_of(middle),
    ]


def surface_message_kernel(viscosity, d7, d6, f7, i7, i6, d7_end, d6_end, f7_end, i7_end, i6_end, up, down):
    sides = ((down, 0, (d7, d6, f7, i7, i6)), (up, TILE - 1, (d7_end, d6_end, f7_end, i7_end, i6_end)))
    for message, near, (a7, a6, g7, k7, k6) in sides:
        far = 1 if near == 0 else near - 1
        h7, h6 = half_viscosity(k7[...], viscosity), half_viscosity(k6[...], viscosity)
        rows = (a7[far], a7[near], a6[near], h7[far], h7[near], h6[near], g7[near])
        for place, row in enumerate(rows):
            message[place] = row
        message[len(rows)] = jnp.zeros_like(rows[0])


def main_message_kernel(viscosity, d, f, index, h, up, down, ring, tops, ends, force_tops, force_ends, sems):
    shells, rows = h.shape[0], h.shape[1]
    components = d.shape[0]
    last = pl.ds(rows - TILE, TILE)
    shell = jnp.where(lax.axis_index("radial") == 0, shells - 1, 0)
    copies = [
        pltpu.make_async_copy(d.at[:, :, pl.ds(0, TILE)], tops, sems.at[0]),
        pltpu.make_async_copy(d.at[:, :, last], ends, sems.at[1]),
        pltpu.make_async_copy(f.at[:, :, pl.ds(0, TILE)], force_tops, sems.at[2]),
        pltpu.make_async_copy(f.at[:, :, last], force_ends, sems.at[3]),
        pltpu.make_async_copy(d.at[:, shell], ring.at[pl.ds(0, components)], sems.at[4]),
    ]
    for copy in copies:
        copy.start()

    def lookup(step, _):
        s, start = step // (rows // TILE), pl.multiple_of(step % (rows // TILE) * TILE, TILE)
        h[s, pl.ds(start, TILE)] = half_viscosity(index[s, pl.ds(start, TILE)], viscosity)
        return 0

    lax.fori_loop(0, shells * (rows // TILE), lookup, 0)
    eta_copy = pltpu.make_async_copy(h.at[shell], ring.at[components], sems.at[5])
    eta_copy.start()
    for copy in copies[:4]:
        copy.wait()
    for message, near, a, g in ((down, 0, tops, force_tops), (up, TILE - 1, ends, force_ends)):
        far = 1 if near == 0 else near - 1
        h_near, h_far = (0, 1) if near == 0 else (rows - 1, rows - 2)
        for s in range(shells):
            for c in range(components):
                message[c * shells + s] = a[c, s, far]
                message[(components + c) * shells + s] = a[c, s, near]
                message[(2 * components + c) * shells + s] = g[c, s, near]
            message[3 * components * shells + s] = h[s, h_far]
            message[(3 * components + 1) * shells + s] = h[s, h_near]
    copies[4].wait()
    eta_copy.wait()


def surface_kernel(d, f, h, before, after, high, low, out, field, force, eta, smoothed, sems):
    shells, rows, count = h.shape
    top = lax.axis_size("radial") - 1

    @pl.when(lax.axis_index("radial") == top)
    def _():
        inner = pl.ds(TILE, rows)
        copies = [
            pltpu.make_async_copy(d.at[0, pl.ds(shells - 3, 3)], field.at[pl.ds(0, 3), inner], sems.at[0]),
            pltpu.make_async_copy(h.at[pl.ds(shells - 3, 3)], eta.at[pl.ds(0, 3), inner], sems.at[1]),
            pltpu.make_async_copy(f.at[0, pl.ds(shells - 2, 2)], force, sems.at[2]),
        ]
        for copy in copies:
            copy.start()
        zeros = jnp.zeros((rows, count), jnp.float32)
        field[3, inner] = zeros
        eta[3, inner] = zeros
        smoothed[2, inner] = zeros
        for message, place in ((before, TILE - 1), (after, rows + TILE)):
            field[2, place] = message[1]
            field[1, place] = message[2]
            eta[2, place] = message[4]
            eta[1, place] = message[5]
        for copy in copies:
            copy.wait()
        lateral = lax.axis_index("lateral")
        inside = (lateral > 0, lateral < lax.axis_size("lateral") - 1)
        for message, own, place, there in (
            (before, TILE, TILE - 1, inside[0]),
            (after, rows + TILE - 1, rows + TILE, inside[1]),
        ):
            row = lambda k: message[pl.ds(k, 1)]
            own_row = lambda ref: ref[2, pl.ds(own, 1)]
            none = jnp.zeros((1, count), jnp.float32)
            weights, factor = relax_weights(
                row(4), [none, row(5), row(3), own_row(eta), west_of(row(4)), east_of(row(4))]
            )
            edge = relax(
                weights,
                factor,
                row(1),
                [none, row(2), row(0), own_row(field), west_of(row(1)), east_of(row(1))],
                row(6),
            )
            smoothed[1, pl.ds(place, 1)] = jnp.where(there, edge, none)

        def first(step, _):
            start = pl.multiple_of(step * TILE, TILE)
            for s in (1, 2):
                weights, factor = relax_weights(*around(eta, (), s, start + TILE))
                middle, others = around(field, (), s, start + TILE)
                smoothed[s - 1, pl.ds(start + TILE, TILE)] = relax(
                    weights, factor, middle, others, force[s - 1, pl.ds(start, TILE)]
                )
            return 0

        lax.fori_loop(0, rows // TILE, first, 0)

        def second(step, _):
            start = pl.multiple_of(step * TILE, TILE)
            weights, factor = relax_weights(*around(eta, (), 2, start + TILE))
            middle, others = around(smoothed, (), 1, start + TILE)
            field[0, pl.ds(start, TILE)] = relax(weights, factor, middle, others, force[1, pl.ds(start, TILE)])
            return 0

        lax.fori_loop(0, rows // TILE, second, 0)
        half = count // 2
        left, right = field[0, pl.ds(0, rows), :half], field[0, pl.ds(0, rows), half:]
        near, far = split(jnp.concatenate([left + right, left - right], axis=0))
        total = dot(jnp.concatenate([near, far], axis=0), high[...])
        total = total[: 2 * rows] + total[2 * rows :] + dot(near, low[...])
        odd = lax.broadcasted_iota(jnp.int32, (rows, total.shape[1]), 1) % 2 == 1
        fourier = jnp.where(odd, total[rows:], total[:rows])
        blocks, width = out.shape[0], out.shape[2]
        for block in range(blocks):
            out[block] = fourier[:, block * width : (block + 1) * width]


def load_tiles(parts, sems, place):
    copies = [pltpu.make_async_copy(source, target, sems.at[place + k]) for k, (source, target) in enumerate(parts)]
    for copy in copies:
        copy.start()
    return copies


def sweep_shells(d, f, h, ring_field, ring_eta, out, field, eta, force, result, sems, after_shell):
    components, shells, rows, count = d.shape
    inner = pl.ds(TILE, rows)
    lower = lax.axis_index("radial") == 0
    ring, nothing = jnp.where(lower, shells + 1, 0), jnp.where(lower, 0, shells + 1)
    halo = [
        pltpu.make_async_copy(source, field.at[c, ring, inner], sems.at[0, c])
        for c, source in enumerate(ring_field)
    ] + [pltpu.make_async_copy(ring_eta, eta.at[ring, inner], sems.at[0, components])]
    for copy in halo:
        copy.start()
    loads = []
    for s in range(shells):
        loads.append(
            [
                pltpu.make_async_copy(d.at[:, s], field.at[:, s + 1, inner], sems.at[s + 1, 0]),
                pltpu.make_async_copy(h.at[s], eta.at[s + 1, inner], sems.at[s + 1, 1]),
                pltpu.make_async_copy(f.at[:, s], force.at[:, s], sems.at[s + 1, 2]),
            ]
        )
        for copy in loads[s]:
            copy.start()
    zeros = jnp.zeros((rows, count), jnp.float32)
    for c in range(components):
        field[c, nothing, inner] = zeros
    eta[nothing, inner] = zeros
    for copy in halo + loads[0]:
        copy.wait()
    stores = []
    for s in range(shells):
        if s + 1 < shells:
            for copy in loads[s + 1]:
                copy.wait()

        def tile(step, _):
            start = pl.multiple_of(step * TILE, TILE)
            weights, factor = relax_weights(*around(eta, (), s + 1, start + TILE))
            for c in range(components):
                middle, others = around(field, (c,), s + 1, start + TILE)
                result[c, s, pl.ds(start, TILE)] = relax(
                    weights, factor, middle, others, force[c, s, pl.ds(start, TILE)]
                )
            return 0

        lax.fori_loop(0, rows // TILE, tile, 0)
        stores.append(pltpu.make_async_copy(result.at[:, s], out.at[:, s], sems.at[s + 1, 3]))
        stores[-1].start()
        after_shell(s)
    for copy in stores:
        copy.wait()


def set_edge(ref, lead, shells, rows, before, after):
    for s in range(shells):
        ref[(*lead, s + 1, TILE - 1)] = before(s)
        ref[(*lead, s + 1, rows + TILE)] = after(s)


def first_kernel(d, f, h, ring, before, after, out, ring_out, field, eta, force, result, edges, sems, ring_sems):
    components, shells, rows, _ = d.shape
    lower = lax.axis_index("radial") == 0
    row = lambda message, kind: lambda s: message[kind * shells + s]
    for c in range(components):
        set_edge(field, (c,), shells, rows, row(before, components + c), row(after, components + c))
    kind = 3 * components + 1
    set_edge(eta, (), shells, rows, row(before, kind), row(after, kind))
    for side, message in enumerate((before, after)):
        for place, k in enumerate([components + c for c in range(components)] + [kind]):
            low, high = message[pl.ds(k * shells, 1)], message[pl.ds((k + 1) * shells - 1, 1)]
            edges[pl.ds(side * (components + 1) + place, 1)] = jnp.where(lower, high, low)
    edge_copy = pltpu.make_async_copy(edges, ring_out.at[pl.ds(components * rows, edges.shape[0])], ring_sems.at[0])
    edge_copy.start()

    def ring_copies(s):
        return [
            pltpu.make_async_copy(result.at[c, s], ring_out.at[pl.ds(c * rows, rows)], ring_sems.at[c + 1])
            for c in range(components)
        ]

    def after_shell(s):
        if s in (0, shells - 1):

            @pl.when(lower if s else jnp.logical_not(lower))
            def _():
                for copy in ring_copies(s):
                    copy.start()

    sweep_shells(
        d, f, h, [ring.at[c] for c in range(components)], ring.at[components],
        out, field, eta, force, result, sems, after_shell,
    )
    for copy in ring_copies(0):
        copy.wait()
    edge_copy.wait()


def second_kernel(
    d, f, h, ring, ring_two, before, after, own_up, own_down, out, field, eta, force, result, edges, sems, ring_sems
):
    components, shells, rows, count = d.shape
    lower = lax.axis_index("radial") == 0
    lateral = lax.axis_index("lateral")
    fetch = pltpu.make_async_copy(ring_two.at[pl.ds(components * rows, edges.shape[0])], edges, ring_sems.at[0])
    fetch.start()
    kind = 3 * components + 1
    row = lambda message, kind: lambda s: message[kind * shells + s]
    set_edge(eta, (), shells, rows, row(before, kind), row(after, kind))
    fetch.wait()
    place = row_number((2 * shells, count))
    pair = lambda a, b, k: jnp.concatenate([a[k * shells : (k + 1) * shells], b[k * shells : (k + 1) * shells]], axis=0)

    def neighbours(inner, outer, part):
        middle = pair(before, after, inner)
        beyond = [edges[pl.ds(side * (components + 1) + part, 1)] for side in range(2)]
        beyond = jnp.where(place < shells, beyond[0], beyond[1])
        none = jnp.zeros_like(beyond)
        above = pltpu.roll(middle, 2 * shells - 1, 0)
        below = pltpu.roll(middle, 1, 0)
        return middle, [
            jnp.where(place % shells == shells - 1, jnp.where(lower, beyond, none), above),
            jnp.where(place % shells == 0, jnp.where(lower, none, beyond), below),
            pair(before, after, outer),
            pair(own_down, own_up, inner),
            west_of(middle),
            east_of(middle),
        ]

    weights, factor = relax_weights(*neighbours(kind, kind - 1, components))
    inside = jnp.where(place < shells, lateral, lax.axis_size("lateral") - 1 - lateral) > 0
    for c in range(components):
        middle, others = neighbours(components + c, c, c)
        edge = relax(weights, factor, middle, others, pair(before, after, 2 * components + c))
        edge = jnp.where(inside, edge, jnp.zeros_like(edge))
        set_edge(field, (c,), shells, rows, lambda s: edge[s], lambda s: edge[shells + s])
    sweep_shells(
        d, f, h, [ring_two.at[pl.ds(c * rows, rows)] for c in range(components)], ring.at[components],
        out, field, eta, force, result, sems, lambda s: None,
    )


def spectrum_kernel(orders, response, wave_high, wave_low, point_high, point_low, coefficients, out):
    radial = lax.axis_size("radial")
    bands, rows, width = orders.shape[0] // radial, orders.shape[1], orders.shape[2]
    fourier = jnp.concatenate([orders[band * radial + radial - 1] for band in range(bands)], axis=0)
    high, low = split(fourier)
    spectrum = dot(wave_high[...], high) + dot(wave_high[...], low) + dot(wave_low[...], high)
    coefficients[...] = spectrum
    own = response[:, :width]
    for place in range(1, radial):
        own = jnp.where(
            lax.axis_index("radial") == place, response[:, place * width : (place + 1) * width], own
        )
    high, low = split(own * spectrum)
    load = dot(point_high[...], high) + dot(point_high[...], low) + dot(point_low[...], high)
    for band in range(bands):
        for place in range(radial):
            out[band * radial + place] = load[band * rows : (band + 1) * rows]


def load_kernel(load, mask, high, low, out):
    blocks, rows, width = load.shape
    half = out.shape[1] // 2
    values = jnp.concatenate([load[block] for block in range(blocks)], axis=1)
    odd = lax.broadcasted_iota(jnp.int32, values.shape, 1) % 2 == 1
    near, far = split(jnp.concatenate([values, jnp.where(odd, -values, values)], axis=0))
    total = dot(jnp.concatenate([near, far], axis=0), high[...])
    total = total[: 2 * rows] + total[2 * rows :] + dot(near, low[...])
    out[:, :half] = total[:rows] * mask[:, :half].astype(jnp.float32)
    out[:, half:] = total[rows:] * mask[:, half:].astype(jnp.float32)


def tile_spec(block, *index):
    return pl.BlockSpec(block, lambda _: index)


def shards(initial_displacement, force, viscosity, layer_index, response, ocean_mask):
    components, shells, rows, count = initial_displacement.shape
    radial, lateral = lax.axis_size("radial"), lax.axis_size("lateral")
    f32 = functools.partial(jax.ShapeDtypeStruct, dtype=jnp.float32)
    scratch = lambda *shape: pltpu.VMEM(shape, jnp.float32)
    width = 2 * MODES // (lateral * radial)
    up = [(i, i + 1) for i in range(lateral - 1)]
    down = [(j, i) for i, j in up]
    top_only = lambda pairs: [(i * radial + radial - 1, j * radial + radial - 1) for i, j in pairs]

    last = rows // TILE - 1
    block4, block3 = (None, None, TILE, count), (None, TILE, count)
    row_specs = [
        [
            tile_spec(block4, 0, shells - 1, row, 0),
            tile_spec(block4, 0, shells - 2, row, 0),
            tile_spec(block4, 0, shells - 1, row, 0),
            tile_spec(block3, shells - 1, row, 0),
            tile_spec(block3, shells - 2, row, 0),
        ]
        for row in (0, last)
    ]
    tensors = (initial_displacement, initial_displacement, force, layer_index, layer_index)
    surface_up, surface_down = pl.pallas_call(
        surface_message_kernel,
        grid=(1,),
        in_specs=[SMEM, *row_specs[0], *row_specs[1]],
        out_specs=[VMEM, VMEM],
        out_shape=[f32((TILE, count))] * 2,
        compiler_params=params(8),
    )(viscosity, *tensors, *tensors)
    both = ("lateral", "radial")
    surface_before = lax.ppermute(surface_up, both, top_only(up))
    surface_after = lax.ppermute(surface_down, both, top_only(down))

    fields = -(-(3 * components + 2) * shells // TILE) * TILE
    edge_rows = scratch(components, shells, TILE, count)
    eta, own_up, own_down, ring = pl.pallas_call(
        main_message_kernel,
        in_specs=[SMEM, ANY, ANY, VMEM],
        out_specs=[VMEM, VMEM, VMEM, ANY],
        out_shape=[
            f32((shells, rows, count)),
            f32((fields, count)),
            f32((fields, count)),
            f32((components + 1, rows, count)),
        ],
        scratch_shapes=[edge_rows] * 4 + [pltpu.SemaphoreType.DMA((6,))],
        compiler_params=params(16),
    )(viscosity, initial_displacement, force, layer_index)
    swap = [(i, radial - 1 - i) for i in range(radial)]
    ring = lax.ppermute(ring, "radial", swap)
    before = lax.ppermute(own_up, "lateral", up)
    after = lax.ppermute(own_down, "lateral", down)

    high, low = longitude_tables(count, MODES)
    orders = pl.pallas_call(
        surface_kernel,
        in_specs=[ANY, ANY, ANY, VMEM, VMEM, VMEM, VMEM],
        out_specs=VMEM,
        out_shape=f32((lateral * radial, rows, width)),
        scratch_shapes=[
            scratch(4, rows + 2 * TILE, count),
            scratch(2, rows, count),
            scratch(4, rows + 2 * TILE, count),
            scratch(3, rows + 2 * TILE, count),
            pltpu.SemaphoreType.DMA((3,)),
        ],
        compiler_params=params(24),
    )(initial_displacement, force, eta, surface_before, surface_after, high, low)
    orders = lax.all_to_all(orders, both, split_axis=0, concat_axis=0, tiled=True)

    sweep_scratch = [
        scratch(components, shells + 2, rows + 2 * TILE, count),
        scratch(shells + 2, rows + 2 * TILE, count),
        scratch(components, shells, rows, count),
        scratch(components, shells, rows, count),
        scratch(2 * (components + 1), count),
        pltpu.SemaphoreType.DMA((shells + 1, 4)),
        pltpu.SemaphoreType.DMA((components + 1,)),
    ]
    cost = pl.CostEstimate(flops=200 * 3 * shells * rows * count, bytes_accessed=16 * MIB, transcendentals=0)
    smoothed, ring_two = pl.pallas_call(
        first_kernel,
        in_specs=[ANY, ANY, ANY, ANY, VMEM, VMEM],
        out_specs=[ANY, ANY],
        out_shape=[
            f32(initial_displacement.shape),
            f32((components * rows + 2 * (components + 1), count)),
        ],
        scratch_shapes=sweep_scratch,
        compiler_params=params(28),
        cost_estimate=cost,
    )(initial_displacement, force, eta, ring, before, after)
    ring_two = lax.ppermute(ring_two, "radial", swap)

    point_high, point_low = colatitude_tables(rows * lateral, MODES)
    coefficients, load = pl.pallas_call(
        spectrum_kernel,
        in_specs=[VMEM] * 6,
        out_specs=[VMEM, VMEM],
        out_shape=[f32((MODES, width)), f32((lateral * radial, rows, width))],
        compiler_params=params(16),
    )(orders, response, point_high.T.copy(), point_low.T.copy(), point_high, point_low)
    load = lax.all_to_all(load, both, split_axis=0, concat_axis=0, tiled=True)

    displacement = pl.pallas_call(
        second_kernel,
        in_specs=[ANY, ANY, ANY, ANY, ANY, VMEM, VMEM, VMEM, VMEM],
        out_specs=ANY,
        out_shape=f32(initial_displacement.shape),
        scratch_shapes=sweep_scratch,
        compiler_params=params(28),
        cost_estimate=cost,
    )(smoothed, force, eta, ring, ring_two, before, after, own_up, own_down)

    sea_load = pl.pallas_call(
        load_kernel,
        in_specs=[VMEM] * 4,
        out_specs=VMEM,
        out_shape=f32((rows, count)),
        compiler_params=params(20),
    )(load, ocean_mask, high.T.copy(), low.T.copy())
    return (displacement, coefficients, sea_load)


def solution(mesh):
    in_specs = (
        P("member", "radial", "lateral", None),
        P("member", "radial", "lateral", None),
        P("member"),
        P("radial", "lateral", None),
        P(None, "lateral"),
        P("lateral", None),
    )
    out_specs = (
        P("member", "radial", "lateral", None),
        P("member", ("lateral", "radial")),
        P("lateral", "member"),
    )
    return jax.shard_map(shards, mesh=mesh, in_specs=in_specs, out_specs=out_specs, check_vma=False)
```

profile of v0, /device:TPU:0, one launch (start us, length us, event | category | flops | bytes accessed | tf_op | source)
XLA Modules:
  0.0 115.3 jit_solution(14119409829212923641)
XLA Ops:
  0.6 1.9 %copy-done = f32[3,4,32,2048]{3,2,1,0:T(8,128)S(1)} copy-done((f32[3,4,32,2048]{3,2,1,0:T(8,128)S(1)}, f32[3,4,32,2048]{3,2,1,0:T(8,128)}, u32[]{:S(2)}) %copy-start) | copy-done | bytes 3145752
  2.5 1.9 %copy-done.2 = f32[3,4,32,2048]{3,2,1,0:T(8,128)S(1)} copy-done((f32[3,4,32,2048]{3,2,1,0:T(8,128)S(1)}, f32[3,4,32,2048]{3,2,1,0:T(8,128)}, u32[]{:S(2)}) %copy-start.2) | copy-done | bytes 3145752
  4.4 1.2 %copy-done.4 = s32[4,32,2048]{2,1,0:T(8,128)S(1)} copy-done((s32[4,32,2048]{2,1,0:T(8,128)S(1)}, s32[4,32,2048]{2,1,0:T(8,128)}, u32[]{:S(2)}) %copy-start.4) | copy-done | bytes 1048600
  6.3 2.1 %shard_map.157 = (f32[4,32,2048]{2,1,0:T(8,128)S(1)}, f32[48,2048]{1,0:T(8,128)S(1)}, f32[48,2048]{1,0:T(8,128)S(1)}, f32[4,32,2048]{2,1,0:T(8,128)S(1)}) custom-call(f32[16]{0:T(128)S(1)} %copy-done.33, f32[3,4,32,2048]{3,2,1,0:T(8,128)S(1)} %copy-done, f32[3,4,32,2048]{3,2,1,0:T(8,128)S(1)} %copy-done.2, s32[4,32,2048]{2,1,0:T(8,128)S(1)} %copy-done.4), custom_call_target="tpu_custom_call" | custom-call | tf_op jit(solution)/shard_map/pallas_call | solution.py:463
  9.0 4.5 %collective-permute-start.1 = (f32[48,2048]{1,0:T(8,128)S(1)}, f32[48,2048]{1,0:T(8,128)S(1)}, u32[]{:S(2)}, u32[]{:S(2)}) collective-permute-start(f32[48,2048]{1,0:T(8,128)S(1)} %get-tuple-element.15.own_up), channel_id=1, source_target_pairs={{0,2},{2,4},{4,6},{6,8},{8,10},{10,12},{12,14},{1,3},{3,5},{5,7},{... | collective-permute-start | bytes 1179656 | tf_op jit(solution)/shard_map/ppermute | solution.py:478
  14.2 1.3 %collective-permute-start.2 = (f32[48,2048]{1,0:T(8,128)S(1)}, f32[48,2048]{1,0:T(8,128)S(1)}, u32[]{:S(2)}, u32[]{:S(2)}) collective-permute-start(f32[48,2048]{1,0:T(8,128)S(1)} %get-tuple-element.16.own_down), channel_id=1, source_target_pairs={{2,0},{4,2},{6,4},{8,6},{10,8},{12,10},{14,12},{3,1},{5,3},{7,5},{... | collective-permute-start | bytes 1179656 | tf_op jit(solution)/shard_map/ppermute | solution.py:479
  16.3 14.6 %collective-permute-done.1.before = f32[48,2048]{1,0:T(8,128)S(1)} collective-permute-done((f32[48,2048]{1,0:T(8,128)S(1)}, f32[48,2048]{1,0:T(8,128)S(1)}, u32[]{:S(2)}, u32[]{:S(2)}) %collective-permute-start.1) | collective-permute-done | bytes 393248 | tf_op jit(solution)/shard_map/ppermute | solution.py:478
  30.9 6.7 %shard_map.158 = (f32[3,4,32,2048]{3,2,1,0:T(8,128)S(1)}, f32[104,2048]{1,0:T(8,128)}) custom-call(f32[3,4,32,2048]{3,2,1,0:T(8,128)S(1)} %copy-done.1, f32[3,4,32,2048]{3,2,1,0:T(8,128)S(1)} %copy-done.3, f32[4,32,2048]{2,1,0:T(8,128)S(1)} %get-tuple-element.13.h, f32[4,32,2048]{2,1,0:T(8,128)S(1)} %collective-permute-done.ring, ...), custom_call_target="tpu_custom_call" | custom-call | flops 157286400 | bytes 16777216 | tf_op jit(solution)/shard_map/pallas_call | solution.py:508
  41.8 1.8 %reshape.6 = f32[16,1,2048]{2,1,0:T(1,128)} reshape(f32[16,32,64]{2,1,0:T(8,128)} %copy-done.18) | data formatting | bytes 262144
  43.5 24.6 %all_to_all.10 = f32[16,1,2048]{2,1,0:T(1,128)} all-to-all(f32[16,1,2048]{2,1,0:T(1,128)} %reshape.6), channel_id=1, replica_groups=mesh['member'=2,'lateral'=8,'radial'=2] {'lateral','radial'}, dimensions={0} | all-to-all | bytes 262144 | tf_op jit(solution)/shard_map/all_to_all | solution.py:496
  68.6 2.4 %reduce = f32[16,2048]{1,0:T(8,128)} reduce(f32[16,1,2048]{2,1,0:T(1,128)} %all_to_all.10, f32[]{:T(128)} %broadcast), dimensions={1}, to_apply=%all_to_all.6.reduce_sub_computation | reduce | bytes 262148 | tf_op jit(solution)/shard_map/all_to_all | solution.py:496
  71.1 1.7 %reshape.7.orders = f32[16,32,64]{2,1,0:T(8,128)} reshape(f32[16,2048]{1,0:T(8,128)} %reduce) | data formatting | bytes 262144
  78.5 1.2 %shard_map.162 = (f32[512,64]{1,0:T(8,128)S(1)}, f32[16,32,64]{2,1,0:T(8,128)S(1)}) custom-call(f32[16,32,64]{2,1,0:T(8,128)S(1)} %copy-done.20, f32[512,128]{1,0:T(8,128)S(1)} %copy-done.28, bf16[512,256]{1,0:T(8,128)(2,1)S(1)} %copy-done.29, bf16[512,256]{1,0:T(8,128)(2,1)S(1)} %copy-done.30, bf16[256,512]{1,0:T(8,128)(2,1)S(1)} %copy-done.31, ...), custom_call_target="tpu_custom_call" | custom-call | tf_op jit(solution)/shard_map/pallas_call | solution.py:523
  81.1 1.8 %reshape.8 = f32[16,1,2048]{2,1,0:T(1,128)} reshape(f32[16,32,64]{2,1,0:T(8,128)} %copy-done.27) | data formatting | bytes 262144
  82.9 4.2 %all-to-all-start.1 = ((f32[16,1,2048]{2,1,0:T(1,128)}), f32[16,1,2048]{2,1,0:T(1,128)}, u32[]{:S(2)}, u32[]{:S(2)}) async-start(f32[16,1,2048]{2,1,0:T(1,128)} %reshape.8), calls=%async_computation.1 | async-start | bytes 262144 | tf_op jit(solution)/shard_map/all_to_all | solution.py:530
  87.0 1.7 %copy.17 = f32[512,64]{0,1:T(8,128)} copy(f32[512,64]{1,0:T(8,128)} %copy-done.26) | data formatting | bytes 262144
  88.8 6.2 %all-to-all-done.1 = f32[16,1,2048]{2,1,0:T(1,128)} async-done(((f32[16,1,2048]{2,1,0:T(1,128)}), f32[16,1,2048]{2,1,0:T(1,128)}, u32[]{:S(2)}, u32[]{:S(2)}) %all-to-all-start.1) | async-done | bytes 131104 | tf_op jit(solution)/shard_map/all_to_all | solution.py:530
  95.0 2.4 %reduce.1 = f32[16,2048]{1,0:T(8,128)} reduce(f32[16,1,2048]{2,1,0:T(1,128)} %all-to-all-done.1, f32[]{:T(128)} %broadcast), dimensions={1}, to_apply=%all_to_all.7.reduce_sub_computation | reduce | bytes 262148 | tf_op jit(solution)/shard_map/all_to_all | solution.py:530
  97.4 1.7 %reshape.9.load = f32[16,32,64]{2,1,0:T(8,128)} reshape(f32[16,2048]{1,0:T(8,128)} %reduce.1) | data formatting | bytes 262144
  99.1 1.6 %copy-done.12 = bf16[1024,1024]{1,0:T(8,128)(2,1)S(1)} copy-done((bf16[1024,1024]{1,0:T(8,128)(2,1)S(1)}, bf16[1024,1024]{1,0:T(8,128)(2,1)}, u32[]{:S(2)}) %copy-start.12) | copy-done | bytes 2097176
  100.7 1.6 %copy-done.13 = bf16[1024,1024]{1,0:T(8,128)(2,1)S(1)} copy-done((bf16[1024,1024]{1,0:T(8,128)(2,1)S(1)}, bf16[1024,1024]{1,0:T(8,128)(2,1)}, u32[]{:S(2)}) %copy-start.13) | copy-done | bytes 2097176
  104.2 1.5 %shard_map.163 = f32[32,2048]{1,0:T(8,128)} custom-call(f32[16,32,64]{2,1,0:T(8,128)S(1)} %copy-done.19, s32[32,2048]{1,0:T(8,128)S(1)} %copy-done.25, bf16[1024,1024]{1,0:T(8,128)(2,1)S(1)} %copy-done.12, bf16[1024,1024]{1,0:T(8,128)(2,1)S(1)} %copy-done.13), custom_call_target="tpu_custom_call" | custom-call | tf_op jit(solution)/shard_map/pallas_call | solution.py:542
  106.2 1.9 %copy-done.11 = f32[3,4,32,2048]{3,2,1,0:T(8,128)S(1)} copy-done((f32[3,4,32,2048]{3,2,1,0:T(8,128)S(1)}, f32[3,4,32,2048]{3,2,1,0:T(8,128)}, u32[]{:S(2)}) %copy-start.11) | copy-done | bytes 3145752
  108.1 7.3 %shard_map.159 = f32[3,4,32,2048]{3,2,1,0:T(8,128)} custom-call(f32[3,4,32,2048]{3,2,1,0:T(8,128)S(1)} %copy-done.11, f32[3,4,32,2048]{3,2,1,0:T(8,128)S(1)} %copy-done.3, f32[4,32,2048]{2,1,0:T(8,128)S(1)} %copy-done.7, f32[4,32,2048]{2,1,0:T(8,128)S(1)} %copy-done.9, f32[104,2048]{1,0:T(8,128)} %collective-permute-done.3.ring_two, ...), custom_call_target="tpu_custom_call" | custom-call | flops 157286400 | bytes 16777216 | tf_op jit(solution)/shard_map/pallas_call | solution.py:532
  (76 shorter events, 16.6 us)
Async XLA Ops:
  0.6 1.9 %copy-start = (f32[3,4,32,2048]{3,2,1,0:T(8,128)S(1)}, f32[3,4,32,2048]{3,2,1,0:T(8,128)}, u32[]{:S(2)}) copy-start(f32[3,4,32,2048]{3,2,1,0:T(8,128)} %d.5) | copy-start | bytes 9437188
  2.5 1.9 %copy-start.2 = (f32[3,4,32,2048]{3,2,1,0:T(8,128)S(1)}, f32[3,4,32,2048]{3,2,1,0:T(8,128)}, u32[]{:S(2)}) copy-start(f32[3,4,32,2048]{3,2,1,0:T(8,128)} %f.7) | copy-start | bytes 9437188
  6.3 24.6 %copy-start.1 = (f32[3,4,32,2048]{3,2,1,0:T(8,128)S(1)}, f32[3,4,32,2048]{3,2,1,0:T(8,128)}, u32[]{:S(2)}) copy-start(f32[3,4,32,2048]{3,2,1,0:T(8,128)} %d.5) | copy-start | bytes 9437188
  6.3 24.6 %copy-start.3 = (f32[3,4,32,2048]{3,2,1,0:T(8,128)S(1)}, f32[3,4,32,2048]{3,2,1,0:T(8,128)}, u32[]{:S(2)}) copy-start(f32[3,4,32,2048]{3,2,1,0:T(8,128)} %f.7) | copy-start | bytes 9437188
  8.4 32.4 %copy-start.6 = (f32[4,32,2048]{2,1,0:T(8,128)}, f32[4,32,2048]{2,1,0:T(8,128)S(1)}, u32[]{:S(2)}) copy-start(f32[4,32,2048]{2,1,0:T(8,128)S(1)} %get-tuple-element.13.h) | copy-start | bytes 3145732
  8.5 22.4 %collective-permute-start = (f32[4,32,2048]{2,1,0:T(8,128)S(1)}, f32[4,32,2048]{2,1,0:T(8,128)S(1)}, u32[]{:S(2)}, u32[]{:S(2)}) collective-permute-start(f32[4,32,2048]{2,1,0:T(8,128)S(1)} %get-tuple-element.14), channel_id=1, source_target_pairs={{0,1},{1,0},{2,3},{3,2},{4,5},{5,4},{6,7},{7,6},{8,9},{9,8},{10,11... | collective-permute-start | bytes 3145736 | tf_op jit(solution)/shard_map/ppermute | solution.py:477
  9.0 21.9 %collective-permute-start.1 = (f32[48,2048]{1,0:T(8,128)S(1)}, f32[48,2048]{1,0:T(8,128)S(1)}, u32[]{:S(2)}, u32[]{:S(2)}) collective-permute-start(f32[48,2048]{1,0:T(8,128)S(1)} %get-tuple-element.15.own_up), channel_id=1, source_target_pairs={{0,2},{2,4},{4,6},{6,8},{8,10},{10,12},{12,14},{1,3},{3,5},{5,7},{... | collective-permute-start | bytes 1179656 | tf_op jit(solution)/shard_map/ppermute | solution.py:478
  14.2 16.6 %collective-permute-start.2 = (f32[48,2048]{1,0:T(8,128)S(1)}, f32[48,2048]{1,0:T(8,128)S(1)}, u32[]{:S(2)}, u32[]{:S(2)}) collective-permute-start(f32[48,2048]{1,0:T(8,128)S(1)} %get-tuple-element.16.own_down), channel_id=1, source_target_pairs={{2,0},{4,2},{6,4},{8,6},{10,8},{12,10},{14,12},{3,1},{5,3},{7,5},{... | collective-permute-start | bytes 1179656 | tf_op jit(solution)/shard_map/ppermute | solution.py:479
  30.9 6.8 %copy-start.16 = (f32[48,2048]{1,0:T(8,128)}, f32[48,2048]{1,0:T(8,128)S(1)}, u32[]{:S(2)}) copy-start(f32[48,2048]{1,0:T(8,128)S(1)} %collective-permute-done.2.after) | copy-start | bytes 1179652
  30.9 6.8 %copy-start.8 = (f32[4,32,2048]{2,1,0:T(8,128)}, f32[4,32,2048]{2,1,0:T(8,128)S(1)}, u32[]{:S(2)}) copy-start(f32[4,32,2048]{2,1,0:T(8,128)S(1)} %collective-permute-done.ring) | copy-start | bytes 3145732
  30.9 6.9 %copy-start.5 = (s32[4,32,2048]{2,1,0:T(8,128)S(1)}, s32[4,32,2048]{2,1,0:T(8,128)}, u32[]{:S(2)}) copy-start(s32[4,32,2048]{2,1,0:T(8,128)} %i6_end.1) | copy-start | bytes 3145732
  30.9 6.9 %copy-start.34 = (f32[16]{0:T(128)S(1)}, f32[16]{0:T(128)}, u32[]{:S(2)}) copy-start(f32[16]{0:T(128)} %viscosity.3) | copy-start | bytes 196
  37.6 1.7 %copy-start.10 = (f32[3,4,32,2048]{3,2,1,0:T(8,128)}, f32[3,4,32,2048]{3,2,1,0:T(8,128)S(1)}, u32[]{:S(2)}) copy-start(f32[3,4,32,2048]{3,2,1,0:T(8,128)S(1)} %get-tuple-element.17.d) | copy-start | bytes 9437188
  37.7 3.2 %copy-start.14 = (bf16[1024,1024]{1,0:T(8,128)(2,1)S(1)}, bf16[1024,1024]{1,0:T(8,128)(2,1)}, u32[]{:S(2)}) copy-start(bf16[1024,1024]{1,0:T(8,128)(2,1)} %constant.16.clone.high) | copy-start | bytes 6291460
  37.7 3.3 %copy-start.15 = (bf16[1024,1024]{1,0:T(8,128)(2,1)S(1)}, bf16[1024,1024]{1,0:T(8,128)(2,1)}, u32[]{:S(2)}) copy-start(bf16[1024,1024]{1,0:T(8,128)(2,1)} %constant.17.clone.low) | copy-start | bytes 6291460
  37.7 68.1 %collective-permute-start.3 = (f32[104,2048]{1,0:T(8,128)}, f32[104,2048]{1,0:T(8,128)}, u32[]{:S(2)}, u32[]{:S(2)}) collective-permute-start(f32[104,2048]{1,0:T(8,128)} %get-tuple-element.18), channel_id=1, source_target_pairs={{0,1},{1,0},{2,3},{3,2},{4,5},{5,4},{6,7},{7,6},{8,9},{9,8},{10,11... | collective-permute-start | bytes 2555912 | tf_op jit(solution)/shard_map/ppermute | solution.py:520
  39.3 1.5 %collective-permute-start.4 = (f32[8,2048]{1,0:T(8,128)S(1)}, f32[8,2048]{1,0:T(8,128)S(1)}, u32[]{:S(2)}, u32[]{:S(2)}) collective-permute-start(f32[8,2048]{1,0:T(8,128)S(1)} %get-tuple-element.19), channel_id=1, source_target_pairs={{1,3},{3,5},{5,7},{7,9},{9,11},{11,13},{13,15},{17,19},{19,21},{21... | collective-permute-start | bytes 196616 | tf_op jit(solution)/shard_map/ppermute | solution.py:458
  40.1 0.7 collective-permute-start.5
  82.9 12.1 %all-to-all-start.1 = ((f32[16,1,2048]{2,1,0:T(1,128)}), f32[16,1,2048]{2,1,0:T(1,128)}, u32[]{:S(2)}, u32[]{:S(2)}) async-start(f32[16,1,2048]{2,1,0:T(1,128)} %reshape.8), calls=%async_computation.1 | async-start | bytes 262144 | tf_op jit(solution)/shard_map/all_to_all | solution.py:530
  99.1 1.6 %copy-start.12 = (bf16[1024,1024]{1,0:T(8,128)(2,1)S(1)}, bf16[1024,1024]{1,0:T(8,128)(2,1)}, u32[]{:S(2)}) copy-start(bf16[1024,1024]{1,0:T(8,128)(2,1)} %constant.22.clone.high) | copy-start | bytes 6291460
  104.2 1.6 %copy-start.17 = (f32[48,2048]{1,0:T(8,128)S(1)}, f32[48,2048]{1,0:T(8,128)}, u32[]{:S(2)}) copy-start(f32[48,2048]{1,0:T(8,128)} %copy-done.16) | copy-start | bytes 1179652
  104.2 1.8 %copy-start.22 = (f32[48,2048]{1,0:T(8,128)S(1)}, f32[48,2048]{1,0:T(8,128)}, u32[]{:S(2)}) copy-start(f32[48,2048]{1,0:T(8,128)} %copy-done.21) | copy-start | bytes 1179652
  104.2 1.9 %copy-start.24 = (f32[48,2048]{1,0:T(8,128)S(1)}, f32[48,2048]{1,0:T(8,128)}, u32[]{:S(2)}) copy-start(f32[48,2048]{1,0:T(8,128)} %copy-done.23) | copy-start | bytes 1179652
  106.2 1.9 %copy-start.11 = (f32[3,4,32,2048]{3,2,1,0:T(8,128)S(1)}, f32[3,4,32,2048]{3,2,1,0:T(8,128)}, u32[]{:S(2)}) copy-start(f32[3,4,32,2048]{3,2,1,0:T(8,128)} %copy-done.10) | copy-start | bytes 9437188
  (18 other events, 17.8 us)
where the time goes:
time: 116 us; the launch traced here: 115 us
  local copies, waits for them, and re-layouts  32.5 us (28%)
  blocking collectives  24.6 us (21%)
  waiting for transfers between devices  20.8 us (18%)
  Pallas kernels  19.7 us (17%)
  starting transfers between devices  11.9 us (10%)
  other arithmetic  4.87 us (4%)
    unnamed x75, local copies, waits for them, and re-layouts  32 us
    all_to_all x1, blocking collectives, shards(): lax.all_to_all(orders, both, split_axis=0, concat_axis=0, tiled=True)  24.6 us
    ppermute x1, waiting for transfers between devices, shards(): before = lax.ppermute(own_up, 'lateral', up)  14.6 us
    pallas_call x1, Pallas kernels, shards(): pl.pallas_call(second_kernel, in_specs=[ANY, ANY, ANY, ANY, ANY, VMEM, VM...  7.26 us
    pallas_call x1, Pallas kernels, shards(): pl.pallas_call(first_kernel, in_specs=[ANY, ANY, ANY, ANY, VMEM, VMEM], o...  6.71 us
    all_to_all x1, waiting for transfers between devices, shards(): load = lax.all_to_all(load, both, split_axis=0, concat_axis=0, tiled=True)  6.22 us
    ppermute x1, starting transfers between devices, shards(): before = lax.ppermute(own_up, 'lateral', up)  4.46 us
    all_to_all x1, starting transfers between devices, shards(): load = lax.all_to_all(load, both, split_axis=0, concat_axis=0, tiled=True)  4.17 us
  transfers between devices with their start and end apart: 7, of which 2 were waited for; matrix products, arithmetic and copies ran while one was open for 12% of the time, Pallas kernels for 3%

commit v1 on v0

v1 whole, which is shorter than its diff:
```python
import functools
import math

import jax
import jax.numpy as jnp
import ml_dtypes
import numpy as np
from jax import lax
from jax.experimental import pallas as pl
from jax.experimental.pallas import tpu as pltpu
from jax.sharding import PartitionSpec as P

MODES = 512
RELAXATION = 0.8
TILE = 8
MIB = 1 << 20
ANY = pl.BlockSpec(memory_space=pl.ANY)
HBM = pl.BlockSpec(memory_space=pltpu.HBM)
SMEM = pl.BlockSpec(memory_space=pltpu.SMEM)
VMEM = pl.BlockSpec(memory_space=pltpu.VMEM)


def params(mib):
    return pltpu.CompilerParams(vmem_limit_bytes=mib * MIB)


def halves(table):
    high = table.astype(ml_dtypes.bfloat16)
    low = (table - high.astype(np.float64)).astype(ml_dtypes.bfloat16)
    return high, low


@functools.lru_cache
def longitude_tables(count, modes):
    points = np.arange(count // 2, dtype=np.int64)[:, None]
    orders = np.arange(modes, dtype=np.int64)[None, :]
    angle = (2.0 * math.pi / count) * (points * orders % count)
    table = np.concatenate([np.cos(angle), np.sin(angle)], axis=1) * math.sqrt(2.0 / count)
    return halves(table)


@functools.lru_cache
def colatitude_tables(count, modes):
    points = np.arange(count, dtype=np.int64)[:, None]
    waves = np.arange(modes, dtype=np.int64)[None, :]
    phase = waves * (2 * points + 1) % (4 * count)
    return halves(np.cos(math.pi / (2 * count) * phase) * math.sqrt(2.0 / count))


def split(values):
    high = values.astype(jnp.bfloat16)
    return high, (values - high.astype(jnp.float32)).astype(jnp.bfloat16)


def dot(a, b):
    return jnp.dot(a, b, preferred_element_type=jnp.float32)


def pack(block):
    rows, width = block.shape
    groups = max(1, 128 // width)
    rows //= groups
    return jnp.concatenate([block[k * rows : (k + 1) * rows] for k in range(groups)], axis=1)


def unpack(block, width):
    groups = max(1, 128 // width)
    return jnp.concatenate([block[:, k * width : (k + 1) * width] for k in range(groups)], axis=0)


def half_viscosity(index, viscosity_ref):
    values = [0.5 * viscosity_ref[k] for k in range(viscosity_ref.shape[0])]
    bit = 1
    while len(values) > 1:
        odd = (index & bit) != 0
        if len(values) % 2:
            values.append(values[-1])
        values = [jnp.where(odd, b, a) for a, b in zip(values[::2], values[1::2])]
        bit *= 2
    return values[0]


def row_number(shape):
    return lax.broadcasted_iota(jnp.int32, shape, 0)


def north_of(above, middle):
    return pltpu.roll(jnp.where(row_number(middle.shape) == TILE - 1, above, middle), 1, 0)


def south_of(below, middle):
    return pltpu.roll(jnp.where(row_number(middle.shape) == 0, below, middle), TILE - 1, 0)


def east_of(values):
    return pltpu.roll(values, values.shape[-1] - 1, values.ndim - 1)


def west_of(values):
    return pltpu.roll(values, 1, values.ndim - 1)


def relax_weights(middle, others):
    weights = [middle + other for other in others]
    diagonal = 1.0 + functools.reduce(jnp.add, weights)
    return weights, RELAXATION / diagonal


def relax(weights, factor, middle, others, force):
    total = force
    for weight, other in zip(weights, others):
        total = total + weight * other
    return (1.0 - RELAXATION) * middle + factor * total


def around(ref, lead, shell, start):
    rows = lambda first: pl.ds(pl.multiple_of(first, TILE), TILE)
    middle = ref[(*lead, shell, rows(start))]
    return middle, [
        ref[(*lead, shell + 1, rows(start))],
        ref[(*lead, shell - 1, rows(start))],
        south_of(ref[(*lead, shell, rows(start + TILE))], middle),
        north_of(ref[(*lead, shell, rows(start - TILE))], middle),
        west_of(middle),
        east_of(middle),
    ]


def surface_message_kernel(viscosity, d, f, index, up, down, fields, forces, layers, sems):
    shells, rows = index.shape[0], index.shape[1]
    top, pair = shells - 1, pl.ds(shells - 2, 2)
    copies = []
    for side, start in enumerate((0, rows - TILE)):
        part = pl.ds(start, TILE)
        copies += [
            pltpu.make_async_copy(d.at[0, pair, part], fields.at[side], sems.at[side, 0]),
            pltpu.make_async_copy(f.at[0, top, part], forces.at[side], sems.at[side, 1]),
            pltpu.make_async_copy(index.at[pair, part], layers.at[side], sems.at[side, 2]),
        ]
    for copy in copies:
        copy.start()
    for copy in copies:
        copy.wait()
    for side, message, near, far in ((0, down, 0, 1), (1, up, TILE - 1, TILE - 2)):
        below, surface = [half_viscosity(layers[side, k], viscosity) for k in range(2)]
        message[0] = fields[side, 1, far]
        message[1] = fields[side, 1, near]
        message[2] = fields[side, 0, near]
        message[3] = surface[far]
        message[4] = surface[near]
        message[5] = below[near]
        message[6] = forces[side, near]
        message[7] = jnp.zeros_like(below[near])


def main_message_kernel(viscosity, d, index_from, h, up, down, ring, tops, ends, index, sems):
    shells, rows = h.shape[0], h.shape[1]
    components = d.shape[0]
    shell = jnp.where(lax.axis_index("radial") == 0, shells - 1, 0)
    copies = [
        pltpu.make_async_copy(d.at[:, :, pl.ds(0, TILE)], tops, sems.at[0]),
        pltpu.make_async_copy(d.at[:, :, pl.ds(rows - TILE, TILE)], ends, sems.at[1]),
        pltpu.make_async_copy(d.at[:, shell], ring.at[pl.ds(0, components)], sems.at[2]),
    ]
    layers = [pltpu.make_async_copy(index_from.at[s], index.at[s], sems.at[4 + s]) for s in range(shells)]
    for copy in layers + copies:
        copy.start()
    for s in range(shells):
        layers[s].wait()

        def lookup(step, _):
            part = pl.ds(pl.multiple_of(step * TILE, TILE), TILE)
            h[s, part] = half_viscosity(index[s, part], viscosity)
            return 0

        lax.fori_loop(0, rows // TILE, lookup, 0)
    eta_copy = pltpu.make_async_copy(h.at[shell], ring.at[components], sems.at[3])
    eta_copy.start()
    for copy in copies[:2]:
        copy.wait()
    for message, row, place, a in ((down, 0, 0, tops), (up, rows - 1, TILE - 1, ends)):
        for s in range(shells):
            for c in range(components):
                message[c * shells + s] = a[c, s, place]
            message[components * shells + s] = h[s, row]
    copies[2].wait()
    eta_copy.wait()


def surface_kernel(d, f, h, before, after, high_from, low_from, out, field, force, eta, smoothed, high, low, sems):
    shells, rows, count = h.shape
    top = lax.axis_size("radial") - 1

    @pl.when(lax.axis_index("radial") == top)
    def _():
        inner = pl.ds(TILE, rows)
        copies = [
            pltpu.make_async_copy(d.at[0, pl.ds(shells - 3, 3)], field.at[pl.ds(0, 3), inner], sems.at[0]),
            pltpu.make_async_copy(h.at[pl.ds(shells - 3, 3)], eta.at[pl.ds(0, 3), inner], sems.at[1]),
            pltpu.make_async_copy(f.at[0, pl.ds(shells - 2, 2)], force, sems.at[2]),
        ]
        tables = [
            pltpu.make_async_copy(high_from, high, sems.at[3]),
            pltpu.make_async_copy(low_from, low, sems.at[4]),
        ]
        for copy in copies + tables:
            copy.start()
        zeros = jnp.zeros((rows, count), jnp.float32)
        field[3, inner] = zeros
        eta[3, inner] = zeros
        smoothed[2, inner] = zeros
        for message, place in ((before, TILE - 1), (after, rows + TILE)):
            field[2, place] = message[1]
            field[1, place] = message[2]
            eta[2, place] = message[4]
            eta[1, place] = message[5]
        for copy in copies:
            copy.wait()
        lateral = lax.axis_index("lateral")
        inside = (lateral > 0, lateral < lax.axis_size("lateral") - 1)
        for message, own, place, there in (
            (before, TILE, TILE - 1, inside[0]),
            (after, rows + TILE - 1, rows + TILE, inside[1]),
        ):
            row = lambda k: message[pl.ds(k, 1)]
            own_row = lambda ref: ref[2, pl.ds(own, 1)]
            none = jnp.zeros((1, count), jnp.float32)
            weights, factor = relax_weights(
                row(4), [none, row(5), row(3), own_row(eta), west_of(row(4)), east_of(row(4))]
            )
            edge = relax(
                weights,
                factor,
                row(1),
                [none, row(2), row(0), own_row(field), west_of(row(1)), east_of(row(1))],
                row(6),
            )
            smoothed[1, pl.ds(place, 1)] = jnp.where(there, edge, none)

        def first(step, _):
            start = pl.multiple_of(step * TILE, TILE)
            for s in (1, 2):
                weights, factor = relax_weights(*around(eta, (), s, start + TILE))
                middle, others = around(field, (), s, start + TILE)
                smoothed[s - 1, pl.ds(start + TILE, TILE)] = relax(
                    weights, factor, middle, others, force[s - 1, pl.ds(start, TILE)]
                )
            return 0

        lax.fori_loop(0, rows // TILE, first, 0)

        def second(step, _):
            start = pl.multiple_of(step * TILE, TILE)
            weights, factor = relax_weights(*around(eta, (), 2, start + TILE))
            middle, others = around(smoothed, (), 1, start + TILE)
            field[0, pl.ds(start, TILE)] = relax(weights, factor, middle, others, force[1, pl.ds(start, TILE)])
            return 0

        lax.fori_loop(0, rows // TILE, second, 0)
        half = count // 2
        left, right = field[0, pl.ds(0, rows), :half], field[0, pl.ds(0, rows), half:]
        near, far = split(jnp.concatenate([left + right, left - right], axis=0))
        for copy in tables:
            copy.wait()
        total = dot(jnp.concatenate([near, far], axis=0), high[...])
        total = total[: 2 * rows] + total[2 * rows :] + dot(near, low[...])
        odd = lax.broadcasted_iota(jnp.int32, (rows, total.shape[1]), 1) % 2 == 1
        fourier = jnp.where(odd, total[rows:], total[:rows])
        blocks = out.shape[0]
        width = fourier.shape[1] // blocks
        for block in range(blocks):
            out[block] = pack(fourier[:, block * width : (block + 1) * width])


def sweep_shells(d, f, h, ring_field, ring_eta, out, field, eta, force, result, sems, after_shell):
    components, shells, rows, count = d.shape
    inner = pl.ds(TILE, rows)
    lower = lax.axis_index("radial") == 0
    ring, nothing = jnp.where(lower, shells + 1, 0), jnp.where(lower, 0, shells + 1)
    halo = [
        pltpu.make_async_copy(source, field.at[c, ring, inner], sems.at[0, c])
        for c, source in enumerate(ring_field)
    ] + [pltpu.make_async_copy(ring_eta, eta.at[ring, inner], sems.at[0, components])]
    for copy in halo:
        copy.start()
    loads = []
    for s in range(shells):
        loads.append(
            [
                pltpu.make_async_copy(d.at[:, s], field.at[:, s + 1, inner], sems.at[s + 1, 0]),
                pltpu.make_async_copy(h.at[s], eta.at[s + 1, inner], sems.at[s + 1, 1]),
                pltpu.make_async_copy(f.at[:, s], force.at[:, s], sems.at[s + 1, 2]),
            ]
        )
        for copy in loads[s]:
            copy.start()
    zeros = jnp.zeros((rows, count), jnp.float32)
    for c in range(components):
        field[c, nothing, inner] = zeros
    eta[nothing, inner] = zeros
    for copy in halo + loads[0]:
        copy.wait()
    stores = []
    for s in range(shells):
        if s + 1 < shells:
            for copy in loads[s + 1]:
                copy.wait()

        def tile(step, _):
            start = pl.multiple_of(step * TILE, TILE)
            weights, factor = relax_weights(*around(eta, (), s + 1, start + TILE))
            for c in range(components):
                middle, others = around(field, (c,), s + 1, start + TILE)
                result[c, s, pl.ds(start, TILE)] = relax(
                    weights, factor, middle, others, force[c, s, pl.ds(start, TILE)]
                )
            return 0

        lax.fori_loop(0, rows // TILE, tile, 0)
        stores.append(pltpu.make_async_copy(result.at[:, s], out.at[:, s], sems.at[s + 1, 3]))
        stores[-1].start()
        after_shell(s)
    for copy in stores:
        copy.wait()


def set_edge(ref, lead, shells, rows, before, after):
    for s in range(shells):
        ref[(*lead, s + 1, TILE - 1)] = before(s)
        ref[(*lead, s + 1, rows + TILE)] = after(s)


def first_kernel(d, f, h, ring, before, after, *refs):
    components, shells, rows, _ = d.shape
    staged = (len(refs) - 11) // 2
    sources, refs = refs[:staged], refs[staged:]
    out, ring_out, up, down, *targets = refs[: 4 + staged]
    field, eta, force, result, sems, ring_sems, stage_sems = refs[4 + staged :]
    stages = [
        pltpu.make_async_copy(source, target, stage_sems.at[k]) for k, (source, target) in enumerate(zip(sources, targets))
    ]
    lower = lax.axis_index("radial") == 0
    row = lambda message, kind: lambda s: message[kind * shells + s]
    for c in range(components):
        set_edge(field, (c,), shells, rows, row(before, c), row(after, c))
    set_edge(eta, (), shells, rows, row(before, components), row(after, components))

    def ring_copies(s):
        return [pltpu.make_async_copy(result.at[:, s], ring_out, ring_sems.at[0])]

    def after_shell(s):
        if s == 0:
            for copy in stages:
                copy.start()
        for c in range(components):
            down[c * shells + s] = result[c, s, 0]
            up[c * shells + s] = result[c, s, rows - 1]
        if s in (0, shells - 1):

            @pl.when(lower if s else jnp.logical_not(lower))
            def _():
                for copy in ring_copies(s):
                    copy.start()

    sweep_shells(
        d, f, h, [ring.at[c] for c in range(components)], ring.at[components],
        out, field, eta, force, result, sems, after_shell,
    )
    for copy in ring_copies(0) + stages:
        copy.wait()


def second_kernel(
    d, f, h, ring, ring_two, eta_before, eta_after, before, after, out, field, eta, force, result, sems
):
    components, shells, rows, _ = d.shape
    row = lambda message, kind: lambda s: message[kind * shells + s]
    for c in range(components):
        set_edge(field, (c,), shells, rows, row(before, c), row(after, c))
    set_edge(eta, (), shells, rows, row(eta_before, components), row(eta_after, components))
    sweep_shells(
        d, f, h, [ring_two.at[c] for c in range(components)], ring.at[components],
        out, field, eta, force, result, sems, lambda s: None,
    )


def spectrum_kernel(orders, response, wave_high, wave_low, point_high, point_low, coefficients, out):
    radial = lax.axis_size("radial")
    width = coefficients.shape[0]
    bands, rows = orders.shape[0] // radial, point_high.shape[0] * radial // orders.shape[0]
    fourier = jnp.concatenate([unpack(orders[band * radial + radial - 1], width) for band in range(bands)], axis=0)
    high, low = split(fourier)
    spectrum = dot(wave_high[...], high) + dot(wave_high[...], low) + dot(wave_low[...], high)
    coefficients[...] = spectrum.T
    own = response[:, :width]
    for place in range(1, radial):
        own = jnp.where(
            lax.axis_index("radial") == place, response[:, place * width : (place + 1) * width], own
        )
    high, low = split(own * spectrum)
    load = dot(point_high[...], high) + dot(point_high[...], low) + dot(point_low[...], high)
    for band in range(bands):
        block = pack(load[band * rows : (band + 1) * rows])
        for place in range(radial):
            out[band * radial + place] = block


def load_kernel(load, mask, high, low, out):
    blocks, rows = load.shape[0], out.shape[0]
    half, width = out.shape[1] // 2, high.shape[0] // blocks
    values = jnp.concatenate([unpack(load[block], width) for block in range(blocks)], axis=1)
    odd = lax.broadcasted_iota(jnp.int32, values.shape, 1) % 2 == 1
    near, far = split(jnp.concatenate([values, jnp.where(odd, -values, values)], axis=0))
    total = dot(jnp.concatenate([near, far], axis=0), high[...])
    total = total[: 2 * rows] + total[2 * rows :] + dot(near, low[...])
    out[:, :half] = total[:rows] * mask[:, :half].astype(jnp.float32)
    out[:, half:] = total[rows:] * mask[:, half:].astype(jnp.float32)


def cost(microseconds):
    return pl.CostEstimate(flops=0, bytes_accessed=3_000_000 * microseconds, transcendentals=0)


def hbm(values):
    return pltpu.with_memory_space_constraint(values, pltpu.HBM)


def shards(initial_displacement, force, viscosity, layer_index, response, ocean_mask):
    components, shells, rows, count = initial_displacement.shape
    radial, lateral = lax.axis_size("radial"), lax.axis_size("lateral")
    f32 = functools.partial(jax.ShapeDtypeStruct, dtype=jnp.float32)
    scratch = lambda *shape: pltpu.VMEM(shape, jnp.float32)
    width = 2 * MODES // (lateral * radial)
    up = [(i, i + 1) for i in range(lateral - 1)]
    down = [(j, i) for i, j in up]
    top_only = lambda pairs: [(i * radial + radial - 1, j * radial + radial - 1) for i, j in pairs]

    tensors = [hbm(a) for a in (initial_displacement, force, layer_index)]
    surface_up, surface_down = pl.pallas_call(
        surface_message_kernel,
        in_specs=[SMEM, HBM, HBM, HBM],
        out_specs=[VMEM, VMEM],
        out_shape=[f32((TILE, count))] * 2,
        scratch_shapes=[
            scratch(2, 2, TILE, count),
            scratch(2, TILE, count),
            pltpu.VMEM((2, 2, TILE, count), jnp.int32),
            pltpu.SemaphoreType.DMA((2, 3)),
        ],
        compiler_params=params(8),
        cost_estimate=cost(2),
    )(viscosity, *tensors)
    both = ("lateral", "radial")
    surface_before = lax.ppermute(surface_up, both, top_only(up))
    surface_after = lax.ppermute(surface_down, both, top_only(down))

    fields = -(-(components + 1) * shells // TILE) * TILE
    message = f32((fields, count))
    edge_rows = scratch(components, shells, TILE, count)
    later, _ = lax.optimization_barrier((viscosity, surface_up))
    eta, own_up, own_down, ring = pl.pallas_call(
        main_message_kernel,
        in_specs=[SMEM, HBM, HBM],
        out_specs=[VMEM, VMEM, VMEM, ANY],
        out_shape=[f32((shells, rows, count)), message, message, f32((components + 1, rows, count))],
        scratch_shapes=[
            edge_rows,
            edge_rows,
            pltpu.VMEM(layer_index.shape, jnp.int32),
            pltpu.SemaphoreType.DMA((4 + shells,)),
        ],
        compiler_params=params(16),
        cost_estimate=cost(4),
    )(later, tensors[0], tensors[2])
    swap = [(i, radial - 1 - i) for i in range(radial)]
    ring = lax.ppermute(ring, "radial", swap)
    before = lax.ppermute(own_up, "lateral", up)
    after = lax.ppermute(own_down, "lateral", down)

    high, low = longitude_tables(count, MODES)
    table = pltpu.VMEM(high.shape, jnp.bfloat16)
    packed = (lateral * radial, rows * width // max(128, width), max(128, width))
    orders = pl.pallas_call(
        surface_kernel,
        in_specs=[HBM, HBM, ANY, VMEM, VMEM, HBM, HBM],
        out_specs=VMEM,
        out_shape=f32(packed),
        scratch_shapes=[
            scratch(4, rows + 2 * TILE, count),
            scratch(2, rows, count),
            scratch(4, rows + 2 * TILE, count),
            scratch(3, rows + 2 * TILE, count),
            table,
            table,
            pltpu.SemaphoreType.DMA((5,)),
        ],
        compiler_params=params(24),
        cost_estimate=cost(6),
    )(*tensors[:2], eta, surface_before, surface_after, hbm(jnp.asarray(high)), hbm(jnp.asarray(low)))
    later, _ = lax.optimization_barrier((eta, orders))
    orders = lax.all_to_all(orders, both, split_axis=0, concat_axis=0, tiled=True)

    sweep_scratch = [
        scratch(components, shells + 2, rows + 2 * TILE, count),
        scratch(shells + 2, rows + 2 * TILE, count),
        scratch(components, shells, rows, count),
        scratch(components, shells, rows, count),
        pltpu.SemaphoreType.DMA((shells + 1, 4)),
    ]
    point_high, point_low = colatitude_tables(rows * lateral, MODES)
    stages = [
        jnp.asarray(a)
        for a in (point_high.T.copy(), point_low.T.copy(), point_high, point_low, high.T.copy(), low.T.copy())
    ] + [response, ocean_mask]
    fields = -(-components * shells // TILE) * TILE
    message = f32((fields, count))
    smoothed, ring_two, next_up, next_down, *staged = pl.pallas_call(
        first_kernel,
        in_specs=[HBM, HBM, ANY, ANY, VMEM, VMEM] + [HBM] * len(stages),
        out_specs=[ANY, ANY, VMEM, VMEM] + [VMEM] * len(stages),
        out_shape=[f32(initial_displacement.shape), f32((components, rows, count)), message, message]
        + [jax.ShapeDtypeStruct(a.shape, a.dtype) for a in stages],
        scratch_shapes=sweep_scratch
        + [pltpu.SemaphoreType.DMA((1,)), pltpu.SemaphoreType.DMA((len(stages),))],
        compiler_params=params(28),
        cost_estimate=cost(10),
    )(*tensors[:2], later, ring, before, after, *(hbm(a) for a in stages))
    ring_two = lax.ppermute(ring_two, "radial", swap)
    next_before = lax.ppermute(next_up, "lateral", up)
    next_after = lax.ppermute(next_down, "lateral", down)

    *points, high, low, response, ocean_mask = staged
    coefficients, load = pl.pallas_call(
        spectrum_kernel,
        in_specs=[VMEM] * 6,
        out_specs=[VMEM, VMEM],
        out_shape=[f32((width, MODES)), f32(packed)],
        compiler_params=params(16),
        cost_estimate=cost(2),
    )(orders, response, *points)
    later, _ = lax.optimization_barrier((eta, load))
    load = lax.all_to_all(load, both, split_axis=0, concat_axis=0, tiled=True)

    displacement = pl.pallas_call(
        second_kernel,
        in_specs=[ANY, HBM, ANY, ANY, ANY, VMEM, VMEM, VMEM, VMEM],
        out_specs=HBM,
        out_shape=pltpu.HBM(initial_displacement.shape, jnp.float32),
        scratch_shapes=sweep_scratch,
        compiler_params=params(28),
        cost_estimate=cost(10),
    )(smoothed, tensors[1], later, ring, ring_two, before, after, next_before, next_after)

    sea_load = pl.pallas_call(
        load_kernel,
        in_specs=[VMEM] * 4,
        out_specs=VMEM,
        out_shape=f32((rows, count)),
        compiler_params=params(20),
        cost_estimate=cost(3),
    )(load, ocean_mask, high, low)
    return (displacement, coefficients.T, sea_load)


def solution(mesh):
    in_specs = (
        P("member", "radial", "lateral", None),
        P("member", "radial", "lateral", None),
        P("member"),
        P("radial", "lateral", None),
        P(None, "lateral"),
        P("lateral", None),
    )
    out_specs = (
        P("member", "radial", "lateral", None),
        P("member", ("lateral", "radial")),
        P("lateral", "member"),
    )
    return jax.shard_map(shards, mesh=mesh, in_specs=in_specs, out_specs=out_specs, check_vma=False)
```

time: 116 us -> 77 us (0.66)
  local copies, waits for them, and re-layouts: 32.5 us -> 9.19 us
  waiting for transfers between devices: 20.8 us -> 7.71 us
  blocking collectives: 24.6 us -> 15.1 us
  starting transfers between devices: 11.9 us -> 20.6 us
  other arithmetic: 4.87 us -> 0 us
  Pallas kernels: 19.7 us -> 23.1 us
    unnamed x75 -> x22, local copies, waits for them, and re-layouts: 32 us -> 9.19 us
    ppermute x1, waiting for transfers between devices: 14.6 us -> 0.64 us  [shards(): before = lax.ppermute(own_up, 'lateral', up)]
    all_to_all x1, blocking collectives: 24.6 us -> 15.1 us  [shards(): lax.all_to_all(orders, both, split_axis=0, concat_axis=0, tiled=True)]
    ppermute x0 -> x2, starting transfers between devices: none -> 5.66 us  [the longest x1 4.38 us: shards(): next_before = lax.ppermute(next_up, 'lateral', up)]
    all_to_all x2 -> x0, other arithmetic: 4.87 us -> none  [the longest x1 2.43 us: shards(): load = lax.all_to_all(load, both, split_axis=0, concat_axis=0, tiled=True)]
    ppermute x1, waiting for transfers between devices: 0.01 us -> 4.82 us  [shards(): after = lax.ppermute(own_down, 'lateral', down)]
    all_to_all x1, waiting for transfers between devices: 6.22 us -> 2.23 us  [shards(): load = lax.all_to_all(load, both, split_axis=0, concat_axis=0, tiled=True)]
    ppermute x1, starting transfers between devices: 0.07 us -> 3.85 us  [shards(): ring_two = lax.ppermute(ring_two, 'radial', swap)]
  transfers between devices with their start and end apart: 7 -> 9, of which waited for: 2 -> 3; matrix products, arithmetic and copies ran while one was open for 12% -> 0% of each run, Pallas kernels for 3% -> 5%
where the time goes in v1:
time: 77 us; the launch traced here: 76.5 us
  Pallas kernels  23.1 us (30%)
  starting transfers between devices  20.6 us (27%)
  blocking collectives  15.1 us (20%)
  local copies, waits for them, and re-layouts  9.19 us (12%)
  waiting for transfers between devices  7.71 us (10%)
  between operations  0.77 us (1%)
    all_to_all x1, blocking collectives, shards(): lax.all_to_all(orders, both, split_axis=0, concat_axis=0, tiled=True)  15.1 us
    unnamed x22, local copies, waits for them, and re-layouts  9.19 us
    pallas_call x1, Pallas kernels, shards(): pl.pallas_call(first_kernel, in_specs=[HBM, HBM, ANY, ANY, VMEM, VMEM] +...  7.51 us
    pallas_call x1, Pallas kernels, shards(): pl.pallas_call(second_kernel, in_specs=[ANY, HBM, ANY, ANY, ANY, VMEM, VM...  7.51 us
    ppermute x1, waiting for transfers between devices, shards(): after = lax.ppermute(own_down, 'lateral', down)  4.82 us
    ppermute x1, starting transfers between devices, shards(): before = lax.ppermute(own_up, 'lateral', up)  4.44 us
    ppermute x1, starting transfers between devices, shards(): next_before = lax.ppermute(next_up, 'lateral', up)  4.38 us
    ppermute x1, starting transfers between devices, shards(): ring_two = lax.ppermute(ring_two, 'radial', swap)  3.85 us
  transfers between devices with their start and end apart: 9, of which 3 were waited for; matrix products, arithmetic and copies ran while one was open for 0% of the time, Pallas kernels for 5%

profile of v1, /device:TPU:0, one launch (start us, length us, event | category | flops | bytes accessed | tf_op | source)
XLA Modules:
  0.0 76.5 jit_solution(17103049773879653089)
XLA Ops:
  0.6 0.6 copy-done.7
  1.3 2.0 %shard_map.157 = (f32[8,2048]{1,0:T(8,128)S(1)}, f32[8,2048]{1,0:T(8,128)S(1)}) custom-call(f32[16]{0:T(128)S(1)} %copy-done.7, f32[3,4,32,2048]{3,2,1,0:T(8,128)} %d.7, f32[3,4,32,2048]{3,2,1,0:T(8,128)} %f.7, s32[4,32,2048]{2,1,0:T(8,128)} %index_from.1), custom_call_target="tpu_custom_call" | custom-call | bytes 6000000 | tf_op jit(solution)/shard_map/pallas_call | solution.py:439
  3.3 2.5 %shard_map.158 = (f32[4,32,2048]{2,1,0:T(8,128)S(1)}, f32[16,2048]{1,0:T(8,128)S(1)}, f32[16,2048]{1,0:T(8,128)S(1)}, f32[4,32,2048]{2,1,0:T(8,128)S(1)}) custom-call(f32[16]{0:T(128)S(1)} %copy-done.8, f32[3,4,32,2048]{3,2,1,0:T(8,128)} %d.7, s32[4,32,2048]{2,1,0:T(8,128)} %index_from.1), custom_call_target="tpu_custom_call" | custom-call | bytes 12000000 | tf_op jit(solution)/shard_map/pallas_call | solution.py:461
  6.4 4.4 %collective-permute-start.3 = (f32[16,2048]{1,0:T(8,128)S(1)}, f32[16,2048]{1,0:T(8,128)S(1)}, u32[]{:S(2)}, u32[]{:S(2)}) collective-permute-start(f32[16,2048]{1,0:T(8,128)S(1)} %get-tuple-element.32), channel_id=1, source_target_pairs={{0,2},{2,4},{4,6},{6,8},{8,10},{10,12},{12,14},{1,3},{3,5},{5,7},{... | collective-permute-start | bytes 393224 | tf_op jit(solution)/shard_map/ppermute | solution.py:477
  10.8 1.3 %collective-permute-start.4 = (f32[16,2048]{1,0:T(8,128)S(1)}, f32[16,2048]{1,0:T(8,128)S(1)}, u32[]{:S(2)}, u32[]{:S(2)}) collective-permute-start(f32[16,2048]{1,0:T(8,128)S(1)} %get-tuple-element.33), channel_id=1, source_target_pairs={{2,0},{4,2},{6,4},{8,6},{10,8},{12,10},{14,12},{3,1},{5,3},{7,5},{... | collective-permute-start | bytes 393224 | tf_op jit(solution)/shard_map/ppermute | solution.py:478
  12.1 0.7 collective-permute-start.1
  12.8 0.7 collective-permute-start
  14.2 4.8 %collective-permute-done.4.after.eta_after = f32[16,2048]{1,0:T(8,128)S(1)} collective-permute-done((f32[16,2048]{1,0:T(8,128)S(1)}, f32[16,2048]{1,0:T(8,128)S(1)}, u32[]{:S(2)}, u32[]{:S(2)}) %collective-permute-start.4) | collective-permute-done | bytes 131104 | tf_op jit(solution)/shard_map/ppermute | solution.py:478
  19.0 7.5 %shard_map.160 = (f32[3,4,32,2048]{3,2,1,0:T(8,128)S(1)}, f32[3,32,2048]{2,1,0:T(8,128)}, f32[16,2048]{1,0:T(8,128)S(1)}, f32[16,2048]{1,0:T(8,128)S(1)}, bf16[5...) custom-call(f32[3,4,32,2048]{3,2,1,0:T(8,128)} %d.7, ...), custom_call_target="tpu_custom_call" | custom-call | bytes 30000000 | tf_op jit(solution)/shard_map/pallas_call | solution.py:517
  26.6 1.7 %copy-done = f32[3,4,32,2048]{3,2,1,0:T(8,128)} copy-done((f32[3,4,32,2048]{3,2,1,0:T(8,128)}, f32[3,4,32,2048]{3,2,1,0:T(8,128)S(1)}, u32[]{:S(2)}) %copy-start) | copy-done | bytes 3145752
  28.2 1.3 %copy-done.2 = bf16[1024,1024]{1,0:T(8,128)(2,1)} copy-done((bf16[1024,1024]{1,0:T(8,128)(2,1)}, bf16[1024,1024]{1,0:T(8,128)(2,1)S(1)}, u32[]{:S(2)}) %copy-start.2) | copy-done | bytes 2097176
  29.6 1.3 %copy-done.4 = bf16[1024,1024]{1,0:T(8,128)(2,1)} copy-done((bf16[1024,1024]{1,0:T(8,128)(2,1)}, bf16[1024,1024]{1,0:T(8,128)(2,1)S(1)}, u32[]{:S(2)}) %copy-start.4) | copy-done | bytes 2097176
  30.9 3.9 %collective-permute-start.5 = (f32[3,32,2048]{2,1,0:T(8,128)}, f32[3,32,2048]{2,1,0:T(8,128)S(1)}, u32[]{:S(2)}, u32[]{:S(2)}) collective-permute-start(f32[3,32,2048]{2,1,0:T(8,128)} %get-tuple-element.42), channel_id=1, source_target_pairs={{0,1},{1,0},{2,3},{3,2},{4,5},{5,4},{6,7},{7,6},{8,9},{9,8},{10,11... | collective-permute-start | bytes 2359304 | tf_op jit(solution)/shard_map/ppermute | solution.py:528
  34.7 15.1 %all_to_all.10.orders = f32[16,16,128]{2,1,0:T(8,128)S(1)} all-to-all(f32[16,16,128]{2,1,0:T(8,128)S(1)} %shard_map.159), channel_id=1, replica_groups=mesh['member'=2,'lateral'=8,'radial'=2] {'lateral','radial'}, dimensions={0} | all-to-all | bytes 262144 | tf_op jit(solution)/shard_map/all_to_all | solution.py:501
  49.8 1.9 %shard_map.161 = (f32[64,512]{1,0:T(8,128)}, f32[16,16,128]{2,1,0:T(8,128)S(1)}) custom-call(f32[16,16,128]{2,1,0:T(8,128)S(1)} %all_to_all.10.orders, f32[512,128]{1,0:T(8,128)S(1)} %get-tuple-element.35.response, bf16[512,256]{1,0:T(8,128)(2,1)S(1)} %get-tuple-element.36.wave_high, bf16[512,256]{1,0:T(8,128)(2,1)S(1)} %get-tuple-element.37.wave_low, ...), custom_call_target="tpu_custom_call" | custom-call | bytes 6000000 | tf_op jit(solution)/shard_map/pallas_call | solution.py:533
  51.7 0.7 copy-done.6
  52.4 3.5 %all-to-all-start.1 = ((f32[16,16,128]{2,1,0:T(8,128)}), f32[16,16,128]{2,1,0:T(8,128)S(1)}, u32[]{:S(2)}, u32[]{:S(2)}) async-start(f32[16,16,128]{2,1,0:T(8,128)} %copy-done.6), calls=%async_computation.1 | async-start | bytes 262144 | tf_op jit(solution)/shard_map/all_to_all | solution.py:542
  55.9 4.4 %collective-permute-start.6 = (f32[16,2048]{1,0:T(8,128)}, f32[16,2048]{1,0:T(8,128)}, u32[]{:S(2)}, u32[]{:S(2)}) collective-permute-start(f32[16,2048]{1,0:T(8,128)} %copy-done.10), channel_id=1, source_target_pairs={{0,2},{2,4},{4,6},{6,8},{8,10},{10,12},{12,14},{1,3},{3,5},{5,7},{... | collective-permute-start | bytes 393224 | tf_op jit(solution)/shard_map/ppermute | solution.py:529
  60.3 1.3 %collective-permute-start.7 = (f32[16,2048]{1,0:T(8,128)}, f32[16,2048]{1,0:T(8,128)}, u32[]{:S(2)}, u32[]{:S(2)}) collective-permute-start(f32[16,2048]{1,0:T(8,128)} %copy-done.9), channel_id=1, source_target_pairs={{2,0},{4,2},{6,4},{8,6},{10,8},{12,10},{14,12},{3,1},{5,3},{7,5},{... | collective-permute-start | bytes 393224 | tf_op jit(solution)/shard_map/ppermute | solution.py:530
  61.6 2.2 %all-to-all-done.1.load = f32[16,16,128]{2,1,0:T(8,128)S(1)} async-done(((f32[16,16,128]{2,1,0:T(8,128)}), f32[16,16,128]{2,1,0:T(8,128)S(1)}, u32[]{:S(2)}, u32[]{:S(2)}) %all-to-all-start.1) | async-done | bytes 131104 | tf_op jit(solution)/shard_map/all_to_all | solution.py:542
  63.8 1.6 %copy-done.3 = bf16[1024,1024]{1,0:T(8,128)(2,1)S(1)} copy-done((bf16[1024,1024]{1,0:T(8,128)(2,1)S(1)}, bf16[1024,1024]{1,0:T(8,128)(2,1)}, u32[]{:S(2)}) %copy-start.3) | copy-done | bytes 2097176
  65.4 1.6 %copy-done.5 = bf16[1024,1024]{1,0:T(8,128)(2,1)S(1)} copy-done((bf16[1024,1024]{1,0:T(8,128)(2,1)S(1)}, bf16[1024,1024]{1,0:T(8,128)(2,1)}, u32[]{:S(2)}) %copy-start.5) | copy-done | bytes 2097176
  67.0 1.6 %shard_map.163 = f32[32,2048]{1,0:T(8,128)} custom-call(f32[16,16,128]{2,1,0:T(8,128)S(1)} %all-to-all-done.1.load, s32[32,2048]{1,0:T(8,128)S(1)} %get-tuple-element.46.mask, bf16[1024,1024]{1,0:T(8,128)(2,1)S(1)} %copy-done.3, bf16[1024,1024]{1,0:T(8,128)(2,1)S(1)} %copy-done.5), custom_call_target="tpu_custom_call" | custom-call | bytes 9000000 | tf_op jit(solution)/shard_map/pallas_call | solution.py:554
  68.9 7.5 %shard_map.162 = f32[3,4,32,2048]{3,2,1,0:T(8,128)} custom-call(f32[3,4,32,2048]{3,2,1,0:T(8,128)S(1)} %copy-done.1, f32[3,4,32,2048]{3,2,1,0:T(8,128)} %f.7, f32[4,32,2048]{2,1,0:T(8,128)S(1)} %get-tuple-element.41.h, f32[4,32,2048]{2,1,0:T(8,128)S(1)} %collective-permute-done.2.ring, f32[3,32,2048]{2,1,0:T(8,128)S(1)} %collective-permute-done.5.ring_two, ...), custom_call_target="tpu_custom_call" | custom-call | bytes 30000000 | tf_op jit(solution)/shard_map/pallas_call | solution.py:544
  (24 shorter events, 1.7 us)
Async XLA Ops:
  0.6 0.7 copy-start.7
  1.3 2.0 %copy-start.8 = (f32[16]{0:T(128)S(1)}, f32[16]{0:T(128)}, u32[]{:S(2)}) copy-start(f32[16]{0:T(128)} %viscosity.2) | copy-start | bytes 196
  5.9 13.2 %collective-permute-start.2 = (f32[4,32,2048]{2,1,0:T(8,128)S(1)}, f32[4,32,2048]{2,1,0:T(8,128)S(1)}, u32[]{:S(2)}, u32[]{:S(2)}) collective-permute-start(f32[4,32,2048]{2,1,0:T(8,128)S(1)} %get-tuple-element.31), channel_id=1, source_target_pairs={{0,1},{1,0},{2,3},{3,2},{4,5},{5,4},{6,7},{7,6},{8,9},{9,8},{10,11... | collective-permute-start | bytes 3145736 | tf_op jit(solution)/shard_map/ppermute | solution.py:476
  6.4 7.8 %collective-permute-start.3 = (f32[16,2048]{1,0:T(8,128)S(1)}, f32[16,2048]{1,0:T(8,128)S(1)}, u32[]{:S(2)}, u32[]{:S(2)}) collective-permute-start(f32[16,2048]{1,0:T(8,128)S(1)} %get-tuple-element.32), channel_id=1, source_target_pairs={{0,2},{2,4},{4,6},{6,8},{8,10},{10,12},{12,14},{1,3},{3,5},{5,7},{... | collective-permute-start | bytes 393224 | tf_op jit(solution)/shard_map/ppermute | solution.py:477
  10.8 8.2 %collective-permute-start.4 = (f32[16,2048]{1,0:T(8,128)S(1)}, f32[16,2048]{1,0:T(8,128)S(1)}, u32[]{:S(2)}, u32[]{:S(2)}) collective-permute-start(f32[16,2048]{1,0:T(8,128)S(1)} %get-tuple-element.33), channel_id=1, source_target_pairs={{2,0},{4,2},{6,4},{8,6},{10,8},{12,10},{14,12},{3,1},{5,3},{7,5},{... | collective-permute-start | bytes 393224 | tf_op jit(solution)/shard_map/ppermute | solution.py:478
  12.1 1.3 %collective-permute-start.1 = (f32[8,2048]{1,0:T(8,128)S(1)}, f32[8,2048]{1,0:T(8,128)S(1)}, u32[]{:S(2)}, u32[]{:S(2)}) collective-permute-start(f32[8,2048]{1,0:T(8,128)S(1)} %get-tuple-element.29), channel_id=1, source_target_pairs={{3,1},{5,3},{7,5},{9,7},{11,9},{13,11},{15,13},{19,17},{21,19},{23... | collective-permute-start | bytes 196616 | tf_op jit(solution)/shard_map/ppermute | solution.py:455
  12.8 0.7 collective-permute-start
  26.6 1.7 %copy-start = (f32[3,4,32,2048]{3,2,1,0:T(8,128)}, f32[3,4,32,2048]{3,2,1,0:T(8,128)S(1)}, u32[]{:S(2)}) copy-start(f32[3,4,32,2048]{3,2,1,0:T(8,128)S(1)} %get-tuple-element.34.d) | copy-start | bytes 9437188
  28.2 1.3 %copy-start.2 = (bf16[1024,1024]{1,0:T(8,128)(2,1)}, bf16[1024,1024]{1,0:T(8,128)(2,1)S(1)}, u32[]{:S(2)}) copy-start(bf16[1024,1024]{1,0:T(8,128)(2,1)S(1)} %get-tuple-element.47.high) | copy-start | bytes 6291460
  29.6 1.3 %copy-start.4 = (bf16[1024,1024]{1,0:T(8,128)(2,1)}, bf16[1024,1024]{1,0:T(8,128)(2,1)S(1)}, u32[]{:S(2)}) copy-start(bf16[1024,1024]{1,0:T(8,128)(2,1)S(1)} %get-tuple-element.48.low) | copy-start | bytes 6291460
  30.9 20.8 %copy-start.9 = (f32[16,2048]{1,0:T(8,128)}, f32[16,2048]{1,0:T(8,128)S(1)}, u32[]{:S(2)}) copy-start(f32[16,2048]{1,0:T(8,128)S(1)} %get-tuple-element.44) | copy-start | bytes 393220
  30.9 20.8 %copy-start.10 = (f32[16,2048]{1,0:T(8,128)}, f32[16,2048]{1,0:T(8,128)S(1)}, u32[]{:S(2)}) copy-start(f32[16,2048]{1,0:T(8,128)S(1)} %get-tuple-element.43) | copy-start | bytes 393220
  30.9 37.7 %collective-permute-start.5 = (f32[3,32,2048]{2,1,0:T(8,128)}, f32[3,32,2048]{2,1,0:T(8,128)S(1)}, u32[]{:S(2)}, u32[]{:S(2)}) collective-permute-start(f32[3,32,2048]{2,1,0:T(8,128)} %get-tuple-element.42), channel_id=1, source_target_pairs={{0,1},{1,0},{2,3},{3,2},{4,5},{5,4},{6,7},{7,6},{8,9},{9,8},{10,11... | collective-permute-start | bytes 2359304 | tf_op jit(solution)/shard_map/ppermute | solution.py:528
  51.7 0.7 copy-start.6
  52.4 11.4 %all-to-all-start.1 = ((f32[16,16,128]{2,1,0:T(8,128)}), f32[16,16,128]{2,1,0:T(8,128)S(1)}, u32[]{:S(2)}, u32[]{:S(2)}) async-start(f32[16,16,128]{2,1,0:T(8,128)} %copy-done.6), calls=%async_computation.1 | async-start | bytes 262144 | tf_op jit(solution)/shard_map/all_to_all | solution.py:542
  55.9 12.7 %collective-permute-start.6 = (f32[16,2048]{1,0:T(8,128)}, f32[16,2048]{1,0:T(8,128)}, u32[]{:S(2)}, u32[]{:S(2)}) collective-permute-start(f32[16,2048]{1,0:T(8,128)} %copy-done.10), channel_id=1, source_target_pairs={{0,2},{2,4},{4,6},{6,8},{8,10},{10,12},{12,14},{1,3},{3,5},{5,7},{... | collective-permute-start | bytes 393224 | tf_op jit(solution)/shard_map/ppermute | solution.py:529
  60.3 8.3 %collective-permute-start.7 = (f32[16,2048]{1,0:T(8,128)}, f32[16,2048]{1,0:T(8,128)}, u32[]{:S(2)}, u32[]{:S(2)}) collective-permute-start(f32[16,2048]{1,0:T(8,128)} %copy-done.9), channel_id=1, source_target_pairs={{2,0},{4,2},{6,4},{8,6},{10,8},{12,10},{14,12},{3,1},{5,3},{7,5},{... | collective-permute-start | bytes 393224 | tf_op jit(solution)/shard_map/ppermute | solution.py:530
  63.8 1.6 %copy-start.3 = (bf16[1024,1024]{1,0:T(8,128)(2,1)S(1)}, bf16[1024,1024]{1,0:T(8,128)(2,1)}, u32[]{:S(2)}) copy-start(bf16[1024,1024]{1,0:T(8,128)(2,1)} %copy-done.2) | copy-start | bytes 6291460
  65.4 1.6 %copy-start.5 = (bf16[1024,1024]{1,0:T(8,128)(2,1)S(1)}, bf16[1024,1024]{1,0:T(8,128)(2,1)}, u32[]{:S(2)}) copy-start(bf16[1024,1024]{1,0:T(8,128)(2,1)} %copy-done.4) | copy-start | bytes 6291460
  67.0 2.0 %copy-start.1 = (f32[3,4,32,2048]{3,2,1,0:T(8,128)S(1)}, f32[3,4,32,2048]{3,2,1,0:T(8,128)}, u32[]{:S(2)}) copy-start(f32[3,4,32,2048]{3,2,1,0:T(8,128)} %copy-done) | copy-start | bytes 9437188

commit v2 on v1

--- a/solution.py
+++ b/solution.py
@@ -13,6 +13,7 @@
 MODES = 512
 RELAXATION = 0.8
 TILE = 8
+RADIX = 8
 MIB = 1 << 20
 ANY = pl.BlockSpec(memory_space=pl.ANY)
 HBM = pl.BlockSpec(memory_space=pltpu.HBM)
@@ -32,7 +33,7 @@
 
 @functools.lru_cache
 def longitude_tables(count, modes):
-    points = np.arange(count // 2, dtype=np.int64)[:, None]
+    points = np.arange(count // RADIX, dtype=np.int64)[:, None]
     orders = np.arange(modes, dtype=np.int64)[None, :]
     angle = (2.0 * math.pi / count) * (points * orders % count)
     table = np.concatenate([np.cos(angle), np.sin(angle)], axis=1) * math.sqrt(2.0 / count)
@@ -66,6 +67,54 @@
 def unpack(block, width):
     groups = max(1, 128 // width)
     return jnp.concatenate([block[:, k * width : (k + 1) * width] for k in range(groups)], axis=0)
+
+
+def weighted_sum(terms):
+    total = None
+    for factor, values in terms:
+        factor = round(factor, 15)
+        if factor == 0.0:
+            continue
+        part = values if abs(factor) == 1.0 else abs(factor) * values
+        if total is None:
+            total = part if factor > 0 else -part
+        else:
+            total = total + part if factor > 0 else total - part
+    return total
+
+
+def turn(number):
+    angle = 2.0 * math.pi * (number % RADIX) / RADIX
+    return math.cos(angle), math.sin(angle)
+
+
+def fold(values):
+    step = values.shape[1] // RADIX
+    parts = [values[:, m * step : (m + 1) * step] for m in range(RADIX)]
+    cosines = [[(turn(k * m)[0], part) for m, part in enumerate(parts)] for k in range(RADIX // 2 + 1)]
+    sines = [[(turn(k * m)[1], part) for m, part in enumerate(parts)] for k in range(1, RADIX // 2)]
+    return [weighted_sum(terms) for terms in cosines + sines]
+
+
+def unfold(blocks):
+    cosines, sines = blocks[: RADIX // 2 + 1], blocks[RADIX // 2 + 1 :]
+    return [
+        weighted_sum(
+            [(turn(k * m)[0], block) for k, block in enumerate(cosines)]
+            + [(turn(k * m)[1], block) for k, block in enumerate(sines, 1)]
+        )
+        for m in range(RADIX)
+    ]
+
+
+def order_class(shape):
+    order = lax.broadcasted_iota(jnp.int32, shape, len(shape) - 1) % RADIX
+    mirrored = order > RADIX // 2
+    return jnp.where(mirrored, RADIX - order, order), mirrored
+
+
+def dot_nt(a, b):
+    return lax.dot_general(a, b, (((1,), (1,)), ((), ())), preferred_element_type=jnp.float32)
 
 
 def half_viscosity(index, viscosity_ref):
@@ -126,7 +175,16 @@
     ]
 
 
-def surface_message_kernel(viscosity, d, f, index, up, down, fields, forces, layers, sems):
+def odd_band():
+    return lax.axis_index("lateral") % 2 == 1
+
+
+def by_parity(one, two):
+    one, two = one[...], two[...]
+    return jnp.where(odd_band(), one, two), jnp.where(odd_band(), two, one)
+
+
+def surface_message_kernel(viscosity_from, d, f, index, one, two, fields, forces, layers, viscosity, sems):
     shells, rows = index.shape[0], index.shape[1]
     top, pair = shells - 1, pl.ds(shells - 2, 2)
     copies = []
@@ -137,25 +195,35 @@
             pltpu.make_async_copy(f.at[0, top, part], forces.at[side], sems.at[side, 1]),
             pltpu.make_async_copy(index.at[pair, part], layers.at[side], sems.at[side, 2]),
         ]
+    copies.append(pltpu.make_async_copy(viscosity_from, viscosity, sems.at[2, 0]))
     for copy in copies:
         copy.start()
     for copy in copies:
         copy.wait()
-    for side, message, near, far in ((0, down, 0, 1), (1, up, TILE - 1, TILE - 2)):
+    messages = []
+    for side, near, far in ((0, 0, 1), (1, TILE - 1, TILE - 2)):
         below, surface = [half_viscosity(layers[side, k], viscosity) for k in range(2)]
-        message[0] = fields[side, 1, far]
-        message[1] = fields[side, 1, near]
-        message[2] = fields[side, 0, near]
-        message[3] = surface[far]
-        message[4] = surface[near]
-        message[5] = below[near]
-        message[6] = forces[side, near]
-        message[7] = jnp.zeros_like(below[near])
-
-
-def main_message_kernel(viscosity, d, index_from, h, up, down, ring, tops, ends, index, sems):
+        messages.append(
+            (
+                fields[side, 1, far],
+                fields[side, 1, near],
+                fields[side, 0, near],
+                surface[far],
+                surface[near],
+                below[near],
+                forces[side, near],
+                jnp.zeros_like(below[near]),
+            )
+        )
+    for place, (down, up) in enumerate(zip(*messages)):
+        one[place] = jnp.where(odd_band(), down, up)
+        two[place] = jnp.where(odd_band(), up, down)
+
+
+def main_message_kernel(viscosity_from, d, index_from, token, h, one, two, ring, tops, ends, index, viscosity, sems):
     shells, rows = h.shape[0], h.shape[1]
     components = d.shape[0]
+    del token
     shell = jnp.where(lax.axis_index("radial") == 0, shells - 1, 0)
     copies = [
         pltpu.make_async_copy(d.at[:, :, pl.ds(0, TILE)], tops, sems.at[0]),
@@ -163,8 +231,10 @@
         pltpu.make_async_copy(d.at[:, shell], ring.at[pl.ds(0, components)], sems.at[2]),
     ]
     layers = [pltpu.make_async_copy(index_from.at[s], index.at[s], sems.at[4 + s]) for s in range(shells)]
-    for copy in layers + copies:
+    values = pltpu.make_async_copy(viscosity_from, viscosity, sems.at[4 + shells])
+    for copy in [values] + layers + copies:
         copy.start()
+    values.wait()
     for s in range(shells):
         layers[s].wait()
 
@@ -178,16 +248,16 @@
     eta_copy.start()
     for copy in copies[:2]:
         copy.wait()
-    for message, row, place, a in ((down, 0, 0, tops), (up, rows - 1, TILE - 1, ends)):
-        for s in range(shells):
-            for c in range(components):
-                message[c * shells + s] = a[c, s, place]
-            message[components * shells + s] = h[s, row]
+    for s in range(shells):
+        pairs = [(tops[c, s, 0], ends[c, s, TILE - 1]) for c in range(components)] + [(h[s, 0], h[s, rows - 1])]
+        for c, (down, up) in enumerate(pairs):
+            one[c * shells + s] = jnp.where(odd_band(), down, up)
+            two[c * shells + s] = jnp.where(odd_band(), up, down)
     copies[2].wait()
     eta_copy.wait()
 
 
-def surface_kernel(d, f, h, before, after, high_from, low_from, out, field, force, eta, smoothed, high, low, sems):
+def surface_kernel(d, f, h, one, two, high_from, low_from, out, field, force, eta, smoothed, high, low, sems):
     shells, rows, count = h.shape
     top = lax.axis_size("radial") - 1
 
@@ -209,6 +279,7 @@
         field[3, inner] = zeros
         eta[3, inner] = zeros
         smoothed[2, inner] = zeros
+        before, after = by_parity(one, two)
         for message, place in ((before, TILE - 1), (after, rows + TILE)):
             field[2, place] = message[1]
             field[1, place] = message[2]
@@ -222,7 +293,7 @@
             (before, TILE, TILE - 1, inside[0]),
             (after, rows + TILE - 1, rows + TILE, inside[1]),
         ):
-            row = lambda k: message[pl.ds(k, 1)]
+            row = lambda k: message[k : k + 1]
             own_row = lambda ref: ref[2, pl.ds(own, 1)]
             none = jnp.zeros((1, count), jnp.float32)
             weights, factor = relax_weights(
@@ -257,15 +328,22 @@
             return 0
 
         lax.fori_loop(0, rows // TILE, second, 0)
-        half = count // 2
-        left, right = field[0, pl.ds(0, rows), :half], field[0, pl.ds(0, rows), half:]
-        near, far = split(jnp.concatenate([left + right, left - right], axis=0))
+        near, far = split(jnp.concatenate(fold(field[0, pl.ds(0, rows), :]), axis=0))
         for copy in tables:
             copy.wait()
-        total = dot(jnp.concatenate([near, far], axis=0), high[...])
-        total = total[: 2 * rows] + total[2 * rows :] + dot(near, low[...])
-        odd = lax.broadcasted_iota(jnp.int32, (rows, total.shape[1]), 1) % 2 == 1
-        fourier = jnp.where(odd, total[rows:], total[:rows])
+        total = dot(near, high[...]) + dot(far, high[...]) + dot(near, low[...])
+        blocks = [total[k * rows : (k + 1) * rows] for k in range(RADIX)]
+        kind, mirrored = order_class((1, total.shape[1]))
+        cosine, sine = blocks[0], jnp.zeros_like(blocks[0])
+        for k in range(1, RADIX // 2 + 1):
+            cosine = jnp.where(kind == k, blocks[k], cosine)
+        for k in range(1, RADIX // 2):
+            sine = jnp.where(kind == k, blocks[RADIX // 2 + k], sine)
+        sine = jnp.where(mirrored, -sine, sine)
+        modes = total.shape[1] // 2
+        fourier = jnp.concatenate(
+            [cosine[:, :modes] - sine[:, modes:], cosine[:, modes:] + sine[:, :modes]], axis=1
+        )
         blocks = out.shape[0]
         width = fourier.shape[1] // blocks
         for block in range(blocks):
@@ -330,11 +408,12 @@
         ref[(*lead, s + 1, rows + TILE)] = after(s)
 
 
-def first_kernel(d, f, h, ring, before, after, *refs):
+def first_kernel(d, f, h, ring, one, two, *refs):
     components, shells, rows, _ = d.shape
     staged = (len(refs) - 11) // 2
     sources, refs = refs[:staged], refs[staged:]
-    out, ring_out, up, down, *targets = refs[: 4 + staged]
+    before, after = by_parity(one, two)
+    out, ring_out, next_one, next_two, *targets = refs[: 4 + staged]
     field, eta, force, result, sems, ring_sems, stage_sems = refs[4 + staged :]
     stages = [
         pltpu.make_async_copy(source, target, stage_sems.at[k]) for k, (source, target) in enumerate(zip(sources, targets))
@@ -353,8 +432,9 @@
             for copy in stages:
                 copy.start()
         for c in range(components):
-            down[c * shells + s] = result[c, s, 0]
-            up[c * shells + s] = result[c, s, rows - 1]
+            down, up = result[c, s, 0], result[c, s, rows - 1]
+            next_one[c * shells + s] = jnp.where(odd_band(), down, up)
+            next_two[c * shells + s] = jnp.where(odd_band(), up, down)
         if s in (0, shells - 1):
 
             @pl.when(lower if s else jnp.logical_not(lower))
@@ -371,9 +451,11 @@
 
 
 def second_kernel(
-    d, f, h, ring, ring_two, eta_before, eta_after, before, after, out, field, eta, force, result, sems
+    d, f, h, ring, ring_two, eta_one, eta_two, one, two, out, token, field, eta, force, result, sems
 ):
     components, shells, rows, _ = d.shape
+    (eta_before, eta_after), (before, after) = by_parity(eta_one, eta_two), by_parity(one, two)
+    token[...] = jnp.zeros_like(token)
     row = lambda message, kind: lambda s: message[kind * shells + s]
     for c in range(components):
         set_edge(field, (c,), shells, rows, row(before, c), row(after, c))
@@ -405,16 +487,31 @@
             out[band * radial + place] = block
 
 
-def load_kernel(load, mask, high, low, out):
+def load_kernel(load, mask, high_from, low_from, token, out, high, low, sems):
+    del token
+    tables = [
+        pltpu.make_async_copy(high_from, high, sems.at[0]),
+        pltpu.make_async_copy(low_from, low, sems.at[1]),
+    ]
+    for copy in tables:
+        copy.start()
     blocks, rows = load.shape[0], out.shape[0]
-    half, width = out.shape[1] // 2, high.shape[0] // blocks
+    step, width = out.shape[1] // RADIX, high.shape[1] // blocks
     values = jnp.concatenate([unpack(load[block], width) for block in range(blocks)], axis=1)
-    odd = lax.broadcasted_iota(jnp.int32, values.shape, 1) % 2 == 1
-    near, far = split(jnp.concatenate([values, jnp.where(odd, -values, values)], axis=0))
-    total = dot(jnp.concatenate([near, far], axis=0), high[...])
-    total = total[: 2 * rows] + total[2 * rows :] + dot(near, low[...])
-    out[:, :half] = total[:rows] * mask[:, :half].astype(jnp.float32)
-    out[:, half:] = total[rows:] * mask[:, half:].astype(jnp.float32)
+    modes = values.shape[1] // 2
+    kind, mirrored = order_class((1, values.shape[1]))
+    crossed = jnp.concatenate([values[:, modes:], -values[:, :modes]], axis=1)
+    crossed = jnp.where(mirrored, -crossed, crossed)
+    zero = jnp.zeros_like(values)
+    stack = [jnp.where(kind == k, values, zero) for k in range(RADIX // 2 + 1)]
+    stack += [jnp.where(kind == k, crossed, zero) for k in range(1, RADIX // 2)]
+    near, far = split(jnp.concatenate(stack, axis=0))
+    for copy in tables:
+        copy.wait()
+    total = dot_nt(near, high[...]) + dot_nt(far, high[...]) + dot_nt(near, low[...])
+    for m, part in enumerate(unfold([total[k * rows : (k + 1) * rows] for k in range(RADIX)])):
+        columns = slice(m * step, (m + 1) * step)
+        out[:, columns] = part * mask[:, columns].astype(jnp.float32)
 
 
 def cost(microseconds):
@@ -431,53 +528,57 @@
     f32 = functools.partial(jax.ShapeDtypeStruct, dtype=jnp.float32)
     scratch = lambda *shape: pltpu.VMEM(shape, jnp.float32)
     width = 2 * MODES // (lateral * radial)
-    up = [(i, i + 1) for i in range(lateral - 1)]
-    down = [(j, i) for i, j in up]
+    first = [p for i in range(0, lateral - 1, 2) for p in ((i, i + 1), (i + 1, i))]
+    second = [p for i in range(1, lateral - 1, 2) for p in ((i, i + 1), (i + 1, i))]
     top_only = lambda pairs: [(i * radial + radial - 1, j * radial + radial - 1) for i, j in pairs]
 
     tensors = [hbm(a) for a in (initial_displacement, force, layer_index)]
-    surface_up, surface_down = pl.pallas_call(
+    viscosity = hbm(viscosity)
+    surface_one, surface_two = pl.pallas_call(
         surface_message_kernel,
-        in_specs=[SMEM, HBM, HBM, HBM],
+        in_specs=[HBM, HBM, HBM, HBM],
         out_specs=[VMEM, VMEM],
         out_shape=[f32((TILE, count))] * 2,
         scratch_shapes=[
             scratch(2, 2, TILE, count),
             scratch(2, TILE, count),
             pltpu.VMEM((2, 2, TILE, count), jnp.int32),
-            pltpu.SemaphoreType.DMA((2, 3)),
+            pltpu.SMEM(viscosity.shape, jnp.float32),
+            pltpu.SemaphoreType.DMA((3, 3)),
         ],
         compiler_params=params(8),
         cost_estimate=cost(2),
     )(viscosity, *tensors)
+    token = surface_one
     both = ("lateral", "radial")
-    surface_before = lax.ppermute(surface_up, both, top_only(up))
-    surface_after = lax.ppermute(surface_down, both, top_only(down))
+    surface_one = lax.ppermute(surface_one, both, top_only(first))
+    surface_two = lax.ppermute(surface_two, both, top_only(second))
 
     fields = -(-(components + 1) * shells // TILE) * TILE
     message = f32((fields, count))
     edge_rows = scratch(components, shells, TILE, count)
-    later, _ = lax.optimization_barrier((viscosity, surface_up))
-    eta, own_up, own_down, ring = pl.pallas_call(
+    eta, one, two, ring = pl.pallas_call(
         main_message_kernel,
-        in_specs=[SMEM, HBM, HBM],
+        in_specs=[HBM, HBM, HBM, ANY],
         out_specs=[VMEM, VMEM, VMEM, ANY],
         out_shape=[f32((shells, rows, count)), message, message, f32((components + 1, rows, count))],
         scratch_shapes=[
             edge_rows,
             edge_rows,
             pltpu.VMEM(layer_index.shape, jnp.int32),
-            pltpu.SemaphoreType.DMA((4 + shells,)),
+            pltpu.SMEM(viscosity.shape, jnp.float32),
+            pltpu.SemaphoreType.DMA((5 + shells,)),
         ],
         compiler_params=params(16),
-        cost_estimate=cost(4),
-    )(later, tensors[0], tensors[2])
+        cost_estimate=cost(20),
+    )(viscosity, tensors[0], tensors[2], token)
     swap = [(i, radial - 1 - i) for i in range(radial)]
     ring = lax.ppermute(ring, "radial", swap)
-    before = lax.ppermute(own_up, "lateral", up)
-    after = lax.ppermute(own_down, "lateral", down)
+    one = lax.ppermute(one, "lateral", first)
+    two = lax.ppermute(two, "lateral", second)
 
     high, low = longitude_tables(count, MODES)
+    high, low = hbm(jnp.asarray(high)), hbm(jnp.asarray(low))
     table = pltpu.VMEM(high.shape, jnp.bfloat16)
     packed = (lateral * radial, rows * width // max(128, width), max(128, width))
     orders = pl.pallas_call(
@@ -495,8 +596,8 @@
             pltpu.SemaphoreType.DMA((5,)),
         ],
         compiler_params=params(24),
-        cost_estimate=cost(6),
-    )(*tensors[:2], eta, surface_before, surface_after, hbm(jnp.asarray(high)), hbm(jnp.asarray(low)))
+        cost_estimate=cost(200),
+    )(*tensors[:2], eta, surface_one, surface_two, high, low)
     later, _ = lax.optimization_barrier((eta, orders))
     orders = lax.all_to_all(orders, both, split_axis=0, concat_axis=0, tiled=True)
 
@@ -510,55 +611,56 @@
     point_high, point_low = colatitude_tables(rows * lateral, MODES)
     stages = [
         jnp.asarray(a)
-        for a in (point_high.T.copy(), point_low.T.copy(), point_high, point_low, high.T.copy(), low.T.copy())
-    ] + [response, ocean_mask]
+        for a in (point_high.T.copy(), point_low.T.copy(), point_high, point_low)
+    ] + [response]
     fields = -(-components * shells // TILE) * TILE
     message = f32((fields, count))
-    smoothed, ring_two, next_up, next_down, *staged = pl.pallas_call(
+    smoothed, ring_two, next_one, next_two, *staged = pl.pallas_call(
         first_kernel,
         in_specs=[HBM, HBM, ANY, ANY, VMEM, VMEM] + [HBM] * len(stages),
-        out_specs=[ANY, ANY, VMEM, VMEM] + [VMEM] * len(stages),
-        out_shape=[f32(initial_displacement.shape), f32((components, rows, count)), message, message]
+        out_specs=[HBM, ANY, VMEM, VMEM] + [VMEM] * len(stages),
+        out_shape=[pltpu.HBM(initial_displacement.shape, jnp.float32), f32((components, rows, count)), message, message]
         + [jax.ShapeDtypeStruct(a.shape, a.dtype) for a in stages],
         scratch_shapes=sweep_scratch
         + [pltpu.SemaphoreType.DMA((1,)), pltpu.SemaphoreType.DMA((len(stages),))],
         compiler_params=params(28),
-        cost_estimate=cost(10),
-    )(*tensors[:2], later, ring, before, after, *(hbm(a) for a in stages))
+        cost_estimate=cost(50),
+    )(*tensors[:2], later, ring, one, two, *(hbm(a) for a in stages))
     ring_two = lax.ppermute(ring_two, "radial", swap)
-    next_before = lax.ppermute(next_up, "lateral", up)
-    next_after = lax.ppermute(next_down, "lateral", down)
-
-    *points, high, low, response, ocean_mask = staged
+    next_one = lax.ppermute(next_one, "lateral", first)
+    next_two = lax.ppermute(next_two, "lateral", second)
+
+    *points, response = staged
     coefficients, load = pl.pallas_call(
         spectrum_kernel,
         in_specs=[VMEM] * 6,
         out_specs=[VMEM, VMEM],
         out_shape=[f32((width, MODES)), f32(packed)],
         compiler_params=params(16),
-        cost_estimate=cost(2),
+        cost_estimate=cost(200),
     )(orders, response, *points)
     later, _ = lax.optimization_barrier((eta, load))
     load = lax.all_to_all(load, both, split_axis=0, concat_axis=0, tiled=True)
 
-    displacement = pl.pallas_call(
+    displacement, token = pl.pallas_call(
         second_kernel,
-        in_specs=[ANY, HBM, ANY, ANY, ANY, VMEM, VMEM, VMEM, VMEM],
-        out_specs=HBM,
-        out_shape=pltpu.HBM(initial_displacement.shape, jnp.float32),
+        in_specs=[HBM, HBM, ANY, ANY, ANY, VMEM, VMEM, VMEM, VMEM],
+        out_specs=[HBM, VMEM],
+        out_shape=[pltpu.HBM(initial_displacement.shape, jnp.float32), f32((TILE, 128))],
         scratch_shapes=sweep_scratch,
         compiler_params=params(28),
-        cost_estimate=cost(10),
-    )(smoothed, tensors[1], later, ring, ring_two, before, after, next_before, next_after)
+        cost_estimate=cost(50),
+    )(smoothed, tensors[1], later, ring, ring_two, one, two, next_one, next_two)
 
     sea_load = pl.pallas_call(
         load_kernel,
-        in_specs=[VMEM] * 4,
+        in_specs=[VMEM, VMEM, HBM, HBM, ANY],
         out_specs=VMEM,
         out_shape=f32((rows, count)),
+        scratch_shapes=[table, table, pltpu.SemaphoreType.DMA((2,))],
         compiler_params=params(20),
         cost_estimate=cost(3),
-    )(load, ocean_mask, high, low)
+    )(load, ocean_mask, high, low, token)
     return (displacement, coefficients.T, sea_load)
 
 

time: 77 us -> 68.2 us (0.89)
  local copies, waits for them, and re-layouts: 9.19 us -> 1.89 us
  blocking collectives: 15.1 us -> 14 us
  Pallas kernels: 23.1 us -> 22.1 us
    unnamed x22 -> x4, local copies, waits for them, and re-layouts: 9.19 us -> 1.89 us
    ppermute x1, starting transfers between devices: 3.85 us -> 9.57 us  [shards(): ring_two = lax.ppermute(ring_two, 'radial', swap)]
    ppermute x6, starting transfers between devices: 12.7 us -> 7.05 us  [the longest x1 2.59 us: shards(): one = lax.ppermute(one, 'lateral', first)]
    ppermute x6, waiting for transfers between devices: 5.48 us -> 8.27 us  [the longest x1 6.27 us: shards(): next_one = lax.ppermute(next_one, 'lateral', first)]
    all_to_all x1, waiting for transfers between devices: 2.23 us -> 0.01 us  [shards(): load = lax.all_to_all(load, both, split_axis=0, concat_axis=0, tiled=True)]
    all_to_all x1, blocking collectives: 15.1 us -> 14 us  [shards(): lax.all_to_all(orders, both, split_axis=0, concat_axis=0, tiled=True)]
    pallas_call x4, Pallas kernels: 13.6 us -> 12.8 us  [the longest x1 6.55 us: shards(): pl.pallas_call(second_kernel, in_specs=[HBM, HBM, ANY, ANY, ANY, VMEM, VM...]
  transfers between devices with their start and end apart: 9 -> 9, of which waited for: 3 -> 2; matrix products, arithmetic and copies ran while one was open for 0% -> 0% of each run, Pallas kernels for 5% -> 13%
where the time goes in v2:
time: 68.2 us; the launch traced here: 67.7 us
  Pallas kernels  22.1 us (32%)
  starting transfers between devices  20.7 us (30%)
  blocking collectives  14 us (21%)
  waiting for transfers between devices  8.28 us (12%)
  local copies, waits for them, and re-layouts  1.89 us (3%)
  between operations  0.75 us (1%)
    all_to_all x1, blocking collectives, shards(): lax.all_to_all(orders, both, split_axis=0, concat_axis=0, tiled=True)  14 us
    ppermute x1, starting transfers between devices, shards(): ring_two = lax.ppermute(ring_two, 'radial', swap)  9.57 us
    pallas_call x1, Pallas kernels, shards(): pl.pallas_call(first_kernel, in_specs=[HBM, HBM, ANY, ANY, VMEM, VMEM] +...  7.25 us
    pallas_call x1, Pallas kernels, shards(): pl.pallas_call(second_kernel, in_specs=[HBM, HBM, ANY, ANY, ANY, VMEM, VM...  6.55 us
    ppermute x1, waiting for transfers between devices, shards(): next_one = lax.ppermute(next_one, 'lateral', first)  6.27 us
    all_to_all x1, starting transfers between devices, shards(): load = lax.all_to_all(load, both, split_axis=0, concat_axis=0, tiled=True)  3.51 us
    pallas_call x1, Pallas kernels, shards(): pl.pallas_call(load_kernel, in_specs=[VMEM, VMEM, HBM, HBM, ANY], out_spe...  2.71 us
    ppermute x1, starting transfers between devices, shards(): one = lax.ppermute(one, 'lateral', first)  2.59 us
  transfers between devices with their start and end apart: 9, of which 2 were waited for; matrix products, arithmetic and copies ran while one was open for 0% of the time, Pallas kernels for 13%

profile of v2, /device:TPU:0, one launch (start us, length us, event | category | flops | bytes accessed | tf_op | source)
XLA Modules:
  0.0 67.7 jit_solution(13374347602603689456)
XLA Ops:
  0.6 1.5 %shard_map.139 = (f32[8,2048]{1,0:T(8,128)S(1)}, f32[8,2048]{1,0:T(8,128)S(1)}) custom-call(f32[16]{0:T(128)} %viscosity_from.3, f32[3,4,32,2048]{3,2,1,0:T(8,128)} %d.7, f32[3,4,32,2048]{3,2,1,0:T(8,128)} %f.7, s32[4,32,2048]{2,1,0:T(8,128)} %index_from.1), custom_call_target="tpu_custom_call" | custom-call | bytes 6000000 | tf_op jit(solution)/shard_map/pallas_call | solution.py:537
  2.2 2.0 %shard_map.140 = (f32[4,32,2048]{2,1,0:T(8,128)S(1)}, f32[16,2048]{1,0:T(8,128)S(1)}, f32[16,2048]{1,0:T(8,128)S(1)}, f32[4,32,2048]{2,1,0:T(8,128)S(1)}) custom-call(f32[16]{0:T(128)} %viscosity_from.3, f32[3,4,32,2048]{3,2,1,0:T(8,128)} %d.7, s32[4,32,2048]{2,1,0:T(8,128)} %index_from.1, f32[8,2048]{1,0:T(8,128)S(1)} %get-tuple-element.24.token), custom_call_target="tpu_custom_call" | custom-call | bytes 60000000 | tf_op jit(solution)/shard_map/pallas_call | solution.py:560
  4.2 0.5 collective-permute-start.2
  4.7 2.6 %collective-permute-start.3 = (f32[16,2048]{1,0:T(8,128)S(1)}, f32[16,2048]{1,0:T(8,128)S(1)}, u32[]{:S(2)}, u32[]{:S(2)}) collective-permute-start(f32[16,2048]{1,0:T(8,128)S(1)} %get-tuple-element.29), channel_id=1, source_target_pairs={{0,2},{2,0},{4,6},{6,4},{8,10},{10,8},{12,14},{14,12},{1,3},{3,1},... | collective-permute-start | bytes 393224 | tf_op jit(solution)/shard_map/ppermute | solution.py:577
  7.3 0.7 collective-permute-start.4
  8.0 0.7 collective-permute-start.1
  8.7 0.7 collective-permute-start
  9.3 0.0 collective-permute-done.1.two
  9.3 0.0 collective-permute-done.one
  9.3 0.1 shard_map.141
  9.4 2.0 %collective-permute-done.3.one.eta_one = f32[16,2048]{1,0:T(8,128)S(1)} collective-permute-done((f32[16,2048]{1,0:T(8,128)S(1)}, f32[16,2048]{1,0:T(8,128)S(1)}, u32[]{:S(2)}, u32[]{:S(2)}) %collective-permute-start.3) | collective-permute-done | bytes 131104 | tf_op jit(solution)/shard_map/ppermute | solution.py:577
  11.4 0.0 collective-permute-done.4.two.eta_two
  11.4 0.0 collective-permute-done.2.ring
  11.4 7.2 %shard_map.142 = (f32[3,4,32,2048]{3,2,1,0:T(8,128)}, f32[3,32,2048]{2,1,0:T(8,128)}, f32[16,2048]{1,0:T(8,128)S(1)}, f32[16,2048]{1,0:T(8,128)S(1)}, bf16[512,2...) custom-call(f32[3,4,32,2048]{3,2,1,0:T(8,128)} %d.7, ...), custom_call_target="tpu_custom_call" | custom-call | bytes 150000000 | tf_op jit(solution)/shard_map/pallas_call | solution.py:618
  18.7 9.6 %collective-permute-start.5 = (f32[3,32,2048]{2,1,0:T(8,128)}, f32[3,32,2048]{2,1,0:T(8,128)S(1)}, u32[]{:S(2)}, u32[]{:S(2)}) collective-permute-start(f32[3,32,2048]{2,1,0:T(8,128)} %get-tuple-element.39), channel_id=1, source_target_pairs={{0,1},{1,0},{2,3},{3,2},{4,5},{5,4},{6,7},{7,6},{8,9},{9,8},{10,11... | collective-permute-start | bytes 2359304 | tf_op jit(solution)/shard_map/ppermute | solution.py:629
  28.2 14.0 %all_to_all.10.orders = f32[16,16,128]{2,1,0:T(8,128)S(1)} all-to-all(f32[16,16,128]{2,1,0:T(8,128)S(1)} %shard_map.141), channel_id=1, replica_groups=mesh['member'=2,'lateral'=8,'radial'=2] {'lateral','radial'}, dimensions={0} | all-to-all | bytes 262144 | tf_op jit(solution)/shard_map/all_to_all | solution.py:602
  42.3 2.0 %shard_map.143 = (f32[64,512]{1,0:T(8,128)}, f32[16,16,128]{2,1,0:T(8,128)}) custom-call(f32[16,16,128]{2,1,0:T(8,128)S(1)} %all_to_all.10.orders, f32[512,128]{1,0:T(8,128)S(1)} %get-tuple-element.32.response, bf16[512,256]{1,0:T(8,128)(2,1)S(1)} %get-tuple-element.33.wave_high, bf16[512,256]{1,0:T(8,128)(2,1)S(1)} %get-tuple-element.34.wave_low, ...), custom_call_target="tpu_custom_call" | custom-call | bytes 600000000 | tf_op jit(solution)/shard_map/pallas_call | solution.py:634
  44.3 3.5 %all-to-all-start.1 = ((f32[16,16,128]{2,1,0:T(8,128)}), f32[16,16,128]{2,1,0:T(8,128)S(1)}, u32[]{:S(2)}, u32[]{:S(2)}) async-start(f32[16,16,128]{2,1,0:T(8,128)} %get-tuple-element.37), calls=%async_computation.1 | async-start | bytes 262144 | tf_op jit(solution)/shard_map/all_to_all | solution.py:643
  47.8 1.8 %collective-permute-start.6 = (f32[16,2048]{1,0:T(8,128)S(1)}, f32[16,2048]{1,0:T(8,128)S(1)}, u32[]{:S(2)}, u32[]{:S(2)}) collective-permute-start(f32[16,2048]{1,0:T(8,128)S(1)} %get-tuple-element.40), channel_id=1, source_target_pairs={{0,2},{2,0},{4,6},{6,4},{8,10},{10,8},{12,14},{14,12},{1,3},{3,1},... | collective-permute-start | bytes 393224 | tf_op jit(solution)/shard_map/ppermute | solution.py:630
  49.6 0.7 collective-permute-start.7
  50.3 6.3 %collective-permute-done.6.one = f32[16,2048]{1,0:T(8,128)S(1)} collective-permute-done((f32[16,2048]{1,0:T(8,128)S(1)}, f32[16,2048]{1,0:T(8,128)S(1)}, u32[]{:S(2)}, u32[]{:S(2)}) %collective-permute-start.6) | collective-permute-done | bytes 131104 | tf_op jit(solution)/shard_map/ppermute | solution.py:630
  56.5 1.9 %copy-done = f32[3,4,32,2048]{3,2,1,0:T(8,128)S(1)} copy-done((f32[3,4,32,2048]{3,2,1,0:T(8,128)S(1)}, f32[3,4,32,2048]{3,2,1,0:T(8,128)}, u32[]{:S(2)}) %copy-start) | copy-done | bytes 3145752
  58.4 6.5 %shard_map.144 = (f32[3,4,32,2048]{3,2,1,0:T(8,128)}, f32[8,128]{1,0:T(8,128)S(1)}) custom-call(f32[3,4,32,2048]{3,2,1,0:T(8,128)S(1)} %copy-done, f32[3,4,32,2048]{3,2,1,0:T(8,128)} %f.7, f32[4,32,2048]{2,1,0:T(8,128)S(1)} %get-tuple-element.38.h, f32[4,32,2048]{2,1,0:T(8,128)S(1)} %collective-permute-done.2.ring, ...), custom_call_target="tpu_custom_call" | custom-call | bytes 150000000 | tf_op jit(solution)/shard_map/pallas_call | solution.py:645
  65.0 2.7 %shard_map.145 = f32[32,2048]{1,0:T(8,128)} custom-call(f32[16,16,128]{2,1,0:T(8,128)S(1)} %all-to-all-done.1.load, s32[32,2048]{1,0:T(8,128)S(1)} %copy-done.1, bf16[256,1024]{1,0:T(8,128)(2,1)} %constant.12.clone.high_from, bf16[256,1024]{1,0:T(8,128)(2,1)} %constant.13.clone.low_from, f32[8,128]{1,0:T(8,128)S(1)} %get-tuple-element.44.token), custom_call_target="tpu_custom_call" | custom-call | bytes 9000000 | tf_op jit(solution)/shard_map/pallas_call | solution.py:655
  (6 shorter events, 0.0 us)
Async XLA Ops:
  4.2 7.2 %collective-permute-start.2 = (f32[4,32,2048]{2,1,0:T(8,128)S(1)}, f32[4,32,2048]{2,1,0:T(8,128)S(1)}, u32[]{:S(2)}, u32[]{:S(2)}) collective-permute-start(f32[4,32,2048]{2,1,0:T(8,128)S(1)} %get-tuple-element.28), channel_id=1, source_target_pairs={{0,1},{1,0},{2,3},{3,2},{4,5},{5,4},{6,7},{7,6},{8,9},{9,8},{10,11... | collective-permute-start | bytes 3145736 | tf_op jit(solution)/shard_map/ppermute | solution.py:576
  4.7 6.7 %collective-permute-start.3 = (f32[16,2048]{1,0:T(8,128)S(1)}, f32[16,2048]{1,0:T(8,128)S(1)}, u32[]{:S(2)}, u32[]{:S(2)}) collective-permute-start(f32[16,2048]{1,0:T(8,128)S(1)} %get-tuple-element.29), channel_id=1, source_target_pairs={{0,2},{2,0},{4,6},{6,4},{8,10},{10,8},{12,14},{14,12},{1,3},{3,1},... | collective-permute-start | bytes 393224 | tf_op jit(solution)/shard_map/ppermute | solution.py:577
  7.3 4.1 %collective-permute-start.4 = (f32[16,2048]{1,0:T(8,128)S(1)}, f32[16,2048]{1,0:T(8,128)S(1)}, u32[]{:S(2)}, u32[]{:S(2)}) collective-permute-start(f32[16,2048]{1,0:T(8,128)S(1)} %get-tuple-element.30), channel_id=1, source_target_pairs={{2,4},{4,2},{6,8},{8,6},{10,12},{12,10},{3,5},{5,3},{7,9},{9,7},{1... | collective-permute-start | bytes 393224 | tf_op jit(solution)/shard_map/ppermute | solution.py:578
  8.0 1.3 %collective-permute-start.1 = (f32[8,2048]{1,0:T(8,128)S(1)}, f32[8,2048]{1,0:T(8,128)S(1)}, u32[]{:S(2)}, u32[]{:S(2)}) collective-permute-start(f32[8,2048]{1,0:T(8,128)S(1)} %get-tuple-element.26), channel_id=1, source_target_pairs={{3,5},{5,3},{7,9},{9,7},{11,13},{13,11},{19,21},{21,19},{23,25},{2... | collective-permute-start | bytes 196616 | tf_op jit(solution)/shard_map/ppermute | solution.py:555
  8.7 0.7 %collective-permute-start = (f32[8,2048]{1,0:T(8,128)S(1)}, f32[8,2048]{1,0:T(8,128)S(1)}, u32[]{:S(2)}, u32[]{:S(2)}) collective-permute-start(f32[8,2048]{1,0:T(8,128)S(1)} %get-tuple-element.24.token), channel_id=1, source_target_pairs={{1,3},{3,1},{5,7},{7,5},{9,11},{11,9},{13,15},{15,13},{17,19},{19,... | collective-permute-start | bytes 196616 | tf_op jit(solution)/shard_map/ppermute | solution.py:554
  18.7 37.9 %collective-permute-start.5 = (f32[3,32,2048]{2,1,0:T(8,128)}, f32[3,32,2048]{2,1,0:T(8,128)S(1)}, u32[]{:S(2)}, u32[]{:S(2)}) collective-permute-start(f32[3,32,2048]{2,1,0:T(8,128)} %get-tuple-element.39), channel_id=1, source_target_pairs={{0,1},{1,0},{2,3},{3,2},{4,5},{5,4},{6,7},{7,6},{8,9},{9,8},{10,11... | collective-permute-start | bytes 2359304 | tf_op jit(solution)/shard_map/ppermute | solution.py:629
  44.3 20.7 %all-to-all-start.1 = ((f32[16,16,128]{2,1,0:T(8,128)}), f32[16,16,128]{2,1,0:T(8,128)S(1)}, u32[]{:S(2)}, u32[]{:S(2)}) async-start(f32[16,16,128]{2,1,0:T(8,128)} %get-tuple-element.37), calls=%async_computation.1 | async-start | bytes 262144 | tf_op jit(solution)/shard_map/all_to_all | solution.py:643
  47.8 8.7 %collective-permute-start.6 = (f32[16,2048]{1,0:T(8,128)S(1)}, f32[16,2048]{1,0:T(8,128)S(1)}, u32[]{:S(2)}, u32[]{:S(2)}) collective-permute-start(f32[16,2048]{1,0:T(8,128)S(1)} %get-tuple-element.40), channel_id=1, source_target_pairs={{0,2},{2,0},{4,6},{6,4},{8,10},{10,8},{12,14},{14,12},{1,3},{3,1},... | collective-permute-start | bytes 393224 | tf_op jit(solution)/shard_map/ppermute | solution.py:630
  49.6 6.9 %collective-permute-start.7 = (f32[16,2048]{1,0:T(8,128)S(1)}, f32[16,2048]{1,0:T(8,128)S(1)}, u32[]{:S(2)}, u32[]{:S(2)}) collective-permute-start(f32[16,2048]{1,0:T(8,128)S(1)} %get-tuple-element.41), channel_id=1, source_target_pairs={{2,4},{4,2},{6,8},{8,6},{10,12},{12,10},{3,5},{5,3},{7,9},{9,7},{1... | collective-permute-start | bytes 393224 | tf_op jit(solution)/shard_map/ppermute | solution.py:631
  56.5 1.9 %copy-start = (f32[3,4,32,2048]{3,2,1,0:T(8,128)S(1)}, f32[3,4,32,2048]{3,2,1,0:T(8,128)}, u32[]{:S(2)}) copy-start(f32[3,4,32,2048]{3,2,1,0:T(8,128)} %get-tuple-element.31.d) | copy-start | bytes 9437188
  58.4 6.6 %copy-start.1 = (s32[32,2048]{1,0:T(8,128)S(1)}, s32[32,2048]{1,0:T(8,128)}, u32[]{:S(2)}) copy-start(s32[32,2048]{1,0:T(8,128)} %mask.1) | copy-start | bytes 786436

commit v3 on v2

--- a/solution.py
+++ b/solution.py
@@ -220,8 +220,10 @@
         two[place] = jnp.where(odd_band(), up, down)
 
 
-def main_message_kernel(viscosity_from, d, index_from, token, h, one, two, ring, tops, ends, index, viscosity, sems):
-    shells, rows = h.shape[0], h.shape[1]
+def main_message_kernel(
+    viscosity_from, d, index_from, token, eta, one, two, ring, h, tops, ends, index, viscosity, sems, eta_sems
+):
+    shells, rows, _ = h.shape
     components = d.shape[0]
     del token
     shell = jnp.where(lax.axis_index("radial") == 0, shells - 1, 0)
@@ -235,6 +237,7 @@
     for copy in [values] + layers + copies:
         copy.start()
     values.wait()
+    stores = []
     for s in range(shells):
         layers[s].wait()
 
@@ -244,8 +247,10 @@
             return 0
 
         lax.fori_loop(0, rows // TILE, lookup, 0)
-    eta_copy = pltpu.make_async_copy(h.at[shell], ring.at[components], sems.at[3])
-    eta_copy.start()
+        stores.append(pltpu.make_async_copy(h.at[s], eta.at[s], eta_sems.at[s]))
+        stores[-1].start()
+    stores.append(pltpu.make_async_copy(h.at[shell], ring.at[components], sems.at[3]))
+    stores[-1].start()
     for copy in copies[:2]:
         copy.wait()
     for s in range(shells):
@@ -253,8 +258,8 @@
         for c, (down, up) in enumerate(pairs):
             one[c * shells + s] = jnp.where(odd_band(), down, up)
             two[c * shells + s] = jnp.where(odd_band(), up, down)
-    copies[2].wait()
-    eta_copy.wait()
+    for copy in copies[2:] + stores:
+        copy.wait()
 
 
 def surface_kernel(d, f, h, one, two, high_from, low_from, out, field, force, eta, smoothed, high, low, sems):
@@ -350,7 +355,7 @@
             out[block] = pack(fourier[:, block * width : (block + 1) * width])
 
 
-def sweep_shells(d, f, h, ring_field, ring_eta, out, field, eta, force, result, sems, after_shell):
+def sweep_shells(d, f, h, ring_field, ring_eta, out, field, eta, force, result, sems, before_first, after_shell):
     components, shells, rows, count = d.shape
     inner = pl.ds(TILE, rows)
     lower = lax.axis_index("radial") == 0
@@ -376,6 +381,7 @@
     for c in range(components):
         field[c, nothing, inner] = zeros
     eta[nothing, inner] = zeros
+    before_first()
     for copy in halo + loads[0]:
         copy.wait()
     stores = []
@@ -408,29 +414,33 @@
         ref[(*lead, s + 1, rows + TILE)] = after(s)
 
 
-def first_kernel(d, f, h, ring, one, two, *refs):
+def load_messages(sources, slots, sems):
+    copies = [pltpu.make_async_copy(source, slots.at[k], sems.at[k]) for k, source in enumerate(sources)]
+    for copy in copies:
+        copy.start()
+    return copies
+
+
+def first_kernel(
+    d, f, h, ring, one, two, out, ring_out, next_one, next_two, field, eta, force, result, messages, sems, more_sems
+):
     components, shells, rows, _ = d.shape
-    staged = (len(refs) - 11) // 2
-    sources, refs = refs[:staged], refs[staged:]
-    before, after = by_parity(one, two)
-    out, ring_out, next_one, next_two, *targets = refs[: 4 + staged]
-    field, eta, force, result, sems, ring_sems, stage_sems = refs[4 + staged :]
-    stages = [
-        pltpu.make_async_copy(source, target, stage_sems.at[k]) for k, (source, target) in enumerate(zip(sources, targets))
-    ]
     lower = lax.axis_index("radial") == 0
-    row = lambda message, kind: lambda s: message[kind * shells + s]
-    for c in range(components):
-        set_edge(field, (c,), shells, rows, row(before, c), row(after, c))
-    set_edge(eta, (), shells, rows, row(before, components), row(after, components))
-
-    def ring_copies(s):
-        return [pltpu.make_async_copy(result.at[:, s], ring_out, ring_sems.at[0])]
+    arrivals = load_messages((one, two), messages, more_sems)
+
+    def before_first():
+        for copy in arrivals:
+            copy.wait()
+        before, after = by_parity(messages.at[0], messages.at[1])
+        row = lambda message, kind: lambda s: message[kind * shells + s]
+        for c in range(components):
+            set_edge(field, (c,), shells, rows, row(before, c), row(after, c))
+        set_edge(eta, (), shells, rows, row(before, components), row(after, components))
+
+    def ring_copy(s):
+        return pltpu.make_async_copy(result.at[:, s], ring_out, more_sems.at[2])
 
     def after_shell(s):
-        if s == 0:
-            for copy in stages:
-                copy.start()
         for c in range(components):
             down, up = result[c, s, 0], result[c, s, rows - 1]
             next_one[c * shells + s] = jnp.where(odd_band(), down, up)
@@ -439,39 +449,54 @@
 
             @pl.when(lower if s else jnp.logical_not(lower))
             def _():
-                for copy in ring_copies(s):
-                    copy.start()
+                ring_copy(s).start()
 
     sweep_shells(
         d, f, h, [ring.at[c] for c in range(components)], ring.at[components],
-        out, field, eta, force, result, sems, after_shell,
+        out, field, eta, force, result, sems, before_first, after_shell,
     )
-    for copy in ring_copies(0) + stages:
-        copy.wait()
+    ring_copy(0).wait()
 
 
 def second_kernel(
-    d, f, h, ring, ring_two, eta_one, eta_two, one, two, out, token, field, eta, force, result, sems
+    d, f, h, ring, ring_two, eta_one, eta_two, one, two, out, token, field, eta, force, result, messages, eta_messages,
+    sems, more_sems
 ):
     components, shells, rows, _ = d.shape
-    (eta_before, eta_after), (before, after) = by_parity(eta_one, eta_two), by_parity(one, two)
     token[...] = jnp.zeros_like(token)
-    row = lambda message, kind: lambda s: message[kind * shells + s]
-    for c in range(components):
-        set_edge(field, (c,), shells, rows, row(before, c), row(after, c))
-    set_edge(eta, (), shells, rows, row(eta_before, components), row(eta_after, components))
+    arrivals = load_messages((one, two), messages, more_sems.at[0]) + load_messages(
+        (eta_one, eta_two), eta_messages, more_sems.at[1]
+    )
+
+    def before_first():
+        for copy in arrivals:
+            copy.wait()
+        before, after = by_parity(messages.at[0], messages.at[1])
+        row = lambda message, kind: lambda s: message[kind * shells + s]
+        for c in range(components):
+            set_edge(field, (c,), shells, rows, row(before, c), row(after, c))
+        before, after = by_parity(eta_messages.at[0], eta_messages.at[1])
+        set_edge(eta, (), shells, rows, row(before, components), row(after, components))
+
     sweep_shells(
         d, f, h, [ring_two.at[c] for c in range(components)], ring.at[components],
-        out, field, eta, force, result, sems, lambda s: None,
+        out, field, eta, force, result, sems, before_first, lambda s: None,
     )
 
 
-def spectrum_kernel(orders, response, wave_high, wave_low, point_high, point_low, coefficients, out):
+def spectrum_kernel(orders, *refs):
+    sources, (coefficients, out), refs = refs[:5], refs[5:7], refs[7:]
+    copies = [pltpu.make_async_copy(source, refs[k], refs[5].at[k]) for k, source in enumerate(sources)]
+    for copy in copies:
+        copy.start()
+    wave_high, wave_low, point_high, point_low, response = refs[:5]
     radial = lax.axis_size("radial")
     width = coefficients.shape[0]
     bands, rows = orders.shape[0] // radial, point_high.shape[0] * radial // orders.shape[0]
     fourier = jnp.concatenate([unpack(orders[band * radial + radial - 1], width) for band in range(bands)], axis=0)
     high, low = split(fourier)
+    for copy in copies:
+        copy.wait()
     spectrum = dot(wave_high[...], high) + dot(wave_high[...], low) + dot(wave_low[...], high)
     coefficients[...] = spectrum.T
     own = response[:, :width]
@@ -527,9 +552,11 @@
     radial, lateral = lax.axis_size("radial"), lax.axis_size("lateral")
     f32 = functools.partial(jax.ShapeDtypeStruct, dtype=jnp.float32)
     scratch = lambda *shape: pltpu.VMEM(shape, jnp.float32)
+    in_hbm = lambda *shape: pltpu.HBM(shape, jnp.float32)
     width = 2 * MODES // (lateral * radial)
     first = [p for i in range(0, lateral - 1, 2) for p in ((i, i + 1), (i + 1, i))]
     second = [p for i in range(1, lateral - 1, 2) for p in ((i, i + 1), (i + 1, i))]
+    both = ("lateral", "radial")
     top_only = lambda pairs: [(i * radial + radial - 1, j * radial + radial - 1) for i, j in pairs]
 
     tensors = [hbm(a) for a in (initial_displacement, force, layer_index)]
@@ -551,8 +578,8 @@
     )(viscosity, *tensors)
     token = surface_one
     both = ("lateral", "radial")
+    surface_two = lax.ppermute(surface_two, both, top_only(second))
     surface_one = lax.ppermute(surface_one, both, top_only(first))
-    surface_two = lax.ppermute(surface_two, both, top_only(second))
 
     fields = -(-(components + 1) * shells // TILE) * TILE
     message = f32((fields, count))
@@ -560,18 +587,21 @@
     eta, one, two, ring = pl.pallas_call(
         main_message_kernel,
         in_specs=[HBM, HBM, HBM, ANY],
-        out_specs=[VMEM, VMEM, VMEM, ANY],
-        out_shape=[f32((shells, rows, count)), message, message, f32((components + 1, rows, count))],
+        out_specs=[HBM, VMEM, VMEM, VMEM],
+        out_shape=[in_hbm(shells, rows, count), message, message, f32((components + 1, rows, count))],
         scratch_shapes=[
+            scratch(shells, rows, count),
             edge_rows,
             edge_rows,
             pltpu.VMEM(layer_index.shape, jnp.int32),
             pltpu.SMEM(viscosity.shape, jnp.float32),
             pltpu.SemaphoreType.DMA((5 + shells,)),
+            pltpu.SemaphoreType.DMA((shells,)),
         ],
         compiler_params=params(16),
         cost_estimate=cost(20),
     )(viscosity, tensors[0], tensors[2], token)
+    one, two, ring, surface_one, surface_two = lax.optimization_barrier((one, two, ring, surface_one, surface_two))
     swap = [(i, radial - 1 - i) for i in range(radial)]
     ring = lax.ppermute(ring, "radial", swap)
     one = lax.ppermute(one, "lateral", first)
@@ -583,7 +613,7 @@
     packed = (lateral * radial, rows * width // max(128, width), max(128, width))
     orders = pl.pallas_call(
         surface_kernel,
-        in_specs=[HBM, HBM, ANY, VMEM, VMEM, HBM, HBM],
+        in_specs=[HBM, HBM, HBM, VMEM, VMEM, HBM, HBM],
         out_specs=VMEM,
         out_shape=f32(packed),
         scratch_shapes=[
@@ -597,8 +627,9 @@
         ],
         compiler_params=params(24),
         cost_estimate=cost(200),
-    )(*tensors[:2], eta, surface_one, surface_two, high, low)
-    later, _ = lax.optimization_barrier((eta, orders))
+    )(*tensors[:2], hbm(eta), surface_one, surface_two, high, low)
+    orders, one, two, ring = lax.optimization_barrier((orders, one, two, ring))
+    one, two, ring, eta = hbm(one), hbm(two), hbm(ring), hbm(eta)
     orders = lax.all_to_all(orders, both, split_axis=0, concat_axis=0, tiled=True)
 
     sweep_scratch = [
@@ -606,51 +637,56 @@
         scratch(shells + 2, rows + 2 * TILE, count),
         scratch(components, shells, rows, count),
         scratch(components, shells, rows, count),
-        pltpu.SemaphoreType.DMA((shells + 1, 4)),
     ]
+    sweep_sems = pltpu.SemaphoreType.DMA((shells + 1, 4))
     point_high, point_low = colatitude_tables(rows * lateral, MODES)
     stages = [
         jnp.asarray(a)
         for a in (point_high.T.copy(), point_low.T.copy(), point_high, point_low)
     ] + [response]
-    fields = -(-components * shells // TILE) * TILE
-    message = f32((fields, count))
-    smoothed, ring_two, next_one, next_two, *staged = pl.pallas_call(
+    message = f32((-(-components * shells // TILE) * TILE, count))
+    smoothed, ring_two, next_one, next_two = pl.pallas_call(
         first_kernel,
-        in_specs=[HBM, HBM, ANY, ANY, VMEM, VMEM] + [HBM] * len(stages),
-        out_specs=[HBM, ANY, VMEM, VMEM] + [VMEM] * len(stages),
-        out_shape=[pltpu.HBM(initial_displacement.shape, jnp.float32), f32((components, rows, count)), message, message]
-        + [jax.ShapeDtypeStruct(a.shape, a.dtype) for a in stages],
-        scratch_shapes=sweep_scratch
-        + [pltpu.SemaphoreType.DMA((1,)), pltpu.SemaphoreType.DMA((len(stages),))],
+        in_specs=[HBM] * 6,
+        out_specs=[HBM, HBM, VMEM, VMEM],
+        out_shape=[in_hbm(*initial_displacement.shape), in_hbm(components, rows, count), message, message],
+        scratch_shapes=[*sweep_scratch, scratch(2, *one.shape), sweep_sems, pltpu.SemaphoreType.DMA((3,))],
         compiler_params=params(28),
         cost_estimate=cost(50),
-    )(*tensors[:2], later, ring, one, two, *(hbm(a) for a in stages))
+    )(*tensors[:2], eta, ring, one, two)
+    ring_two, next_one, next_two, orders = lax.optimization_barrier((ring_two, next_one, next_two, orders))
     ring_two = lax.ppermute(ring_two, "radial", swap)
     next_one = lax.ppermute(next_one, "lateral", first)
     next_two = lax.ppermute(next_two, "lateral", second)
 
-    *points, response = staged
     coefficients, load = pl.pallas_call(
         spectrum_kernel,
-        in_specs=[VMEM] * 6,
+        in_specs=[VMEM] + [HBM] * 5,
         out_specs=[VMEM, VMEM],
         out_shape=[f32((width, MODES)), f32(packed)],
+        scratch_shapes=[pltpu.VMEM(a.shape, a.dtype) for a in stages] + [pltpu.SemaphoreType.DMA((5,))],
         compiler_params=params(16),
         cost_estimate=cost(200),
-    )(orders, response, *points)
-    later, _ = lax.optimization_barrier((eta, load))
+    )(orders, *(hbm(a) for a in stages))
+    load, ring_two, next_one, next_two = lax.optimization_barrier((load, ring_two, next_one, next_two))
+    eta, load = lax.optimization_barrier((eta, load))
     load = lax.all_to_all(load, both, split_axis=0, concat_axis=0, tiled=True)
 
     displacement, token = pl.pallas_call(
         second_kernel,
-        in_specs=[HBM, HBM, ANY, ANY, ANY, VMEM, VMEM, VMEM, VMEM],
+        in_specs=[HBM] * 9,
         out_specs=[HBM, VMEM],
-        out_shape=[pltpu.HBM(initial_displacement.shape, jnp.float32), f32((TILE, 128))],
-        scratch_shapes=sweep_scratch,
+        out_shape=[in_hbm(*initial_displacement.shape), f32((TILE, 128))],
+        scratch_shapes=[
+            *sweep_scratch,
+            scratch(2, *next_one.shape),
+            scratch(2, *one.shape),
+            sweep_sems,
+            pltpu.SemaphoreType.DMA((2, 2)),
+        ],
         compiler_params=params(28),
         cost_estimate=cost(50),
-    )(smoothed, tensors[1], later, ring, ring_two, one, two, next_one, next_two)
+    )(hbm(smoothed), tensors[1], *(hbm(a) for a in (eta, ring, ring_two, one, two, next_one, next_two)))
 
     sea_load = pl.pallas_call(
         load_kernel,

time: 68.2 us -> 61.1 us (0.90)
  blocking collectives: 14 us -> 0 us
  starting transfers between devices: 20.7 us -> 28.5 us
  Pallas kernels: 22.1 us -> 27.6 us
  waiting for transfers between devices: 8.28 us -> 3.68 us
  local copies, waits for them, and re-layouts: 1.89 us -> 0.03 us
    all_to_all x1 -> x0, blocking collectives: 14 us -> none  [shards(): lax.all_to_all(orders, both, split_axis=0, concat_axis=0, tiled=True)]
    ppermute x1, starting transfers between devices: 9.57 us -> 0.22 us  [shards(): ring_two = lax.ppermute(ring_two, 'radial', swap)]
    all_to_all x0 -> x1, starting transfers between devices: none -> 7.92 us  [shards(): lax.all_to_all(orders, both, split_axis=0, concat_axis=0, tiled=True)]
    ppermute x1, waiting for transfers between devices: 6.27 us -> 0.19 us  [shards(): next_one = lax.ppermute(next_one, 'lateral', first)]
    ppermute x1, starting transfers between devices: 0.52 us -> 6.31 us  [shards(): ring = lax.ppermute(ring, 'radial', swap)]
    all_to_all x1, starting transfers between devices: 3.51 us -> 8.9 us  [shards(): load = lax.all_to_all(load, both, split_axis=0, concat_axis=0, tiled=True)]
    pallas_call x4, Pallas kernels: 15.8 us -> 20.7 us  [the longest x1 8.47 us: shards(): pl.pallas_call(first_kernel, in_specs=[HBM] * 6, out_specs=[HBM, HBM, VME...]
    ppermute x1, starting transfers between devices: 2.59 us -> 0.62 us  [shards(): one = lax.ppermute(one, 'lateral', first)]
  transfers between devices with their start and end apart: 9 -> 10, of which waited for: 2 -> 2; matrix products, arithmetic and copies ran while one was open for 0% -> 0% of each run, Pallas kernels for 13% -> 39%
where the time goes in v3:
time: 61.1 us; the launch traced here: 60.6 us
  starting transfers between devices  28.5 us (47%)
  Pallas kernels  27.6 us (45%)
  waiting for transfers between devices  3.68 us (6%)
  between operations  0.85 us (1%)
    all_to_all x1, starting transfers between devices, shards(): load = lax.all_to_all(load, both, split_axis=0, concat_axis=0, tiled=True)  8.9 us
    pallas_call x1, Pallas kernels, shards(): pl.pallas_call(first_kernel, in_specs=[HBM] * 6, out_specs=[HBM, HBM, VME...  8.47 us
    pallas_call x1, Pallas kernels, shards(): pl.pallas_call(second_kernel, in_specs=[HBM] * 9, out_specs=[HBM, VMEM],...  8.29 us
    all_to_all x1, starting transfers between devices, shards(): lax.all_to_all(orders, both, split_axis=0, concat_axis=0, tiled=True)  7.92 us
    ppermute x1, starting transfers between devices, shards(): ring = lax.ppermute(ring, 'radial', swap)  6.31 us
    ppermute x1, waiting for transfers between devices, shards(): one = lax.ppermute(one, 'lateral', first)  3.47 us
    pallas_call x1, Pallas kernels, shards(): pl.pallas_call(spectrum_kernel, in_specs=[VMEM] + [HBM] * 5, out_specs=[V...  3.23 us
    pallas_call x1, Pallas kernels, shards(): pl.pallas_call(load_kernel, in_specs=[VMEM, VMEM, HBM, HBM, ANY], out_spe...  2.68 us
  transfers between devices with their start and end apart: 10, of which 2 were waited for; matrix products, arithmetic and copies ran while one was open for 0% of the time, Pallas kernels for 39%

profile of v3, /device:TPU:0, one launch (start us, length us, event | category | flops | bytes accessed | tf_op | source)
XLA Modules:
  0.0 60.6 jit_solution(8311167601016161211)
XLA Ops:
  0.6 1.5 %shard_map.139 = (f32[8,2048]{1,0:T(8,128)S(1)}, f32[8,2048]{1,0:T(8,128)S(1)}) custom-call(f32[16]{0:T(128)} %viscosity_from.3, f32[3,4,32,2048]{3,2,1,0:T(8,128)} %d.7, f32[3,4,32,2048]{3,2,1,0:T(8,128)} %f.7, s32[4,32,2048]{2,1,0:T(8,128)} %index_from.1), custom_call_target="tpu_custom_call" | custom-call | bytes 6000000 | tf_op jit(solution)/shard_map/pallas_call | solution.py:564
  2.2 0.7 %collective-permute-start.1 = (f32[8,2048]{1,0:T(8,128)S(1)}, f32[8,2048]{1,0:T(8,128)S(1)}, u32[]{:S(2)}, u32[]{:S(2)}) collective-permute-start(f32[8,2048]{1,0:T(8,128)S(1)} %get-tuple-element.41), channel_id=1, source_target_pairs={{3,5},{5,3},{7,9},{9,7},{11,13},{13,11},{19,21},{21,19},{23,25},{2... | collective-permute-start | bytes 196616 | tf_op jit(solution)/shard_map/ppermute | solution.py:581
  2.9 0.7 %collective-permute-start = (f32[8,2048]{1,0:T(8,128)S(1)}, f32[8,2048]{1,0:T(8,128)S(1)}, u32[]{:S(2)}, u32[]{:S(2)}) collective-permute-start(f32[8,2048]{1,0:T(8,128)S(1)} %get-tuple-element.36.token), channel_id=1, source_target_pairs={{1,3},{3,1},{5,7},{7,5},{9,11},{11,9},{13,15},{15,13},{17,19},{19,... | collective-permute-start | bytes 196616 | tf_op jit(solution)/shard_map/ppermute | solution.py:582
  3.5 2.7 %shard_map.140 = (f32[4,32,2048]{2,1,0:T(8,128)}, f32[16,2048]{1,0:T(8,128)S(1)}, f32[16,2048]{1,0:T(8,128)S(1)}, f32[4,32,2048]{2,1,0:T(8,128)S(1)}) custom-call(f32[16]{0:T(128)} %viscosity_from.3, f32[3,4,32,2048]{3,2,1,0:T(8,128)} %d.7, s32[4,32,2048]{2,1,0:T(8,128)} %index_from.1, f32[8,2048]{1,0:T(8,128)S(1)} %get-tuple-element.36.token), custom_call_target="tpu_custom_call" | custom-call | bytes 60000000 | tf_op jit(solution)/shard_map/pallas_call | solution.py:587
  6.2 0.0 collective-permute-done.1.two
  6.2 0.0 collective-permute-done.one
  6.2 6.3 %collective-permute-start.4 = (f32[4,32,2048]{2,1,0:T(8,128)S(1)}, f32[4,32,2048]{2,1,0:T(8,128)S(1)}, u32[]{:S(2)}, u32[]{:S(2)}) collective-permute-start(f32[4,32,2048]{2,1,0:T(8,128)S(1)} %get-tuple-element.46), channel_id=1, source_target_pairs={{0,1},{1,0},{2,3},{3,2},{4,5},{5,4},{6,7},{7,6},{8,9},{9,8},{10,11... | collective-permute-start | bytes 3145736 | tf_op jit(solution)/shard_map/ppermute | solution.py:606
  12.5 0.6 %collective-permute-start.2 = (f32[16,2048]{1,0:T(8,128)S(1)}, f32[16,2048]{1,0:T(8,128)S(1)}, u32[]{:S(2)}, u32[]{:S(2)}) collective-permute-start(f32[16,2048]{1,0:T(8,128)S(1)} %get-tuple-element.44), channel_id=1, source_target_pairs={{0,2},{2,0},{4,6},{6,4},{8,10},{10,8},{12,14},{14,12},{1,3},{3,1},... | collective-permute-start | bytes 393224 | tf_op jit(solution)/shard_map/ppermute | solution.py:607
  13.1 0.7 %collective-permute-start.3 = (f32[16,2048]{1,0:T(8,128)S(1)}, f32[16,2048]{1,0:T(8,128)S(1)}, u32[]{:S(2)}, u32[]{:S(2)}) collective-permute-start(f32[16,2048]{1,0:T(8,128)S(1)} %get-tuple-element.45), channel_id=1, source_target_pairs={{2,4},{4,2},{6,8},{8,6},{10,12},{12,10},{3,5},{5,3},{7,9},{9,7},{1... | collective-permute-start | bytes 393224 | tf_op jit(solution)/shard_map/ppermute | solution.py:608
  13.8 0.7 %shard_map.141 = f32[16,16,128]{2,1,0:T(8,128)} custom-call(f32[3,4,32,2048]{3,2,1,0:T(8,128)} %d.7, f32[3,4,32,2048]{3,2,1,0:T(8,128)} %f.7, f32[4,32,2048]{2,1,0:T(8,128)} %get-tuple-element.61.h, f32[8,2048]{1,0:T(8,128)S(1)} %collective-permute-done.one, f32[8,2048]{1,0:T(8,128)S(1)} %collective-permute-done.1.two, ...), custom_call_target="tpu_custom_call" | custom-call | bytes 600000000 | tf_op jit(solution)/shard_map/pallas_call | solution.py:614
  14.5 3.5 %collective-permute-done.2.one.eta_one = f32[16,2048]{1,0:T(8,128)S(1)} collective-permute-done((f32[16,2048]{1,0:T(8,128)S(1)}, f32[16,2048]{1,0:T(8,128)S(1)}, u32[]{:S(2)}, u32[]{:S(2)}) %collective-permute-start.2) | collective-permute-done | bytes 131104 | tf_op jit(solution)/shard_map/ppermute | solution.py:607
  18.0 0.0 collective-permute-done.3.two.eta_two
  18.0 0.0 collective-permute-done.4.ring
  18.0 7.9 %all-to-all-start = ((f32[16,16,128]{2,1,0:T(8,128)}), f32[16,16,128]{2,1,0:T(8,128)S(1)}, u32[]{:S(2)}, u32[]{:S(2)}) async-start(f32[16,16,128]{2,1,0:T(8,128)} %shard_map.141), calls=%async_computation | async-start | bytes 262144 | tf_op jit(solution)/shard_map/all_to_all | solution.py:633
  26.0 8.5 %shard_map.142 = (f32[3,4,32,2048]{3,2,1,0:T(8,128)}, f32[3,32,2048]{2,1,0:T(8,128)}, f32[16,2048]{1,0:T(8,128)S(1)}, f32[16,2048]{1,0:T(8,128)S(1)}) custom-call(f32[3,4,32,2048]{3,2,1,0:T(8,128)} %d.7, f32[3,4,32,2048]{3,2,1,0:T(8,128)} %f.7, f32[4,32,2048]{2,1,0:T(8,128)} %get-tuple-element.61.h, f32[4,32,2048]{2,1,0:T(8,128)} %copy-done.1, ...), custom_call_target="tpu_custom_call" | custom-call | bytes 150000000 | tf_op jit(solution)/shard_map/pallas_call | solution.py:648
  34.5 0.2 collective-permute-start.5
  34.7 1.8 %collective-permute-start.6 = (f32[16,2048]{1,0:T(8,128)S(1)}, f32[16,2048]{1,0:T(8,128)S(1)}, u32[]{:S(2)}, u32[]{:S(2)}) collective-permute-start(f32[16,2048]{1,0:T(8,128)S(1)} %get-tuple-element.58), channel_id=1, source_target_pairs={{0,2},{2,0},{4,6},{6,4},{8,10},{10,8},{12,14},{14,12},{1,3},{3,1},... | collective-permute-start | bytes 393224 | tf_op jit(solution)/shard_map/ppermute | solution.py:659
  36.5 0.7 %collective-permute-start.7 = (f32[16,2048]{1,0:T(8,128)S(1)}, f32[16,2048]{1,0:T(8,128)S(1)}, u32[]{:S(2)}, u32[]{:S(2)}) collective-permute-start(f32[16,2048]{1,0:T(8,128)S(1)} %get-tuple-element.59), channel_id=1, source_target_pairs={{2,4},{4,2},{6,8},{8,6},{10,12},{12,10},{3,5},{5,3},{7,9},{9,7},{1... | collective-permute-start | bytes 393224 | tf_op jit(solution)/shard_map/ppermute | solution.py:660
  37.2 3.2 %shard_map.143 = (f32[64,512]{1,0:T(8,128)}, f32[16,16,128]{2,1,0:T(8,128)}) custom-call(f32[16,16,128]{2,1,0:T(8,128)S(1)} %all-to-all-done.orders, bf16[512,256]{1,0:T(8,128)(2,1)} %constant.14.clone.refs_0_, bf16[512,256]{1,0:T(8,128)(2,1)} %constant.15.clone.refs_1_, bf16[256,512]{1,0:T(8,128)(2,1)} %constant.16.clone.refs_2_, ...), custom_call_target="tpu_custom_call" | custom-call | bytes 600000000 | tf_op jit(solution)/shard_map/pallas_call | solution.py:662
  40.4 0.2 collective-permute-done.6.one
  40.7 8.9 %all-to-all-start.1 = ((f32[16,16,128]{2,1,0:T(8,128)}), f32[16,16,128]{2,1,0:T(8,128)S(1)}, u32[]{:S(2)}, u32[]{:S(2)}) async-start(f32[16,16,128]{2,1,0:T(8,128)} %get-tuple-element.67), calls=%async_computation.1 | async-start | bytes 262144 | tf_op jit(solution)/shard_map/all_to_all | solution.py:673
  49.6 0.0 copy-start
  49.6 8.3 %shard_map.144 = (f32[3,4,32,2048]{3,2,1,0:T(8,128)}, f32[8,128]{1,0:T(8,128)S(1)}) custom-call(f32[3,4,32,2048]{3,2,1,0:T(8,128)} %get-tuple-element.50.d, f32[3,4,32,2048]{3,2,1,0:T(8,128)} %f.7, f32[4,32,2048]{2,1,0:T(8,128)} %get-tuple-element.61.h, f32[4,32,2048]{2,1,0:T(8,128)} %copy-done.1, f32[3,32,2048]{2,1,0:T(8,128)} %copy-done.2, ...), custom_call_target="tpu_custom_call" | custom-call | bytes 150000000 | tf_op jit(solution)/shard_map/pallas_call | solution.py:675
  57.9 2.7 %shard_map.145 = f32[32,2048]{1,0:T(8,128)} custom-call(f32[16,16,128]{2,1,0:T(8,128)S(1)} %all-to-all-done.1.load, s32[32,2048]{1,0:T(8,128)S(1)} %copy-done, bf16[256,1024]{1,0:T(8,128)(2,1)} %constant.12.clone.high_from, bf16[256,1024]{1,0:T(8,128)(2,1)} %constant.13.clone.low_from, f32[8,128]{1,0:T(8,128)S(1)} %get-tuple-element.68.token), custom_call_target="tpu_custom_call" | custom-call | bytes 9000000 | tf_op jit(solution)/shard_map/pallas_call | solution.py:691
  (17 shorter events, 0.0 us)
Async XLA Ops:
  2.2 4.0 %collective-permute-start.1 = (f32[8,2048]{1,0:T(8,128)S(1)}, f32[8,2048]{1,0:T(8,128)S(1)}, u32[]{:S(2)}, u32[]{:S(2)}) collective-permute-start(f32[8,2048]{1,0:T(8,128)S(1)} %get-tuple-element.41), channel_id=1, source_target_pairs={{3,5},{5,3},{7,9},{9,7},{11,13},{13,11},{19,21},{21,19},{23,25},{2... | collective-permute-start | bytes 196616 | tf_op jit(solution)/shard_map/ppermute | solution.py:581
  2.9 3.4 %collective-permute-start = (f32[8,2048]{1,0:T(8,128)S(1)}, f32[8,2048]{1,0:T(8,128)S(1)}, u32[]{:S(2)}, u32[]{:S(2)}) collective-permute-start(f32[8,2048]{1,0:T(8,128)S(1)} %get-tuple-element.36.token), channel_id=1, source_target_pairs={{1,3},{3,1},{5,7},{7,5},{9,11},{11,9},{13,15},{15,13},{17,19},{19,... | collective-permute-start | bytes 196616 | tf_op jit(solution)/shard_map/ppermute | solution.py:582
  6.2 11.8 %collective-permute-start.4 = (f32[4,32,2048]{2,1,0:T(8,128)S(1)}, f32[4,32,2048]{2,1,0:T(8,128)S(1)}, u32[]{:S(2)}, u32[]{:S(2)}) collective-permute-start(f32[4,32,2048]{2,1,0:T(8,128)S(1)} %get-tuple-element.46), channel_id=1, source_target_pairs={{0,1},{1,0},{2,3},{3,2},{4,5},{5,4},{6,7},{7,6},{8,9},{9,8},{10,11... | collective-permute-start | bytes 3145736 | tf_op jit(solution)/shard_map/ppermute | solution.py:606
  12.5 5.5 %collective-permute-start.2 = (f32[16,2048]{1,0:T(8,128)S(1)}, f32[16,2048]{1,0:T(8,128)S(1)}, u32[]{:S(2)}, u32[]{:S(2)}) collective-permute-start(f32[16,2048]{1,0:T(8,128)S(1)} %get-tuple-element.44), channel_id=1, source_target_pairs={{0,2},{2,0},{4,6},{6,4},{8,10},{10,8},{12,14},{14,12},{1,3},{3,1},... | collective-permute-start | bytes 393224 | tf_op jit(solution)/shard_map/ppermute | solution.py:607
  13.1 4.9 %collective-permute-start.3 = (f32[16,2048]{1,0:T(8,128)S(1)}, f32[16,2048]{1,0:T(8,128)S(1)}, u32[]{:S(2)}, u32[]{:S(2)}) collective-permute-start(f32[16,2048]{1,0:T(8,128)S(1)} %get-tuple-element.45), channel_id=1, source_target_pairs={{2,4},{4,2},{6,8},{8,6},{10,12},{12,10},{3,5},{5,3},{7,9},{9,7},{1... | collective-permute-start | bytes 393224 | tf_op jit(solution)/shard_map/ppermute | solution.py:608
  18.0 8.0 %copy-start.3 = (f32[16,2048]{1,0:T(8,128)}, f32[16,2048]{1,0:T(8,128)S(1)}, u32[]{:S(2)}) copy-start(f32[16,2048]{1,0:T(8,128)S(1)} %collective-permute-done.2.one.eta_one) | copy-start | bytes 393220
  18.0 8.0 %copy-start.4 = (f32[16,2048]{1,0:T(8,128)}, f32[16,2048]{1,0:T(8,128)S(1)}, u32[]{:S(2)}) copy-start(f32[16,2048]{1,0:T(8,128)S(1)} %collective-permute-done.3.two.eta_two) | copy-start | bytes 393220
  18.0 8.0 %copy-start.1 = (f32[4,32,2048]{2,1,0:T(8,128)}, f32[4,32,2048]{2,1,0:T(8,128)S(1)}, u32[]{:S(2)}) copy-start(f32[4,32,2048]{2,1,0:T(8,128)S(1)} %collective-permute-done.4.ring) | copy-start | bytes 3145732
  18.0 16.4 %all-to-all-start = ((f32[16,16,128]{2,1,0:T(8,128)}), f32[16,16,128]{2,1,0:T(8,128)S(1)}, u32[]{:S(2)}, u32[]{:S(2)}) async-start(f32[16,16,128]{2,1,0:T(8,128)} %shard_map.141), calls=%async_computation | async-start | bytes 262144 | tf_op jit(solution)/shard_map/all_to_all | solution.py:633
  34.5 6.2 %collective-permute-start.5 = (f32[3,32,2048]{2,1,0:T(8,128)}, f32[3,32,2048]{2,1,0:T(8,128)S(1)}, u32[]{:S(2)}, u32[]{:S(2)}) collective-permute-start(f32[3,32,2048]{2,1,0:T(8,128)} %get-tuple-element.57), channel_id=1, source_target_pairs={{0,1},{1,0},{2,3},{3,2},{4,5},{5,4},{6,7},{7,6},{8,9},{9,8},{10,11... | collective-permute-start | bytes 2359304 | tf_op jit(solution)/shard_map/ppermute | solution.py:658
  34.7 5.9 %collective-permute-start.6 = (f32[16,2048]{1,0:T(8,128)S(1)}, f32[16,2048]{1,0:T(8,128)S(1)}, u32[]{:S(2)}, u32[]{:S(2)}) collective-permute-start(f32[16,2048]{1,0:T(8,128)S(1)} %get-tuple-element.58), channel_id=1, source_target_pairs={{0,2},{2,0},{4,6},{6,4},{8,10},{10,8},{12,14},{14,12},{1,3},{3,1},... | collective-permute-start | bytes 393224 | tf_op jit(solution)/shard_map/ppermute | solution.py:659
  36.5 4.1 %collective-permute-start.7 = (f32[16,2048]{1,0:T(8,128)S(1)}, f32[16,2048]{1,0:T(8,128)S(1)}, u32[]{:S(2)}, u32[]{:S(2)}) collective-permute-start(f32[16,2048]{1,0:T(8,128)S(1)} %get-tuple-element.59), channel_id=1, source_target_pairs={{2,4},{4,2},{6,8},{8,6},{10,12},{12,10},{3,5},{5,3},{7,9},{9,7},{1... | collective-permute-start | bytes 393224 | tf_op jit(solution)/shard_map/ppermute | solution.py:660
  40.6 8.9 %copy-start.5 = (f32[16,2048]{1,0:T(8,128)}, f32[16,2048]{1,0:T(8,128)S(1)}, u32[]{:S(2)}) copy-start(f32[16,2048]{1,0:T(8,128)S(1)} %collective-permute-done.6.one) | copy-start | bytes 393220
  40.6 8.9 %copy-start.6 = (f32[16,2048]{1,0:T(8,128)}, f32[16,2048]{1,0:T(8,128)S(1)}, u32[]{:S(2)}) copy-start(f32[16,2048]{1,0:T(8,128)S(1)} %collective-permute-done.7.two) | copy-start | bytes 393220
  40.6 8.9 %copy-start.2 = (f32[3,32,2048]{2,1,0:T(8,128)}, f32[3,32,2048]{2,1,0:T(8,128)S(1)}, u32[]{:S(2)}) copy-start(f32[3,32,2048]{2,1,0:T(8,128)S(1)} %collective-permute-done.5.ring_two) | copy-start | bytes 2359300
  40.7 17.2 %all-to-all-start.1 = ((f32[16,16,128]{2,1,0:T(8,128)}), f32[16,16,128]{2,1,0:T(8,128)S(1)}, u32[]{:S(2)}, u32[]{:S(2)}) async-start(f32[16,16,128]{2,1,0:T(8,128)} %get-tuple-element.67), calls=%async_computation.1 | async-start | bytes 262144 | tf_op jit(solution)/shard_map/all_to_all | solution.py:673
  49.6 8.3 %copy-start = (s32[32,2048]{1,0:T(8,128)S(1)}, s32[32,2048]{1,0:T(8,128)}, u32[]{:S(2)}) copy-start(s32[32,2048]{1,0:T(8,128)} %mask.1) | copy-start | bytes 786436

commit v4 on v3

v4 whole, which is shorter than its diff:
```python
import functools
import math

import jax
import jax.numpy as jnp
import ml_dtypes
import numpy as np
from jax import lax
from jax.experimental import pallas as pl
from jax.experimental.pallas import tpu as pltpu
from jax.sharding import PartitionSpec as P

MODES = 512
RELAXATION = 0.8
TILE = 8
RADIX = 8
MIB = 1 << 20
ANY = pl.BlockSpec(memory_space=pl.ANY)
HBM = pl.BlockSpec(memory_space=pltpu.HBM)
SMEM = pl.BlockSpec(memory_space=pltpu.SMEM)
VMEM = pl.BlockSpec(memory_space=pltpu.VMEM)


def params(mib):
    return pltpu.CompilerParams(vmem_limit_bytes=mib * MIB)


def halves(table):
    high = table.astype(ml_dtypes.bfloat16)
    low = (table - high.astype(np.float64)).astype(ml_dtypes.bfloat16)
    return high, low


@functools.lru_cache
def longitude_tables(count, modes):
    points = np.arange(count // RADIX, dtype=np.int64)[:, None]
    orders = np.arange(modes, dtype=np.int64)[None, :]
    angle = (2.0 * math.pi / count) * (points * orders % count)
    table = np.concatenate([np.cos(angle), np.sin(angle)], axis=1) * math.sqrt(2.0 / count)
    return halves(table)


@functools.lru_cache
def colatitude_tables(count, modes):
    points = np.arange(count, dtype=np.int64)[:, None]
    waves = np.arange(modes, dtype=np.int64)[None, :]
    phase = waves * (2 * points + 1) % (4 * count)
    return halves(np.cos(math.pi / (2 * count) * phase) * math.sqrt(2.0 / count))


def split(values):
    high = values.astype(jnp.bfloat16)
    return high, (values - high.astype(jnp.float32)).astype(jnp.bfloat16)


def dot(a, b):
    return jnp.dot(a, b, preferred_element_type=jnp.float32)


def pack(block):
    rows, width = block.shape
    groups = max(1, 128 // width)
    rows //= groups
    return jnp.concatenate([block[k * rows : (k + 1) * rows] for k in range(groups)], axis=1)


def unpack(block, width):
    groups = max(1, 128 // width)
    return jnp.concatenate([block[:, k * width : (k + 1) * width] for k in range(groups)], axis=0)


def weighted_sum(terms):
    total = None
    for factor, values in terms:
        factor = round(factor, 15)
        if factor == 0.0:
            continue
        part = values if abs(factor) == 1.0 else abs(factor) * values
        if total is None:
            total = part if factor > 0 else -part
        else:
            total = total + part if factor > 0 else total - part
    return total


def turn(number):
    angle = 2.0 * math.pi * (number % RADIX) / RADIX
    return math.cos(angle), math.sin(angle)


def fold(values):
    step = values.shape[1] // RADIX
    parts = [values[:, m * step : (m + 1) * step] for m in range(RADIX)]
    cosines = [[(turn(k * m)[0], part) for m, part in enumerate(parts)] for k in range(RADIX // 2 + 1)]
    sines = [[(turn(k * m)[1], part) for m, part in enumerate(parts)] for k in range(1, RADIX // 2)]
    return [weighted_sum(terms) for terms in cosines + sines]


def unfold(blocks):
    cosines, sines = blocks[: RADIX // 2 + 1], blocks[RADIX // 2 + 1 :]
    return [
        weighted_sum(
            [(turn(k * m)[0], block) for k, block in enumerate(cosines)]
            + [(turn(k * m)[1], block) for k, block in enumerate(sines, 1)]
        )
        for m in range(RADIX)
    ]


def order_class(shape):
    order = lax.broadcasted_iota(jnp.int32, shape, len(shape) - 1) % RADIX
    mirrored = order > RADIX // 2
    return jnp.where(mirrored, RADIX - order, order), mirrored


def dot_nt(a, b):
    return lax.dot_general(a, b, (((1,), (1,)), ((), ())), preferred_element_type=jnp.float32)


def half_viscosity(index, viscosity_ref):
    values = [0.5 * viscosity_ref[k] for k in range(viscosity_ref.shape[0])]
    bit = 1
    while len(values) > 1:
        odd = (index & bit) != 0
        if len(values) % 2:
            values.append(values[-1])
        values = [jnp.where(odd, b, a) for a, b in zip(values[::2], values[1::2])]
        bit *= 2
    return values[0]


def row_number(shape):
    return lax.broadcasted_iota(jnp.int32, shape, 0)


def north_of(above, middle):
    return pltpu.roll(jnp.where(row_number(middle.shape) == TILE - 1, above, middle), 1, 0)


def south_of(below, middle):
    return pltpu.roll(jnp.where(row_number(middle.shape) == 0, below, middle), TILE - 1, 0)


def east_of(values):
    return pltpu.roll(values, values.shape[-1] - 1, values.ndim - 1)


def west_of(values):
    return pltpu.roll(values, 1, values.ndim - 1)


def relax_weights(middle, others):
    weights = [middle + other for other in others]
    diagonal = 1.0 + functools.reduce(jnp.add, weights)
    return weights, RELAXATION / diagonal


def relax(weights, factor, middle, others, force):
    total = force
    for weight, other in zip(weights, others):
        total = total + weight * other
    return (1.0 - RELAXATION) * middle + factor * total


def around(ref, lead, shell, start):
    rows = lambda first: pl.ds(pl.multiple_of(first, TILE), TILE)
    middle = ref[(*lead, shell, rows(start))]
    return middle, [
        ref[(*lead, shell + 1, rows(start))],
        ref[(*lead, shell - 1, rows(start))],
        south_of(ref[(*lead, shell, rows(start + TILE))], middle),
        north_of(ref[(*lead, shell, rows(start - TILE))], middle),
        west_of(middle),
        east_of(middle),
    ]


def odd_band():
    return lax.axis_index("lateral") % 2 == 1


def by_parity(one, two):
    one, two = one[...], two[...]
    return jnp.where(odd_band(), one, two), jnp.where(odd_band(), two, one)


def message_kernel(viscosity_from, d, f, index, one, two, fields, forces, layers, rows_of, viscosity, sems):
    components, shells, rows, count = d.shape
    copies = [pltpu.make_async_copy(viscosity_from, viscosity, sems.at[0])]
    for side, start in enumerate((0, rows - TILE)):
        part = pl.ds(start, TILE)
        copies += [
            pltpu.make_async_copy(index.at[:, part], layers.at[side], sems.at[1 + side]),
            pltpu.make_async_copy(d.at[:, :, part], fields.at[side], sems.at[3 + side]),
            pltpu.make_async_copy(f.at[:, :, part], forces.at[side], sems.at[5 + side]),
        ]
    for copy in copies:
        copy.start()
    for copy in copies[:2] + copies[4:5]:
        copy.wait()
    near_eta, far_eta = 2 * components, 2 * components + 1
    for side, near, far in ((0, 0, 1), (1, TILE - 1, TILE - 2)):
        for s in range(shells):
            eta = half_viscosity(layers[side, s], viscosity)
            rows_of[near_eta, side * shells + s] = eta[near]
            rows_of[far_eta, side * shells + s] = eta[far]
    for copy in copies[2:4] + copies[5:]:
        copy.wait()
    for side, near, far in ((0, 0, 1), (1, TILE - 1, TILE - 2)):
        for s in range(shells):
            for c in range(components):
                rows_of[c, side * shells + s] = fields[side, c, s, near]
                rows_of[components + c, side * shells + s] = fields[side, c, s, far]
                rows_of[far_eta + 1 + c, side * shells + s] = forces[side, c, s, near]
    radial = lax.axis_index("radial")
    place = row_number((2 * shells, count)) % shells
    highest, lowest = place == shells - 1, place == 0
    zero = jnp.zeros((2 * shells, count), jnp.float32)

    def beside(near, far):
        middle = rows_of[near]
        return middle, [
            jnp.where(highest, zero, pltpu.roll(middle, 2 * shells - 1, 0)),
            jnp.where(lowest, zero, pltpu.roll(middle, 1, 0)),
            rows_of[far],
            west_of(middle),
            east_of(middle),
        ]

    eta, others = beside(near_eta, far_eta)
    weights = [eta + other for other in others]
    inside = (radial < lax.axis_size("radial") - 1, radial > 0)
    weights[0] = jnp.where(jnp.logical_and(highest, inside[0]), zero, weights[0])
    weights[1] = jnp.where(jnp.logical_and(lowest, inside[1]), zero, weights[1])
    diagonal = 1.0 + functools.reduce(jnp.add, weights)
    values, sums = [], []
    for c in range(components):
        middle, others = beside(c, components + c)
        total = rows_of[far_eta + 1 + c]
        for weight, other in zip(weights, others):
            total = total + weight * other
        values.append(middle)
        sums.append(total)
    for place, field in enumerate(values + [eta] + sums + [diagonal]):
        both = jnp.where(odd_band(), field, pltpu.roll(field, shells, 0))
        one[pl.ds(place * shells, shells)] = both[:shells]
        two[pl.ds(place * shells, shells)] = both[shells:]


def viscosity_kernel(viscosity_from, d, index_from, token, eta, ring, h, index, viscosity, sems, eta_sems):
    del token
    shells, rows, _ = h.shape
    components = d.shape[0]
    shell = jnp.where(lax.axis_index("radial") == 0, shells - 1, 0)
    copies = [
        pltpu.make_async_copy(viscosity_from, viscosity, sems.at[shells]),
        pltpu.make_async_copy(d.at[:, shell], ring.at[pl.ds(0, components)], sems.at[shells + 1]),
    ]
    layers = [pltpu.make_async_copy(index_from.at[s], index.at[s], sems.at[s]) for s in range(shells)]
    for copy in copies[:1] + layers + copies[1:]:
        copy.start()
    copies[0].wait()
    stores = []
    for s in range(shells):
        layers[s].wait()

        def lookup(step, _):
            part = pl.ds(pl.multiple_of(step * TILE, TILE), TILE)
            h[s, part] = half_viscosity(index[s, part], viscosity)
            return 0

        lax.fori_loop(0, rows // TILE, lookup, 0)
        stores.append(pltpu.make_async_copy(h.at[s], eta.at[s], eta_sems.at[s]))
        stores[-1].start()
    stores.append(pltpu.make_async_copy(h.at[shell], ring.at[components], eta_sems.at[shells]))
    stores[-1].start()
    for copy in copies[1:] + stores:
        copy.wait()


def surface_kernel(d, f, h, one, two, high_from, low_from, out, field, force, eta, smoothed, high, low, sems):
    shells, rows, count = h.shape
    top = lax.axis_size("radial") - 1

    @pl.when(lax.axis_index("radial") == top)
    def _():
        block = pl.ds(TILE, rows)
        copies = [
            pltpu.make_async_copy(d.at[0, pl.ds(shells - 3, 3)], field.at[pl.ds(0, 3), block], sems.at[0]),
            pltpu.make_async_copy(h.at[pl.ds(shells - 3, 3)], eta.at[pl.ds(0, 3), block], sems.at[1]),
            pltpu.make_async_copy(f.at[0, pl.ds(shells - 2, 2)], force, sems.at[2]),
        ]
        tables = [
            pltpu.make_async_copy(high_from, high, sems.at[3]),
            pltpu.make_async_copy(low_from, low, sems.at[4]),
        ]
        for copy in copies + tables:
            copy.start()
        zeros = jnp.zeros((rows, count), jnp.float32)
        field[3, block] = zeros
        eta[3, block] = zeros
        smoothed[2, block] = zeros
        components = d.shape[0]
        before, after = by_parity(one, two)
        inner, weight, partial, diagonal = [
            k * shells for k in (0, components, components + 1, 2 * components + 1)
        ]
        for message, place in ((before, TILE - 1), (after, rows + TILE)):
            for k in (1, 2):
                field[k, place] = message[inner + shells - 3 + k]
                eta[k, place] = message[weight + shells - 3 + k]
        for copy in copies:
            copy.wait()
        lateral = lax.axis_index("lateral")
        inside = (lateral > 0, lateral < lax.axis_size("lateral") - 1)
        for message, own, place, there in (
            (before, TILE, TILE - 1, inside[0]),
            (after, rows + TILE - 1, rows + TILE, inside[1]),
        ):
            row = lambda start: message[start + shells - 1 : start + shells]
            last = row(weight) + eta[2, pl.ds(own, 1)]
            total = row(partial) + last * field[2, pl.ds(own, 1)]
            edge = (1.0 - RELAXATION) * row(inner) + RELAXATION / (row(diagonal) + last) * total
            smoothed[1, pl.ds(place, 1)] = jnp.where(there, edge, jnp.zeros_like(edge))

        def first(step, _):
            start = pl.multiple_of(step * TILE, TILE)
            for s in (1, 2):
                weights, factor = relax_weights(*around(eta, (), s, start + TILE))
                middle, others = around(field, (), s, start + TILE)
                smoothed[s - 1, pl.ds(start + TILE, TILE)] = relax(
                    weights, factor, middle, others, force[s - 1, pl.ds(start, TILE)]
                )
            return 0

        lax.fori_loop(0, rows // TILE, first, 0)

        def second(step, _):
            start = pl.multiple_of(step * TILE, TILE)
            weights, factor = relax_weights(*around(eta, (), 2, start + TILE))
            middle, others = around(smoothed, (), 1, start + TILE)
            field[0, pl.ds(start, TILE)] = relax(weights, factor, middle, others, force[1, pl.ds(start, TILE)])
            return 0

        lax.fori_loop(0, rows // TILE, second, 0)
        near, far = split(jnp.concatenate(fold(field[0, pl.ds(0, rows), :]), axis=0))
        for copy in tables:
            copy.wait()
        total = dot(near, high[...]) + dot(far, high[...]) + dot(near, low[...])
        blocks = [total[k * rows : (k + 1) * rows] for k in range(RADIX)]
        kind, mirrored = order_class((1, total.shape[1]))
        cosine, sine = blocks[0], jnp.zeros_like(blocks[0])
        for k in range(1, RADIX // 2 + 1):
            cosine = jnp.where(kind == k, blocks[k], cosine)
        for k in range(1, RADIX // 2):
            sine = jnp.where(kind == k, blocks[RADIX // 2 + k], sine)
        sine = jnp.where(mirrored, -sine, sine)
        modes = total.shape[1] // 2
        fourier = jnp.concatenate(
            [cosine[:, :modes] - sine[:, modes:], cosine[:, modes:] + sine[:, :modes]], axis=1
        )
        blocks = out.shape[0]
        width = fourier.shape[1] // blocks
        for block in range(blocks):
            out[block] = pack(fourier[:, block * width : (block + 1) * width])


def sweep_shells(d, f, h, ring_field, ring_eta, out, field, eta, force, result, sems, before_first, after_shell):
    components, shells, rows, count = d.shape
    inner = pl.ds(TILE, rows)
    lower = lax.axis_index("radial") == 0
    shell = lambda k: jnp.where(lower, k, shells - 1 - k)
    ring, nothing = jnp.where(lower, shells + 1, 0), jnp.where(lower, 0, shells + 1)

    def field_loads(k):
        if k == shells:
            return [
                pltpu.make_async_copy(ring_eta, eta.at[ring, inner], sems.at[k, components]),
                *(
                    pltpu.make_async_copy(source, field.at[c, ring, inner], sems.at[k, c])
                    for c, source in enumerate(ring_field)
                ),
            ]
        s = shell(k)
        return [
            pltpu.make_async_copy(d.at[:, s], field.at[:, s + 1, inner], sems.at[k, 0]),
            pltpu.make_async_copy(h.at[s], eta.at[s + 1, inner], sems.at[k, 1]),
        ]

    def force_load(k):
        return [pltpu.make_async_copy(f.at[:, shell(k)], force.at[:, shell(k)], sems.at[k, 2])]

    loads = [start_all(field_loads(0)), start_all(field_loads(1))]
    forces = [start_all(force_load(0))]
    loads.append(start_all(field_loads(2)))
    forces.append(start_all(force_load(1)))
    zeros = jnp.zeros((rows, count), jnp.float32)
    for c in range(components):
        field[c, nothing, inner] = zeros
    eta[nothing, inner] = zeros
    before_first()
    for copy in loads[0]:
        copy.wait()
    stores = []
    for k in range(shells):
        s = shell(k)
        if k + 3 <= shells:
            loads.append(start_all(field_loads(k + 3)))
        if k + 2 < shells:
            forces.append(start_all(force_load(k + 2)))
        for copy in loads[k + 1] + forces[k]:
            copy.wait()

        def tile(step, _):
            first = pl.multiple_of(step * TILE, TILE)
            weights, factor = relax_weights(*around(eta, (), s + 1, first + TILE))
            for c in range(components):
                middle, others = around(field, (c,), s + 1, first + TILE)
                result[c, s, pl.ds(first, TILE)] = relax(
                    weights, factor, middle, others, force[c, s, pl.ds(first, TILE)]
                )
            return 0

        lax.fori_loop(0, rows // TILE, tile, 0)
        stores += start_all([pltpu.make_async_copy(result.at[:, s], out.at[:, s], sems.at[k, 3])])
        after_shell(s, k)
    for copy in stores:
        copy.wait()


def set_edge(ref, lead, shells, rows, before, after):
    for s in range(shells):
        ref[(*lead, s + 1, TILE - 1)] = before(s)
        ref[(*lead, s + 1, rows + TILE)] = after(s)


def start_all(copies):
    for copy in copies:
        copy.start()
    return copies


def load_messages(sources, lower_sources, slots, sems):
    lower = lax.axis_index("radial") < lax.axis_size("radial") - 1
    part = pl.ds(0, slots.shape[1])
    copies = lambda refs: [pltpu.make_async_copy(ref.at[part], slots.at[k], sems.at[k]) for k, ref in enumerate(refs)]
    pl.when(lower)(lambda: [copy.start() for copy in copies(lower_sources)] and None)
    pl.when(jnp.logical_not(lower))(lambda: [copy.start() for copy in copies(sources)] and None)
    return copies(sources)


def first_kernel(d, f, h, ring, one, two, lower_one, lower_two, *refs):
    components, shells, rows, _ = d.shape
    staged = (len(refs) - 12) // 2
    sources, refs = refs[:staged], refs[staged:]
    out, ring_out, own_out, *targets = refs[: 3 + staged]
    field, eta, force, result, messages, edges, own, sems, more_sems = refs[3 + staged :]
    arrivals = load_messages((one, two), (lower_one, lower_two), messages, more_sems)
    lower = lax.axis_index("radial") == 0
    copies = []

    def before_first():
        for copy in arrivals:
            copy.wait()
        before, after = by_parity(messages.at[0], messages.at[1])
        row = lambda message, kind: lambda s: message[kind * shells + s]
        for c in range(components):
            set_edge(field, (c,), shells, rows, row(before, c), row(after, c))
        set_edge(eta, (), shells, rows, row(before, components), row(after, components))
        for side, message in enumerate((before, after)):
            for k in range(components + 1):
                edges[side * (components + 1) + k] = jnp.where(
                    lower, message[(k + 1) * shells - 1], message[k * shells]
                )
        tail = ring_out.at[pl.ds(components * rows, edges.shape[0])]
        copies.extend(start_all([pltpu.make_async_copy(edges, tail, more_sems.at[2])]))

    def after_shell(s, k):
        if k == 0:
            stages = [
                pltpu.make_async_copy(source, target, more_sems.at[4 + components + n])
                for n, (source, target) in enumerate(zip(sources, targets))
            ]
            copies.extend(start_all(stages))
        for side, place in enumerate((TILE, TILE + rows - 1)):
            for c in range(components):
                own[c, side * shells + s] = field[c, s + 1, place]
            own[components, side * shells + s] = eta[s + 1, place]
        if k == shells - 1:
            copies.extend(start_all([pltpu.make_async_copy(own, own_out, more_sems.at[3])]))
            copies.extend(
                start_all(
                    [
                        pltpu.make_async_copy(
                            result.at[c, s], ring_out.at[pl.ds(c * rows, rows)], more_sems.at[4 + c]
                        )
                        for c in range(components)
                    ]
                )
            )

    sweep_shells(
        d, f, h, [ring.at[c] for c in range(components)], ring.at[components],
        out, field, eta, force, result, sems, before_first, after_shell,
    )
    for copy in copies:
        copy.wait()


def second_kernel(d, f, h, ring, ring_two, one, two, lower_one, lower_two, own_from, *refs):
    components, shells, rows, count = d.shape
    staged = (len(refs) - 11) // 2
    sources, refs = refs[:staged], refs[staged:]
    out, token, *targets = refs[: 2 + staged]
    field, eta, force, result, messages, edges, own, sems, more_sems = refs[2 + staged :]
    token[...] = jnp.zeros_like(token)
    arrivals = load_messages((one, two), (lower_one, lower_two), messages, more_sems)
    tail = ring_two.at[pl.ds(components * rows, edges.shape[0])]
    arrivals += start_all(
        [
            pltpu.make_async_copy(tail, edges, more_sems.at[2]),
            pltpu.make_async_copy(own_from, own, more_sems.at[3]),
        ]
    )
    radial, lateral = lax.axis_index("radial"), lax.axis_index("lateral")
    copies = []

    def before_first():
        for copy in arrivals:
            copy.wait()
        before, after = by_parity(messages.at[0], messages.at[1])
        pair = lambda k: jnp.concatenate(
            [before[k * shells : (k + 1) * shells], after[k * shells : (k + 1) * shells]], axis=0
        )
        place = row_number((2 * shells, count))
        zero = jnp.zeros((2 * shells, count), jnp.float32)
        shared = place % shells == jnp.where(radial == 0, shells - 1, 0)
        beyond = lambda k: jnp.where(
            place < shells, edges[pl.ds(k, 1)], edges[pl.ds(components + 1 + k, 1)]
        )
        inside = jnp.where(place < shells, lateral, lax.axis_size("lateral") - 1 - lateral) > 0
        middle = pair(components)
        weight = middle + own[components]
        across = jnp.where(shared, middle + beyond(components), zero)
        factor = RELAXATION / (pair(2 * components + 1) + weight + across)
        for c in range(components):
            total = pair(components + 1 + c) + weight * own[c] + across * beyond(c)
            edge = jnp.where(inside, (1.0 - RELAXATION) * pair(c) + factor * total, zero)
            set_edge(field, (c,), shells, rows, lambda s: edge[s], lambda s: edge[shells + s])
        set_edge(eta, (), shells, rows, lambda s: middle[s], lambda s: middle[shells + s])

    def after_shell(s, k):
        if k == 0:
            stages = [
                pltpu.make_async_copy(source, target, more_sems.at[4 + n])
                for n, (source, target) in enumerate(zip(sources, targets))
            ]
            copies.extend(start_all(stages))

    sweep_shells(
        d, f, h, [ring_two.at[pl.ds(c * rows, rows)] for c in range(components)], ring.at[components],
        out, field, eta, force, result, sems, before_first, after_shell,
    )
    for copy in copies:
        copy.wait()


def spectrum_kernel(orders, wave_high, wave_low, point_high, point_low, response, coefficients, out):
    radial = lax.axis_size("radial")
    width = coefficients.shape[0]
    bands, rows = orders.shape[0] // radial, point_high.shape[0] * radial // orders.shape[0]
    fourier = jnp.concatenate([unpack(orders[band * radial + radial - 1], width) for band in range(bands)], axis=0)
    high, low = split(fourier)
    spectrum = dot(wave_high[...], high) + dot(wave_high[...], low) + dot(wave_low[...], high)
    coefficients[...] = spectrum.T
    own = response[:, :width]
    for place in range(1, radial):
        own = jnp.where(
            lax.axis_index("radial") == place, response[:, place * width : (place + 1) * width], own
        )
    high, low = split(own * spectrum)
    load = dot(point_high[...], high) + dot(point_high[...], low) + dot(point_low[...], high)
    for band in range(bands):
        block = pack(load[band * rows : (band + 1) * rows])
        for place in range(radial):
            out[band * radial + place] = block


def load_kernel(load, high, low, mask, out):
    blocks, rows = load.shape[0], out.shape[0]
    step, width = out.shape[1] // RADIX, high.shape[1] // blocks
    values = jnp.concatenate([unpack(load[block], width) for block in range(blocks)], axis=1)
    modes = values.shape[1] // 2
    kind, mirrored = order_class((1, values.shape[1]))
    crossed = jnp.concatenate([values[:, modes:], -values[:, :modes]], axis=1)
    crossed = jnp.where(mirrored, -crossed, crossed)
    zero = jnp.zeros_like(values)
    stack = [jnp.where(kind == k, values, zero) for k in range(RADIX // 2 + 1)]
    stack += [jnp.where(kind == k, crossed, zero) for k in range(1, RADIX // 2)]
    near, far = split(jnp.concatenate(stack, axis=0))
    total = dot_nt(near, high[...]) + dot_nt(far, high[...]) + dot_nt(near, low[...])
    for m, part in enumerate(unfold([total[k * rows : (k + 1) * rows] for k in range(RADIX)])):
        columns = slice(m * step, (m + 1) * step)
        out[:, columns] = part * mask[:, columns].astype(jnp.float32)


def cost(microseconds):
    return pl.CostEstimate(flops=0, bytes_accessed=3_000_000 * microseconds, transcendentals=0)


def hbm(values):
    return pltpu.with_memory_space_constraint(values, pltpu.HBM)


def shards(initial_displacement, force, viscosity, layer_index, response, ocean_mask):
    components, shells, rows, count = initial_displacement.shape
    radial, lateral = lax.axis_size("radial"), lax.axis_size("lateral")
    f32 = functools.partial(jax.ShapeDtypeStruct, dtype=jnp.float32)
    scratch = lambda *shape: pltpu.VMEM(shape, jnp.float32)
    in_hbm = lambda *shape: pltpu.HBM(shape, jnp.float32)
    width = 2 * MODES // (lateral * radial)
    first = [p for i in range(0, lateral - 1, 2) for p in ((i, i + 1), (i + 1, i))]
    second = [p for i in range(1, lateral - 1, 2) for p in ((i, i + 1), (i + 1, i))]
    both = ("lateral", "radial")
    top_only = lambda pairs: [(i * radial + radial - 1, j * radial + radial - 1) for i, j in pairs]

    lower_only = lambda pairs: [(i * radial + k, j * radial + k) for i, j in pairs for k in range(radial - 1)]
    tensors = [hbm(a) for a in (initial_displacement, force, layer_index)]
    viscosity = hbm(viscosity)
    message = f32((2 * (components + 1) * shells, count))
    sides = lambda *shape: scratch(2, *shape)
    mine = pl.pallas_call(
        message_kernel,
        in_specs=[HBM] * 4,
        out_specs=[VMEM] * 2,
        out_shape=[message] * 2,
        scratch_shapes=[
            sides(components, shells, TILE, count),
            sides(components, shells, TILE, count),
            pltpu.VMEM((2, shells, TILE, count), jnp.int32),
            scratch(3 * components + 2, 2 * shells, count),
            pltpu.SMEM(viscosity.shape, jnp.float32),
            pltpu.SemaphoreType.DMA((7,)),
        ],
        compiler_params=params(16),
        cost_estimate=cost(20),
    )(viscosity, *tensors)
    two = lax.ppermute(mine[1], both, top_only(second))
    one = lax.ppermute(mine[0], both, top_only(first))
    eta, ring = pl.pallas_call(
        viscosity_kernel,
        in_specs=[HBM, HBM, HBM, ANY],
        out_specs=[HBM, VMEM],
        out_shape=[in_hbm(shells, rows, count), f32((components + 1, rows, count))],
        scratch_shapes=[
            scratch(shells, rows, count),
            pltpu.VMEM(layer_index.shape, jnp.int32),
            pltpu.SMEM(viscosity.shape, jnp.float32),
            pltpu.SemaphoreType.DMA((2 + shells,)),
            pltpu.SemaphoreType.DMA((1 + shells,)),
        ],
        compiler_params=params(12),
        cost_estimate=cost(20),
    )(viscosity, tensors[0], tensors[2], mine[0])
    ring, lower_one, lower_two, one, two = lax.optimization_barrier((ring, *mine, one, two))
    swap = [(i, radial - 1 - i) for i in range(radial)]
    ring = lax.ppermute(ring, "radial", swap)
    lower_one = lax.ppermute(lower_one, both, lower_only(first))
    lower_two = lax.ppermute(lower_two, both, lower_only(second))

    high, low = longitude_tables(count, MODES)
    high, low = hbm(jnp.asarray(high)), hbm(jnp.asarray(low))
    table = pltpu.VMEM(high.shape, jnp.bfloat16)
    packed = (lateral * radial, rows * width // max(128, width), max(128, width))
    orders = pl.pallas_call(
        surface_kernel,
        in_specs=[HBM, HBM, HBM, VMEM, VMEM, HBM, HBM],
        out_specs=VMEM,
        out_shape=f32(packed),
        scratch_shapes=[
            scratch(4, rows + 2 * TILE, count),
            scratch(2, rows, count),
            scratch(4, rows + 2 * TILE, count),
            scratch(3, rows + 2 * TILE, count),
            table,
            table,
            pltpu.SemaphoreType.DMA((5,)),
        ],
        compiler_params=params(24),
        cost_estimate=cost(200),
    )(*tensors[:2], hbm(eta), one, two, high, low)
    orders, ring, lower_one, lower_two = lax.optimization_barrier((orders, ring, lower_one, lower_two))
    messages = [hbm(a) for a in (one, two, lower_one, lower_two)]
    ring, eta = hbm(ring), hbm(eta)
    orders = lax.all_to_all(orders, both, split_axis=0, concat_axis=0, tiled=True)

    sweep_scratch = [
        scratch(components, shells + 2, rows + 2 * TILE, count),
        scratch(shells + 2, rows + 2 * TILE, count),
        scratch(components, shells, rows, count),
        scratch(components, shells, rows, count),
    ]
    sweep_sems = pltpu.SemaphoreType.DMA((shells + 1, components + 1))
    point_high, point_low = colatitude_tables(rows * lateral, MODES)
    stages = [
        jnp.asarray(a)
        for a in (point_high.T.copy(), point_low.T.copy(), point_high, point_low)
    ] + [response]
    ring_rows = components * rows + 2 * (components + 1)
    own_rows = scratch(components + 1, 2 * shells, count)
    smoothed, ring_two, own, *staged = pl.pallas_call(
        first_kernel,
        in_specs=[HBM] * (8 + len(stages)),
        out_specs=[HBM] * 3 + [VMEM] * len(stages),
        out_shape=[
            in_hbm(*initial_displacement.shape),
            in_hbm(ring_rows, count),
            in_hbm(components + 1, 2 * shells, count),
            *(jax.ShapeDtypeStruct(a.shape, a.dtype) for a in stages),
        ],
        scratch_shapes=[
            *sweep_scratch,
            sides((components + 1) * shells, count),
            scratch(2 * (components + 1), count),
            own_rows,
            sweep_sems,
            pltpu.SemaphoreType.DMA((4 + components + len(stages),)),
        ],
        compiler_params=params(28),
        cost_estimate=cost(50),
    )(*tensors[:2], eta, ring, *messages, *(hbm(a) for a in stages))
    ring_two, orders = lax.optimization_barrier((ring_two, orders))
    ring_two = lax.ppermute(ring_two, "radial", swap)
    coefficients, load = pl.pallas_call(
        spectrum_kernel,
        in_specs=[VMEM] * 6,
        out_specs=[VMEM, VMEM],
        out_shape=[f32((width, MODES)), f32(packed)],
        compiler_params=params(16),
        cost_estimate=cost(200),
    )(orders, *staged)
    load, ring_two = lax.optimization_barrier((load, ring_two))
    eta, load = lax.optimization_barrier((eta, load))
    load = lax.all_to_all(load, both, split_axis=0, concat_axis=0, tiled=True)

    stages = [high, low, hbm(ocean_mask)]
    displacement, token, *staged = pl.pallas_call(
        second_kernel,
        in_specs=[HBM] * (10 + len(stages)),
        out_specs=[HBM, VMEM] + [VMEM] * len(stages),
        out_shape=[
            in_hbm(*initial_displacement.shape),
            f32((TILE, 128)),
            *(jax.ShapeDtypeStruct(a.shape, a.dtype) for a in stages),
        ],
        scratch_shapes=[
            *sweep_scratch,
            sides(message.shape[0], count),
            scratch(2 * (components + 1), count),
            own_rows,
            sweep_sems,
            pltpu.SemaphoreType.DMA((4 + len(stages),)),
        ],
        compiler_params=params(28),
        cost_estimate=cost(50),
    )(hbm(smoothed), tensors[1], hbm(eta), ring, hbm(ring_two), *messages, hbm(own), *stages)

    sea_load = pl.pallas_call(
        load_kernel,
        in_specs=[VMEM] * 4,
        out_specs=VMEM,
        out_shape=f32((rows, count)),
        compiler_params=params(20),
        cost_estimate=cost(3),
    )(load, *staged)
    return (displacement, coefficients.T, sea_load)


def solution(mesh):
    in_specs = (
        P("member", "radial", "lateral", None),
        P("member", "radial", "lateral", None),
        P("member"),
        P("radial", "lateral", None),
        P(None, "lateral"),
        P("lateral", None),
    )
    out_specs = (
        P("member", "radial", "lateral", None),
        P("member", ("lateral", "radial")),
        P("lateral", "member"),
    )
    return jax.shard_map(shards, mesh=mesh, in_specs=in_specs, out_specs=out_specs, check_vma=False)
```

time: 61.1 us -> 58.9 us (0.964)
  Pallas kernels: 27.6 us -> 25.7 us
    all_to_all x1, starting transfers between devices: 8.9 us -> 5.76 us  [shards(): load = lax.all_to_all(load, both, split_axis=0, concat_axis=0, tiled=True)]
    pallas_call x6, Pallas kernels: 26.9 us -> 24.9 us  [the longest x1 8.63 us: shards(): pl.pallas_call(second_kernel, in_specs=[HBM] * (10 + len(stages)), out_sp...]
    ppermute x1, starting transfers between devices: 6.31 us -> 7.39 us  [shards(): ring = lax.ppermute(ring, 'radial', swap)]
    ppermute x6 -> x4, starting transfers between devices: 5.11 us -> 6.11 us  [the longest x1 4.08 us: shards(): lower_one = lax.ppermute(lower_one, both, lower_only(first))]
    all_to_all x1, starting transfers between devices: 7.92 us -> 8.79 us  [shards(): lax.all_to_all(orders, both, split_axis=0, concat_axis=0, tiled=True)]
    ppermute x6 -> x4, waiting for transfers between devices: 3.67 us -> 2.92 us  [the longest x1 2.91 us: shards(): lower_one = lax.ppermute(lower_one, both, lower_only(first))]
  transfers between devices with their start and end apart: 10 -> 8, of which waited for: 2 -> 3; matrix products, arithmetic and copies ran while one was open for 0% -> 0% of each run, Pallas kernels for 39% -> 37%
where the time goes in v4:
time: 58.9 us; the launch traced here: 58.5 us
  starting transfers between devices  28.8 us (49%)
  Pallas kernels  25.7 us (44%)
  waiting for transfers between devices  3.22 us (5%)
  between operations  0.82 us (1%)
    all_to_all x1, starting transfers between devices, shards(): lax.all_to_all(orders, both, split_axis=0, concat_axis=0, tiled=True)  8.79 us
    pallas_call x1, Pallas kernels, shards(): pl.pallas_call(second_kernel, in_specs=[HBM] * (10 + len(stages)), out_sp...  8.63 us
    pallas_call x1, Pallas kernels, shards(): pl.pallas_call(first_kernel, in_specs=[HBM] * (8 + len(stages)), out_spec...  7.83 us
    ppermute x1, starting transfers between devices, shards(): ring = lax.ppermute(ring, 'radial', swap)  7.39 us
    all_to_all x1, starting transfers between devices, shards(): load = lax.all_to_all(load, both, split_axis=0, concat_axis=0, tiled=True)  5.76 us
    ppermute x1, starting transfers between devices, shards(): lower_one = lax.ppermute(lower_one, both, lower_only(first))  4.08 us
    ppermute x1, waiting for transfers between devices, shards(): lower_one = lax.ppermute(lower_one, both, lower_only(first))  2.91 us
    pallas_call x1, Pallas kernels, shards(): pl.pallas_call(viscosity_kernel, in_specs=[HBM, HBM, HBM, ANY], out_specs...  2.63 us
  transfers between devices with their start and end apart: 8, of which 3 were waited for; matrix products, arithmetic and copies ran while one was open for 0% of the time, Pallas kernels for 37%

profile of v4, /device:TPU:0, one launch (start us, length us, event | category | flops | bytes accessed | tf_op | source)
XLA Modules:
  0.0 58.5 jit_solution(183693631838507849)
XLA Ops:
  0.6 2.4 %shard_map.139 = (f32[32,2048]{1,0:T(8,128)S(1)}, f32[32,2048]{1,0:T(8,128)S(1)}) custom-call(f32[16]{0:T(128)} %viscosity_from.3, f32[3,4,32,2048]{3,2,1,0:T(8,128)} %d.7, f32[3,4,32,2048]{3,2,1,0:T(8,128)} %f.7, s32[4,32,2048]{2,1,0:T(8,128)} %index_from.1), custom_call_target="tpu_custom_call" | custom-call | bytes 60000000 | tf_op jit(solution)/shard_map/pallas_call | solution.py:632
  3.1 0.7 %collective-permute-start.1 = (f32[32,2048]{1,0:T(8,128)S(1)}, f32[32,2048]{1,0:T(8,128)S(1)}, u32[]{:S(2)}, u32[]{:S(2)}) collective-permute-start(f32[32,2048]{1,0:T(8,128)S(1)} %get-tuple-element.44), channel_id=1, source_target_pairs={{3,5},{5,3},{7,9},{9,7},{11,13},{13,11},{19,21},{21,19},{23,25},{2... | collective-permute-start | bytes 786440 | tf_op jit(solution)/shard_map/ppermute | solution.py:648
  3.8 0.7 %collective-permute-start = (f32[32,2048]{1,0:T(8,128)S(1)}, f32[32,2048]{1,0:T(8,128)S(1)}, u32[]{:S(2)}, u32[]{:S(2)}) collective-permute-start(f32[32,2048]{1,0:T(8,128)S(1)} %get-tuple-element.43.token), channel_id=1, source_target_pairs={{1,3},{3,1},{5,7},{7,5},{9,11},{11,9},{13,15},{15,13},{17,19},{19,... | collective-permute-start | bytes 786440 | tf_op jit(solution)/shard_map/ppermute | solution.py:649
  4.4 2.6 %shard_map.140 = (f32[4,32,2048]{2,1,0:T(8,128)}, f32[4,32,2048]{2,1,0:T(8,128)S(1)}) custom-call(f32[16]{0:T(128)} %viscosity_from.3, f32[3,4,32,2048]{3,2,1,0:T(8,128)} %d.7, s32[4,32,2048]{2,1,0:T(8,128)} %index_from.1, f32[32,2048]{1,0:T(8,128)S(1)} %get-tuple-element.43.token), custom_call_target="tpu_custom_call" | custom-call | bytes 60000000 | tf_op jit(solution)/shard_map/pallas_call | solution.py:650
  7.1 0.0 collective-permute-done.1.two
  7.1 0.0 collective-permute-done.one
  7.1 0.0 copy-start.1
  7.1 7.4 %collective-permute-start.2 = (f32[4,32,2048]{2,1,0:T(8,128)S(1)}, f32[4,32,2048]{2,1,0:T(8,128)S(1)}, u32[]{:S(2)}, u32[]{:S(2)}) collective-permute-start(f32[4,32,2048]{2,1,0:T(8,128)S(1)} %get-tuple-element.42), channel_id=1, source_target_pairs={{0,1},{1,0},{2,3},{3,2},{4,5},{5,4},{6,7},{7,6},{8,9},{9,8},{10,11... | collective-permute-start | bytes 3145736 | tf_op jit(solution)/shard_map/ppermute | solution.py:667
  14.5 4.1 %collective-permute-start.3 = (f32[32,2048]{1,0:T(8,128)S(1)}, f32[32,2048]{1,0:T(8,128)S(1)}, u32[]{:S(2)}, u32[]{:S(2)}) collective-permute-start(f32[32,2048]{1,0:T(8,128)S(1)} %get-tuple-element.43.token), channel_id=1, source_target_pairs={{0,2},{2,0},{4,6},{6,4},{8,10},{10,8},{12,14},{14,12},{16,18},{18,... | collective-permute-start | bytes 786440 | tf_op jit(solution)/shard_map/ppermute | solution.py:668
  18.6 0.7 %collective-permute-start.4 = (f32[32,2048]{1,0:T(8,128)S(1)}, f32[32,2048]{1,0:T(8,128)S(1)}, u32[]{:S(2)}, u32[]{:S(2)}) collective-permute-start(f32[32,2048]{1,0:T(8,128)S(1)} %get-tuple-element.44), channel_id=1, source_target_pairs={{2,4},{4,2},{6,8},{8,6},{10,12},{12,10},{18,20},{20,18},{22,24},{2... | collective-permute-start | bytes 786440 | tf_op jit(solution)/shard_map/ppermute | solution.py:669
  19.3 0.7 %shard_map.141 = f32[16,16,128]{2,1,0:T(8,128)} custom-call(f32[3,4,32,2048]{3,2,1,0:T(8,128)} %d.7, f32[3,4,32,2048]{3,2,1,0:T(8,128)} %f.7, f32[4,32,2048]{2,1,0:T(8,128)} %get-tuple-element.60.h, f32[32,2048]{1,0:T(8,128)S(1)} %collective-permute-done.one, f32[32,2048]{1,0:T(8,128)S(1)} %collective-permute-done.1.two, ...), custom_call_target="tpu_custom_call" | custom-call | bytes 600000000 | tf_op jit(solution)/shard_map/pallas_call | solution.py:675
  20.0 2.9 %collective-permute-done.3.lower_one = f32[32,2048]{1,0:T(8,128)S(1)} collective-permute-done((f32[32,2048]{1,0:T(8,128)S(1)}, f32[32,2048]{1,0:T(8,128)S(1)}, u32[]{:S(2)}, u32[]{:S(2)}) %collective-permute-start.3) | collective-permute-done | bytes 262176 | tf_op jit(solution)/shard_map/ppermute | solution.py:668
  22.9 0.0 collective-permute-done.4.lower_two
  23.0 0.0 collective-permute-done.2.ring
  23.0 8.8 %all-to-all-start = ((f32[16,16,128]{2,1,0:T(8,128)}), f32[16,16,128]{2,1,0:T(8,128)S(1)}, u32[]{:S(2)}, u32[]{:S(2)}) async-start(f32[16,16,128]{2,1,0:T(8,128)} %shard_map.141), calls=%async_computation | async-start | bytes 262144 | tf_op jit(solution)/shard_map/all_to_all | solution.py:695
  31.8 7.8 %shard_map.142 = (f32[3,4,32,2048]{3,2,1,0:T(8,128)}, f32[104,2048]{1,0:T(8,128)}, f32[4,8,2048]{2,1,0:T(8,128)}, bf16[512,256]{1,0:T(8,128)(2,1)S(1)}, bf16[512...) custom-call(f32[3,4,32,2048]{3,2,1,0:T(8,128)} %d.7, ...), custom_call_target="tpu_custom_call" | custom-call | bytes 150000000 | tf_op jit(solution)/shard_map/pallas_call | solution.py:711
  39.6 0.1 all-to-all-done.orders
  39.7 0.7 %collective-permute-start.5 = (f32[104,2048]{1,0:T(8,128)}, f32[104,2048]{1,0:T(8,128)S(1)}, u32[]{:S(2)}, u32[]{:S(2)}) collective-permute-start(f32[104,2048]{1,0:T(8,128)} %get-tuple-element.58), channel_id=1, source_target_pairs={{0,1},{1,0},{2,3},{3,2},{4,5},{5,4},{6,7},{7,6},{8,9},{9,8},{10,11... | collective-permute-start | bytes 2555912 | tf_op jit(solution)/shard_map/ppermute | solution.py:733
  40.4 2.0 %shard_map.143 = (f32[64,512]{1,0:T(8,128)}, f32[16,16,128]{2,1,0:T(8,128)}) custom-call(f32[16,16,128]{2,1,0:T(8,128)S(1)} %all-to-all-done.orders, bf16[512,256]{1,0:T(8,128)(2,1)S(1)} %get-tuple-element.52.wave_high, bf16[512,256]{1,0:T(8,128)(2,1)S(1)} %get-tuple-element.53.wave_low, bf16[256,512]{1,0:T(8,128)(2,1)S(1)} %get-tuple-element.54.point_high, ...), custom_call_target="tpu_custom_call" | custom-call | bytes 600000000 | tf_op jit(solution)/shard_map/pallas_call | solution.py:734
  42.4 0.2 collective-permute-done.5.ring_two
  42.7 5.8 %all-to-all-start.1 = ((f32[16,16,128]{2,1,0:T(8,128)}), f32[16,16,128]{2,1,0:T(8,128)S(1)}, u32[]{:S(2)}, u32[]{:S(2)}) async-start(f32[16,16,128]{2,1,0:T(8,128)} %get-tuple-element.65), calls=%async_computation.1 | async-start | bytes 262144 | tf_op jit(solution)/shard_map/all_to_all | solution.py:744
  48.4 8.6 %shard_map.144 = (f32[3,4,32,2048]{3,2,1,0:T(8,128)}, f32[8,128]{1,0:T(8,128)}, bf16[256,1024]{1,0:T(8,128)(2,1)S(1)}, bf16[256,1024]{1,0:T(8,128)(2,1)S(1)}, s32[32,2048]{1,0:T(8,128)S(1)}) custom-call(f32[3,4,32,2048]{3,2,1,0:T(8,128)} %get-tuple-element.48.d, f32[3,4,32,2048]{3,2,1,0:T(8,128)} %f.7, f32[4,32,2048]{2,1,0:T(8,128)} %get-tuple-element.60.h, ...), custom_call_target="tpu_custom_call" | custom-call | bytes 150000000 | tf_op jit(solution)/shard_map/pallas_call | solution.py:747
  57.1 0.0 all-to-all-done.1.load
  57.1 1.4 %shard_map.145 = f32[32,2048]{1,0:T(8,128)} custom-call(f32[16,16,128]{2,1,0:T(8,128)S(1)} %all-to-all-done.1.load, bf16[256,1024]{1,0:T(8,128)(2,1)S(1)} %get-tuple-element.66.high, bf16[256,1024]{1,0:T(8,128)(2,1)S(1)} %get-tuple-element.67.low, s32[32,2048]{1,0:T(8,128)S(1)} %get-tuple-element.68.mask), custom_call_target="tpu_custom_call" | custom-call | bytes 9000000 | tf_op jit(solution)/shard_map/pallas_call | solution.py:768
  (11 shorter events, 0.0 us)
Async XLA Ops:
  3.1 4.0 %collective-permute-start.1 = (f32[32,2048]{1,0:T(8,128)S(1)}, f32[32,2048]{1,0:T(8,128)S(1)}, u32[]{:S(2)}, u32[]{:S(2)}) collective-permute-start(f32[32,2048]{1,0:T(8,128)S(1)} %get-tuple-element.44), channel_id=1, source_target_pairs={{3,5},{5,3},{7,9},{9,7},{11,13},{13,11},{19,21},{21,19},{23,25},{2... | collective-permute-start | bytes 786440 | tf_op jit(solution)/shard_map/ppermute | solution.py:648
  3.8 3.4 %collective-permute-start = (f32[32,2048]{1,0:T(8,128)S(1)}, f32[32,2048]{1,0:T(8,128)S(1)}, u32[]{:S(2)}, u32[]{:S(2)}) collective-permute-start(f32[32,2048]{1,0:T(8,128)S(1)} %get-tuple-element.43.token), channel_id=1, source_target_pairs={{1,3},{3,1},{5,7},{7,5},{9,11},{11,9},{13,15},{15,13},{17,19},{19,... | collective-permute-start | bytes 786440 | tf_op jit(solution)/shard_map/ppermute | solution.py:649
  7.1 12.9 %copy-start = (f32[32,2048]{1,0:T(8,128)}, f32[32,2048]{1,0:T(8,128)S(1)}, u32[]{:S(2)}) copy-start(f32[32,2048]{1,0:T(8,128)S(1)} %collective-permute-done.1.two) | copy-start | bytes 786436
  7.1 12.9 %copy-start.1 = (f32[32,2048]{1,0:T(8,128)}, f32[32,2048]{1,0:T(8,128)S(1)}, u32[]{:S(2)}) copy-start(f32[32,2048]{1,0:T(8,128)S(1)} %collective-permute-done.one) | copy-start | bytes 786436
  7.1 15.8 %collective-permute-start.2 = (f32[4,32,2048]{2,1,0:T(8,128)S(1)}, f32[4,32,2048]{2,1,0:T(8,128)S(1)}, u32[]{:S(2)}, u32[]{:S(2)}) collective-permute-start(f32[4,32,2048]{2,1,0:T(8,128)S(1)} %get-tuple-element.42), channel_id=1, source_target_pairs={{0,1},{1,0},{2,3},{3,2},{4,5},{5,4},{6,7},{7,6},{8,9},{9,8},{10,11... | collective-permute-start | bytes 3145736 | tf_op jit(solution)/shard_map/ppermute | solution.py:667
  14.5 8.4 %collective-permute-start.3 = (f32[32,2048]{1,0:T(8,128)S(1)}, f32[32,2048]{1,0:T(8,128)S(1)}, u32[]{:S(2)}, u32[]{:S(2)}) collective-permute-start(f32[32,2048]{1,0:T(8,128)S(1)} %get-tuple-element.43.token), channel_id=1, source_target_pairs={{0,2},{2,0},{4,6},{6,4},{8,10},{10,8},{12,14},{14,12},{16,18},{18,... | collective-permute-start | bytes 786440 | tf_op jit(solution)/shard_map/ppermute | solution.py:668
  18.6 4.3 %collective-permute-start.4 = (f32[32,2048]{1,0:T(8,128)S(1)}, f32[32,2048]{1,0:T(8,128)S(1)}, u32[]{:S(2)}, u32[]{:S(2)}) collective-permute-start(f32[32,2048]{1,0:T(8,128)S(1)} %get-tuple-element.44), channel_id=1, source_target_pairs={{2,4},{4,2},{6,8},{8,6},{10,12},{12,10},{18,20},{20,18},{22,24},{2... | collective-permute-start | bytes 786440 | tf_op jit(solution)/shard_map/ppermute | solution.py:669
  22.9 8.8 %copy-start.3 = (f32[32,2048]{1,0:T(8,128)}, f32[32,2048]{1,0:T(8,128)S(1)}, u32[]{:S(2)}) copy-start(f32[32,2048]{1,0:T(8,128)S(1)} %collective-permute-done.3.lower_one) | copy-start | bytes 786436
  22.9 8.8 %copy-start.4 = (f32[32,2048]{1,0:T(8,128)}, f32[32,2048]{1,0:T(8,128)S(1)}, u32[]{:S(2)}) copy-start(f32[32,2048]{1,0:T(8,128)S(1)} %collective-permute-done.4.lower_two) | copy-start | bytes 786436
  23.0 8.8 %copy-start.2 = (f32[4,32,2048]{2,1,0:T(8,128)}, f32[4,32,2048]{2,1,0:T(8,128)S(1)}, u32[]{:S(2)}) copy-start(f32[4,32,2048]{2,1,0:T(8,128)S(1)} %collective-permute-done.2.ring) | copy-start | bytes 3145732
  23.0 16.7 %all-to-all-start = ((f32[16,16,128]{2,1,0:T(8,128)}), f32[16,16,128]{2,1,0:T(8,128)S(1)}, u32[]{:S(2)}, u32[]{:S(2)}) async-start(f32[16,16,128]{2,1,0:T(8,128)} %shard_map.141), calls=%async_computation | async-start | bytes 262144 | tf_op jit(solution)/shard_map/all_to_all | solution.py:695
  39.7 2.9 %collective-permute-start.5 = (f32[104,2048]{1,0:T(8,128)}, f32[104,2048]{1,0:T(8,128)S(1)}, u32[]{:S(2)}, u32[]{:S(2)}) collective-permute-start(f32[104,2048]{1,0:T(8,128)} %get-tuple-element.58), channel_id=1, source_target_pairs={{0,1},{1,0},{2,3},{3,2},{4,5},{5,4},{6,7},{7,6},{8,9},{9,8},{10,11... | collective-permute-start | bytes 2555912 | tf_op jit(solution)/shard_map/ppermute | solution.py:733
  42.7 5.8 %copy-start.5 = (f32[104,2048]{1,0:T(8,128)}, f32[104,2048]{1,0:T(8,128)S(1)}, u32[]{:S(2)}) copy-start(f32[104,2048]{1,0:T(8,128)S(1)} %collective-permute-done.5.ring_two) | copy-start | bytes 2555908
  42.7 14.4 %all-to-all-start.1 = ((f32[16,16,128]{2,1,0:T(8,128)}), f32[16,16,128]{2,1,0:T(8,128)S(1)}, u32[]{:S(2)}, u32[]{:S(2)}) async-start(f32[16,16,128]{2,1,0:T(8,128)} %get-tuple-element.65), calls=%async_computation.1 | async-start | bytes 262144 | tf_op jit(solution)/shard_map/all_to_all | solution.py:744

commit v5 on v4

--- a/solution.py
+++ b/solution.py
@@ -247,103 +247,105 @@
         two[pl.ds(place * shells, shells)] = both[shells:]
 
 
-def viscosity_kernel(viscosity_from, d, index_from, token, eta, ring, h, index, viscosity, sems, eta_sems):
+def viscosity_kernel(
+    viscosity_from, d, f, index_from, token, eta_out, surface_swept, surface_eta, surface_force,
+    index, eta, field, force, viscosity, sems, eta_sems,
+):
     del token
-    shells, rows, _ = h.shape
-    components = d.shape[0]
-    shell = jnp.where(lax.axis_index("radial") == 0, shells - 1, 0)
-    copies = [
-        pltpu.make_async_copy(viscosity_from, viscosity, sems.at[shells]),
-        pltpu.make_async_copy(d.at[:, shell], ring.at[pl.ds(0, components)], sems.at[shells + 1]),
+    _, shells, rows, count = d.shape
+    block = pl.ds(TILE, rows)
+    value_copy = pltpu.make_async_copy(viscosity_from, viscosity, sems.at[shells])
+    layers = [pltpu.make_async_copy(index_from.at[s], index.at[s], sems.at[s]) for s in range(shells)]
+    surface_copies = [
+        pltpu.make_async_copy(d.at[0, pl.ds(shells - 3, 3)], field.at[pl.ds(0, 3), block], sems.at[shells + 1]),
+        pltpu.make_async_copy(f.at[0, pl.ds(shells - 2, 2)], force, sems.at[shells + 2]),
     ]
-    layers = [pltpu.make_async_copy(index_from.at[s], index.at[s], sems.at[s]) for s in range(shells)]
-    for copy in copies[:1] + layers + copies[1:]:
-        copy.start()
-    copies[0].wait()
+    start_all([value_copy, *layers, *surface_copies])
+    zeros = jnp.zeros((rows, count), jnp.float32)
+    field[3, block] = zeros
+    eta[shells, block] = zeros
+    value_copy.wait()
     stores = []
     for s in range(shells):
         layers[s].wait()
 
         def lookup(step, _):
-            part = pl.ds(pl.multiple_of(step * TILE, TILE), TILE)
-            h[s, part] = half_viscosity(index[s, part], viscosity)
+            start = pl.multiple_of(step * TILE, TILE)
+            eta[s, pl.ds(start + TILE, TILE)] = half_viscosity(index[s, pl.ds(start, TILE)], viscosity)
             return 0
 
         lax.fori_loop(0, rows // TILE, lookup, 0)
-        stores.append(pltpu.make_async_copy(h.at[s], eta.at[s], eta_sems.at[s]))
-        stores[-1].start()
-    stores.append(pltpu.make_async_copy(h.at[shell], ring.at[components], eta_sems.at[shells]))
-    stores[-1].start()
-    for copy in copies[1:] + stores:
+        stores += start_all([pltpu.make_async_copy(eta.at[s, block], eta_out.at[s], eta_sems.at[s])])
+    for copy in surface_copies:
         copy.wait()
 
-
-def surface_kernel(d, f, h, one, two, high_from, low_from, out, field, force, eta, smoothed, high, low, sems):
-    shells, rows, count = h.shape
-    top = lax.axis_size("radial") - 1
-
-    @pl.when(lax.axis_index("radial") == top)
+    def sweep(step, _):
+        start = pl.multiple_of(step * TILE, TILE)
+        part = pl.ds(start, TILE)
+        for k in range(2):
+            weights, factor = relax_weights(*around(eta, (), shells - 2 + k, start + TILE))
+            middle, others = around(field, (), k + 1, start + TILE)
+            surface_swept[k, part] = relax(weights, factor, middle, others, force[k, part])
+            surface_eta[k, part] = eta[shells - 2 + k, pl.ds(start + TILE, TILE)]
+        surface_force[part] = force[1, part]
+        return 0
+
+    lax.fori_loop(0, rows // TILE, sweep, 0)
+    for copy in stores:
+        copy.wait()
+
+
+def surface_kernel(
+    surface_swept, surface_eta, force, own_one, own_two, one, two, high_from, low_from, out,
+    swept, eta, surface, high, low, sems, components,
+):
+    rows, count = force.shape
+
+    @pl.when(lax.axis_index("radial") == lax.axis_size("radial") - 1)
     def _():
+        tables = start_all(
+            [
+                pltpu.make_async_copy(high_from, high, sems.at[0]),
+                pltpu.make_async_copy(low_from, low, sems.at[1]),
+            ]
+        )
         block = pl.ds(TILE, rows)
-        copies = [
-            pltpu.make_async_copy(d.at[0, pl.ds(shells - 3, 3)], field.at[pl.ds(0, 3), block], sems.at[0]),
-            pltpu.make_async_copy(h.at[pl.ds(shells - 3, 3)], eta.at[pl.ds(0, 3), block], sems.at[1]),
-            pltpu.make_async_copy(f.at[0, pl.ds(shells - 2, 2)], force, sems.at[2]),
-        ]
-        tables = [
-            pltpu.make_async_copy(high_from, high, sems.at[3]),
-            pltpu.make_async_copy(low_from, low, sems.at[4]),
-        ]
-        for copy in copies + tables:
-            copy.start()
-        zeros = jnp.zeros((rows, count), jnp.float32)
-        field[3, block] = zeros
-        eta[3, block] = zeros
-        smoothed[2, block] = zeros
-        components = d.shape[0]
-        before, after = by_parity(one, two)
-        inner, weight, partial, diagonal = [
-            k * shells for k in (0, components, components + 1, 2 * components + 1)
-        ]
-        for message, place in ((before, TILE - 1), (after, rows + TILE)):
-            for k in (1, 2):
-                field[k, place] = message[inner + shells - 3 + k]
-                eta[k, place] = message[weight + shells - 3 + k]
-        for copy in copies:
-            copy.wait()
+        for k in range(2):
+            swept[k, block] = surface_swept[k]
+            eta[k, block] = surface_eta[k]
+        swept[2, block] = jnp.zeros((rows, count), jnp.float32)
+        eta[2, block] = jnp.zeros((rows, count), jnp.float32)
+        fields = one.shape[0]
+        shells = fields // (2 * (components + 1))
         lateral = lax.axis_index("lateral")
         inside = (lateral > 0, lateral < lax.axis_size("lateral") - 1)
-        for message, own, place, there in (
-            (before, TILE, TILE - 1, inside[0]),
-            (after, rows + TILE - 1, rows + TILE, inside[1]),
+        for beside, own, place, own_place, there in zip(
+            by_parity(one, two), by_parity(own_one, own_two), (TILE - 1, rows + TILE), (TILE, rows + TILE - 1), inside
         ):
-            row = lambda start: message[start + shells - 1 : start + shells]
-            last = row(weight) + eta[2, pl.ds(own, 1)]
-            total = row(partial) + last * field[2, pl.ds(own, 1)]
-            edge = (1.0 - RELAXATION) * row(inner) + RELAXATION / (row(diagonal) + last) * total
-            smoothed[1, pl.ds(place, 1)] = jnp.where(there, edge, jnp.zeros_like(edge))
-
-        def first(step, _):
-            start = pl.multiple_of(step * TILE, TILE)
-            for s in (1, 2):
-                weights, factor = relax_weights(*around(eta, (), s, start + TILE))
-                middle, others = around(field, (), s, start + TILE)
-                smoothed[s - 1, pl.ds(start + TILE, TILE)] = relax(
-                    weights, factor, middle, others, force[s - 1, pl.ds(start, TILE)]
-                )
-            return 0
-
-        lax.fori_loop(0, rows // TILE, first, 0)
+            for k in range(2):
+                row = lambda message, kind: message[kind * shells + shells - 2 + k : kind * shells + shells - 1 + k]
+                weight = row(beside, components) + row(own, components)
+
+                def finish(message, other):
+                    total = row(message, components + 1) + weight * row(other, 0)
+                    factor = RELAXATION / (row(message, 2 * components + 1) + weight)
+                    return (1.0 - RELAXATION) * row(message, 0) + factor * total
+
+                swept[k, pl.ds(own_place, 1)] = finish(own, beside)
+                if k == 1:
+                    edge = finish(beside, own)
+                    swept[k, pl.ds(place, 1)] = jnp.where(there, edge, jnp.zeros_like(edge))
+                    eta[k, pl.ds(place, 1)] = row(beside, components)
 
         def second(step, _):
             start = pl.multiple_of(step * TILE, TILE)
-            weights, factor = relax_weights(*around(eta, (), 2, start + TILE))
-            middle, others = around(smoothed, (), 1, start + TILE)
-            field[0, pl.ds(start, TILE)] = relax(weights, factor, middle, others, force[1, pl.ds(start, TILE)])
+            weights, factor = relax_weights(*around(eta, (), 1, start + TILE))
+            middle, others = around(swept, (), 1, start + TILE)
+            surface[pl.ds(start, TILE)] = relax(weights, factor, middle, others, force[pl.ds(start, TILE)])
             return 0
 
         lax.fori_loop(0, rows // TILE, second, 0)
-        near, far = split(jnp.concatenate(fold(field[0, pl.ds(0, rows), :]), axis=0))
+        near, far = split(jnp.concatenate(fold(surface[...]), axis=0))
         for copy in tables:
             copy.wait()
         total = dot(near, high[...]) + dot(far, high[...]) + dot(near, low[...])
@@ -365,26 +367,19 @@
             out[block] = pack(fourier[:, block * width : (block + 1) * width])
 
 
-def sweep_shells(d, f, h, ring_field, ring_eta, out, field, eta, force, result, sems, before_first, after_shell):
+def sweep_shells(d, f, h, out, field, eta, force, result, sems, before_first, last_loads, arrived, finish, after_shell):
     components, shells, rows, count = d.shape
     inner = pl.ds(TILE, rows)
     lower = lax.axis_index("radial") == 0
     shell = lambda k: jnp.where(lower, k, shells - 1 - k)
-    ring, nothing = jnp.where(lower, shells + 1, 0), jnp.where(lower, 0, shells + 1)
+    nothing = jnp.where(lower, 0, shells + 1)
 
     def field_loads(k):
-        if k == shells:
-            return [
-                pltpu.make_async_copy(ring_eta, eta.at[ring, inner], sems.at[k, components]),
-                *(
-                    pltpu.make_async_copy(source, field.at[c, ring, inner], sems.at[k, c])
-                    for c, source in enumerate(ring_field)
-                ),
-            ]
         s = shell(k)
         return [
             pltpu.make_async_copy(d.at[:, s], field.at[:, s + 1, inner], sems.at[k, 0]),
             pltpu.make_async_copy(h.at[s], eta.at[s + 1, inner], sems.at[k, 1]),
+            *(last_loads if k == shells - 1 else []),
         ]
 
     def force_load(k):
@@ -392,37 +387,42 @@
 
     loads = [start_all(field_loads(0)), start_all(field_loads(1))]
     forces = [start_all(force_load(0))]
-    loads.append(start_all(field_loads(2)))
-    forces.append(start_all(force_load(1)))
     zeros = jnp.zeros((rows, count), jnp.float32)
     for c in range(components):
         field[c, nothing, inner] = zeros
     eta[nothing, inner] = zeros
     before_first()
+    loads.append(start_all(field_loads(2)))
+    forces.append(start_all(force_load(1)))
     for copy in loads[0]:
         copy.wait()
     stores = []
     for k in range(shells):
         s = shell(k)
-        if k + 3 <= shells:
+        if k + 3 < shells:
             loads.append(start_all(field_loads(k + 3)))
         if k + 2 < shells:
             forces.append(start_all(force_load(k + 2)))
-        for copy in loads[k + 1] + forces[k]:
+        for copy in (loads[k + 1] if k + 1 < shells else []) + forces[k]:
             copy.wait()
+        if k == shells - 2:
+            arrived()
 
         def tile(step, _):
             first = pl.multiple_of(step * TILE, TILE)
-            weights, factor = relax_weights(*around(eta, (), s + 1, first + TILE))
-            for c in range(components):
-                middle, others = around(field, (c,), s + 1, first + TILE)
-                result[c, s, pl.ds(first, TILE)] = relax(
-                    weights, factor, middle, others, force[c, s, pl.ds(first, TILE)]
-                )
+            part = pl.ds(first, TILE)
+            if k == shells - 1:
+                finish(s, first)
+            else:
+                weights, factor = relax_weights(*around(eta, (), s + 1, first + TILE))
+                for c in range(components):
+                    middle, others = around(field, (c,), s + 1, first + TILE)
+                    result[c, s, part] = relax(weights, factor, middle, others, force[c, s, part])
+            pltpu.make_async_copy(result.at[:, s, part], out.at[:, s, part], sems.at[k, 3]).start()
             return 0
 
         lax.fori_loop(0, rows // TILE, tile, 0)
-        stores += start_all([pltpu.make_async_copy(result.at[:, s], out.at[:, s], sems.at[k, 3])])
+        stores.append(pltpu.make_async_copy(result.at[:, s], out.at[:, s], sems.at[k, 3]))
         after_shell(s, k)
     for copy in stores:
         copy.wait()
@@ -442,21 +442,21 @@
 
 def load_messages(sources, lower_sources, slots, sems):
     lower = lax.axis_index("radial") < lax.axis_size("radial") - 1
-    part = pl.ds(0, slots.shape[1])
-    copies = lambda refs: [pltpu.make_async_copy(ref.at[part], slots.at[k], sems.at[k]) for k, ref in enumerate(refs)]
+    copies = lambda refs: [pltpu.make_async_copy(ref, slots.at[k], sems.at[k]) for k, ref in enumerate(refs)]
     pl.when(lower)(lambda: [copy.start() for copy in copies(lower_sources)] and None)
     pl.when(jnp.logical_not(lower))(lambda: [copy.start() for copy in copies(sources)] and None)
     return copies(sources)
 
 
-def first_kernel(d, f, h, ring, one, two, lower_one, lower_two, *refs):
-    components, shells, rows, _ = d.shape
-    staged = (len(refs) - 12) // 2
+def first_kernel(d, f, h, one, two, lower_one, lower_two, *refs):
+    components, shells, rows, count = d.shape
+    staged = (len(refs) - 14) // 2
     sources, refs = refs[:staged], refs[staged:]
-    out, ring_out, own_out, *targets = refs[: 3 + staged]
-    field, eta, force, result, messages, edges, own, sems, more_sems = refs[3 + staged :]
+    out, diagonal_out, ring_out, own_out, beside_out, *targets = refs[: 5 + staged]
+    field, eta, force, result, messages, edges, own, diagonal, sems, more_sems = refs[5 + staged :]
     arrivals = load_messages((one, two), (lower_one, lower_two), messages, more_sems)
     lower = lax.axis_index("radial") == 0
+    last = jnp.where(lower, shells - 1, 0)
     copies = []
 
     def before_first():
@@ -472,57 +472,120 @@
                 edges[side * (components + 1) + k] = jnp.where(
                     lower, message[(k + 1) * shells - 1], message[k * shells]
                 )
-        tail = ring_out.at[pl.ds(components * rows, edges.shape[0])]
-        copies.extend(start_all([pltpu.make_async_copy(edges, tail, more_sems.at[2])]))
+        tail = ring_out.at[pl.ds(2 * (components + 1) * rows, edges.shape[0])]
+        copies.extend(
+            start_all(
+                [
+                    pltpu.make_async_copy(edges, tail, more_sems.at[2]),
+                    pltpu.make_async_copy(messages, beside_out, more_sems.at[3]),
+                ]
+            )
+        )
+
+    def arrived():
+        block = pl.ds(TILE, rows)
+        zeros = jnp.zeros((rows, count), jnp.float32)
+        beyond = jnp.where(lower, shells + 1, 0)
+        for c in range(components):
+            field[c, beyond, block] = zeros
+        eta[beyond, block] = zeros
+        sources = [field.at[c, last + 1, block] for c in range(components)] + [eta.at[last + 1, block]]
+        copies.extend(
+            start_all(
+                [
+                    pltpu.make_async_copy(source, ring_out.at[pl.ds(k * rows, rows)], more_sems.at[4 + k])
+                    for k, source in enumerate(sources)
+                ]
+            )
+        )
+
+    def finish(s, first):
+        part = pl.ds(first, TILE)
+        middle, others = around(eta, (), s + 1, first + TILE)
+        weights = [middle + other for other in others]
+        zero = jnp.zeros_like(middle)
+        weights[0] = jnp.where(lower, zero, weights[0])
+        weights[1] = jnp.where(lower, weights[1], zero)
+        diagonal[part] = 1.0 + functools.reduce(jnp.add, weights)
+        for c in range(components):
+            total = force[c, s, part]
+            for weight, other in zip(weights, around(field, (c,), s + 1, first + TILE)[1]):
+                total = total + weight * other
+            result[c, s, part] = total
 
     def after_shell(s, k):
         if k == 0:
-            stages = [
-                pltpu.make_async_copy(source, target, more_sems.at[4 + components + n])
-                for n, (source, target) in enumerate(zip(sources, targets))
-            ]
-            copies.extend(start_all(stages))
+            copies.extend(
+                start_all(
+                    [
+                        pltpu.make_async_copy(source, target, more_sems.at[7 + 2 * components + n])
+                        for n, (source, target) in enumerate(zip(sources, targets))
+                    ]
+                )
+            )
         for side, place in enumerate((TILE, TILE + rows - 1)):
             for c in range(components):
                 own[c, side * shells + s] = field[c, s + 1, place]
             own[components, side * shells + s] = eta[s + 1, place]
         if k == shells - 1:
-            copies.extend(start_all([pltpu.make_async_copy(own, own_out, more_sems.at[3])]))
+            sums = [result.at[c, s] for c in range(components)] + [diagonal]
             copies.extend(
                 start_all(
                     [
                         pltpu.make_async_copy(
-                            result.at[c, s], ring_out.at[pl.ds(c * rows, rows)], more_sems.at[4 + c]
+                            source,
+                            ring_out.at[pl.ds((components + 1 + n) * rows, rows)],
+                            more_sems.at[5 + components + n],
                         )
-                        for c in range(components)
+                        for n, source in enumerate(sums)
+                    ]
+                    + [
+                        pltpu.make_async_copy(diagonal, diagonal_out, more_sems.at[6 + 2 * components]),
+                        pltpu.make_async_copy(own, own_out, more_sems.at[0]),
                     ]
                 )
             )
 
     sweep_shells(
-        d, f, h, [ring.at[c] for c in range(components)], ring.at[components],
-        out, field, eta, force, result, sems, before_first, after_shell,
+        d, f, h, out, field, eta, force, result, sems, before_first, [], arrived, finish, after_shell
     )
     for copy in copies:
         copy.wait()
 
 
-def second_kernel(d, f, h, ring, ring_two, one, two, lower_one, lower_two, own_from, *refs):
+def second_kernel(d, f, h, start, diagonal_from, ring, beside, own_from, *refs):
     components, shells, rows, count = d.shape
-    staged = (len(refs) - 11) // 2
+    staged = (len(refs) - 14) // 2
     sources, refs = refs[:staged], refs[staged:]
     out, token, *targets = refs[: 2 + staged]
-    field, eta, force, result, messages, edges, own, sems, more_sems = refs[2 + staged :]
+    field, eta, force, result, messages, edges, own, diagonal, raw, ring_diagonal, sems, more_sems = refs[2 + staged :]
     token[...] = jnp.zeros_like(token)
-    arrivals = load_messages((one, two), (lower_one, lower_two), messages, more_sems)
-    tail = ring_two.at[pl.ds(components * rows, edges.shape[0])]
-    arrivals += start_all(
+    tail = ring.at[pl.ds(2 * (components + 1) * rows, edges.shape[0])]
+    arrivals = start_all(
         [
-            pltpu.make_async_copy(tail, edges, more_sems.at[2]),
-            pltpu.make_async_copy(own_from, own, more_sems.at[3]),
+            pltpu.make_async_copy(beside, messages, more_sems.at[0]),
+            pltpu.make_async_copy(tail, edges, more_sems.at[1]),
+            pltpu.make_async_copy(own_from, own, more_sems.at[2]),
         ]
     )
     radial, lateral = lax.axis_index("radial"), lax.axis_index("lateral")
+    lower = radial == 0
+    last, beyond = jnp.where(lower, shells - 1, 0), jnp.where(lower, shells + 1, 0)
+    block = pl.ds(TILE, rows)
+    from_ring = lambda k, target, sem: pltpu.make_async_copy(
+        ring.at[pl.ds(k * rows, rows)], target, more_sems.at[sem]
+    )
+    last_loads = [
+        pltpu.make_async_copy(start.at[:, last], raw.at[pl.ds(0, components)], more_sems.at[3]),
+        pltpu.make_async_copy(diagonal_from, diagonal, more_sems.at[4]),
+        *(from_ring(c, raw.at[components + c], 5 + c) for c in range(components)),
+        from_ring(components, eta.at[beyond, block], 5 + components),
+        *(
+            from_ring(components + 1 + c, field.at[c, beyond, block], 6 + components + c)
+            for c in range(components)
+        ),
+        from_ring(2 * components + 1, ring_diagonal, 6 + 2 * components),
+    ]
     copies = []
 
     def before_first():
@@ -534,38 +597,69 @@
         )
         place = row_number((2 * shells, count))
         zero = jnp.zeros((2 * shells, count), jnp.float32)
-        shared = place % shells == jnp.where(radial == 0, shells - 1, 0)
-        beyond = lambda k: jnp.where(
+        shared = place % shells == last
+        across_of = lambda k: jnp.where(
             place < shells, edges[pl.ds(k, 1)], edges[pl.ds(components + 1 + k, 1)]
         )
         inside = jnp.where(place < shells, lateral, lax.axis_size("lateral") - 1 - lateral) > 0
         middle = pair(components)
         weight = middle + own[components]
-        across = jnp.where(shared, middle + beyond(components), zero)
+        across = jnp.where(shared, middle + across_of(components), zero)
         factor = RELAXATION / (pair(2 * components + 1) + weight + across)
         for c in range(components):
-            total = pair(components + 1 + c) + weight * own[c] + across * beyond(c)
+            total = pair(components + 1 + c) + weight * own[c] + across * across_of(c)
             edge = jnp.where(inside, (1.0 - RELAXATION) * pair(c) + factor * total, zero)
             set_edge(field, (c,), shells, rows, lambda s: edge[s], lambda s: edge[shells + s])
         set_edge(eta, (), shells, rows, lambda s: middle[s], lambda s: middle[shells + s])
 
+    def arrived():
+        def tile(step, _):
+            first = pl.multiple_of(step * TILE, TILE)
+            part, place = pl.ds(first, TILE), pl.ds(first + TILE, TILE)
+            weight = eta[last + 1, place] + eta[beyond, place]
+            here, there = RELAXATION / (diagonal[part] + weight), RELAXATION / (ring_diagonal[part] + weight)
+            for c in range(components):
+                mine, other = raw[c, part], raw[components + c, part]
+                field[c, last + 1, place] = (1.0 - RELAXATION) * mine + here * (
+                    field[c, last + 1, place] + weight * other
+                )
+                field[c, beyond, place] = (1.0 - RELAXATION) * other + there * (
+                    field[c, beyond, place] + weight * mine
+                )
+            return 0
+
+        lax.fori_loop(0, rows // TILE, tile, 0)
+
+    def finish(s, first):
+        part = pl.ds(first, TILE)
+        weights, factor = relax_weights(*around(eta, (), s + 1, first + TILE))
+        for c in range(components):
+            middle, others = around(field, (c,), s + 1, first + TILE)
+            result[c, s, part] = relax(weights, factor, middle, others, force[c, s, part])
+
     def after_shell(s, k):
         if k == 0:
-            stages = [
-                pltpu.make_async_copy(source, target, more_sems.at[4 + n])
-                for n, (source, target) in enumerate(zip(sources, targets))
-            ]
-            copies.extend(start_all(stages))
+            copies.extend(
+                start_all(
+                    [
+                        pltpu.make_async_copy(source, target, more_sems.at[7 + 2 * components + n])
+                        for n, (source, target) in enumerate(zip(sources, targets))
+                    ]
+                )
+            )
 
     sweep_shells(
-        d, f, h, [ring_two.at[pl.ds(c * rows, rows)] for c in range(components)], ring.at[components],
-        out, field, eta, force, result, sems, before_first, after_shell,
+        d, f, h, out, field, eta, force, result, sems, before_first, last_loads, arrived, finish, after_shell
     )
     for copy in copies:
         copy.wait()
 
 
-def spectrum_kernel(orders, wave_high, wave_low, point_high, point_low, response, coefficients, out):
+def spectrum_kernel(
+    orders, wave_high, wave_low, point_high, point_low, response_from, coefficients, out, response, sem
+):
+    copy = pltpu.make_async_copy(response_from, response, sem)
+    copy.start()
     radial = lax.axis_size("radial")
     width = coefficients.shape[0]
     bands, rows = orders.shape[0] // radial, point_high.shape[0] * radial // orders.shape[0]
@@ -573,6 +667,7 @@
     high, low = split(fourier)
     spectrum = dot(wave_high[...], high) + dot(wave_high[...], low) + dot(wave_low[...], high)
     coefficients[...] = spectrum.T
+    copy.wait()
     own = response[:, :width]
     for place in range(1, radial):
         own = jnp.where(
@@ -586,7 +681,9 @@
             out[band * radial + place] = block
 
 
-def load_kernel(load, high, low, mask, out):
+def load_kernel(load, high, low, mask_from, out, mask, sem):
+    copy = pltpu.make_async_copy(mask_from, mask, sem)
+    copy.start()
     blocks, rows = load.shape[0], out.shape[0]
     step, width = out.shape[1] // RADIX, high.shape[1] // blocks
     values = jnp.concatenate([unpack(load[block], width) for block in range(blocks)], axis=1)
@@ -599,6 +696,7 @@
     stack += [jnp.where(kind == k, crossed, zero) for k in range(1, RADIX // 2)]
     near, far = split(jnp.concatenate(stack, axis=0))
     total = dot_nt(near, high[...]) + dot_nt(far, high[...]) + dot_nt(near, low[...])
+    copy.wait()
     for m, part in enumerate(unfold([total[k * rows : (k + 1) * rows] for k in range(RADIX)])):
         columns = slice(m * step, (m + 1) * step)
         out[:, columns] = part * mask[:, columns].astype(jnp.float32)
@@ -625,6 +723,7 @@
     top_only = lambda pairs: [(i * radial + radial - 1, j * radial + radial - 1) for i, j in pairs]
 
     lower_only = lambda pairs: [(i * radial + k, j * radial + k) for i, j in pairs for k in range(radial - 1)]
+    swap = [(i, radial - 1 - i) for i in range(radial)]
     tensors = [hbm(a) for a in (initial_displacement, force, layer_index)]
     viscosity = hbm(viscosity)
     message = f32((2 * (components + 1) * shells, count))
@@ -647,24 +746,29 @@
     )(viscosity, *tensors)
     two = lax.ppermute(mine[1], both, top_only(second))
     one = lax.ppermute(mine[0], both, top_only(first))
-    eta, ring = pl.pallas_call(
+    eta, *surface = pl.pallas_call(
         viscosity_kernel,
-        in_specs=[HBM, HBM, HBM, ANY],
-        out_specs=[HBM, VMEM],
-        out_shape=[in_hbm(shells, rows, count), f32((components + 1, rows, count))],
+        in_specs=[HBM] * 4 + [ANY],
+        out_specs=[HBM, VMEM, VMEM, VMEM],
+        out_shape=[
+            in_hbm(shells, rows, count),
+            f32((2, rows, count)),
+            f32((2, rows, count)),
+            f32((rows, count)),
+        ],
         scratch_shapes=[
-            scratch(shells, rows, count),
             pltpu.VMEM(layer_index.shape, jnp.int32),
+            scratch(shells + 1, rows + 2 * TILE, count),
+            scratch(4, rows + 2 * TILE, count),
+            scratch(2, rows, count),
             pltpu.SMEM(viscosity.shape, jnp.float32),
-            pltpu.SemaphoreType.DMA((2 + shells,)),
-            pltpu.SemaphoreType.DMA((1 + shells,)),
+            pltpu.SemaphoreType.DMA((3 + shells,)),
+            pltpu.SemaphoreType.DMA((shells,)),
         ],
-        compiler_params=params(12),
+        compiler_params=params(16),
         cost_estimate=cost(20),
-    )(viscosity, tensors[0], tensors[2], mine[0])
-    ring, lower_one, lower_two, one, two = lax.optimization_barrier((ring, *mine, one, two))
-    swap = [(i, radial - 1 - i) for i in range(radial)]
-    ring = lax.ppermute(ring, "radial", swap)
+    )(viscosity, *tensors, mine[0])
+    lower_one, lower_two, eta = lax.optimization_barrier((*mine, eta))
     lower_one = lax.ppermute(lower_one, both, lower_only(first))
     lower_two = lax.ppermute(lower_two, both, lower_only(second))
 
@@ -673,26 +777,24 @@
     table = pltpu.VMEM(high.shape, jnp.bfloat16)
     packed = (lateral * radial, rows * width // max(128, width), max(128, width))
     orders = pl.pallas_call(
-        surface_kernel,
-        in_specs=[HBM, HBM, HBM, VMEM, VMEM, HBM, HBM],
+        functools.partial(surface_kernel, components=components),
+        in_specs=[VMEM] * 7 + [HBM, HBM],
         out_specs=VMEM,
         out_shape=f32(packed),
         scratch_shapes=[
-            scratch(4, rows + 2 * TILE, count),
-            scratch(2, rows, count),
-            scratch(4, rows + 2 * TILE, count),
             scratch(3, rows + 2 * TILE, count),
+            scratch(3, rows + 2 * TILE, count),
+            scratch(rows, count),
             table,
             table,
-            pltpu.SemaphoreType.DMA((5,)),
+            pltpu.SemaphoreType.DMA((2,)),
         ],
-        compiler_params=params(24),
+        compiler_params=params(16),
         cost_estimate=cost(200),
-    )(*tensors[:2], hbm(eta), one, two, high, low)
-    orders, ring, lower_one, lower_two = lax.optimization_barrier((orders, ring, lower_one, lower_two))
-    messages = [hbm(a) for a in (one, two, lower_one, lower_two)]
-    ring, eta = hbm(ring), hbm(eta)
+    )(*surface, *mine, one, two, high, low)
+    eta, _ = lax.optimization_barrier((eta, orders))
     orders = lax.all_to_all(orders, both, split_axis=0, concat_axis=0, tiled=True)
+    eta = hbm(eta)
 
     sweep_scratch = [
         scratch(components, shells + 2, rows + 2 * TILE, count),
@@ -700,53 +802,57 @@
         scratch(components, shells, rows, count),
         scratch(components, shells, rows, count),
     ]
-    sweep_sems = pltpu.SemaphoreType.DMA((shells + 1, components + 1))
+    sweep_sems = pltpu.SemaphoreType.DMA((shells, 4))
     point_high, point_low = colatitude_tables(rows * lateral, MODES)
     stages = [
         jnp.asarray(a)
         for a in (point_high.T.copy(), point_low.T.copy(), point_high, point_low)
-    ] + [response]
-    ring_rows = components * rows + 2 * (components + 1)
-    own_rows = scratch(components + 1, 2 * shells, count)
-    smoothed, ring_two, own, *staged = pl.pallas_call(
+    ]
+    ring_rows = 2 * (components + 1) * (rows + 1)
+    sweep_scratch += [
+        sides(*message.shape),
+        scratch(2 * (components + 1), count),
+        scratch(components + 1, 2 * shells, count),
+        scratch(rows, count),
+    ]
+    smoothed, diagonal, ring, own, beside, *staged = pl.pallas_call(
         first_kernel,
-        in_specs=[HBM] * (8 + len(stages)),
-        out_specs=[HBM] * 3 + [VMEM] * len(stages),
+        in_specs=[HBM] * 3 + [ANY] * 4 + [HBM] * len(stages),
+        out_specs=[HBM] * 5 + [VMEM] * len(stages),
         out_shape=[
             in_hbm(*initial_displacement.shape),
+            in_hbm(rows, count),
             in_hbm(ring_rows, count),
             in_hbm(components + 1, 2 * shells, count),
+            in_hbm(2, *message.shape),
             *(jax.ShapeDtypeStruct(a.shape, a.dtype) for a in stages),
         ],
         scratch_shapes=[
             *sweep_scratch,
-            sides((components + 1) * shells, count),
-            scratch(2 * (components + 1), count),
-            own_rows,
             sweep_sems,
-            pltpu.SemaphoreType.DMA((4 + components + len(stages),)),
+            pltpu.SemaphoreType.DMA((7 + 2 * components + len(stages),)),
         ],
         compiler_params=params(28),
         cost_estimate=cost(50),
-    )(*tensors[:2], eta, ring, *messages, *(hbm(a) for a in stages))
-    ring_two, orders = lax.optimization_barrier((ring_two, orders))
-    ring_two = lax.ppermute(ring_two, "radial", swap)
+    )(*tensors[:2], eta, one, two, lower_one, lower_two, *(hbm(a) for a in stages))
+    ring, orders = lax.optimization_barrier((ring, orders))
+    ring = lax.ppermute(ring, "radial", swap)
     coefficients, load = pl.pallas_call(
         spectrum_kernel,
-        in_specs=[VMEM] * 6,
+        in_specs=[VMEM] * 5 + [HBM],
         out_specs=[VMEM, VMEM],
         out_shape=[f32((width, MODES)), f32(packed)],
+        scratch_shapes=[pltpu.VMEM(response.shape, jnp.float32), pltpu.SemaphoreType.DMA],
         compiler_params=params(16),
         cost_estimate=cost(200),
-    )(orders, *staged)
-    load, ring_two = lax.optimization_barrier((load, ring_two))
+    )(orders, *staged, hbm(response))
     eta, load = lax.optimization_barrier((eta, load))
     load = lax.all_to_all(load, both, split_axis=0, concat_axis=0, tiled=True)
 
-    stages = [high, low, hbm(ocean_mask)]
+    stages = [high, low]
     displacement, token, *staged = pl.pallas_call(
         second_kernel,
-        in_specs=[HBM] * (10 + len(stages)),
+        in_specs=[HBM] * 5 + [ANY] + [HBM] * (2 + len(stages)),
         out_specs=[HBM, VMEM] + [VMEM] * len(stages),
         out_shape=[
             in_hbm(*initial_displacement.shape),
@@ -755,24 +861,29 @@
         ],
         scratch_shapes=[
             *sweep_scratch,
-            sides(message.shape[0], count),
-            scratch(2 * (components + 1), count),
-            own_rows,
+            scratch(2 * components, rows, count),
+            scratch(rows, count),
             sweep_sems,
-            pltpu.SemaphoreType.DMA((4 + len(stages),)),
+            pltpu.SemaphoreType.DMA((7 + 2 * components + len(stages),)),
         ],
         compiler_params=params(28),
         cost_estimate=cost(50),
-    )(hbm(smoothed), tensors[1], hbm(eta), ring, hbm(ring_two), *messages, hbm(own), *stages)
+    )(
+        *(hbm(a) for a in (smoothed, tensors[1], eta, tensors[0], diagonal)),
+        ring,
+        *(hbm(a) for a in (beside, own)),
+        *stages,
+    )
 
     sea_load = pl.pallas_call(
         load_kernel,
-        in_specs=[VMEM] * 4,
+        in_specs=[VMEM] * 3 + [HBM],
         out_specs=VMEM,
         out_shape=f32((rows, count)),
+        scratch_shapes=[pltpu.VMEM(ocean_mask.shape, ocean_mask.dtype), pltpu.SemaphoreType.DMA],
         compiler_params=params(20),
         cost_estimate=cost(3),
-    )(load, *staged)
+    )(load, *staged, hbm(ocean_mask))
     return (displacement, coefficients.T, sea_load)
 
 

time: 58.9 us -> 50.9 us (0.86)
  starting transfers between devices: 28.8 us -> 22.7 us
  waiting for transfers between devices: 3.22 us -> 0.54 us
  Pallas kernels: 25.7 us -> 26.5 us
    ppermute x1, starting transfers between devices: 7.39 us -> 0.01 us  [shards(): ring = lax.ppermute(ring, 'radial', swap)]
    ppermute x1, waiting for transfers between devices: 2.91 us -> 0.01 us  [shards(): lower_one = lax.ppermute(lower_one, both, lower_only(first))]
    all_to_all x1, starting transfers between devices: 8.79 us -> 10 us  [shards(): lax.all_to_all(orders, both, split_axis=0, concat_axis=0, tiled=True)]
    pallas_call x6, Pallas kernels: 23.2 us -> 24 us  [the longest x1 7.93 us: shards(): pl.pallas_call(second_kernel, in_specs=[HBM] * 5 + [ANY] + [HBM] * (2 + l...]
    ppermute x1, starting transfers between devices: 4.08 us -> 4.88 us  [shards(): lower_one = lax.ppermute(lower_one, both, lower_only(first))]
    ppermute x1 -> x0, starting transfers between devices: 0.73 us -> none  [shards(): ring_two = lax.ppermute(ring_two, 'radial', swap)]
  transfers between devices with their start and end apart: 8 -> 7, of which waited for: 3 -> 1; matrix products, arithmetic and copies ran while one was open for 0% -> 0% of each run, Pallas kernels for 37% -> 43%
where the time goes in v5:
time: 50.9 us; the launch traced here: 50.4 us
  Pallas kernels  26.5 us (52%)
  starting transfers between devices  22.7 us (45%)
  between operations  0.77 us (2%)
  waiting for transfers between devices  0.54 us (1%)
    all_to_all x1, starting transfers between devices, shards(): lax.all_to_all(orders, both, split_axis=0, concat_axis=0, tiled=True)  10 us
    pallas_call x1, Pallas kernels, shards(): pl.pallas_call(second_kernel, in_specs=[HBM] * 5 + [ANY] + [HBM] * (2 + l...  7.93 us
    pallas_call x1, Pallas kernels, shards(): pl.pallas_call(first_kernel, in_specs=[HBM] * 3 + [ANY] * 4 + [HBM] * len...  7.39 us
    all_to_all x1, starting transfers between devices, shards(): load = lax.all_to_all(load, both, split_axis=0, concat_axis=0, tiled=True)  5.73 us
    ppermute x1, starting transfers between devices, shards(): lower_one = lax.ppermute(lower_one, both, lower_only(first))  4.88 us
    pallas_call x1, Pallas kernels, shards(): pl.pallas_call(spectrum_kernel, in_specs=[VMEM] * 5 + [HBM], out_specs=[V...  2.92 us
    pallas_call x1, Pallas kernels, shards(): pl.pallas_call(viscosity_kernel, in_specs=[HBM] * 4 + [ANY], out_specs=[H...  2.9 us
    pallas_call x1, Pallas kernels, shards(): pl.pallas_call(message_kernel, in_specs=[HBM] * 4, out_specs=[VMEM] * 2,...  2.44 us
  transfers between devices with their start and end apart: 7, of which 1 were waited for; matrix products, arithmetic and copies ran while one was open for 0% of the time, Pallas kernels for 43%

profile of v5, /device:TPU:0, one launch (start us, length us, event | category | flops | bytes accessed | tf_op | source)
XLA Modules:
  0.0 50.4 jit_solution(6622488821319187783)
XLA Ops:
  0.6 2.4 %shard_map.139 = (f32[32,2048]{1,0:T(8,128)S(1)}, f32[32,2048]{1,0:T(8,128)S(1)}) custom-call(f32[16]{0:T(128)} %viscosity_from.3, f32[3,4,32,2048]{3,2,1,0:T(8,128)} %start.1, f32[3,4,32,2048]{3,2,1,0:T(8,128)} %f.7, s32[4,32,2048]{2,1,0:T(8,128)} %index_from.1), custom_call_target="tpu_custom_call" | custom-call | bytes 60000000 | tf_op jit(solution)/shard_map/pallas_call | solution.py:731
  3.1 0.7 %collective-permute-start.1 = (f32[32,2048]{1,0:T(8,128)S(1)}, f32[32,2048]{1,0:T(8,128)S(1)}, u32[]{:S(2)}, u32[]{:S(2)}) collective-permute-start(f32[32,2048]{1,0:T(8,128)S(1)} %get-tuple-element.40.own_two), channel_id=1, source_target_pairs={{3,5},{5,3},{7,9},{9,7},{11,13},{13,11},{19,21},{21,19},{23,25},{2... | collective-permute-start | bytes 786440 | tf_op jit(solution)/shard_map/ppermute | solution.py:747
  3.8 0.7 %collective-permute-start = (f32[32,2048]{1,0:T(8,128)S(1)}, f32[32,2048]{1,0:T(8,128)S(1)}, u32[]{:S(2)}, u32[]{:S(2)}) collective-permute-start(f32[32,2048]{1,0:T(8,128)S(1)} %get-tuple-element.39.token.own_one), channel_id=1, source_target_pairs={{1,3},{3,1},{5,7},{7,5},{9,11},{11,9},{13,15},{15,13},{17,19},{19,... | collective-permute-start | bytes 786440 | tf_op jit(solution)/shard_map/ppermute | solution.py:748
  4.4 2.9 %shard_map.140 = (f32[4,32,2048]{2,1,0:T(8,128)}, f32[2,32,2048]{2,1,0:T(8,128)S(1)}, f32[2,32,2048]{2,1,0:T(8,128)S(1)}, f32[32,2048]{1,0:T(8,128)S(1)}) custom-call(f32[16]{0:T(128)} %viscosity_from.3, f32[3,4,32,2048]{3,2,1,0:T(8,128)} %start.1, f32[3,4,32,2048]{3,2,1,0:T(8,128)} %f.7, s32[4,32,2048]{2,1,0:T(8,128)} %index_from.1, ...), custom_call_target="tpu_custom_call" | custom-call | bytes 60000000 | tf_op jit(solution)/shard_map/pallas_call | solution.py:749
  7.3 4.9 %collective-permute-start.2 = (f32[32,2048]{1,0:T(8,128)S(1)}, f32[32,2048]{1,0:T(8,128)S(1)}, u32[]{:S(2)}, u32[]{:S(2)}) collective-permute-start(f32[32,2048]{1,0:T(8,128)S(1)} %get-tuple-element.39.token.own_one), channel_id=1, source_target_pairs={{0,2},{2,0},{4,6},{6,4},{8,10},{10,8},{12,14},{14,12},{16,18},{18,... | collective-permute-start | bytes 786440 | tf_op jit(solution)/shard_map/ppermute | solution.py:772
  12.2 0.7 %collective-permute-start.3 = (f32[32,2048]{1,0:T(8,128)S(1)}, f32[32,2048]{1,0:T(8,128)S(1)}, u32[]{:S(2)}, u32[]{:S(2)}) collective-permute-start(f32[32,2048]{1,0:T(8,128)S(1)} %get-tuple-element.40.own_two), channel_id=1, source_target_pairs={{2,4},{4,2},{6,8},{8,6},{10,12},{12,10},{18,20},{20,18},{22,24},{2... | collective-permute-start | bytes 786440 | tf_op jit(solution)/shard_map/ppermute | solution.py:773
  12.9 0.0 collective-permute-done.1.two
  12.9 0.0 collective-permute-done.one
  12.9 0.7 %shard_map.141 = f32[16,16,128]{2,1,0:T(8,128)} custom-call(f32[2,32,2048]{2,1,0:T(8,128)S(1)} %get-tuple-element.35.surface_swept, f32[2,32,2048]{2,1,0:T(8,128)S(1)} %get-tuple-element.36.surface_eta, f32[32,2048]{1,0:T(8,128)S(1)} %get-tuple-element.37.force, f32[32,2048]{1,0:T(8,128)S(1)} %get-tuple-element.39.token.own_one, ...), custom_call_target="tpu_custom_call" | custom-call | bytes 600000000 | tf_op jit(solution)/shard_map/pallas_call | solution.py:779
  13.6 10.0 %all-to-all-start = ((f32[16,16,128]{2,1,0:T(8,128)}), f32[16,16,128]{2,1,0:T(8,128)S(1)}, u32[]{:S(2)}, u32[]{:S(2)}) async-start(f32[16,16,128]{2,1,0:T(8,128)} %shard_map.141), calls=%async_computation | async-start | bytes 262144 | tf_op jit(solution)/shard_map/all_to_all | solution.py:796
  23.7 0.0 collective-permute-done.2.lower_one
  23.7 0.0 collective-permute-done.3.lower_two
  23.7 7.4 %shard_map.142 = (f32[3,4,32,2048]{3,2,1,0:T(8,128)}, f32[32,2048]{1,0:T(8,128)}, f32[264,2048]{1,0:T(8,128)}, f32[4,8,2048]{2,1,0:T(8,128)}, f32[2,32,2048]{2,1...) custom-call(f32[3,4,32,2048]{3,2,1,0:T(8,128)} %start.1, ...), custom_call_target="tpu_custom_call" | custom-call | bytes 150000000 | tf_op jit(solution)/shard_map/pallas_call | solution.py:818
  31.1 0.5 %all-to-all-done.orders = f32[16,16,128]{2,1,0:T(8,128)S(1)} async-done(((f32[16,16,128]{2,1,0:T(8,128)}), f32[16,16,128]{2,1,0:T(8,128)S(1)}, u32[]{:S(2)}, u32[]{:S(2)}) %all-to-all-start) | async-done | bytes 131104 | tf_op jit(solution)/shard_map/all_to_all | solution.py:796
  31.6 0.0 collective-permute-start.4
  31.6 2.9 %shard_map.143 = (f32[64,512]{1,0:T(8,128)}, f32[16,16,128]{2,1,0:T(8,128)}) custom-call(f32[16,16,128]{2,1,0:T(8,128)S(1)} %all-to-all-done.orders, bf16[512,256]{1,0:T(8,128)(2,1)S(1)} %get-tuple-element.44.wave_high, bf16[512,256]{1,0:T(8,128)(2,1)S(1)} %get-tuple-element.45.wave_low, bf16[256,512]{1,0:T(8,128)(2,1)S(1)} %get-tuple-element.46.point_high, ...), custom_call_target="tpu_custom_call" | custom-call | bytes 600000000 | tf_op jit(solution)/shard_map/pallas_call | solution.py:840
  34.5 5.7 %all-to-all-start.1 = ((f32[16,16,128]{2,1,0:T(8,128)}), f32[16,16,128]{2,1,0:T(8,128)S(1)}, u32[]{:S(2)}, u32[]{:S(2)}) async-start(f32[16,16,128]{2,1,0:T(8,128)} %get-tuple-element.56), calls=%async_computation.1 | async-start | bytes 262144 | tf_op jit(solution)/shard_map/all_to_all | solution.py:850
  40.3 0.0 collective-permute-done.4.ring
  40.3 7.9 %shard_map.144 = (f32[3,4,32,2048]{3,2,1,0:T(8,128)}, f32[8,128]{1,0:T(8,128)}, bf16[256,1024]{1,0:T(8,128)(2,1)S(1)}, bf16[256,1024]{1,0:T(8,128)(2,1)S(1)}) custom-call(f32[3,4,32,2048]{3,2,1,0:T(8,128)} %get-tuple-element.41.d, f32[3,4,32,2048]{3,2,1,0:T(8,128)} %f.7, f32[4,32,2048]{2,1,0:T(8,128)} %get-tuple-element.49.h, f32[3,4,32,2048]{3,2,1,0:T(8,128)} %start.1, ...), custom_call_target="tpu_custom_call" | custom-call | bytes 150000000 | tf_op jit(solution)/shard_map/pallas_call | solution.py:853
  48.2 0.0 all-to-all-done.1.load
  48.2 2.2 %shard_map.145 = f32[32,2048]{1,0:T(8,128)} custom-call(f32[16,16,128]{2,1,0:T(8,128)S(1)} %all-to-all-done.1.load, bf16[256,1024]{1,0:T(8,128)(2,1)S(1)} %get-tuple-element.57.high, bf16[256,1024]{1,0:T(8,128)(2,1)S(1)} %get-tuple-element.58.low, s32[32,2048]{1,0:T(8,128)} %mask_from.1), custom_call_target="tpu_custom_call" | custom-call | bytes 9000000 | tf_op jit(solution)/shard_map/pallas_call | solution.py:878
Async XLA Ops:
  3.1 9.8 %collective-permute-start.1 = (f32[32,2048]{1,0:T(8,128)S(1)}, f32[32,2048]{1,0:T(8,128)S(1)}, u32[]{:S(2)}, u32[]{:S(2)}) collective-permute-start(f32[32,2048]{1,0:T(8,128)S(1)} %get-tuple-element.40.own_two), channel_id=1, source_target_pairs={{3,5},{5,3},{7,9},{9,7},{11,13},{13,11},{19,21},{21,19},{23,25},{2... | collective-permute-start | bytes 786440 | tf_op jit(solution)/shard_map/ppermute | solution.py:747
  3.8 9.2 %collective-permute-start = (f32[32,2048]{1,0:T(8,128)S(1)}, f32[32,2048]{1,0:T(8,128)S(1)}, u32[]{:S(2)}, u32[]{:S(2)}) collective-permute-start(f32[32,2048]{1,0:T(8,128)S(1)} %get-tuple-element.39.token.own_one), channel_id=1, source_target_pairs={{1,3},{3,1},{5,7},{7,5},{9,11},{11,9},{13,15},{15,13},{17,19},{19,... | collective-permute-start | bytes 786440 | tf_op jit(solution)/shard_map/ppermute | solution.py:748
  7.3 16.3 %collective-permute-start.2 = (f32[32,2048]{1,0:T(8,128)S(1)}, f32[32,2048]{1,0:T(8,128)S(1)}, u32[]{:S(2)}, u32[]{:S(2)}) collective-permute-start(f32[32,2048]{1,0:T(8,128)S(1)} %get-tuple-element.39.token.own_one), channel_id=1, source_target_pairs={{0,2},{2,0},{4,6},{6,4},{8,10},{10,8},{12,14},{14,12},{16,18},{18,... | collective-permute-start | bytes 786440 | tf_op jit(solution)/shard_map/ppermute | solution.py:772
  12.2 11.4 %collective-permute-start.3 = (f32[32,2048]{1,0:T(8,128)S(1)}, f32[32,2048]{1,0:T(8,128)S(1)}, u32[]{:S(2)}, u32[]{:S(2)}) collective-permute-start(f32[32,2048]{1,0:T(8,128)S(1)} %get-tuple-element.40.own_two), channel_id=1, source_target_pairs={{2,4},{4,2},{6,8},{8,6},{10,12},{12,10},{18,20},{20,18},{22,24},{2... | collective-permute-start | bytes 786440 | tf_op jit(solution)/shard_map/ppermute | solution.py:773
  13.6 18.0 %all-to-all-start = ((f32[16,16,128]{2,1,0:T(8,128)}), f32[16,16,128]{2,1,0:T(8,128)S(1)}, u32[]{:S(2)}, u32[]{:S(2)}) async-start(f32[16,16,128]{2,1,0:T(8,128)} %shard_map.141), calls=%async_computation | async-start | bytes 262144 | tf_op jit(solution)/shard_map/all_to_all | solution.py:796
  31.6 8.7 %collective-permute-start.4 = (f32[264,2048]{1,0:T(8,128)}, f32[264,2048]{1,0:T(8,128)S(1)}, u32[]{:S(2)}, u32[]{:S(2)}) collective-permute-start(f32[264,2048]{1,0:T(8,128)} %get-tuple-element.51), channel_id=1, source_target_pairs={{0,1},{1,0},{2,3},{3,2},{4,5},{5,4},{6,7},{7,6},{8,9},{9,8},{10,11... | collective-permute-start | bytes 6488072 | tf_op jit(solution)/shard_map/ppermute | solution.py:839
  34.5 13.7 %all-to-all-start.1 = ((f32[16,16,128]{2,1,0:T(8,128)}), f32[16,16,128]{2,1,0:T(8,128)S(1)}, u32[]{:S(2)}, u32[]{:S(2)}) async-start(f32[16,16,128]{2,1,0:T(8,128)} %get-tuple-element.56), calls=%async_computation.1 | async-start | bytes 262144 | tf_op jit(solution)/shard_map/all_to_all | solution.py:850

commit v6 on v5

--- a/solution.py
+++ b/solution.py
@@ -421,7 +421,7 @@
             pltpu.make_async_copy(result.at[:, s, part], out.at[:, s, part], sems.at[k, 3]).start()
             return 0
 
-        lax.fori_loop(0, rows // TILE, tile, 0)
+        lax.fori_loop(0, rows // TILE, tile, 0, unroll=2)
         stores.append(pltpu.make_async_copy(result.at[:, s], out.at[:, s], sems.at[k, 3]))
         after_shell(s, k)
     for copy in stores:
@@ -555,10 +555,12 @@
 
 def second_kernel(d, f, h, start, diagonal_from, ring, beside, own_from, *refs):
     components, shells, rows, count = d.shape
-    staged = (len(refs) - 14) // 2
-    sources, refs = refs[:staged], refs[staged:]
-    out, token, *targets = refs[: 2 + staged]
-    field, eta, force, result, messages, edges, own, diagonal, raw, ring_diagonal, sems, more_sems = refs[2 + staged :]
+    staged = (len(refs) - 17) // 2
+    mask_from, *sources = refs[: 1 + staged]
+    out, token, mask_out, *targets = refs[1 + staged : 4 + 2 * staged]
+    (
+        field, eta, force, result, messages, edges, own, diagonal, raw, ring_diagonal, mask, sems, more_sems
+    ) = refs[4 + 2 * staged :]
     token[...] = jnp.zeros_like(token)
     tail = ring.at[pl.ds(2 * (components + 1) * rows, edges.shape[0])]
     arrivals = start_all(
@@ -587,6 +589,7 @@
         from_ring(2 * components + 1, ring_diagonal, 6 + 2 * components),
     ]
     copies = []
+    mask_copy = pltpu.make_async_copy(mask_from, mask, more_sems.at[7 + 2 * components])
 
     def before_first():
         for copy in arrivals:
@@ -642,11 +645,15 @@
             copies.extend(
                 start_all(
                     [
-                        pltpu.make_async_copy(source, target, more_sems.at[7 + 2 * components + n])
+                        pltpu.make_async_copy(source, target, more_sems.at[8 + 2 * components + n])
                         for n, (source, target) in enumerate(zip(sources, targets))
                     ]
                 )
             )
+            mask_copy.start()
+        if k == shells - 2:
+            mask_copy.wait()
+            mask_out[...] = mask[...].astype(jnp.float32).astype(jnp.bfloat16)
 
     sweep_shells(
         d, f, h, out, field, eta, force, result, sems, before_first, last_loads, arrived, finish, after_shell
@@ -655,35 +662,28 @@
         copy.wait()
 
 
-def spectrum_kernel(
-    orders, wave_high, wave_low, point_high, point_low, response_from, coefficients, out, response, sem
-):
-    copy = pltpu.make_async_copy(response_from, response, sem)
-    copy.start()
+def spectrum_kernel(orders, high, low, response, coefficients, out):
     radial = lax.axis_size("radial")
     width = coefficients.shape[0]
-    bands, rows = orders.shape[0] // radial, point_high.shape[0] * radial // orders.shape[0]
+    bands, rows = orders.shape[0] // radial, high.shape[0] * radial // orders.shape[0]
     fourier = jnp.concatenate([unpack(orders[band * radial + radial - 1], width) for band in range(bands)], axis=0)
-    high, low = split(fourier)
-    spectrum = dot(wave_high[...], high) + dot(wave_high[...], low) + dot(wave_low[...], high)
-    coefficients[...] = spectrum.T
-    copy.wait()
+    near, far = split(fourier.T)
+    spectrum = dot(near, high[...]) + dot(far, high[...]) + dot(near, low[...])
+    coefficients[...] = spectrum
     own = response[:, :width]
     for place in range(1, radial):
         own = jnp.where(
             lax.axis_index("radial") == place, response[:, place * width : (place + 1) * width], own
         )
-    high, low = split(own * spectrum)
-    load = dot(point_high[...], high) + dot(point_high[...], low) + dot(point_low[...], high)
+    near, far = split(own.T * spectrum)
+    load = (dot_nt(near, high[...]) + dot_nt(far, high[...]) + dot_nt(near, low[...])).T
     for band in range(bands):
         block = pack(load[band * rows : (band + 1) * rows])
         for place in range(radial):
             out[band * radial + place] = block
 
 
-def load_kernel(load, high, low, mask_from, out, mask, sem):
-    copy = pltpu.make_async_copy(mask_from, mask, sem)
-    copy.start()
+def load_kernel(load, high, low, mask, out):
     blocks, rows = load.shape[0], out.shape[0]
     step, width = out.shape[1] // RADIX, high.shape[1] // blocks
     values = jnp.concatenate([unpack(load[block], width) for block in range(blocks)], axis=1)
@@ -696,7 +696,6 @@
     stack += [jnp.where(kind == k, crossed, zero) for k in range(1, RADIX // 2)]
     near, far = split(jnp.concatenate(stack, axis=0))
     total = dot_nt(near, high[...]) + dot_nt(far, high[...]) + dot_nt(near, low[...])
-    copy.wait()
     for m, part in enumerate(unfold([total[k * rows : (k + 1) * rows] for k in range(RADIX)])):
         columns = slice(m * step, (m + 1) * step)
         out[:, columns] = part * mask[:, columns].astype(jnp.float32)
@@ -804,10 +803,7 @@
     ]
     sweep_sems = pltpu.SemaphoreType.DMA((shells, 4))
     point_high, point_low = colatitude_tables(rows * lateral, MODES)
-    stages = [
-        jnp.asarray(a)
-        for a in (point_high.T.copy(), point_low.T.copy(), point_high, point_low)
-    ]
+    stages = [jnp.asarray(point_high), jnp.asarray(point_low)] + [response]
     ring_rows = 2 * (components + 1) * (rows + 1)
     sweep_scratch += [
         sides(*message.shape),
@@ -839,51 +835,51 @@
     ring = lax.ppermute(ring, "radial", swap)
     coefficients, load = pl.pallas_call(
         spectrum_kernel,
-        in_specs=[VMEM] * 5 + [HBM],
+        in_specs=[VMEM] * 4,
         out_specs=[VMEM, VMEM],
         out_shape=[f32((width, MODES)), f32(packed)],
-        scratch_shapes=[pltpu.VMEM(response.shape, jnp.float32), pltpu.SemaphoreType.DMA],
         compiler_params=params(16),
         cost_estimate=cost(200),
-    )(orders, *staged, hbm(response))
+    )(orders, *staged)
     eta, load = lax.optimization_barrier((eta, load))
     load = lax.all_to_all(load, both, split_axis=0, concat_axis=0, tiled=True)
 
     stages = [high, low]
-    displacement, token, *staged = pl.pallas_call(
+    displacement, token, mask, *staged = pl.pallas_call(
         second_kernel,
-        in_specs=[HBM] * 5 + [ANY] + [HBM] * (2 + len(stages)),
-        out_specs=[HBM, VMEM] + [VMEM] * len(stages),
+        in_specs=[HBM] * 5 + [ANY] + [HBM] * (3 + len(stages)),
+        out_specs=[HBM, VMEM, VMEM] + [VMEM] * len(stages),
         out_shape=[
             in_hbm(*initial_displacement.shape),
             f32((TILE, 128)),
+            jax.ShapeDtypeStruct(ocean_mask.shape, jnp.bfloat16),
             *(jax.ShapeDtypeStruct(a.shape, a.dtype) for a in stages),
         ],
         scratch_shapes=[
             *sweep_scratch,
             scratch(2 * components, rows, count),
             scratch(rows, count),
+            pltpu.VMEM(ocean_mask.shape, ocean_mask.dtype),
             sweep_sems,
-            pltpu.SemaphoreType.DMA((7 + 2 * components + len(stages),)),
+            pltpu.SemaphoreType.DMA((8 + 2 * components + len(stages),)),
         ],
         compiler_params=params(28),
         cost_estimate=cost(50),
     )(
         *(hbm(a) for a in (smoothed, tensors[1], eta, tensors[0], diagonal)),
         ring,
-        *(hbm(a) for a in (beside, own)),
+        *(hbm(a) for a in (beside, own, ocean_mask)),
         *stages,
     )
 
     sea_load = pl.pallas_call(
         load_kernel,
-        in_specs=[VMEM] * 3 + [HBM],
+        in_specs=[VMEM] * 4,
         out_specs=VMEM,
         out_shape=f32((rows, count)),
-        scratch_shapes=[pltpu.VMEM(ocean_mask.shape, ocean_mask.dtype), pltpu.SemaphoreType.DMA],
         compiler_params=params(20),
         cost_estimate=cost(3),
-    )(load, *staged, hbm(ocean_mask))
+    )(load, *staged, mask)
     return (displacement, coefficients.T, sea_load)
 
 

time: 50.9 us -> 48.1 us (0.945)
  Pallas kernels: 26.5 us -> 23.7 us
  waiting for transfers between devices: 0.54 us -> 1.06 us
    pallas_call x3, Pallas kernels: 13.1 us -> 10.8 us  [the longest x1 7.85 us: shards(): pl.pallas_call(second_kernel, in_specs=[HBM] * 5 + [ANY] + [HBM] * (3 + l...]
  transfers between devices with their start and end apart: 7 -> 7, of which waited for: 1 -> 2; matrix products, arithmetic and copies ran while one was open for 0% -> 0% of each run, Pallas kernels for 43% -> 42%
where the time goes in v6:
time: 48.1 us; the launch traced here: 47.7 us
  Pallas kernels  23.7 us (49%)
  starting transfers between devices  22.2 us (46%)
  waiting for transfers between devices  1.06 us (2%)
  between operations  0.76 us (2%)
    all_to_all x1, starting transfers between devices, shards(): lax.all_to_all(orders, both, split_axis=0, concat_axis=0, tiled=True)  10 us
    pallas_call x1, Pallas kernels, shards(): pl.pallas_call(second_kernel, in_specs=[HBM] * 5 + [ANY] + [HBM] * (3 + l...  7.85 us
    pallas_call x1, Pallas kernels, shards(): pl.pallas_call(first_kernel, in_specs=[HBM] * 3 + [ANY] * 4 + [HBM] * len...  6.93 us
    all_to_all x1, starting transfers between devices, shards(): load = lax.all_to_all(load, both, split_axis=0, concat_axis=0, tiled=True)  5.26 us
    ppermute x1, starting transfers between devices, shards(): lower_one = lax.ppermute(lower_one, both, lower_only(first))  4.88 us
    pallas_call x1, Pallas kernels, shards(): pl.pallas_call(viscosity_kernel, in_specs=[HBM] * 4 + [ANY], out_specs=[H...  2.9 us
    pallas_call x1, Pallas kernels, shards(): pl.pallas_call(message_kernel, in_specs=[HBM] * 4, out_specs=[VMEM] * 2,...  2.44 us
    pallas_call x1, Pallas kernels, shards(): pl.pallas_call(spectrum_kernel, in_specs=[VMEM] * 4, out_specs=[VMEM, VME...  1.51 us
  transfers between devices with their start and end apart: 7, of which 2 were waited for; matrix products, arithmetic and copies ran while one was open for 0% of the time, Pallas kernels for 42%

profile of v6, /device:TPU:0, one launch (start us, length us, event | category | flops | bytes accessed | tf_op | source)
XLA Modules:
  0.0 47.7 jit_solution(6569440044976786036)
XLA Ops:
  0.6 2.4 %shard_map.121 = (f32[32,2048]{1,0:T(8,128)S(1)}, f32[32,2048]{1,0:T(8,128)S(1)}) custom-call(f32[16]{0:T(128)} %viscosity_from.3, f32[3,4,32,2048]{3,2,1,0:T(8,128)} %start.1, f32[3,4,32,2048]{3,2,1,0:T(8,128)} %f.7, s32[4,32,2048]{2,1,0:T(8,128)} %index_from.1), custom_call_target="tpu_custom_call" | custom-call | bytes 60000000 | tf_op jit(solution)/shard_map/pallas_call | solution.py:730
  3.1 0.7 %collective-permute-start.1 = (f32[32,2048]{1,0:T(8,128)S(1)}, f32[32,2048]{1,0:T(8,128)S(1)}, u32[]{:S(2)}, u32[]{:S(2)}) collective-permute-start(f32[32,2048]{1,0:T(8,128)S(1)} %get-tuple-element.40.own_two), channel_id=1, source_target_pairs={{3,5},{5,3},{7,9},{9,7},{11,13},{13,11},{19,21},{21,19},{23,25},{2... | collective-permute-start | bytes 786440 | tf_op jit(solution)/shard_map/ppermute | solution.py:746
  3.8 0.7 %collective-permute-start = (f32[32,2048]{1,0:T(8,128)S(1)}, f32[32,2048]{1,0:T(8,128)S(1)}, u32[]{:S(2)}, u32[]{:S(2)}) collective-permute-start(f32[32,2048]{1,0:T(8,128)S(1)} %get-tuple-element.39.token.own_one), channel_id=1, source_target_pairs={{1,3},{3,1},{5,7},{7,5},{9,11},{11,9},{13,15},{15,13},{17,19},{19,... | collective-permute-start | bytes 786440 | tf_op jit(solution)/shard_map/ppermute | solution.py:747
  4.4 2.9 %shard_map.122 = (f32[4,32,2048]{2,1,0:T(8,128)}, f32[2,32,2048]{2,1,0:T(8,128)S(1)}, f32[2,32,2048]{2,1,0:T(8,128)S(1)}, f32[32,2048]{1,0:T(8,128)S(1)}) custom-call(f32[16]{0:T(128)} %viscosity_from.3, f32[3,4,32,2048]{3,2,1,0:T(8,128)} %start.1, f32[3,4,32,2048]{3,2,1,0:T(8,128)} %f.7, s32[4,32,2048]{2,1,0:T(8,128)} %index_from.1, ...), custom_call_target="tpu_custom_call" | custom-call | bytes 60000000 | tf_op jit(solution)/shard_map/pallas_call | solution.py:748
  7.3 4.9 %collective-permute-start.2 = (f32[32,2048]{1,0:T(8,128)S(1)}, f32[32,2048]{1,0:T(8,128)S(1)}, u32[]{:S(2)}, u32[]{:S(2)}) collective-permute-start(f32[32,2048]{1,0:T(8,128)S(1)} %get-tuple-element.39.token.own_one), channel_id=1, source_target_pairs={{0,2},{2,0},{4,6},{6,4},{8,10},{10,8},{12,14},{14,12},{16,18},{18,... | collective-permute-start | bytes 786440 | tf_op jit(solution)/shard_map/ppermute | solution.py:771
  12.2 0.7 %collective-permute-start.3 = (f32[32,2048]{1,0:T(8,128)S(1)}, f32[32,2048]{1,0:T(8,128)S(1)}, u32[]{:S(2)}, u32[]{:S(2)}) collective-permute-start(f32[32,2048]{1,0:T(8,128)S(1)} %get-tuple-element.40.own_two), channel_id=1, source_target_pairs={{2,4},{4,2},{6,8},{8,6},{10,12},{12,10},{18,20},{20,18},{22,24},{2... | collective-permute-start | bytes 786440 | tf_op jit(solution)/shard_map/ppermute | solution.py:772
  12.9 0.0 collective-permute-done.1.two
  12.9 0.0 collective-permute-done.one
  12.9 0.7 %shard_map.123 = f32[16,16,128]{2,1,0:T(8,128)} custom-call(f32[2,32,2048]{2,1,0:T(8,128)S(1)} %get-tuple-element.35.surface_swept, f32[2,32,2048]{2,1,0:T(8,128)S(1)} %get-tuple-element.36.surface_eta, f32[32,2048]{1,0:T(8,128)S(1)} %get-tuple-element.37.force, f32[32,2048]{1,0:T(8,128)S(1)} %get-tuple-element.39.token.own_one, ...), custom_call_target="tpu_custom_call" | custom-call | bytes 600000000 | tf_op jit(solution)/shard_map/pallas_call | solution.py:778
  13.6 10.0 %all-to-all-start = ((f32[16,16,128]{2,1,0:T(8,128)}), f32[16,16,128]{2,1,0:T(8,128)S(1)}, u32[]{:S(2)}, u32[]{:S(2)}) async-start(f32[16,16,128]{2,1,0:T(8,128)} %shard_map.123), calls=%async_computation | async-start | bytes 262144 | tf_op jit(solution)/shard_map/all_to_all | solution.py:795
  23.7 0.0 collective-permute-done.2.lower_one
  23.7 0.0 collective-permute-done.3.lower_two
  23.7 6.9 %shard_map.124 = (f32[3,4,32,2048]{3,2,1,0:T(8,128)}, f32[32,2048]{1,0:T(8,128)}, f32[264,2048]{1,0:T(8,128)}, f32[4,8,2048]{2,1,0:T(8,128)}, f32[2,32,2048]{2,1...) custom-call(f32[3,4,32,2048]{3,2,1,0:T(8,128)} %start.1, ...), custom_call_target="tpu_custom_call" | custom-call | bytes 150000000 | tf_op jit(solution)/shard_map/pallas_call | solution.py:814
  30.6 1.0 %all-to-all-done.orders = f32[16,16,128]{2,1,0:T(8,128)S(1)} async-done(((f32[16,16,128]{2,1,0:T(8,128)}), f32[16,16,128]{2,1,0:T(8,128)S(1)}, u32[]{:S(2)}, u32[]{:S(2)}) %all-to-all-start) | async-done | bytes 131104 | tf_op jit(solution)/shard_map/all_to_all | solution.py:795
  31.6 0.0 collective-permute-start.4
  31.6 1.5 %shard_map.125 = (f32[64,512]{1,0:T(8,128)}, f32[16,16,128]{2,1,0:T(8,128)}) custom-call(f32[16,16,128]{2,1,0:T(8,128)S(1)} %all-to-all-done.orders, bf16[256,512]{1,0:T(8,128)(2,1)S(1)} %get-tuple-element.44.high, bf16[256,512]{1,0:T(8,128)(2,1)S(1)} %get-tuple-element.45.low, f32[512,128]{1,0:T(8,128)S(1)} %get-tuple-element.46.response), custom_call_target="tpu_custom_call" | custom-call | bytes 600000000 | tf_op jit(solution)/shard_map/pallas_call | solution.py:836
  33.1 5.3 %all-to-all-start.1 = ((f32[16,16,128]{2,1,0:T(8,128)}), f32[16,16,128]{2,1,0:T(8,128)S(1)}, u32[]{:S(2)}, u32[]{:S(2)}) async-start(f32[16,16,128]{2,1,0:T(8,128)} %get-tuple-element.55), calls=%async_computation.1 | async-start | bytes 262144 | tf_op jit(solution)/shard_map/all_to_all | solution.py:845
  38.4 0.0 collective-permute-done.4.ring
  38.4 7.8 %shard_map.126 = (f32[3,4,32,2048]{3,2,1,0:T(8,128)}, f32[8,128]{1,0:T(8,128)}, bf16[32,2048]{1,0:T(8,128)(2,1)S(1)}, bf16[256,1024]{1,0:T(8,128)(2,1)S(1)}, bf16[256,1024]{1,0:T(8,128)(2,1)S(1)}) custom-call(f32[3,4,32,2048]{3,2,1,0:T(8,128)} %get-tuple-element.41.d, f32[3,4,32,2048]{3,2,1,0:T(8,128)} %f.7, f32[4,32,2048]{2,1,0:T(8,128)} %get-tuple-element.48.h, ...), custom_call_target="tpu_custom_call" | custom-call | bytes 150000000 | tf_op jit(solution)/shard_map/pallas_call | solution.py:848
  46.2 0.1 all-to-all-done.1.load
  46.3 1.4 %shard_map.127 = f32[32,2048]{1,0:T(8,128)} custom-call(f32[16,16,128]{2,1,0:T(8,128)S(1)} %all-to-all-done.1.load, bf16[256,1024]{1,0:T(8,128)(2,1)S(1)} %get-tuple-element.56.high, bf16[256,1024]{1,0:T(8,128)(2,1)S(1)} %get-tuple-element.57.low, bf16[32,2048]{1,0:T(8,128)(2,1)S(1)} %get-tuple-element.58.mask), custom_call_target="tpu_custom_call" | custom-call | bytes 9000000 | tf_op jit(solution)/shard_map/pallas_call | solution.py:875
Async XLA Ops:
  3.1 9.8 %collective-permute-start.1 = (f32[32,2048]{1,0:T(8,128)S(1)}, f32[32,2048]{1,0:T(8,128)S(1)}, u32[]{:S(2)}, u32[]{:S(2)}) collective-permute-start(f32[32,2048]{1,0:T(8,128)S(1)} %get-tuple-element.40.own_two), channel_id=1, source_target_pairs={{3,5},{5,3},{7,9},{9,7},{11,13},{13,11},{19,21},{21,19},{23,25},{2... | collective-permute-start | bytes 786440 | tf_op jit(solution)/shard_map/ppermute | solution.py:746
  3.8 9.2 %collective-permute-start = (f32[32,2048]{1,0:T(8,128)S(1)}, f32[32,2048]{1,0:T(8,128)S(1)}, u32[]{:S(2)}, u32[]{:S(2)}) collective-permute-start(f32[32,2048]{1,0:T(8,128)S(1)} %get-tuple-element.39.token.own_one), channel_id=1, source_target_pairs={{1,3},{3,1},{5,7},{7,5},{9,11},{11,9},{13,15},{15,13},{17,19},{19,... | collective-permute-start | bytes 786440 | tf_op jit(solution)/shard_map/ppermute | solution.py:747
  7.3 16.3 %collective-permute-start.2 = (f32[32,2048]{1,0:T(8,128)S(1)}, f32[32,2048]{1,0:T(8,128)S(1)}, u32[]{:S(2)}, u32[]{:S(2)}) collective-permute-start(f32[32,2048]{1,0:T(8,128)S(1)} %get-tuple-element.39.token.own_one), channel_id=1, source_target_pairs={{0,2},{2,0},{4,6},{6,4},{8,10},{10,8},{12,14},{14,12},{16,18},{18,... | collective-permute-start | bytes 786440 | tf_op jit(solution)/shard_map/ppermute | solution.py:771
  12.2 11.4 %collective-permute-start.3 = (f32[32,2048]{1,0:T(8,128)S(1)}, f32[32,2048]{1,0:T(8,128)S(1)}, u32[]{:S(2)}, u32[]{:S(2)}) collective-permute-start(f32[32,2048]{1,0:T(8,128)S(1)} %get-tuple-element.40.own_two), channel_id=1, source_target_pairs={{2,4},{4,2},{6,8},{8,6},{10,12},{12,10},{18,20},{20,18},{22,24},{2... | collective-permute-start | bytes 786440 | tf_op jit(solution)/shard_map/ppermute | solution.py:772
  13.6 18.0 %all-to-all-start = ((f32[16,16,128]{2,1,0:T(8,128)}), f32[16,16,128]{2,1,0:T(8,128)S(1)}, u32[]{:S(2)}, u32[]{:S(2)}) async-start(f32[16,16,128]{2,1,0:T(8,128)} %shard_map.123), calls=%async_computation | async-start | bytes 262144 | tf_op jit(solution)/shard_map/all_to_all | solution.py:795
  31.6 6.8 %collective-permute-start.4 = (f32[264,2048]{1,0:T(8,128)}, f32[264,2048]{1,0:T(8,128)S(1)}, u32[]{:S(2)}, u32[]{:S(2)}) collective-permute-start(f32[264,2048]{1,0:T(8,128)} %get-tuple-element.50), channel_id=1, source_target_pairs={{0,1},{1,0},{2,3},{3,2},{4,5},{5,4},{6,7},{7,6},{8,9},{9,8},{10,11... | collective-permute-start | bytes 6488072 | tf_op jit(solution)/shard_map/ppermute | solution.py:835
  33.1 13.2 %all-to-all-start.1 = ((f32[16,16,128]{2,1,0:T(8,128)}), f32[16,16,128]{2,1,0:T(8,128)S(1)}, u32[]{:S(2)}, u32[]{:S(2)}) async-start(f32[16,16,128]{2,1,0:T(8,128)} %get-tuple-element.55), calls=%async_computation.1 | async-start | bytes 262144 | tf_op jit(solution)/shard_map/all_to_all | solution.py:845

commit v7 on v6

--- a/solution.py
+++ b/solution.py
@@ -14,6 +14,7 @@
 RELAXATION = 0.8
 TILE = 8
 RADIX = 8
+EARLY = 2
 MIB = 1 << 20
 ANY = pl.BlockSpec(memory_space=pl.ANY)
 HBM = pl.BlockSpec(memory_space=pltpu.HBM)
@@ -247,50 +248,68 @@
         two[pl.ds(place * shells, shells)] = both[shells:]
 
 
+def shell_order(shells):
+    lower = lax.axis_index("radial") == 0
+    return lambda k: jnp.where(lower, k, shells - 1 - k)
+
+
 def viscosity_kernel(
-    viscosity_from, d, f, index_from, token, eta_out, surface_swept, surface_eta, surface_force,
-    index, eta, field, force, viscosity, sems, eta_sems,
+    viscosity_from, d, f, index_from, token, eta_out, out, surface_swept, surface_eta, surface_force,
+    index, eta, field, force, result, viscosity, sems, more_sems,
 ):
     del token
     _, shells, rows, count = d.shape
+    components = d.shape[0]
     block = pl.ds(TILE, rows)
+    shell = shell_order(shells)
     value_copy = pltpu.make_async_copy(viscosity_from, viscosity, sems.at[shells])
-    layers = [pltpu.make_async_copy(index_from.at[s], index.at[s], sems.at[s]) for s in range(shells)]
-    surface_copies = [
-        pltpu.make_async_copy(d.at[0, pl.ds(shells - 3, 3)], field.at[pl.ds(0, 3), block], sems.at[shells + 1]),
-        pltpu.make_async_copy(f.at[0, pl.ds(shells - 2, 2)], force, sems.at[shells + 2]),
+    layers = [pltpu.make_async_copy(index_from.at[shell(k)], index.at[k], sems.at[k]) for k in range(shells)]
+    fields = [
+        pltpu.make_async_copy(d.at[:, shell(k)], field.at[:, k + 1, block], more_sems.at[k]) for k in range(EARLY + 1)
     ]
-    start_all([value_copy, *layers, *surface_copies])
+    forces = [
+        pltpu.make_async_copy(f.at[:, shell(k)], force.at[:, k], more_sems.at[EARLY + 1 + k]) for k in range(EARLY)
+    ]
+    start_all([value_copy, *layers, *fields, *forces])
     zeros = jnp.zeros((rows, count), jnp.float32)
-    field[3, block] = zeros
-    eta[shells, block] = zeros
+    for c in range(components):
+        field[c, 0, block] = zeros
+    eta[0, block] = zeros
     value_copy.wait()
     stores = []
-    for s in range(shells):
-        layers[s].wait()
+    for k in range(shells):
+        layers[k].wait()
 
         def lookup(step, _):
             start = pl.multiple_of(step * TILE, TILE)
-            eta[s, pl.ds(start + TILE, TILE)] = half_viscosity(index[s, pl.ds(start, TILE)], viscosity)
+            eta[k + 1, pl.ds(start + TILE, TILE)] = half_viscosity(index[k, pl.ds(start, TILE)], viscosity)
             return 0
 
         lax.fori_loop(0, rows // TILE, lookup, 0)
-        stores += start_all([pltpu.make_async_copy(eta.at[s, block], eta_out.at[s], eta_sems.at[s])])
-    for copy in surface_copies:
-        copy.wait()
-
-    def sweep(step, _):
-        start = pl.multiple_of(step * TILE, TILE)
-        part = pl.ds(start, TILE)
-        for k in range(2):
-            weights, factor = relax_weights(*around(eta, (), shells - 2 + k, start + TILE))
-            middle, others = around(field, (), k + 1, start + TILE)
-            surface_swept[k, part] = relax(weights, factor, middle, others, force[k, part])
-            surface_eta[k, part] = eta[shells - 2 + k, pl.ds(start + TILE, TILE)]
-        surface_force[part] = force[1, part]
-        return 0
-
-    lax.fori_loop(0, rows // TILE, sweep, 0)
+        stores += start_all(
+            [pltpu.make_async_copy(eta.at[k + 1, block], eta_out.at[shell(k)], more_sems.at[2 * EARLY + 1 + k])]
+        )
+    for k in range(EARLY):
+        for copy in (fields[: EARLY + 1] if k == 0 else []) + forces[k : k + 1]:
+            copy.wait()
+
+        def sweep(step, _):
+            start = pl.multiple_of(step * TILE, TILE)
+            part = pl.ds(start, TILE)
+            weights, factor = relax_weights(*around(eta, (), k + 1, start + TILE))
+            for c in range(components):
+                middle, others = around(field, (c,), k + 1, start + TILE)
+                result[c, k, part] = relax(weights, factor, middle, others, force[c, k, part])
+            surface_swept[1 - k, part] = result[0, k, part]
+            surface_eta[1 - k, part] = eta[k + 1, pl.ds(start + TILE, TILE)]
+            if k == 0:
+                surface_force[part] = force[0, 0, part]
+            return 0
+
+        lax.fori_loop(0, rows // TILE, sweep, 0, unroll=2)
+        stores += start_all(
+            [pltpu.make_async_copy(result.at[:, k], out.at[:, k], more_sems.at[2 * EARLY + 1 + shells + k])]
+        )
     for copy in stores:
         copy.wait()
 
@@ -367,17 +386,17 @@
             out[block] = pack(fourier[:, block * width : (block + 1) * width])
 
 
-def sweep_shells(d, f, h, out, field, eta, force, result, sems, before_first, last_loads, arrived, finish, after_shell):
-    components, shells, rows, count = d.shape
+def sweep_shells(
+    begin, source, f, h, store, field, eta, force, result, sems, before_first, last_loads, arrived, finish, after_shell
+):
+    components, shells, rows, count = f.shape
     inner = pl.ds(TILE, rows)
-    lower = lax.axis_index("radial") == 0
-    shell = lambda k: jnp.where(lower, k, shells - 1 - k)
-    nothing = jnp.where(lower, 0, shells + 1)
+    shell = shell_order(shells)
 
     def field_loads(k):
         s = shell(k)
         return [
-            pltpu.make_async_copy(d.at[:, s], field.at[:, s + 1, inner], sems.at[k, 0]),
+            pltpu.make_async_copy(source(k), field.at[:, s + 1, inner], sems.at[k, 0]),
             pltpu.make_async_copy(h.at[s], eta.at[s + 1, inner], sems.at[k, 1]),
             *(last_loads if k == shells - 1 else []),
         ]
@@ -385,28 +404,36 @@
     def force_load(k):
         return [pltpu.make_async_copy(f.at[:, shell(k)], force.at[:, shell(k)], sems.at[k, 2])]
 
-    loads = [start_all(field_loads(0)), start_all(field_loads(1))]
-    forces = [start_all(force_load(0))]
-    zeros = jnp.zeros((rows, count), jnp.float32)
-    for c in range(components):
-        field[c, nothing, inner] = zeros
-    eta[nothing, inner] = zeros
+    loads = {k: start_all(field_loads(k)) for k in range(max(begin - 1, 0), begin + 2)}
+    forces = {begin: start_all(force_load(begin))}
+    if begin == 0:
+        nothing = jnp.where(lax.axis_index("radial") == 0, 0, shells + 1)
+        zeros = jnp.zeros((rows, count), jnp.float32)
+        for c in range(components):
+            field[c, nothing, inner] = zeros
+        eta[nothing, inner] = zeros
     before_first()
-    loads.append(start_all(field_loads(2)))
-    forces.append(start_all(force_load(1)))
-    for copy in loads[0]:
-        copy.wait()
-    stores = []
-    for k in range(shells):
+
+    def start_until(k):
+        for ahead in range(begin, shells):
+            if ahead <= k and ahead not in loads:
+                loads[ahead] = start_all(field_loads(ahead))
+            if ahead < k and ahead not in forces:
+                forces[ahead] = start_all(force_load(ahead))
+
+    start_until(begin + 2)
+    stores, there = [], set()
+    for k in range(begin, shells):
         s = shell(k)
-        if k + 3 < shells:
-            loads.append(start_all(field_loads(k + 3)))
-        if k + 2 < shells:
-            forces.append(start_all(force_load(k + 2)))
-        for copy in (loads[k + 1] if k + 1 < shells else []) + forces[k]:
+        start_until(k + 3)
+        for near in range(max(k - 1, 0), min(k + 2, shells)):
+            if near not in there:
+                there.add(near)
+                for copy in loads[near]:
+                    copy.wait()
+                arrived(near)
+        for copy in forces[k]:
             copy.wait()
-        if k == shells - 2:
-            arrived()
 
         def tile(step, _):
             first = pl.multiple_of(step * TILE, TILE)
@@ -418,11 +445,11 @@
                 for c in range(components):
                     middle, others = around(field, (c,), s + 1, first + TILE)
                     result[c, s, part] = relax(weights, factor, middle, others, force[c, s, part])
-            pltpu.make_async_copy(result.at[:, s, part], out.at[:, s, part], sems.at[k, 3]).start()
+            pltpu.make_async_copy(result.at[:, s, part], store(k).at[:, part], sems.at[k, 3]).start()
             return 0
 
         lax.fori_loop(0, rows // TILE, tile, 0, unroll=2)
-        stores.append(pltpu.make_async_copy(result.at[:, s], out.at[:, s], sems.at[k, 3]))
+        stores.append(pltpu.make_async_copy(result.at[:, s], store(k), sems.at[k, 3]))
         after_shell(s, k)
     for copy in stores:
         copy.wait()
@@ -448,18 +475,29 @@
     return copies(sources)
 
 
-def first_kernel(d, f, h, one, two, lower_one, lower_two, *refs):
+def first_kernel(d, f, h, one, two, lower_one, lower_two, mine_one, mine_two, *refs):
     components, shells, rows, count = d.shape
-    staged = (len(refs) - 14) // 2
+    staged = (len(refs) - 13) // 2
     sources, refs = refs[:staged], refs[staged:]
     out, diagonal_out, ring_out, own_out, beside_out, *targets = refs[: 5 + staged]
-    field, eta, force, result, messages, edges, own, diagonal, sems, more_sems = refs[5 + staged :]
+    field, eta, force, result, messages, edges, diagonal, sems, more_sems = refs[5 + staged :]
     arrivals = load_messages((one, two), (lower_one, lower_two), messages, more_sems)
     lower = lax.axis_index("radial") == 0
-    last = jnp.where(lower, shells - 1, 0)
-    copies = []
+    last, beyond = jnp.where(lower, shells - 1, 0), jnp.where(lower, shells + 1, 0)
+    values = pl.ds(0, own_out.shape[1])
+    copies = start_all(
+        [
+            pltpu.make_async_copy(mine.at[values], own_out.at[k], more_sems.at[4 + components + k])
+            for k, mine in enumerate((mine_one, mine_two))
+        ]
+    )
 
     def before_first():
+        block = pl.ds(TILE, rows)
+        zeros = jnp.zeros((rows, count), jnp.float32)
+        for c in range(components):
+            field[c, beyond, block] = zeros
+        eta[beyond, block] = zeros
         for copy in arrivals:
             copy.wait()
         before, after = by_parity(messages.at[0], messages.at[1])
@@ -482,18 +520,15 @@
             )
         )
 
-    def arrived():
+    def arrived(k):
+        if k < shells - 1:
+            return
         block = pl.ds(TILE, rows)
-        zeros = jnp.zeros((rows, count), jnp.float32)
-        beyond = jnp.where(lower, shells + 1, 0)
-        for c in range(components):
-            field[c, beyond, block] = zeros
-        eta[beyond, block] = zeros
         sources = [field.at[c, last + 1, block] for c in range(components)] + [eta.at[last + 1, block]]
         copies.extend(
             start_all(
                 [
-                    pltpu.make_async_copy(source, ring_out.at[pl.ds(k * rows, rows)], more_sems.at[4 + k])
+                    pltpu.make_async_copy(source, ring_out.at[pl.ds(k * rows, rows)], more_sems.at[6 + components + k])
                     for k, source in enumerate(sources)
                 ]
             )
@@ -514,19 +549,15 @@
             result[c, s, part] = total
 
     def after_shell(s, k):
-        if k == 0:
+        if k == EARLY:
             copies.extend(
                 start_all(
                     [
-                        pltpu.make_async_copy(source, target, more_sems.at[7 + 2 * components + n])
+                        pltpu.make_async_copy(source, target, more_sems.at[8 + 3 * components + n])
                         for n, (source, target) in enumerate(zip(sources, targets))
                     ]
                 )
             )
-        for side, place in enumerate((TILE, TILE + rows - 1)):
-            for c in range(components):
-                own[c, side * shells + s] = field[c, s + 1, place]
-            own[components, side * shells + s] = eta[s + 1, place]
         if k == shells - 1:
             sums = [result.at[c, s] for c in range(components)] + [diagonal]
             copies.extend(
@@ -535,31 +566,30 @@
                         pltpu.make_async_copy(
                             source,
                             ring_out.at[pl.ds((components + 1 + n) * rows, rows)],
-                            more_sems.at[5 + components + n],
+                            more_sems.at[7 + 2 * components + n],
                         )
                         for n, source in enumerate(sums)
                     ]
-                    + [
-                        pltpu.make_async_copy(diagonal, diagonal_out, more_sems.at[6 + 2 * components]),
-                        pltpu.make_async_copy(own, own_out, more_sems.at[0]),
-                    ]
+                    + [pltpu.make_async_copy(diagonal, diagonal_out, more_sems.at[0])]
                 )
             )
 
+    shell = shell_order(shells)
     sweep_shells(
-        d, f, h, out, field, eta, force, result, sems, before_first, [], arrived, finish, after_shell
+        EARLY, lambda k: d.at[:, shell(k)], f, h, lambda k: out.at[:, k - EARLY],
+        field, eta, force, result, sems, before_first, [], arrived, finish, after_shell,
     )
     for copy in copies:
         copy.wait()
 
 
-def second_kernel(d, f, h, start, diagonal_from, ring, beside, own_from, *refs):
-    components, shells, rows, count = d.shape
-    staged = (len(refs) - 17) // 2
+def second_kernel(early, late, f, h, start, diagonal_from, ring, beside, own_from, *refs):
+    components, shells, rows, count = f.shape
+    staged = (len(refs) - 18) // 2
     mask_from, *sources = refs[: 1 + staged]
     out, token, mask_out, *targets = refs[1 + staged : 4 + 2 * staged]
     (
-        field, eta, force, result, messages, edges, own, diagonal, raw, ring_diagonal, mask, sems, more_sems
+        field, eta, force, result, messages, edges, own, diagonal, raw, ring_diagonal, mask, ends, sems, more_sems
     ) = refs[4 + 2 * staged :]
     token[...] = jnp.zeros_like(token)
     tail = ring.at[pl.ds(2 * (components + 1) * rows, edges.shape[0])]
@@ -574,6 +604,7 @@
     lower = radial == 0
     last, beyond = jnp.where(lower, shells - 1, 0), jnp.where(lower, shells + 1, 0)
     block = pl.ds(TILE, rows)
+    shell = shell_order(shells)
     from_ring = lambda k, target, sem: pltpu.make_async_copy(
         ring.at[pl.ds(k * rows, rows)], target, more_sems.at[sem]
     )
@@ -605,17 +636,30 @@
             place < shells, edges[pl.ds(k, 1)], edges[pl.ds(components + 1 + k, 1)]
         )
         inside = jnp.where(place < shells, lateral, lax.axis_size("lateral") - 1 - lateral) > 0
+        mine = by_parity(own.at[0], own.at[1])
+        own_row = lambda k: jnp.concatenate([part[k * shells : (k + 1) * shells] for part in mine], axis=0)
         middle = pair(components)
-        weight = middle + own[components]
+        weight = middle + own_row(components)
         across = jnp.where(shared, middle + across_of(components), zero)
         factor = RELAXATION / (pair(2 * components + 1) + weight + across)
+        own_factor = RELAXATION / (own_row(2 * components + 1) + weight)
         for c in range(components):
-            total = pair(components + 1 + c) + weight * own[c] + across * across_of(c)
+            total = pair(components + 1 + c) + weight * own_row(c) + across * across_of(c)
             edge = jnp.where(inside, (1.0 - RELAXATION) * pair(c) + factor * total, zero)
+            total = own_row(components + 1 + c) + weight * pair(c)
+            ends[c] = (1.0 - RELAXATION) * own_row(c) + own_factor * total
             set_edge(field, (c,), shells, rows, lambda s: edge[s], lambda s: edge[shells + s])
         set_edge(eta, (), shells, rows, lambda s: middle[s], lambda s: middle[shells + s])
 
-    def arrived():
+    def arrived(k):
+        if k < EARLY:
+            s = shell(k)
+            for side, place in enumerate((TILE, TILE + rows - 1)):
+                for c in range(components):
+                    field[c, s + 1, pl.ds(place, 1)] = ends[c, pl.ds(side * shells + s, 1)]
+        if k < shells - 1:
+            return
+
         def tile(step, _):
             first = pl.multiple_of(step * TILE, TILE)
             part, place = pl.ds(first, TILE), pl.ds(first + TILE, TILE)
@@ -656,7 +700,8 @@
             mask_out[...] = mask[...].astype(jnp.float32).astype(jnp.bfloat16)
 
     sweep_shells(
-        d, f, h, out, field, eta, force, result, sems, before_first, last_loads, arrived, finish, after_shell
+        0, lambda k: early.at[:, k] if k < EARLY else late.at[:, k - EARLY], f, h, lambda k: out.at[:, shell(k)],
+        field, eta, force, result, sems, before_first, last_loads, arrived, finish, after_shell,
     )
     for copy in copies:
         copy.wait()
@@ -745,12 +790,13 @@
     )(viscosity, *tensors)
     two = lax.ppermute(mine[1], both, top_only(second))
     one = lax.ppermute(mine[0], both, top_only(first))
-    eta, *surface = pl.pallas_call(
+    eta, early, *surface = pl.pallas_call(
         viscosity_kernel,
         in_specs=[HBM] * 4 + [ANY],
-        out_specs=[HBM, VMEM, VMEM, VMEM],
+        out_specs=[HBM, HBM, VMEM, VMEM, VMEM],
         out_shape=[
             in_hbm(shells, rows, count),
+            in_hbm(components, EARLY, rows, count),
             f32((2, rows, count)),
             f32((2, rows, count)),
             f32((rows, count)),
@@ -758,13 +804,14 @@
         scratch_shapes=[
             pltpu.VMEM(layer_index.shape, jnp.int32),
             scratch(shells + 1, rows + 2 * TILE, count),
-            scratch(4, rows + 2 * TILE, count),
-            scratch(2, rows, count),
+            scratch(components, EARLY + 2, rows + 2 * TILE, count),
+            scratch(components, EARLY, rows, count),
+            scratch(components, EARLY, rows, count),
             pltpu.SMEM(viscosity.shape, jnp.float32),
-            pltpu.SemaphoreType.DMA((3 + shells,)),
-            pltpu.SemaphoreType.DMA((shells,)),
+            pltpu.SemaphoreType.DMA((1 + shells,)),
+            pltpu.SemaphoreType.DMA((3 * EARLY + 1 + shells,)),
         ],
-        compiler_params=params(16),
+        compiler_params=params(24),
         cost_estimate=cost(20),
     )(viscosity, *tensors, mine[0])
     lower_one, lower_two, eta = lax.optimization_barrier((*mine, eta))
@@ -808,29 +855,29 @@
     sweep_scratch += [
         sides(*message.shape),
         scratch(2 * (components + 1), count),
-        scratch(components + 1, 2 * shells, count),
-        scratch(rows, count),
     ]
-    smoothed, diagonal, ring, own, beside, *staged = pl.pallas_call(
+    own_shape = (2, *message.shape)
+    late, diagonal, ring, own, beside, *staged = pl.pallas_call(
         first_kernel,
-        in_specs=[HBM] * 3 + [ANY] * 4 + [HBM] * len(stages),
+        in_specs=[HBM] * 3 + [ANY] * 6 + [HBM] * len(stages),
         out_specs=[HBM] * 5 + [VMEM] * len(stages),
         out_shape=[
-            in_hbm(*initial_displacement.shape),
+            in_hbm(components, shells - EARLY, rows, count),
             in_hbm(rows, count),
             in_hbm(ring_rows, count),
-            in_hbm(components + 1, 2 * shells, count),
+            in_hbm(*own_shape),
             in_hbm(2, *message.shape),
             *(jax.ShapeDtypeStruct(a.shape, a.dtype) for a in stages),
         ],
         scratch_shapes=[
             *sweep_scratch,
+            scratch(rows, count),
             sweep_sems,
-            pltpu.SemaphoreType.DMA((7 + 2 * components + len(stages),)),
+            pltpu.SemaphoreType.DMA((8 + 3 * components + len(stages),)),
         ],
         compiler_params=params(28),
         cost_estimate=cost(50),
-    )(*tensors[:2], eta, one, two, lower_one, lower_two, *(hbm(a) for a in stages))
+    )(*tensors[:2], hbm(eta), one, two, lower_one, lower_two, *mine, *(hbm(a) for a in stages))
     ring, orders = lax.optimization_barrier((ring, orders))
     ring = lax.ppermute(ring, "radial", swap)
     coefficients, load = pl.pallas_call(
@@ -847,7 +894,7 @@
     stages = [high, low]
     displacement, token, mask, *staged = pl.pallas_call(
         second_kernel,
-        in_specs=[HBM] * 5 + [ANY] + [HBM] * (3 + len(stages)),
+        in_specs=[HBM] * 6 + [ANY] + [HBM] * (3 + len(stages)),
         out_specs=[HBM, VMEM, VMEM] + [VMEM] * len(stages),
         out_shape=[
             in_hbm(*initial_displacement.shape),
@@ -857,16 +904,19 @@
         ],
         scratch_shapes=[
             *sweep_scratch,
+            scratch(*own_shape),
+            scratch(rows, count),
             scratch(2 * components, rows, count),
             scratch(rows, count),
             pltpu.VMEM(ocean_mask.shape, ocean_mask.dtype),
+            scratch(components, 2 * shells, count),
             sweep_sems,
             pltpu.SemaphoreType.DMA((8 + 2 * components + len(stages),)),
         ],
         compiler_params=params(28),
         cost_estimate=cost(50),
     )(
-        *(hbm(a) for a in (smoothed, tensors[1], eta, tensors[0], diagonal)),
+        *(hbm(a) for a in (early, late, tensors[1], eta, tensors[0], diagonal)),
         ring,
         *(hbm(a) for a in (beside, own, ocean_mask)),
         *stages,

time: 48.1 us -> 47.5 us (0.988)
  starting transfers between devices: 22.2 us -> 19.1 us
  waiting for transfers between devices: 1.06 us -> 2.34 us
  Pallas kernels: 23.7 us -> 24.9 us
    pallas_call x1, Pallas kernels: 2.9 us -> 5.15 us  [shards(): pl.pallas_call(viscosity_kernel, in_specs=[HBM] * 4 + [ANY], out_specs=[H...]
    all_to_all x1, starting transfers between devices: 10 us -> 8.31 us  [shards(): lax.all_to_all(orders, both, split_axis=0, concat_axis=0, tiled=True)]
    all_to_all x1, waiting for transfers between devices: 0.98 us -> 2.32 us  [shards(): lax.all_to_all(orders, both, split_axis=0, concat_axis=0, tiled=True)]
    all_to_all x1, starting transfers between devices: 5.26 us -> 3.92 us  [shards(): load = lax.all_to_all(load, both, split_axis=0, concat_axis=0, tiled=True)]
    pallas_call x2, Pallas kernels: 14.8 us -> 13.7 us  [the longest x1 8.09 us: shards(): pl.pallas_call(second_kernel, in_specs=[HBM] * 6 + [ANY] + [HBM] * (3 + l...]
  transfers between devices with their start and end apart: 7 -> 7, of which waited for: 2 -> 1; matrix products, arithmetic and copies ran while one was open for 0% -> 0% of each run, Pallas kernels for 42% -> 45%
where the time goes in v7:
time: 47.5 us; the launch traced here: 47.1 us
  Pallas kernels  24.9 us (52%)
  starting transfers between devices  19.1 us (40%)
  waiting for transfers between devices  2.34 us (5%)
  between operations  0.77 us (2%)
    all_to_all x1, starting transfers between devices, shards(): lax.all_to_all(orders, both, split_axis=0, concat_axis=0, tiled=True)  8.31 us
    pallas_call x1, Pallas kernels, shards(): pl.pallas_call(second_kernel, in_specs=[HBM] * 6 + [ANY] + [HBM] * (3 + l...  8.09 us
    pallas_call x1, Pallas kernels, shards(): pl.pallas_call(first_kernel, in_specs=[HBM] * 3 + [ANY] * 6 + [HBM] * len...  5.58 us
    pallas_call x1, Pallas kernels, shards(): pl.pallas_call(viscosity_kernel, in_specs=[HBM] * 4 + [ANY], out_specs=[H...  5.15 us
    ppermute x1, starting transfers between devices, shards(): lower_one = lax.ppermute(lower_one, both, lower_only(first))  4.88 us
    all_to_all x1, starting transfers between devices, shards(): load = lax.all_to_all(load, both, split_axis=0, concat_axis=0, tiled=True)  3.92 us
    pallas_call x1, Pallas kernels, shards(): pl.pallas_call(message_kernel, in_specs=[HBM] * 4, out_specs=[VMEM] * 2,...  2.44 us
    all_to_all x1, waiting for transfers between devices, shards(): lax.all_to_all(orders, both, split_axis=0, concat_axis=0, tiled=True)  2.32 us
  transfers between devices with their start and end apart: 7, of which 1 were waited for; matrix products, arithmetic and copies ran while one was open for 0% of the time, Pallas kernels for 45%

profile of v7, /device:TPU:0, one launch (start us, length us, event | category | flops | bytes accessed | tf_op | source)
XLA Modules:
  0.0 47.1 jit_solution(13474331114172129528)
XLA Ops:
  0.6 2.4 %shard_map.121 = (f32[32,2048]{1,0:T(8,128)S(1)}, f32[32,2048]{1,0:T(8,128)S(1)}) custom-call(f32[16]{0:T(128)} %viscosity_from.3, f32[3,4,32,2048]{3,2,1,0:T(8,128)} %start.1, f32[3,4,32,2048]{3,2,1,0:T(8,128)} %f.7, s32[4,32,2048]{2,1,0:T(8,128)} %index_from.1), custom_call_target="tpu_custom_call" | custom-call | bytes 60000000 | tf_op jit(solution)/shard_map/pallas_call | solution.py:775
  3.1 0.7 %collective-permute-start.1 = (f32[32,2048]{1,0:T(8,128)S(1)}, f32[32,2048]{1,0:T(8,128)S(1)}, u32[]{:S(2)}, u32[]{:S(2)}) collective-permute-start(f32[32,2048]{1,0:T(8,128)S(1)} %get-tuple-element.42.own_two.mine_two), channel_id=1, source_target_pairs={{3,5},{5,3},{7,9},{9,7},{11,13},{13,11},{19,21},{21,19},{23,25},{2... | collective-permute-start | bytes 786440 | tf_op jit(solution)/shard_map/ppermute | solution.py:791
  3.8 0.7 %collective-permute-start = (f32[32,2048]{1,0:T(8,128)S(1)}, f32[32,2048]{1,0:T(8,128)S(1)}, u32[]{:S(2)}, u32[]{:S(2)}) collective-permute-start(f32[32,2048]{1,0:T(8,128)S(1)} %get-tuple-element.41.token.own_one.mine_one), channel_id=1, source_target_pairs={{1,3},{3,1},{5,7},{7,5},{9,11},{11,9},{13,15},{15,13},{17,19},{19,... | collective-permute-start | bytes 786440 | tf_op jit(solution)/shard_map/ppermute | solution.py:792
  4.4 5.2 %shard_map.122 = (f32[4,32,2048]{2,1,0:T(8,128)}, f32[3,2,32,2048]{3,2,1,0:T(8,128)}, f32[2,32,2048]{2,1,0:T(8,128)S(1)}, f32[2,32,2048]{2,1,0:T(8,128)S(1)}, f32[32,2048]{1,0:T(8,128)S(1)}) custom-call(f32[16]{0:T(128)} %viscosity_from.3, f32[3,4,32,2048]{3,2,1,0:T(8,128)} %start.1, f32[3,4,32,2048]{3,2,1,0:T(8,128)} %f.7, s32[4,32,2048]{2,1,0:T(8,128)} %index_from.1, ...), custom_call_target="tpu_custom_call" | custom-call | bytes 60000000 | tf_op jit(solution)/shard_map/pallas_call | solution.py:793
  9.6 4.9 %collective-permute-start.2 = (f32[32,2048]{1,0:T(8,128)S(1)}, f32[32,2048]{1,0:T(8,128)S(1)}, u32[]{:S(2)}, u32[]{:S(2)}) collective-permute-start(f32[32,2048]{1,0:T(8,128)S(1)} %get-tuple-element.41.token.own_one.mine_one), channel_id=1, source_target_pairs={{0,2},{2,0},{4,6},{6,4},{8,10},{10,8},{12,14},{14,12},{16,18},{18,... | collective-permute-start | bytes 786440 | tf_op jit(solution)/shard_map/ppermute | solution.py:818
  14.5 0.7 %collective-permute-start.3 = (f32[32,2048]{1,0:T(8,128)S(1)}, f32[32,2048]{1,0:T(8,128)S(1)}, u32[]{:S(2)}, u32[]{:S(2)}) collective-permute-start(f32[32,2048]{1,0:T(8,128)S(1)} %get-tuple-element.42.own_two.mine_two), channel_id=1, source_target_pairs={{2,4},{4,2},{6,8},{8,6},{10,12},{12,10},{18,20},{20,18},{22,24},{2... | collective-permute-start | bytes 786440 | tf_op jit(solution)/shard_map/ppermute | solution.py:819
  15.2 0.0 collective-permute-done.1.two
  15.2 0.0 collective-permute-done.one
  15.2 0.7 %shard_map.123 = f32[16,16,128]{2,1,0:T(8,128)} custom-call(f32[2,32,2048]{2,1,0:T(8,128)S(1)} %get-tuple-element.37.surface_swept, f32[2,32,2048]{2,1,0:T(8,128)S(1)} %get-tuple-element.38.surface_eta, f32[32,2048]{1,0:T(8,128)S(1)} %get-tuple-element.39.force, f32[32,2048]{1,0:T(8,128)S(1)} %get-tuple-element.41.token.own_one.mine_one, ...), custom_call_target="tpu_custom_call" | custom-call | bytes 600000000 | tf_op jit(solution)/shard_map/pallas_call | solution.py:825
  15.9 8.3 %all-to-all-start = ((f32[16,16,128]{2,1,0:T(8,128)}), f32[16,16,128]{2,1,0:T(8,128)S(1)}, u32[]{:S(2)}, u32[]{:S(2)}) async-start(f32[16,16,128]{2,1,0:T(8,128)} %shard_map.123), calls=%async_computation | async-start | bytes 262144 | tf_op jit(solution)/shard_map/all_to_all | solution.py:842
  24.2 0.0 collective-permute-done.2.lower_one
  24.2 0.0 collective-permute-done.3.lower_two
  24.2 5.6 %shard_map.124 = (f32[3,2,32,2048]{3,2,1,0:T(8,128)}, f32[32,2048]{1,0:T(8,128)}, f32[264,2048]{1,0:T(8,128)}, f32[2,32,2048]{2,1,0:T(8,128)}, f32[2,32,2048]{2,...) custom-call(f32[3,4,32,2048]{3,2,1,0:T(8,128)} %start.1, ...), custom_call_target="tpu_custom_call" | custom-call | bytes 150000000 | tf_op jit(solution)/shard_map/pallas_call | solution.py:860
  29.8 2.3 %all-to-all-done.orders = f32[16,16,128]{2,1,0:T(8,128)S(1)} async-done(((f32[16,16,128]{2,1,0:T(8,128)}), f32[16,16,128]{2,1,0:T(8,128)S(1)}, u32[]{:S(2)}, u32[]{:S(2)}) %all-to-all-start) | async-done | bytes 131104 | tf_op jit(solution)/shard_map/all_to_all | solution.py:842
  32.1 0.0 collective-permute-start.4
  32.1 1.5 %shard_map.125 = (f32[64,512]{1,0:T(8,128)}, f32[16,16,128]{2,1,0:T(8,128)}) custom-call(f32[16,16,128]{2,1,0:T(8,128)S(1)} %all-to-all-done.orders, bf16[256,512]{1,0:T(8,128)(2,1)S(1)} %get-tuple-element.46.high, bf16[256,512]{1,0:T(8,128)(2,1)S(1)} %get-tuple-element.47.low, f32[512,128]{1,0:T(8,128)S(1)} %get-tuple-element.48.response), custom_call_target="tpu_custom_call" | custom-call | bytes 600000000 | tf_op jit(solution)/shard_map/pallas_call | solution.py:883
  33.6 3.9 %all-to-all-start.1 = ((f32[16,16,128]{2,1,0:T(8,128)}), f32[16,16,128]{2,1,0:T(8,128)S(1)}, u32[]{:S(2)}, u32[]{:S(2)}) async-start(f32[16,16,128]{2,1,0:T(8,128)} %get-tuple-element.57), calls=%async_computation.1 | async-start | bytes 262144 | tf_op jit(solution)/shard_map/all_to_all | solution.py:892
  37.6 0.0 collective-permute-done.4.ring
  37.6 8.1 %shard_map.126 = (f32[3,4,32,2048]{3,2,1,0:T(8,128)}, f32[8,128]{1,0:T(8,128)}, bf16[32,2048]{1,0:T(8,128)(2,1)S(1)}, bf16[256,1024]{1,0:T(8,128)(2,1)S(1)}, bf16[256,1024]{1,0:T(8,128)(2,1)S(1)}) custom-call(f32[3,2,32,2048]{3,2,1,0:T(8,128)} %get-tuple-element.33.early, f32[3,2,32,2048]{3,2,1,0:T(8,128)} %get-tuple-element.43.late, f32[3,4,32,2048]{3,2,1,0:T(8,128)} %f.7, ...), custom_call_target="tpu_custom_call" | custom-call | bytes 150000000 | tf_op jit(solution)/shard_map/pallas_call | solution.py:895
  45.7 0.0 all-to-all-done.1.load
  45.7 1.4 %shard_map.127 = f32[32,2048]{1,0:T(8,128)} custom-call(f32[16,16,128]{2,1,0:T(8,128)S(1)} %all-to-all-done.1.load, bf16[256,1024]{1,0:T(8,128)(2,1)S(1)} %get-tuple-element.58.high, bf16[256,1024]{1,0:T(8,128)(2,1)S(1)} %get-tuple-element.59.low, bf16[32,2048]{1,0:T(8,128)(2,1)S(1)} %get-tuple-element.60.mask), custom_call_target="tpu_custom_call" | custom-call | bytes 9000000 | tf_op jit(solution)/shard_map/pallas_call | solution.py:925
Async XLA Ops:
  3.1 12.1 %collective-permute-start.1 = (f32[32,2048]{1,0:T(8,128)S(1)}, f32[32,2048]{1,0:T(8,128)S(1)}, u32[]{:S(2)}, u32[]{:S(2)}) collective-permute-start(f32[32,2048]{1,0:T(8,128)S(1)} %get-tuple-element.42.own_two.mine_two), channel_id=1, source_target_pairs={{3,5},{5,3},{7,9},{9,7},{11,13},{13,11},{19,21},{21,19},{23,25},{2... | collective-permute-start | bytes 786440 | tf_op jit(solution)/shard_map/ppermute | solution.py:791
  3.8 11.4 %collective-permute-start = (f32[32,2048]{1,0:T(8,128)S(1)}, f32[32,2048]{1,0:T(8,128)S(1)}, u32[]{:S(2)}, u32[]{:S(2)}) collective-permute-start(f32[32,2048]{1,0:T(8,128)S(1)} %get-tuple-element.41.token.own_one.mine_one), channel_id=1, source_target_pairs={{1,3},{3,1},{5,7},{7,5},{9,11},{11,9},{13,15},{15,13},{17,19},{19,... | collective-permute-start | bytes 786440 | tf_op jit(solution)/shard_map/ppermute | solution.py:792
  9.6 14.6 %collective-permute-start.2 = (f32[32,2048]{1,0:T(8,128)S(1)}, f32[32,2048]{1,0:T(8,128)S(1)}, u32[]{:S(2)}, u32[]{:S(2)}) collective-permute-start(f32[32,2048]{1,0:T(8,128)S(1)} %get-tuple-element.41.token.own_one.mine_one), channel_id=1, source_target_pairs={{0,2},{2,0},{4,6},{6,4},{8,10},{10,8},{12,14},{14,12},{16,18},{18,... | collective-permute-start | bytes 786440 | tf_op jit(solution)/shard_map/ppermute | solution.py:818
  14.5 9.7 %collective-permute-start.3 = (f32[32,2048]{1,0:T(8,128)S(1)}, f32[32,2048]{1,0:T(8,128)S(1)}, u32[]{:S(2)}, u32[]{:S(2)}) collective-permute-start(f32[32,2048]{1,0:T(8,128)S(1)} %get-tuple-element.42.own_two.mine_two), channel_id=1, source_target_pairs={{2,4},{4,2},{6,8},{8,6},{10,12},{12,10},{18,20},{20,18},{22,24},{2... | collective-permute-start | bytes 786440 | tf_op jit(solution)/shard_map/ppermute | solution.py:819
  15.9 16.2 %all-to-all-start = ((f32[16,16,128]{2,1,0:T(8,128)}), f32[16,16,128]{2,1,0:T(8,128)S(1)}, u32[]{:S(2)}, u32[]{:S(2)}) async-start(f32[16,16,128]{2,1,0:T(8,128)} %shard_map.123), calls=%async_computation | async-start | bytes 262144 | tf_op jit(solution)/shard_map/all_to_all | solution.py:842
  32.1 5.4 %collective-permute-start.4 = (f32[264,2048]{1,0:T(8,128)}, f32[264,2048]{1,0:T(8,128)S(1)}, u32[]{:S(2)}, u32[]{:S(2)}) collective-permute-start(f32[264,2048]{1,0:T(8,128)} %get-tuple-element.52), channel_id=1, source_target_pairs={{0,1},{1,0},{2,3},{3,2},{4,5},{5,4},{6,7},{7,6},{8,9},{9,8},{10,11... | collective-permute-start | bytes 6488072 | tf_op jit(solution)/shard_map/ppermute | solution.py:882
  33.6 12.0 %all-to-all-start.1 = ((f32[16,16,128]{2,1,0:T(8,128)}), f32[16,16,128]{2,1,0:T(8,128)S(1)}, u32[]{:S(2)}, u32[]{:S(2)}) async-start(f32[16,16,128]{2,1,0:T(8,128)} %get-tuple-element.57), calls=%async_computation.1 | async-start | bytes 262144 | tf_op jit(solution)/shard_map/all_to_all | solution.py:892

commit v8 on v7

--- a/solution.py
+++ b/solution.py
@@ -174,15 +174,6 @@
         west_of(middle),
         east_of(middle),
     ]
-
-
-def odd_band():
-    return lax.axis_index("lateral") % 2 == 1
-
-
-def by_parity(one, two):
-    one, two = one[...], two[...]
-    return jnp.where(odd_band(), one, two), jnp.where(odd_band(), two, one)
 
 
 def message_kernel(viscosity_from, d, f, index, one, two, fields, forces, layers, rows_of, viscosity, sems):
@@ -243,7 +234,7 @@
         values.append(middle)
         sums.append(total)
     for place, field in enumerate(values + [eta] + sums + [diagonal]):
-        both = jnp.where(odd_band(), field, pltpu.roll(field, shells, 0))
+        both = pltpu.roll(field, shells, 0)
         one[pl.ds(place * shells, shells)] = both[:shells]
         two[pl.ds(place * shells, shells)] = both[shells:]
 
@@ -304,12 +295,12 @@
             surface_eta[1 - k, part] = eta[k + 1, pl.ds(start + TILE, TILE)]
             if k == 0:
                 surface_force[part] = force[0, 0, part]
+            sem = more_sems.at[2 * EARLY + 1 + shells + k]
+            pltpu.make_async_copy(result.at[:, k, part], out.at[:, k, part], sem).start()
             return 0
 
         lax.fori_loop(0, rows // TILE, sweep, 0, unroll=2)
-        stores += start_all(
-            [pltpu.make_async_copy(result.at[:, k], out.at[:, k], more_sems.at[2 * EARLY + 1 + shells + k])]
-        )
+        stores.append(pltpu.make_async_copy(result.at[:, k], out.at[:, k], more_sems.at[2 * EARLY + 1 + shells + k]))
     for copy in stores:
         copy.wait()
 
@@ -339,7 +330,7 @@
         lateral = lax.axis_index("lateral")
         inside = (lateral > 0, lateral < lax.axis_size("lateral") - 1)
         for beside, own, place, own_place, there in zip(
-            by_parity(one, two), by_parity(own_one, own_two), (TILE - 1, rows + TILE), (TILE, rows + TILE - 1), inside
+            (one[...], two[...]), (own_two[...], own_one[...]), (TILE - 1, rows + TILE), (TILE, rows + TILE - 1), inside
         ):
             for k in range(2):
                 row = lambda message, kind: message[kind * shells + shells - 2 + k : kind * shells + shells - 1 + k]
@@ -363,7 +354,7 @@
             surface[pl.ds(start, TILE)] = relax(weights, factor, middle, others, force[pl.ds(start, TILE)])
             return 0
 
-        lax.fori_loop(0, rows // TILE, second, 0)
+        lax.fori_loop(0, rows // TILE, second, 0, unroll=2)
         near, far = split(jnp.concatenate(fold(surface[...]), axis=0))
         for copy in tables:
             copy.wait()
@@ -500,7 +491,7 @@
         eta[beyond, block] = zeros
         for copy in arrivals:
             copy.wait()
-        before, after = by_parity(messages.at[0], messages.at[1])
+        before, after = messages[0], messages[1]
         row = lambda message, kind: lambda s: message[kind * shells + s]
         for c in range(components):
             set_edge(field, (c,), shells, rows, row(before, c), row(after, c))
@@ -625,7 +616,7 @@
     def before_first():
         for copy in arrivals:
             copy.wait()
-        before, after = by_parity(messages.at[0], messages.at[1])
+        before, after = messages[0], messages[1]
         pair = lambda k: jnp.concatenate(
             [before[k * shells : (k + 1) * shells], after[k * shells : (k + 1) * shells]], axis=0
         )
@@ -636,7 +627,7 @@
             place < shells, edges[pl.ds(k, 1)], edges[pl.ds(components + 1 + k, 1)]
         )
         inside = jnp.where(place < shells, lateral, lax.axis_size("lateral") - 1 - lateral) > 0
-        mine = by_parity(own.at[0], own.at[1])
+        mine = (own[1], own[0])
         own_row = lambda k: jnp.concatenate([part[k * shells : (k + 1) * shells] for part in mine], axis=0)
         middle = pair(components)
         weight = middle + own_row(components)
@@ -761,8 +752,8 @@
     scratch = lambda *shape: pltpu.VMEM(shape, jnp.float32)
     in_hbm = lambda *shape: pltpu.HBM(shape, jnp.float32)
     width = 2 * MODES // (lateral * radial)
-    first = [p for i in range(0, lateral - 1, 2) for p in ((i, i + 1), (i + 1, i))]
-    second = [p for i in range(1, lateral - 1, 2) for p in ((i, i + 1), (i + 1, i))]
+    first = [(i, i + 1) for i in range(lateral - 1)]
+    second = [(i + 1, i) for i in range(lateral - 1)]
     both = ("lateral", "radial")
     top_only = lambda pairs: [(i * radial + radial - 1, j * radial + radial - 1) for i, j in pairs]
 

time: 47.5 us -> 47.3 us (level)
    all_to_all x1, starting transfers between devices: 8.31 us -> 7.68 us  [shards(): lax.all_to_all(orders, both, split_axis=0, concat_axis=0, tiled=True)]
    ppermute x1, starting transfers between devices: 0.68 us -> 1.29 us  [shards(): lower_two = lax.ppermute(lower_two, both, lower_only(second))]
  transfers between devices with their start and end apart: 7 -> 7, of which waited for: 1 -> 1; matrix products, arithmetic and copies ran while one was open for 0% -> 0% of each run, Pallas kernels for 45% -> 44%
where the time goes in v8:
time: 47.3 us; the launch traced here: 46.9 us
  Pallas kernels  24.7 us (52%)
  starting transfers between devices  19.1 us (40%)
  waiting for transfers between devices  2.35 us (5%)
  between operations  0.77 us (2%)
    pallas_call x1, Pallas kernels, shards(): pl.pallas_call(second_kernel, in_specs=[HBM] * 6 + [ANY] + [HBM] * (3 + l...  8.1 us
    all_to_all x1, starting transfers between devices, shards(): lax.all_to_all(orders, both, split_axis=0, concat_axis=0, tiled=True)  7.68 us
    pallas_call x1, Pallas kernels, shards(): pl.pallas_call(first_kernel, in_specs=[HBM] * 3 + [ANY] * 6 + [HBM] * len...  5.58 us
    pallas_call x1, Pallas kernels, shards(): pl.pallas_call(viscosity_kernel, in_specs=[HBM] * 4 + [ANY], out_specs=[H...  4.95 us
    ppermute x1, starting transfers between devices, shards(): lower_one = lax.ppermute(lower_one, both, lower_only(first))  4.89 us
    all_to_all x1, starting transfers between devices, shards(): load = lax.all_to_all(load, both, split_axis=0, concat_axis=0, tiled=True)  3.91 us
    pallas_call x1, Pallas kernels, shards(): pl.pallas_call(message_kernel, in_specs=[HBM] * 4, out_specs=[VMEM] * 2,...  2.43 us
    all_to_all x1, waiting for transfers between devices, shards(): lax.all_to_all(orders, both, split_axis=0, concat_axis=0, tiled=True)  2.33 us
  transfers between devices with their start and end apart: 7, of which 1 were waited for; matrix products, arithmetic and copies ran while one was open for 0% of the time, Pallas kernels for 44%

profile of v8, /device:TPU:0, one launch (start us, length us, event | category | flops | bytes accessed | tf_op | source)
XLA Modules:
  0.0 46.9 jit_solution(7794846235790483357)
XLA Ops:
  0.6 2.4 %shard_map.121 = (f32[32,2048]{1,0:T(8,128)S(1)}, f32[32,2048]{1,0:T(8,128)S(1)}) custom-call(f32[16]{0:T(128)} %viscosity_from.3, f32[3,4,32,2048]{3,2,1,0:T(8,128)} %start.1, f32[3,4,32,2048]{3,2,1,0:T(8,128)} %f.7, s32[4,32,2048]{2,1,0:T(8,128)} %index_from.1), custom_call_target="tpu_custom_call" | custom-call | bytes 60000000 | tf_op jit(solution)/shard_map/pallas_call | solution.py:766
  3.1 0.7 %collective-permute-start.1 = (f32[32,2048]{1,0:T(8,128)S(1)}, f32[32,2048]{1,0:T(8,128)S(1)}, u32[]{:S(2)}, u32[]{:S(2)}) collective-permute-start(f32[32,2048]{1,0:T(8,128)S(1)} %get-tuple-element.42.own_two.mine_two), channel_id=1, source_target_pairs={{3,1},{5,3},{7,5},{9,7},{11,9},{13,11},{15,13},{19,17},{21,19},{23... | collective-permute-start | bytes 786440 | tf_op jit(solution)/shard_map/ppermute | solution.py:782
  3.8 0.7 %collective-permute-start = (f32[32,2048]{1,0:T(8,128)S(1)}, f32[32,2048]{1,0:T(8,128)S(1)}, u32[]{:S(2)}, u32[]{:S(2)}) collective-permute-start(f32[32,2048]{1,0:T(8,128)S(1)} %get-tuple-element.41.token.own_one.mine_one), channel_id=1, source_target_pairs={{1,3},{3,5},{5,7},{7,9},{9,11},{11,13},{13,15},{17,19},{19,21},{21... | collective-permute-start | bytes 786440 | tf_op jit(solution)/shard_map/ppermute | solution.py:783
  4.4 4.9 %shard_map.122 = (f32[4,32,2048]{2,1,0:T(8,128)}, f32[3,2,32,2048]{3,2,1,0:T(8,128)}, f32[2,32,2048]{2,1,0:T(8,128)S(1)}, f32[2,32,2048]{2,1,0:T(8,128)S(1)}, f32[32,2048]{1,0:T(8,128)S(1)}) custom-call(f32[16]{0:T(128)} %viscosity_from.3, f32[3,4,32,2048]{3,2,1,0:T(8,128)} %start.1, f32[3,4,32,2048]{3,2,1,0:T(8,128)} %f.7, s32[4,32,2048]{2,1,0:T(8,128)} %index_from.1, ...), custom_call_target="tpu_custom_call" | custom-call | bytes 60000000 | tf_op jit(solution)/shard_map/pallas_call | solution.py:784
  9.4 4.9 %collective-permute-start.2 = (f32[32,2048]{1,0:T(8,128)S(1)}, f32[32,2048]{1,0:T(8,128)S(1)}, u32[]{:S(2)}, u32[]{:S(2)}) collective-permute-start(f32[32,2048]{1,0:T(8,128)S(1)} %get-tuple-element.41.token.own_one.mine_one), channel_id=1, source_target_pairs={{0,2},{2,4},{4,6},{6,8},{8,10},{10,12},{12,14},{16,18},{18,20},{20... | collective-permute-start | bytes 786440 | tf_op jit(solution)/shard_map/ppermute | solution.py:809
  14.3 1.3 %collective-permute-start.3 = (f32[32,2048]{1,0:T(8,128)S(1)}, f32[32,2048]{1,0:T(8,128)S(1)}, u32[]{:S(2)}, u32[]{:S(2)}) collective-permute-start(f32[32,2048]{1,0:T(8,128)S(1)} %get-tuple-element.42.own_two.mine_two), channel_id=1, source_target_pairs={{2,0},{4,2},{6,4},{8,6},{10,8},{12,10},{14,12},{18,16},{20,18},{22... | collective-permute-start | bytes 786440 | tf_op jit(solution)/shard_map/ppermute | solution.py:810
  15.6 0.0 collective-permute-done.1.two
  15.6 0.0 collective-permute-done.one
  15.6 0.7 %shard_map.123 = f32[16,16,128]{2,1,0:T(8,128)} custom-call(f32[2,32,2048]{2,1,0:T(8,128)S(1)} %get-tuple-element.37.surface_swept, f32[2,32,2048]{2,1,0:T(8,128)S(1)} %get-tuple-element.38.surface_eta, f32[32,2048]{1,0:T(8,128)S(1)} %get-tuple-element.39.force, f32[32,2048]{1,0:T(8,128)S(1)} %get-tuple-element.41.token.own_one.mine_one, ...), custom_call_target="tpu_custom_call" | custom-call | bytes 600000000 | tf_op jit(solution)/shard_map/pallas_call | solution.py:816
  16.3 7.7 %all-to-all-start = ((f32[16,16,128]{2,1,0:T(8,128)}), f32[16,16,128]{2,1,0:T(8,128)S(1)}, u32[]{:S(2)}, u32[]{:S(2)}) async-start(f32[16,16,128]{2,1,0:T(8,128)} %shard_map.123), calls=%async_computation | async-start | bytes 262144 | tf_op jit(solution)/shard_map/all_to_all | solution.py:833
  24.0 0.0 collective-permute-done.2.lower_one
  24.0 0.0 collective-permute-done.3.lower_two
  24.0 5.6 %shard_map.124 = (f32[3,2,32,2048]{3,2,1,0:T(8,128)}, f32[32,2048]{1,0:T(8,128)}, f32[264,2048]{1,0:T(8,128)}, f32[2,32,2048]{2,1,0:T(8,128)}, f32[2,32,2048]{2,...) custom-call(f32[3,4,32,2048]{3,2,1,0:T(8,128)} %start.1, ...), custom_call_target="tpu_custom_call" | custom-call | bytes 150000000 | tf_op jit(solution)/shard_map/pallas_call | solution.py:851
  29.6 2.3 %all-to-all-done.orders = f32[16,16,128]{2,1,0:T(8,128)S(1)} async-done(((f32[16,16,128]{2,1,0:T(8,128)}), f32[16,16,128]{2,1,0:T(8,128)S(1)}, u32[]{:S(2)}, u32[]{:S(2)}) %all-to-all-start) | async-done | bytes 131104 | tf_op jit(solution)/shard_map/all_to_all | solution.py:833
  31.9 0.0 collective-permute-start.4
  31.9 1.5 %shard_map.125 = (f32[64,512]{1,0:T(8,128)}, f32[16,16,128]{2,1,0:T(8,128)}) custom-call(f32[16,16,128]{2,1,0:T(8,128)S(1)} %all-to-all-done.orders, bf16[256,512]{1,0:T(8,128)(2,1)S(1)} %get-tuple-element.46.high, bf16[256,512]{1,0:T(8,128)(2,1)S(1)} %get-tuple-element.47.low, f32[512,128]{1,0:T(8,128)S(1)} %get-tuple-element.48.response), custom_call_target="tpu_custom_call" | custom-call | bytes 600000000 | tf_op jit(solution)/shard_map/pallas_call | solution.py:874
  33.4 3.9 %all-to-all-start.1 = ((f32[16,16,128]{2,1,0:T(8,128)}), f32[16,16,128]{2,1,0:T(8,128)S(1)}, u32[]{:S(2)}, u32[]{:S(2)}) async-start(f32[16,16,128]{2,1,0:T(8,128)} %get-tuple-element.57), calls=%async_computation.1 | async-start | bytes 262144 | tf_op jit(solution)/shard_map/all_to_all | solution.py:883
  37.4 0.0 collective-permute-done.4.ring
  37.4 8.1 %shard_map.126 = (f32[3,4,32,2048]{3,2,1,0:T(8,128)}, f32[8,128]{1,0:T(8,128)}, bf16[32,2048]{1,0:T(8,128)(2,1)S(1)}, bf16[256,1024]{1,0:T(8,128)(2,1)S(1)}, bf16[256,1024]{1,0:T(8,128)(2,1)S(1)}) custom-call(f32[3,2,32,2048]{3,2,1,0:T(8,128)} %get-tuple-element.33.early, f32[3,2,32,2048]{3,2,1,0:T(8,128)} %get-tuple-element.43.late, f32[3,4,32,2048]{3,2,1,0:T(8,128)} %f.7, ...), custom_call_target="tpu_custom_call" | custom-call | bytes 150000000 | tf_op jit(solution)/shard_map/pallas_call | solution.py:886
  45.5 0.0 all-to-all-done.1.load
  45.5 1.4 %shard_map.127 = f32[32,2048]{1,0:T(8,128)} custom-call(f32[16,16,128]{2,1,0:T(8,128)S(1)} %all-to-all-done.1.load, bf16[256,1024]{1,0:T(8,128)(2,1)S(1)} %get-tuple-element.58.high, bf16[256,1024]{1,0:T(8,128)(2,1)S(1)} %get-tuple-element.59.low, bf16[32,2048]{1,0:T(8,128)(2,1)S(1)} %get-tuple-element.60.mask), custom_call_target="tpu_custom_call" | custom-call | bytes 9000000 | tf_op jit(solution)/shard_map/pallas_call | solution.py:916
Async XLA Ops:
  3.1 12.5 %collective-permute-start.1 = (f32[32,2048]{1,0:T(8,128)S(1)}, f32[32,2048]{1,0:T(8,128)S(1)}, u32[]{:S(2)}, u32[]{:S(2)}) collective-permute-start(f32[32,2048]{1,0:T(8,128)S(1)} %get-tuple-element.42.own_two.mine_two), channel_id=1, source_target_pairs={{3,1},{5,3},{7,5},{9,7},{11,9},{13,11},{15,13},{19,17},{21,19},{23... | collective-permute-start | bytes 786440 | tf_op jit(solution)/shard_map/ppermute | solution.py:782
  3.8 11.8 %collective-permute-start = (f32[32,2048]{1,0:T(8,128)S(1)}, f32[32,2048]{1,0:T(8,128)S(1)}, u32[]{:S(2)}, u32[]{:S(2)}) collective-permute-start(f32[32,2048]{1,0:T(8,128)S(1)} %get-tuple-element.41.token.own_one.mine_one), channel_id=1, source_target_pairs={{1,3},{3,5},{5,7},{7,9},{9,11},{11,13},{13,15},{17,19},{19,21},{21... | collective-permute-start | bytes 786440 | tf_op jit(solution)/shard_map/ppermute | solution.py:783
  9.4 14.6 %collective-permute-start.2 = (f32[32,2048]{1,0:T(8,128)S(1)}, f32[32,2048]{1,0:T(8,128)S(1)}, u32[]{:S(2)}, u32[]{:S(2)}) collective-permute-start(f32[32,2048]{1,0:T(8,128)S(1)} %get-tuple-element.41.token.own_one.mine_one), channel_id=1, source_target_pairs={{0,2},{2,4},{4,6},{6,8},{8,10},{10,12},{12,14},{16,18},{18,20},{20... | collective-permute-start | bytes 786440 | tf_op jit(solution)/shard_map/ppermute | solution.py:809
  14.3 9.7 %collective-permute-start.3 = (f32[32,2048]{1,0:T(8,128)S(1)}, f32[32,2048]{1,0:T(8,128)S(1)}, u32[]{:S(2)}, u32[]{:S(2)}) collective-permute-start(f32[32,2048]{1,0:T(8,128)S(1)} %get-tuple-element.42.own_two.mine_two), channel_id=1, source_target_pairs={{2,0},{4,2},{6,4},{8,6},{10,8},{12,10},{14,12},{18,16},{20,18},{22... | collective-permute-start | bytes 786440 | tf_op jit(solution)/shard_map/ppermute | solution.py:810
  16.3 15.6 %all-to-all-start = ((f32[16,16,128]{2,1,0:T(8,128)}), f32[16,16,128]{2,1,0:T(8,128)S(1)}, u32[]{:S(2)}, u32[]{:S(2)}) async-start(f32[16,16,128]{2,1,0:T(8,128)} %shard_map.123), calls=%async_computation | async-start | bytes 262144 | tf_op jit(solution)/shard_map/all_to_all | solution.py:833
  31.9 5.4 %collective-permute-start.4 = (f32[264,2048]{1,0:T(8,128)}, f32[264,2048]{1,0:T(8,128)S(1)}, u32[]{:S(2)}, u32[]{:S(2)}) collective-permute-start(f32[264,2048]{1,0:T(8,128)} %get-tuple-element.52), channel_id=1, source_target_pairs={{0,1},{1,0},{2,3},{3,2},{4,5},{5,4},{6,7},{7,6},{8,9},{9,8},{10,11... | collective-permute-start | bytes 6488072 | tf_op jit(solution)/shard_map/ppermute | solution.py:873
  33.4 12.0 %all-to-all-start.1 = ((f32[16,16,128]{2,1,0:T(8,128)}), f32[16,16,128]{2,1,0:T(8,128)S(1)}, u32[]{:S(2)}, u32[]{:S(2)}) async-start(f32[16,16,128]{2,1,0:T(8,128)} %get-tuple-element.57), calls=%async_computation.1 | async-start | bytes 262144 | tf_op jit(solution)/shard_map/all_to_all | solution.py:883

commit v9 on v8

--- a/solution.py
+++ b/solution.py
@@ -245,7 +245,7 @@
 
 
 def viscosity_kernel(
-    viscosity_from, d, f, index_from, token, eta_out, out, surface_swept, surface_eta, surface_force,
+    viscosity_from, d, f, index_from, token, table_from, eta_out, out, surface_swept, surface_eta, surface_force, table,
     index, eta, field, force, result, viscosity, sems, more_sems,
 ):
     del token
@@ -261,13 +261,14 @@
     forces = [
         pltpu.make_async_copy(f.at[:, shell(k)], force.at[:, k], more_sems.at[EARLY + 1 + k]) for k in range(EARLY)
     ]
+    table_copy = pltpu.make_async_copy(table_from, table, sems.at[shells + 1])
     start_all([value_copy, *layers, *fields, *forces])
     zeros = jnp.zeros((rows, count), jnp.float32)
     for c in range(components):
         field[c, 0, block] = zeros
     eta[0, block] = zeros
     value_copy.wait()
-    stores = []
+    stores = start_all([table_copy])
     for k in range(shells):
         layers[k].wait()
 
@@ -306,19 +307,15 @@
 
 
 def surface_kernel(
-    surface_swept, surface_eta, force, own_one, own_two, one, two, high_from, low_from, out,
-    swept, eta, surface, high, low, sems, components,
+    surface_swept, surface_eta, force, own_one, own_two, one, two, high, low_from, out,
+    swept, eta, surface, low, sem, components,
 ):
     rows, count = force.shape
 
     @pl.when(lax.axis_index("radial") == lax.axis_size("radial") - 1)
     def _():
-        tables = start_all(
-            [
-                pltpu.make_async_copy(high_from, high, sems.at[0]),
-                pltpu.make_async_copy(low_from, low, sems.at[1]),
-            ]
-        )
+        low_copy = pltpu.make_async_copy(low_from, low, sem)
+        low_copy.start()
         block = pl.ds(TILE, rows)
         for k in range(2):
             swept[k, block] = surface_swept[k]
@@ -356,9 +353,9 @@
 
         lax.fori_loop(0, rows // TILE, second, 0, unroll=2)
         near, far = split(jnp.concatenate(fold(surface[...]), axis=0))
-        for copy in tables:
-            copy.wait()
-        total = dot(near, high[...]) + dot(far, high[...]) + dot(near, low[...])
+        total = dot(near, high[...]) + dot(far, high[...])
+        low_copy.wait()
+        total = total + dot(near, low[...])
         blocks = [total[k * rows : (k + 1) * rows] for k in range(RADIX)]
         kind, mirrored = order_class((1, total.shape[1]))
         cosine, sine = blocks[0], jnp.zeros_like(blocks[0])
@@ -781,16 +778,19 @@
     )(viscosity, *tensors)
     two = lax.ppermute(mine[1], both, top_only(second))
     one = lax.ppermute(mine[0], both, top_only(first))
-    eta, early, *surface = pl.pallas_call(
+    high, low = longitude_tables(count, MODES)
+    high, low = hbm(jnp.asarray(high)), hbm(jnp.asarray(low))
+    eta, early, *surface, table = pl.pallas_call(
         viscosity_kernel,
-        in_specs=[HBM] * 4 + [ANY],
-        out_specs=[HBM, HBM, VMEM, VMEM, VMEM],
+        in_specs=[HBM] * 4 + [ANY, HBM],
+        out_specs=[HBM, HBM, VMEM, VMEM, VMEM, VMEM],
         out_shape=[
             in_hbm(shells, rows, count),
             in_hbm(components, EARLY, rows, count),
             f32((2, rows, count)),
             f32((2, rows, count)),
             f32((rows, count)),
+            jax.ShapeDtypeStruct(high.shape, high.dtype),
         ],
         scratch_shapes=[
             pltpu.VMEM(layer_index.shape, jnp.int32),
@@ -799,36 +799,32 @@
             scratch(components, EARLY, rows, count),
             scratch(components, EARLY, rows, count),
             pltpu.SMEM(viscosity.shape, jnp.float32),
-            pltpu.SemaphoreType.DMA((1 + shells,)),
+            pltpu.SemaphoreType.DMA((2 + shells,)),
             pltpu.SemaphoreType.DMA((3 * EARLY + 1 + shells,)),
         ],
         compiler_params=params(24),
         cost_estimate=cost(20),
-    )(viscosity, *tensors, mine[0])
+    )(viscosity, *tensors, mine[0], high)
     lower_one, lower_two, eta = lax.optimization_barrier((*mine, eta))
     lower_one = lax.ppermute(lower_one, both, lower_only(first))
     lower_two = lax.ppermute(lower_two, both, lower_only(second))
 
-    high, low = longitude_tables(count, MODES)
-    high, low = hbm(jnp.asarray(high)), hbm(jnp.asarray(low))
-    table = pltpu.VMEM(high.shape, jnp.bfloat16)
     packed = (lateral * radial, rows * width // max(128, width), max(128, width))
     orders = pl.pallas_call(
         functools.partial(surface_kernel, components=components),
-        in_specs=[VMEM] * 7 + [HBM, HBM],
+        in_specs=[VMEM] * 8 + [HBM],
         out_specs=VMEM,
         out_shape=f32(packed),
         scratch_shapes=[
             scratch(3, rows + 2 * TILE, count),
             scratch(3, rows + 2 * TILE, count),
             scratch(rows, count),
-            table,
-            table,
-            pltpu.SemaphoreType.DMA((2,)),
+            pltpu.VMEM(low.shape, low.dtype),
+            pltpu.SemaphoreType.DMA,
         ],
         compiler_params=params(16),
         cost_estimate=cost(200),
-    )(*surface, *mine, one, two, high, low)
+    )(*surface, *mine, one, two, table, low)
     eta, _ = lax.optimization_barrier((eta, orders))
     orders = lax.all_to_all(orders, both, split_axis=0, concat_axis=0, tiled=True)
     eta = hbm(eta)

time: 47.3 us -> 46.9 us (level)
  transfers between devices with their start and end apart: 7 -> 7, of which waited for: 1 -> 1; matrix products, arithmetic and copies ran while one was open for 0% -> 0% of each run, Pallas kernels for 44% -> 45%
where the time goes in v9:
time: 46.9 us; the launch traced here: 46.5 us
  Pallas kernels  24.7 us (53%)
  starting transfers between devices  18.7 us (40%)
  waiting for transfers between devices  2.35 us (5%)
  between operations  0.77 us (2%)
    pallas_call x1, Pallas kernels, shards(): pl.pallas_call(second_kernel, in_specs=[HBM] * 6 + [ANY] + [HBM] * (3 + l...  8.1 us
    all_to_all x1, starting transfers between devices, shards(): lax.all_to_all(orders, both, split_axis=0, concat_axis=0, tiled=True)  7.25 us
    pallas_call x1, Pallas kernels, shards(): pl.pallas_call(first_kernel, in_specs=[HBM] * 3 + [ANY] * 6 + [HBM] * len...  5.58 us
    pallas_call x1, Pallas kernels, shards(): pl.pallas_call(viscosity_kernel, in_specs=[HBM] * 4 + [ANY, HBM], out_spe...  4.96 us
    ppermute x1, starting transfers between devices, shards(): lower_one = lax.ppermute(lower_one, both, lower_only(first))  4.89 us
    all_to_all x1, starting transfers between devices, shards(): load = lax.all_to_all(load, both, split_axis=0, concat_axis=0, tiled=True)  3.91 us
    pallas_call x1, Pallas kernels, shards(): pl.pallas_call(message_kernel, in_specs=[HBM] * 4, out_specs=[VMEM] * 2,...  2.43 us
    all_to_all x1, waiting for transfers between devices, shards(): lax.all_to_all(orders, both, split_axis=0, concat_axis=0, tiled=True)  2.33 us
  transfers between devices with their start and end apart: 7, of which 1 were waited for; matrix products, arithmetic and copies ran while one was open for 0% of the time, Pallas kernels for 45%

profile of v9, /device:TPU:0, one launch (start us, length us, event | category | flops | bytes accessed | tf_op | source)
XLA Modules:
  0.0 46.5 jit_solution(15766875886740563862)
XLA Ops:
  0.6 2.4 %shard_map.121 = (f32[32,2048]{1,0:T(8,128)S(1)}, f32[32,2048]{1,0:T(8,128)S(1)}) custom-call(f32[16]{0:T(128)} %viscosity_from.3, f32[3,4,32,2048]{3,2,1,0:T(8,128)} %start.1, f32[3,4,32,2048]{3,2,1,0:T(8,128)} %f.7, s32[4,32,2048]{2,1,0:T(8,128)} %index_from.1), custom_call_target="tpu_custom_call" | custom-call | bytes 60000000 | tf_op jit(solution)/shard_map/pallas_call | solution.py:763
  3.1 0.7 %collective-permute-start.1 = (f32[32,2048]{1,0:T(8,128)S(1)}, f32[32,2048]{1,0:T(8,128)S(1)}, u32[]{:S(2)}, u32[]{:S(2)}) collective-permute-start(f32[32,2048]{1,0:T(8,128)S(1)} %get-tuple-element.44.own_two.mine_two), channel_id=1, source_target_pairs={{3,1},{5,3},{7,5},{9,7},{11,9},{13,11},{15,13},{19,17},{21,19},{23... | collective-permute-start | bytes 786440 | tf_op jit(solution)/shard_map/ppermute | solution.py:779
  3.8 0.7 %collective-permute-start = (f32[32,2048]{1,0:T(8,128)S(1)}, f32[32,2048]{1,0:T(8,128)S(1)}, u32[]{:S(2)}, u32[]{:S(2)}) collective-permute-start(f32[32,2048]{1,0:T(8,128)S(1)} %get-tuple-element.43.token.own_one.mine_one), channel_id=1, source_target_pairs={{1,3},{3,5},{5,7},{7,9},{9,11},{11,13},{13,15},{17,19},{19,21},{21... | collective-permute-start | bytes 786440 | tf_op jit(solution)/shard_map/ppermute | solution.py:780
  4.4 5.0 %shard_map.122 = (f32[4,32,2048]{2,1,0:T(8,128)}, f32[3,2,32,2048]{3,2,1,0:T(8,128)}, f32[2,32,2048]{2,1,0:T(8,128)S(1)}, f32[2,32,2048]{2,1,0:T(8,128)S(1)}, f3...) custom-call(f32[16]{0:T(128)} %viscosity_from.3, f32[3,4,32,2048]{3,2,1,0:T(8,128)} %start.1, f32[3,4,32,2048]{3,2,1,0:T(8,128)} %f.7, ...), custom_call_target="tpu_custom_call" | custom-call | bytes 60000000 | tf_op jit(solution)/shard_map/pallas_call | solution.py:783
  9.4 4.9 %collective-permute-start.2 = (f32[32,2048]{1,0:T(8,128)S(1)}, f32[32,2048]{1,0:T(8,128)S(1)}, u32[]{:S(2)}, u32[]{:S(2)}) collective-permute-start(f32[32,2048]{1,0:T(8,128)S(1)} %get-tuple-element.43.token.own_one.mine_one), channel_id=1, source_target_pairs={{0,2},{2,4},{4,6},{6,8},{8,10},{10,12},{12,14},{16,18},{18,20},{20... | collective-permute-start | bytes 786440 | tf_op jit(solution)/shard_map/ppermute | solution.py:809
  14.3 1.3 %collective-permute-start.3 = (f32[32,2048]{1,0:T(8,128)S(1)}, f32[32,2048]{1,0:T(8,128)S(1)}, u32[]{:S(2)}, u32[]{:S(2)}) collective-permute-start(f32[32,2048]{1,0:T(8,128)S(1)} %get-tuple-element.44.own_two.mine_two), channel_id=1, source_target_pairs={{2,0},{4,2},{6,4},{8,6},{10,8},{12,10},{14,12},{18,16},{20,18},{22... | collective-permute-start | bytes 786440 | tf_op jit(solution)/shard_map/ppermute | solution.py:810
  15.6 0.0 collective-permute-done.1.two
  15.6 0.0 collective-permute-done.one
  15.6 0.7 %shard_map.123 = f32[16,16,128]{2,1,0:T(8,128)} custom-call(f32[2,32,2048]{2,1,0:T(8,128)S(1)} %get-tuple-element.38.surface_swept, f32[2,32,2048]{2,1,0:T(8,128)S(1)} %get-tuple-element.39.surface_eta, f32[32,2048]{1,0:T(8,128)S(1)} %get-tuple-element.40.force, f32[32,2048]{1,0:T(8,128)S(1)} %get-tuple-element.43.token.own_one.mine_one, ...), custom_call_target="tpu_custom_call" | custom-call | bytes 600000000 | tf_op jit(solution)/shard_map/pallas_call | solution.py:813
  16.3 7.2 %all-to-all-start = ((f32[16,16,128]{2,1,0:T(8,128)}), f32[16,16,128]{2,1,0:T(8,128)S(1)}, u32[]{:S(2)}, u32[]{:S(2)}) async-start(f32[16,16,128]{2,1,0:T(8,128)} %shard_map.123), calls=%async_computation | async-start | bytes 262144 | tf_op jit(solution)/shard_map/all_to_all | solution.py:829
  23.6 0.0 collective-permute-done.2.lower_one
  23.6 0.0 collective-permute-done.3.lower_two
  23.6 5.6 %shard_map.124 = (f32[3,2,32,2048]{3,2,1,0:T(8,128)}, f32[32,2048]{1,0:T(8,128)}, f32[264,2048]{1,0:T(8,128)}, f32[2,32,2048]{2,1,0:T(8,128)}, f32[2,32,2048]{2,...) custom-call(f32[3,4,32,2048]{3,2,1,0:T(8,128)} %start.1, ...), custom_call_target="tpu_custom_call" | custom-call | bytes 150000000 | tf_op jit(solution)/shard_map/pallas_call | solution.py:847
  29.2 2.3 %all-to-all-done.orders = f32[16,16,128]{2,1,0:T(8,128)S(1)} async-done(((f32[16,16,128]{2,1,0:T(8,128)}), f32[16,16,128]{2,1,0:T(8,128)S(1)}, u32[]{:S(2)}, u32[]{:S(2)}) %all-to-all-start) | async-done | bytes 131104 | tf_op jit(solution)/shard_map/all_to_all | solution.py:829
  31.5 0.0 collective-permute-start.4
  31.5 1.5 %shard_map.125 = (f32[64,512]{1,0:T(8,128)}, f32[16,16,128]{2,1,0:T(8,128)}) custom-call(f32[16,16,128]{2,1,0:T(8,128)S(1)} %all-to-all-done.orders, bf16[256,512]{1,0:T(8,128)(2,1)S(1)} %get-tuple-element.48.high, bf16[256,512]{1,0:T(8,128)(2,1)S(1)} %get-tuple-element.49.low, f32[512,128]{1,0:T(8,128)S(1)} %get-tuple-element.50.response), custom_call_target="tpu_custom_call" | custom-call | bytes 600000000 | tf_op jit(solution)/shard_map/pallas_call | solution.py:870
  33.0 3.9 %all-to-all-start.1 = ((f32[16,16,128]{2,1,0:T(8,128)}), f32[16,16,128]{2,1,0:T(8,128)S(1)}, u32[]{:S(2)}, u32[]{:S(2)}) async-start(f32[16,16,128]{2,1,0:T(8,128)} %get-tuple-element.59), calls=%async_computation.1 | async-start | bytes 262144 | tf_op jit(solution)/shard_map/all_to_all | solution.py:879
  36.9 0.0 collective-permute-done.4.ring
  36.9 8.1 %shard_map.126 = (f32[3,4,32,2048]{3,2,1,0:T(8,128)}, f32[8,128]{1,0:T(8,128)}, bf16[32,2048]{1,0:T(8,128)(2,1)S(1)}, bf16[256,1024]{1,0:T(8,128)(2,1)S(1)}, bf16[256,1024]{1,0:T(8,128)(2,1)S(1)}) custom-call(f32[3,2,32,2048]{3,2,1,0:T(8,128)} %get-tuple-element.34.early, f32[3,2,32,2048]{3,2,1,0:T(8,128)} %get-tuple-element.45.late, f32[3,4,32,2048]{3,2,1,0:T(8,128)} %f.7, ...), custom_call_target="tpu_custom_call" | custom-call | bytes 150000000 | tf_op jit(solution)/shard_map/pallas_call | solution.py:882
  45.0 0.0 all-to-all-done.1.load
  45.0 1.4 %shard_map.127 = f32[32,2048]{1,0:T(8,128)} custom-call(f32[16,16,128]{2,1,0:T(8,128)S(1)} %all-to-all-done.1.load, bf16[256,1024]{1,0:T(8,128)(2,1)S(1)} %get-tuple-element.60.high, bf16[256,1024]{1,0:T(8,128)(2,1)S(1)} %get-tuple-element.61.low, bf16[32,2048]{1,0:T(8,128)(2,1)S(1)} %get-tuple-element.62.mask), custom_call_target="tpu_custom_call" | custom-call | bytes 9000000 | tf_op jit(solution)/shard_map/pallas_call | solution.py:912
Async XLA Ops:
  3.1 12.5 %collective-permute-start.1 = (f32[32,2048]{1,0:T(8,128)S(1)}, f32[32,2048]{1,0:T(8,128)S(1)}, u32[]{:S(2)}, u32[]{:S(2)}) collective-permute-start(f32[32,2048]{1,0:T(8,128)S(1)} %get-tuple-element.44.own_two.mine_two), channel_id=1, source_target_pairs={{3,1},{5,3},{7,5},{9,7},{11,9},{13,11},{15,13},{19,17},{21,19},{23... | collective-permute-start | bytes 786440 | tf_op jit(solution)/shard_map/ppermute | solution.py:779
  3.8 11.9 %collective-permute-start = (f32[32,2048]{1,0:T(8,128)S(1)}, f32[32,2048]{1,0:T(8,128)S(1)}, u32[]{:S(2)}, u32[]{:S(2)}) collective-permute-start(f32[32,2048]{1,0:T(8,128)S(1)} %get-tuple-element.43.token.own_one.mine_one), channel_id=1, source_target_pairs={{1,3},{3,5},{5,7},{7,9},{9,11},{11,13},{13,15},{17,19},{19,21},{21... | collective-permute-start | bytes 786440 | tf_op jit(solution)/shard_map/ppermute | solution.py:780
  9.4 14.2 %collective-permute-start.2 = (f32[32,2048]{1,0:T(8,128)S(1)}, f32[32,2048]{1,0:T(8,128)S(1)}, u32[]{:S(2)}, u32[]{:S(2)}) collective-permute-start(f32[32,2048]{1,0:T(8,128)S(1)} %get-tuple-element.43.token.own_one.mine_one), channel_id=1, source_target_pairs={{0,2},{2,4},{4,6},{6,8},{8,10},{10,12},{12,14},{16,18},{18,20},{20... | collective-permute-start | bytes 786440 | tf_op jit(solution)/shard_map/ppermute | solution.py:809
  14.3 9.3 %collective-permute-start.3 = (f32[32,2048]{1,0:T(8,128)S(1)}, f32[32,2048]{1,0:T(8,128)S(1)}, u32[]{:S(2)}, u32[]{:S(2)}) collective-permute-start(f32[32,2048]{1,0:T(8,128)S(1)} %get-tuple-element.44.own_two.mine_two), channel_id=1, source_target_pairs={{2,0},{4,2},{6,4},{8,6},{10,8},{12,10},{14,12},{18,16},{20,18},{22... | collective-permute-start | bytes 786440 | tf_op jit(solution)/shard_map/ppermute | solution.py:810
  16.3 15.2 %all-to-all-start = ((f32[16,16,128]{2,1,0:T(8,128)}), f32[16,16,128]{2,1,0:T(8,128)S(1)}, u32[]{:S(2)}, u32[]{:S(2)}) async-start(f32[16,16,128]{2,1,0:T(8,128)} %shard_map.123), calls=%async_computation | async-start | bytes 262144 | tf_op jit(solution)/shard_map/all_to_all | solution.py:829
  31.5 5.4 %collective-permute-start.4 = (f32[264,2048]{1,0:T(8,128)}, f32[264,2048]{1,0:T(8,128)S(1)}, u32[]{:S(2)}, u32[]{:S(2)}) collective-permute-start(f32[264,2048]{1,0:T(8,128)} %get-tuple-element.54), channel_id=1, source_target_pairs={{0,1},{1,0},{2,3},{3,2},{4,5},{5,4},{6,7},{7,6},{8,9},{9,8},{10,11... | collective-permute-start | bytes 6488072 | tf_op jit(solution)/shard_map/ppermute | solution.py:869
  33.0 12.0 %all-to-all-start.1 = ((f32[16,16,128]{2,1,0:T(8,128)}), f32[16,16,128]{2,1,0:T(8,128)S(1)}, u32[]{:S(2)}, u32[]{:S(2)}) async-start(f32[16,16,128]{2,1,0:T(8,128)} %get-tuple-element.59), calls=%async_computation.1 | async-start | bytes 262144 | tf_op jit(solution)/shard_map/all_to_all | solution.py:879

commit v10 on v9

--- a/solution.py
+++ b/solution.py
@@ -112,6 +112,11 @@
     order = lax.broadcasted_iota(jnp.int32, shape, len(shape) - 1) % RADIX
     mirrored = order > RADIX // 2
     return jnp.where(mirrored, RADIX - order, order), mirrored
+
+
+def three_pass(product, near, far, high, low):
+    both = product(jnp.concatenate([near, far], axis=0), high[...])
+    return both[: near.shape[0]] + both[near.shape[0] :] + product(near, low[...])
 
 
 def dot_nt(a, b):
@@ -277,7 +282,7 @@
             eta[k + 1, pl.ds(start + TILE, TILE)] = half_viscosity(index[k, pl.ds(start, TILE)], viscosity)
             return 0
 
-        lax.fori_loop(0, rows // TILE, lookup, 0)
+        lax.fori_loop(0, rows // TILE, lookup, 0, unroll=2)
         stores += start_all(
             [pltpu.make_async_copy(eta.at[k + 1, block], eta_out.at[shell(k)], more_sems.at[2 * EARLY + 1 + k])]
         )
@@ -400,7 +405,6 @@
         for c in range(components):
             field[c, nothing, inner] = zeros
         eta[nothing, inner] = zeros
-    before_first()
 
     def start_until(k):
         for ahead in range(begin, shells):
@@ -410,6 +414,7 @@
                 forces[ahead] = start_all(force_load(ahead))
 
     start_until(begin + 2)
+    before_first()
     stores, there = [], set()
     for k in range(begin, shells):
         s = shell(k)
@@ -673,7 +678,7 @@
             result[c, s, part] = relax(weights, factor, middle, others, force[c, s, part])
 
     def after_shell(s, k):
-        if k == 0:
+        if k == shells - 2:
             copies.extend(
                 start_all(
                     [
@@ -683,7 +688,7 @@
                 )
             )
             mask_copy.start()
-        if k == shells - 2:
+        if k == shells - 1:
             mask_copy.wait()
             mask_out[...] = mask[...].astype(jnp.float32).astype(jnp.bfloat16)
 
@@ -701,7 +706,7 @@
     bands, rows = orders.shape[0] // radial, high.shape[0] * radial // orders.shape[0]
     fourier = jnp.concatenate([unpack(orders[band * radial + radial - 1], width) for band in range(bands)], axis=0)
     near, far = split(fourier.T)
-    spectrum = dot(near, high[...]) + dot(far, high[...]) + dot(near, low[...])
+    spectrum = three_pass(dot, near, far, high, low)
     coefficients[...] = spectrum
     own = response[:, :width]
     for place in range(1, radial):
@@ -709,7 +714,7 @@
             lax.axis_index("radial") == place, response[:, place * width : (place + 1) * width], own
         )
     near, far = split(own.T * spectrum)
-    load = (dot_nt(near, high[...]) + dot_nt(far, high[...]) + dot_nt(near, low[...])).T
+    load = three_pass(dot_nt, near, far, high, low).T
     for band in range(bands):
         block = pack(load[band * rows : (band + 1) * rows])
         for place in range(radial):

time: 46.9 us -> 46.6 us (level)
  transfers between devices with their start and end apart: 7 -> 7, of which waited for: 1 -> 1; matrix products, arithmetic and copies ran while one was open for 0% -> 0% of each run, Pallas kernels for 45% -> 44%
where the time goes in v10:
time: 46.6 us; the launch traced here: 46.2 us
  Pallas kernels  24.3 us (52%)
  starting transfers between devices  18.7 us (40%)
  waiting for transfers between devices  2.39 us (5%)
  between operations  0.76 us (2%)
    pallas_call x1, Pallas kernels, shards(): pl.pallas_call(second_kernel, in_specs=[HBM] * 6 + [ANY] + [HBM] * (3 + l...  7.87 us
    all_to_all x1, starting transfers between devices, shards(): lax.all_to_all(orders, both, split_axis=0, concat_axis=0, tiled=True)  7.25 us
    pallas_call x1, Pallas kernels, shards(): pl.pallas_call(first_kernel, in_specs=[HBM] * 3 + [ANY] * 6 + [HBM] * len...  5.58 us
    pallas_call x1, Pallas kernels, shards(): pl.pallas_call(viscosity_kernel, in_specs=[HBM] * 4 + [ANY, HBM], out_spe...  4.94 us
    ppermute x1, starting transfers between devices, shards(): lower_one = lax.ppermute(lower_one, both, lower_only(first))  4.89 us
    all_to_all x1, starting transfers between devices, shards(): load = lax.all_to_all(load, both, split_axis=0, concat_axis=0, tiled=True)  3.91 us
    pallas_call x1, Pallas kernels, shards(): pl.pallas_call(message_kernel, in_specs=[HBM] * 4, out_specs=[VMEM] * 2,...  2.43 us
    all_to_all x1, waiting for transfers between devices, shards(): lax.all_to_all(orders, both, split_axis=0, concat_axis=0, tiled=True)  2.33 us
  transfers between devices with their start and end apart: 7, of which 1 were waited for; matrix products, arithmetic and copies ran while one was open for 0% of the time, Pallas kernels for 44%

profile of v10, /device:TPU:0, one launch (start us, length us, event | category | flops | bytes accessed | tf_op | source)
XLA Modules:
  0.0 46.2 jit_solution(4085022917223326193)
XLA Ops:
  0.6 2.4 %shard_map.121 = (f32[32,2048]{1,0:T(8,128)S(1)}, f32[32,2048]{1,0:T(8,128)S(1)}) custom-call(f32[16]{0:T(128)} %viscosity_from.3, f32[3,4,32,2048]{3,2,1,0:T(8,128)} %start.1, f32[3,4,32,2048]{3,2,1,0:T(8,128)} %f.7, s32[4,32,2048]{2,1,0:T(8,128)} %index_from.1), custom_call_target="tpu_custom_call" | custom-call | bytes 60000000 | tf_op jit(solution)/shard_map/pallas_call | solution.py:768
  3.1 0.7 %collective-permute-start.1 = (f32[32,2048]{1,0:T(8,128)S(1)}, f32[32,2048]{1,0:T(8,128)S(1)}, u32[]{:S(2)}, u32[]{:S(2)}) collective-permute-start(f32[32,2048]{1,0:T(8,128)S(1)} %get-tuple-element.44.own_two.mine_two), channel_id=1, source_target_pairs={{3,1},{5,3},{7,5},{9,7},{11,9},{13,11},{15,13},{19,17},{21,19},{23... | collective-permute-start | bytes 786440 | tf_op jit(solution)/shard_map/ppermute | solution.py:784
  3.8 0.7 %collective-permute-start = (f32[32,2048]{1,0:T(8,128)S(1)}, f32[32,2048]{1,0:T(8,128)S(1)}, u32[]{:S(2)}, u32[]{:S(2)}) collective-permute-start(f32[32,2048]{1,0:T(8,128)S(1)} %get-tuple-element.43.token.own_one.mine_one), channel_id=1, source_target_pairs={{1,3},{3,5},{5,7},{7,9},{9,11},{11,13},{13,15},{17,19},{19,21},{21... | collective-permute-start | bytes 786440 | tf_op jit(solution)/shard_map/ppermute | solution.py:785
  4.4 4.9 %shard_map.122 = (f32[4,32,2048]{2,1,0:T(8,128)}, f32[3,2,32,2048]{3,2,1,0:T(8,128)}, f32[2,32,2048]{2,1,0:T(8,128)S(1)}, f32[2,32,2048]{2,1,0:T(8,128)S(1)}, f3...) custom-call(f32[16]{0:T(128)} %viscosity_from.3, f32[3,4,32,2048]{3,2,1,0:T(8,128)} %start.1, f32[3,4,32,2048]{3,2,1,0:T(8,128)} %f.7, ...), custom_call_target="tpu_custom_call" | custom-call | bytes 60000000 | tf_op jit(solution)/shard_map/pallas_call | solution.py:788
  9.4 4.9 %collective-permute-start.2 = (f32[32,2048]{1,0:T(8,128)S(1)}, f32[32,2048]{1,0:T(8,128)S(1)}, u32[]{:S(2)}, u32[]{:S(2)}) collective-permute-start(f32[32,2048]{1,0:T(8,128)S(1)} %get-tuple-element.43.token.own_one.mine_one), channel_id=1, source_target_pairs={{0,2},{2,4},{4,6},{6,8},{8,10},{10,12},{12,14},{16,18},{18,20},{20... | collective-permute-start | bytes 786440 | tf_op jit(solution)/shard_map/ppermute | solution.py:814
  14.3 1.3 %collective-permute-start.3 = (f32[32,2048]{1,0:T(8,128)S(1)}, f32[32,2048]{1,0:T(8,128)S(1)}, u32[]{:S(2)}, u32[]{:S(2)}) collective-permute-start(f32[32,2048]{1,0:T(8,128)S(1)} %get-tuple-element.44.own_two.mine_two), channel_id=1, source_target_pairs={{2,0},{4,2},{6,4},{8,6},{10,8},{12,10},{14,12},{18,16},{20,18},{22... | collective-permute-start | bytes 786440 | tf_op jit(solution)/shard_map/ppermute | solution.py:815
  15.6 0.0 collective-permute-done.1.two
  15.6 0.0 collective-permute-done.one
  15.6 0.7 %shard_map.123 = f32[16,16,128]{2,1,0:T(8,128)} custom-call(f32[2,32,2048]{2,1,0:T(8,128)S(1)} %get-tuple-element.38.surface_swept, f32[2,32,2048]{2,1,0:T(8,128)S(1)} %get-tuple-element.39.surface_eta, f32[32,2048]{1,0:T(8,128)S(1)} %get-tuple-element.40.force, f32[32,2048]{1,0:T(8,128)S(1)} %get-tuple-element.43.token.own_one.mine_one, ...), custom_call_target="tpu_custom_call" | custom-call | bytes 600000000 | tf_op jit(solution)/shard_map/pallas_call | solution.py:818
  16.3 7.2 %all-to-all-start = ((f32[16,16,128]{2,1,0:T(8,128)}), f32[16,16,128]{2,1,0:T(8,128)S(1)}, u32[]{:S(2)}, u32[]{:S(2)}) async-start(f32[16,16,128]{2,1,0:T(8,128)} %shard_map.123), calls=%async_computation | async-start | bytes 262144 | tf_op jit(solution)/shard_map/all_to_all | solution.py:834
  23.6 0.0 collective-permute-done.2.lower_one
  23.6 0.0 collective-permute-done.3.lower_two
  23.6 5.6 %shard_map.124 = (f32[3,2,32,2048]{3,2,1,0:T(8,128)}, f32[32,2048]{1,0:T(8,128)}, f32[264,2048]{1,0:T(8,128)}, f32[2,32,2048]{2,1,0:T(8,128)}, f32[2,32,2048]{2,...) custom-call(f32[3,4,32,2048]{3,2,1,0:T(8,128)} %start.1, ...), custom_call_target="tpu_custom_call" | custom-call | bytes 150000000 | tf_op jit(solution)/shard_map/pallas_call | solution.py:852
  29.2 2.3 %all-to-all-done.orders = f32[16,16,128]{2,1,0:T(8,128)S(1)} async-done(((f32[16,16,128]{2,1,0:T(8,128)}), f32[16,16,128]{2,1,0:T(8,128)S(1)}, u32[]{:S(2)}, u32[]{:S(2)}) %all-to-all-start) | async-done | bytes 131104 | tf_op jit(solution)/shard_map/all_to_all | solution.py:834
  31.5 0.0 collective-permute-start.4
  31.5 1.4 %shard_map.125 = (f32[64,512]{1,0:T(8,128)}, f32[16,16,128]{2,1,0:T(8,128)}) custom-call(f32[16,16,128]{2,1,0:T(8,128)S(1)} %all-to-all-done.orders, bf16[256,512]{1,0:T(8,128)(2,1)S(1)} %get-tuple-element.48.high, bf16[256,512]{1,0:T(8,128)(2,1)S(1)} %get-tuple-element.49.low, f32[512,128]{1,0:T(8,128)S(1)} %get-tuple-element.50.response), custom_call_target="tpu_custom_call" | custom-call | bytes 600000000 | tf_op jit(solution)/shard_map/pallas_call | solution.py:875
  32.9 3.9 %all-to-all-start.1 = ((f32[16,16,128]{2,1,0:T(8,128)}), f32[16,16,128]{2,1,0:T(8,128)S(1)}, u32[]{:S(2)}, u32[]{:S(2)}) async-start(f32[16,16,128]{2,1,0:T(8,128)} %get-tuple-element.59), calls=%async_computation.1 | async-start | bytes 262144 | tf_op jit(solution)/shard_map/all_to_all | solution.py:884
  36.8 0.0 collective-permute-done.4.ring
  36.8 7.9 %shard_map.126 = (f32[3,4,32,2048]{3,2,1,0:T(8,128)}, f32[8,128]{1,0:T(8,128)}, bf16[32,2048]{1,0:T(8,128)(2,1)S(1)}, bf16[256,1024]{1,0:T(8,128)(2,1)S(1)}, bf16[256,1024]{1,0:T(8,128)(2,1)S(1)}) custom-call(f32[3,2,32,2048]{3,2,1,0:T(8,128)} %get-tuple-element.34.early, f32[3,2,32,2048]{3,2,1,0:T(8,128)} %get-tuple-element.45.late, f32[3,4,32,2048]{3,2,1,0:T(8,128)} %f.7, ...), custom_call_target="tpu_custom_call" | custom-call | bytes 150000000 | tf_op jit(solution)/shard_map/pallas_call | solution.py:887
  44.7 0.0 all-to-all-done.1.load
  44.8 1.4 %shard_map.127 = f32[32,2048]{1,0:T(8,128)} custom-call(f32[16,16,128]{2,1,0:T(8,128)S(1)} %all-to-all-done.1.load, bf16[256,1024]{1,0:T(8,128)(2,1)S(1)} %get-tuple-element.60.high, bf16[256,1024]{1,0:T(8,128)(2,1)S(1)} %get-tuple-element.61.low, bf16[32,2048]{1,0:T(8,128)(2,1)S(1)} %get-tuple-element.62.mask), custom_call_target="tpu_custom_call" | custom-call | bytes 9000000 | tf_op jit(solution)/shard_map/pallas_call | solution.py:917
Async XLA Ops:
  3.1 12.5 %collective-permute-start.1 = (f32[32,2048]{1,0:T(8,128)S(1)}, f32[32,2048]{1,0:T(8,128)S(1)}, u32[]{:S(2)}, u32[]{:S(2)}) collective-permute-start(f32[32,2048]{1,0:T(8,128)S(1)} %get-tuple-element.44.own_two.mine_two), channel_id=1, source_target_pairs={{3,1},{5,3},{7,5},{9,7},{11,9},{13,11},{15,13},{19,17},{21,19},{23... | collective-permute-start | bytes 786440 | tf_op jit(solution)/shard_map/ppermute | solution.py:784
  3.8 11.8 %collective-permute-start = (f32[32,2048]{1,0:T(8,128)S(1)}, f32[32,2048]{1,0:T(8,128)S(1)}, u32[]{:S(2)}, u32[]{:S(2)}) collective-permute-start(f32[32,2048]{1,0:T(8,128)S(1)} %get-tuple-element.43.token.own_one.mine_one), channel_id=1, source_target_pairs={{1,3},{3,5},{5,7},{7,9},{9,11},{11,13},{13,15},{17,19},{19,21},{21... | collective-permute-start | bytes 786440 | tf_op jit(solution)/shard_map/ppermute | solution.py:785
  9.4 14.2 %collective-permute-start.2 = (f32[32,2048]{1,0:T(8,128)S(1)}, f32[32,2048]{1,0:T(8,128)S(1)}, u32[]{:S(2)}, u32[]{:S(2)}) collective-permute-start(f32[32,2048]{1,0:T(8,128)S(1)} %get-tuple-element.43.token.own_one.mine_one), channel_id=1, source_target_pairs={{0,2},{2,4},{4,6},{6,8},{8,10},{10,12},{12,14},{16,18},{18,20},{20... | collective-permute-start | bytes 786440 | tf_op jit(solution)/shard_map/ppermute | solution.py:814
  14.3 9.3 %collective-permute-start.3 = (f32[32,2048]{1,0:T(8,128)S(1)}, f32[32,2048]{1,0:T(8,128)S(1)}, u32[]{:S(2)}, u32[]{:S(2)}) collective-permute-start(f32[32,2048]{1,0:T(8,128)S(1)} %get-tuple-element.44.own_two.mine_two), channel_id=1, source_target_pairs={{2,0},{4,2},{6,4},{8,6},{10,8},{12,10},{14,12},{18,16},{20,18},{22... | collective-permute-start | bytes 786440 | tf_op jit(solution)/shard_map/ppermute | solution.py:815
  16.3 15.2 %all-to-all-start = ((f32[16,16,128]{2,1,0:T(8,128)}), f32[16,16,128]{2,1,0:T(8,128)S(1)}, u32[]{:S(2)}, u32[]{:S(2)}) async-start(f32[16,16,128]{2,1,0:T(8,128)} %shard_map.123), calls=%async_computation | async-start | bytes 262144 | tf_op jit(solution)/shard_map/all_to_all | solution.py:834
  31.5 5.3 %collective-permute-start.4 = (f32[264,2048]{1,0:T(8,128)}, f32[264,2048]{1,0:T(8,128)S(1)}, u32[]{:S(2)}, u32[]{:S(2)}) collective-permute-start(f32[264,2048]{1,0:T(8,128)} %get-tuple-element.54), channel_id=1, source_target_pairs={{0,1},{1,0},{2,3},{3,2},{4,5},{5,4},{6,7},{7,6},{8,9},{9,8},{10,11... | collective-permute-start | bytes 6488072 | tf_op jit(solution)/shard_map/ppermute | solution.py:874
  32.9 11.9 %all-to-all-start.1 = ((f32[16,16,128]{2,1,0:T(8,128)}), f32[16,16,128]{2,1,0:T(8,128)S(1)}, u32[]{:S(2)}, u32[]{:S(2)}) async-start(f32[16,16,128]{2,1,0:T(8,128)} %get-tuple-element.59), calls=%async_computation.1 | async-start | bytes 262144 | tf_op jit(solution)/shard_map/all_to_all | solution.py:884

commit v11 on v10

--- a/solution.py
+++ b/solution.py
@@ -478,7 +478,8 @@
     lower = lax.axis_index("radial") == 0
     last, beyond = jnp.where(lower, shells - 1, 0), jnp.where(lower, shells + 1, 0)
     values = pl.ds(0, own_out.shape[1])
-    copies = start_all(
+    copies = []
+    own_copies = lambda: start_all(
         [
             pltpu.make_async_copy(mine.at[values], own_out.at[k], more_sems.at[4 + components + k])
             for k, mine in enumerate((mine_one, mine_two))
@@ -508,7 +509,6 @@
             start_all(
                 [
                     pltpu.make_async_copy(edges, tail, more_sems.at[2]),
-                    pltpu.make_async_copy(messages, beside_out, more_sems.at[3]),
                 ]
             )
         )
@@ -543,6 +543,8 @@
 
     def after_shell(s, k):
         if k == EARLY:
+            copies.extend(own_copies())
+            copies.extend(start_all([pltpu.make_async_copy(messages, beside_out, more_sems.at[3])]))
             copies.extend(
                 start_all(
                     [

time: 46.6 us -> 46.3 us (level)
  no operation moved by 1% of the time
where the time goes in v11:
time: 46.3 us; the launch traced here: 45.8 us
  Pallas kernels  24 us (52%)
  starting transfers between devices  18.3 us (40%)
  waiting for transfers between devices  2.76 us (6%)
  between operations  0.76 us (2%)
    pallas_call x1, Pallas kernels, shards(): pl.pallas_call(second_kernel, in_specs=[HBM] * 6 + [ANY] + [HBM] * (3 + l...  7.87 us
    all_to_all x1, starting transfers between devices, shards(): lax.all_to_all(orders, both, split_axis=0, concat_axis=0, tiled=True)  7.25 us
    pallas_call x1, Pallas kernels, shards(): pl.pallas_call(first_kernel, in_specs=[HBM] * 3 + [ANY] * 6 + [HBM] * len...  5.2 us
    pallas_call x1, Pallas kernels, shards(): pl.pallas_call(viscosity_kernel, in_specs=[HBM] * 4 + [ANY, HBM], out_spe...  4.94 us
    ppermute x1, starting transfers between devices, shards(): lower_one = lax.ppermute(lower_one, both, lower_only(first))  4.89 us
    all_to_all x1, starting transfers between devices, shards(): load = lax.all_to_all(load, both, split_axis=0, concat_axis=0, tiled=True)  3.54 us
    all_to_all x1, waiting for transfers between devices, shards(): lax.all_to_all(orders, both, split_axis=0, concat_axis=0, tiled=True)  2.7 us
    pallas_call x1, Pallas kernels, shards(): pl.pallas_call(message_kernel, in_specs=[HBM] * 4, out_specs=[VMEM] * 2,...  2.43 us
  transfers between devices with their start and end apart: 7, of which 1 were waited for; matrix products, arithmetic and copies ran while one was open for 0% of the time, Pallas kernels for 44%

profile of v11, /device:TPU:0, one launch (start us, length us, event | category | flops | bytes accessed | tf_op | source)
XLA Modules:
  0.0 45.8 jit_solution(5743936680563297958)
XLA Ops:
  0.6 2.4 %shard_map.121 = (f32[32,2048]{1,0:T(8,128)S(1)}, f32[32,2048]{1,0:T(8,128)S(1)}) custom-call(f32[16]{0:T(128)} %viscosity_from.3, f32[3,4,32,2048]{3,2,1,0:T(8,128)} %start.1, f32[3,4,32,2048]{3,2,1,0:T(8,128)} %f.7, s32[4,32,2048]{2,1,0:T(8,128)} %index_from.1), custom_call_target="tpu_custom_call" | custom-call | bytes 60000000 | tf_op jit(solution)/shard_map/pallas_call | solution.py:770
  3.1 0.7 %collective-permute-start.1 = (f32[32,2048]{1,0:T(8,128)S(1)}, f32[32,2048]{1,0:T(8,128)S(1)}, u32[]{:S(2)}, u32[]{:S(2)}) collective-permute-start(f32[32,2048]{1,0:T(8,128)S(1)} %get-tuple-element.44.own_two.mine_two), channel_id=1, source_target_pairs={{3,1},{5,3},{7,5},{9,7},{11,9},{13,11},{15,13},{19,17},{21,19},{23... | collective-permute-start | bytes 786440 | tf_op jit(solution)/shard_map/ppermute | solution.py:786
  3.8 0.7 %collective-permute-start = (f32[32,2048]{1,0:T(8,128)S(1)}, f32[32,2048]{1,0:T(8,128)S(1)}, u32[]{:S(2)}, u32[]{:S(2)}) collective-permute-start(f32[32,2048]{1,0:T(8,128)S(1)} %get-tuple-element.43.token.own_one.mine_one), channel_id=1, source_target_pairs={{1,3},{3,5},{5,7},{7,9},{9,11},{11,13},{13,15},{17,19},{19,21},{21... | collective-permute-start | bytes 786440 | tf_op jit(solution)/shard_map/ppermute | solution.py:787
  4.4 4.9 %shard_map.122 = (f32[4,32,2048]{2,1,0:T(8,128)}, f32[3,2,32,2048]{3,2,1,0:T(8,128)}, f32[2,32,2048]{2,1,0:T(8,128)S(1)}, f32[2,32,2048]{2,1,0:T(8,128)S(1)}, f3...) custom-call(f32[16]{0:T(128)} %viscosity_from.3, f32[3,4,32,2048]{3,2,1,0:T(8,128)} %start.1, f32[3,4,32,2048]{3,2,1,0:T(8,128)} %f.7, ...), custom_call_target="tpu_custom_call" | custom-call | bytes 60000000 | tf_op jit(solution)/shard_map/pallas_call | solution.py:790
  9.4 4.9 %collective-permute-start.2 = (f32[32,2048]{1,0:T(8,128)S(1)}, f32[32,2048]{1,0:T(8,128)S(1)}, u32[]{:S(2)}, u32[]{:S(2)}) collective-permute-start(f32[32,2048]{1,0:T(8,128)S(1)} %get-tuple-element.43.token.own_one.mine_one), channel_id=1, source_target_pairs={{0,2},{2,4},{4,6},{6,8},{8,10},{10,12},{12,14},{16,18},{18,20},{20... | collective-permute-start | bytes 786440 | tf_op jit(solution)/shard_map/ppermute | solution.py:816
  14.3 1.3 %collective-permute-start.3 = (f32[32,2048]{1,0:T(8,128)S(1)}, f32[32,2048]{1,0:T(8,128)S(1)}, u32[]{:S(2)}, u32[]{:S(2)}) collective-permute-start(f32[32,2048]{1,0:T(8,128)S(1)} %get-tuple-element.44.own_two.mine_two), channel_id=1, source_target_pairs={{2,0},{4,2},{6,4},{8,6},{10,8},{12,10},{14,12},{18,16},{20,18},{22... | collective-permute-start | bytes 786440 | tf_op jit(solution)/shard_map/ppermute | solution.py:817
  15.6 0.0 collective-permute-done.1.two
  15.6 0.0 collective-permute-done.one
  15.6 0.7 %shard_map.123 = f32[16,16,128]{2,1,0:T(8,128)} custom-call(f32[2,32,2048]{2,1,0:T(8,128)S(1)} %get-tuple-element.38.surface_swept, f32[2,32,2048]{2,1,0:T(8,128)S(1)} %get-tuple-element.39.surface_eta, f32[32,2048]{1,0:T(8,128)S(1)} %get-tuple-element.40.force, f32[32,2048]{1,0:T(8,128)S(1)} %get-tuple-element.43.token.own_one.mine_one, ...), custom_call_target="tpu_custom_call" | custom-call | bytes 600000000 | tf_op jit(solution)/shard_map/pallas_call | solution.py:820
  16.3 7.2 %all-to-all-start = ((f32[16,16,128]{2,1,0:T(8,128)}), f32[16,16,128]{2,1,0:T(8,128)S(1)}, u32[]{:S(2)}, u32[]{:S(2)}) async-start(f32[16,16,128]{2,1,0:T(8,128)} %shard_map.123), calls=%async_computation | async-start | bytes 262144 | tf_op jit(solution)/shard_map/all_to_all | solution.py:836
  23.6 0.0 collective-permute-done.2.lower_one
  23.6 0.0 collective-permute-done.3.lower_two
  23.6 5.2 %shard_map.124 = (f32[3,2,32,2048]{3,2,1,0:T(8,128)}, f32[32,2048]{1,0:T(8,128)}, f32[264,2048]{1,0:T(8,128)}, f32[2,32,2048]{2,1,0:T(8,128)}, f32[2,32,2048]{2,...) custom-call(f32[3,4,32,2048]{3,2,1,0:T(8,128)} %start.1, ...), custom_call_target="tpu_custom_call" | custom-call | bytes 150000000 | tf_op jit(solution)/shard_map/pallas_call | solution.py:854
  28.8 2.7 %all-to-all-done.orders = f32[16,16,128]{2,1,0:T(8,128)S(1)} async-done(((f32[16,16,128]{2,1,0:T(8,128)}), f32[16,16,128]{2,1,0:T(8,128)S(1)}, u32[]{:S(2)}, u32[]{:S(2)}) %all-to-all-start) | async-done | bytes 131104 | tf_op jit(solution)/shard_map/all_to_all | solution.py:836
  31.5 0.0 collective-permute-start.4
  31.5 1.4 %shard_map.125 = (f32[64,512]{1,0:T(8,128)}, f32[16,16,128]{2,1,0:T(8,128)}) custom-call(f32[16,16,128]{2,1,0:T(8,128)S(1)} %all-to-all-done.orders, bf16[256,512]{1,0:T(8,128)(2,1)S(1)} %get-tuple-element.48.high, bf16[256,512]{1,0:T(8,128)(2,1)S(1)} %get-tuple-element.49.low, f32[512,128]{1,0:T(8,128)S(1)} %get-tuple-element.50.response), custom_call_target="tpu_custom_call" | custom-call | bytes 600000000 | tf_op jit(solution)/shard_map/pallas_call | solution.py:877
  32.9 3.5 %all-to-all-start.1 = ((f32[16,16,128]{2,1,0:T(8,128)}), f32[16,16,128]{2,1,0:T(8,128)S(1)}, u32[]{:S(2)}, u32[]{:S(2)}) async-start(f32[16,16,128]{2,1,0:T(8,128)} %get-tuple-element.59), calls=%async_computation.1 | async-start | bytes 262144 | tf_op jit(solution)/shard_map/all_to_all | solution.py:886
  36.4 0.0 collective-permute-done.4.ring
  36.5 7.9 %shard_map.126 = (f32[3,4,32,2048]{3,2,1,0:T(8,128)}, f32[8,128]{1,0:T(8,128)}, bf16[32,2048]{1,0:T(8,128)(2,1)S(1)}, bf16[256,1024]{1,0:T(8,128)(2,1)S(1)}, bf16[256,1024]{1,0:T(8,128)(2,1)S(1)}) custom-call(f32[3,2,32,2048]{3,2,1,0:T(8,128)} %get-tuple-element.34.early, f32[3,2,32,2048]{3,2,1,0:T(8,128)} %get-tuple-element.45.late, f32[3,4,32,2048]{3,2,1,0:T(8,128)} %f.7, ...), custom_call_target="tpu_custom_call" | custom-call | bytes 150000000 | tf_op jit(solution)/shard_map/pallas_call | solution.py:889
  44.3 0.0 all-to-all-done.1.load
  44.4 1.4 %shard_map.127 = f32[32,2048]{1,0:T(8,128)} custom-call(f32[16,16,128]{2,1,0:T(8,128)S(1)} %all-to-all-done.1.load, bf16[256,1024]{1,0:T(8,128)(2,1)S(1)} %get-tuple-element.60.high, bf16[256,1024]{1,0:T(8,128)(2,1)S(1)} %get-tuple-element.61.low, bf16[32,2048]{1,0:T(8,128)(2,1)S(1)} %get-tuple-element.62.mask), custom_call_target="tpu_custom_call" | custom-call | bytes 9000000 | tf_op jit(solution)/shard_map/pallas_call | solution.py:919
Async XLA Ops:
  3.1 12.5 %collective-permute-start.1 = (f32[32,2048]{1,0:T(8,128)S(1)}, f32[32,2048]{1,0:T(8,128)S(1)}, u32[]{:S(2)}, u32[]{:S(2)}) collective-permute-start(f32[32,2048]{1,0:T(8,128)S(1)} %get-tuple-element.44.own_two.mine_two), channel_id=1, source_target_pairs={{3,1},{5,3},{7,5},{9,7},{11,9},{13,11},{15,13},{19,17},{21,19},{23... | collective-permute-start | bytes 786440 | tf_op jit(solution)/shard_map/ppermute | solution.py:786
  3.8 11.8 %collective-permute-start = (f32[32,2048]{1,0:T(8,128)S(1)}, f32[32,2048]{1,0:T(8,128)S(1)}, u32[]{:S(2)}, u32[]{:S(2)}) collective-permute-start(f32[32,2048]{1,0:T(8,128)S(1)} %get-tuple-element.43.token.own_one.mine_one), channel_id=1, source_target_pairs={{1,3},{3,5},{5,7},{7,9},{9,11},{11,13},{13,15},{17,19},{19,21},{21... | collective-permute-start | bytes 786440 | tf_op jit(solution)/shard_map/ppermute | solution.py:787
  9.4 14.2 %collective-permute-start.2 = (f32[32,2048]{1,0:T(8,128)S(1)}, f32[32,2048]{1,0:T(8,128)S(1)}, u32[]{:S(2)}, u32[]{:S(2)}) collective-permute-start(f32[32,2048]{1,0:T(8,128)S(1)} %get-tuple-element.43.token.own_one.mine_one), channel_id=1, source_target_pairs={{0,2},{2,4},{4,6},{6,8},{8,10},{10,12},{12,14},{16,18},{18,20},{20... | collective-permute-start | bytes 786440 | tf_op jit(solution)/shard_map/ppermute | solution.py:816
  14.3 9.3 %collective-permute-start.3 = (f32[32,2048]{1,0:T(8,128)S(1)}, f32[32,2048]{1,0:T(8,128)S(1)}, u32[]{:S(2)}, u32[]{:S(2)}) collective-permute-start(f32[32,2048]{1,0:T(8,128)S(1)} %get-tuple-element.44.own_two.mine_two), channel_id=1, source_target_pairs={{2,0},{4,2},{6,4},{8,6},{10,8},{12,10},{14,12},{18,16},{20,18},{22... | collective-permute-start | bytes 786440 | tf_op jit(solution)/shard_map/ppermute | solution.py:817
  16.3 15.2 %all-to-all-start = ((f32[16,16,128]{2,1,0:T(8,128)}), f32[16,16,128]{2,1,0:T(8,128)S(1)}, u32[]{:S(2)}, u32[]{:S(2)}) async-start(f32[16,16,128]{2,1,0:T(8,128)} %shard_map.123), calls=%async_computation | async-start | bytes 262144 | tf_op jit(solution)/shard_map/all_to_all | solution.py:836
  31.5 5.0 %collective-permute-start.4 = (f32[264,2048]{1,0:T(8,128)}, f32[264,2048]{1,0:T(8,128)S(1)}, u32[]{:S(2)}, u32[]{:S(2)}) collective-permute-start(f32[264,2048]{1,0:T(8,128)} %get-tuple-element.54), channel_id=1, source_target_pairs={{0,1},{1,0},{2,3},{3,2},{4,5},{5,4},{6,7},{7,6},{8,9},{9,8},{10,11... | collective-permute-start | bytes 6488072 | tf_op jit(solution)/shard_map/ppermute | solution.py:876
  32.9 11.5 %all-to-all-start.1 = ((f32[16,16,128]{2,1,0:T(8,128)}), f32[16,16,128]{2,1,0:T(8,128)S(1)}, u32[]{:S(2)}, u32[]{:S(2)}) async-start(f32[16,16,128]{2,1,0:T(8,128)} %get-tuple-element.59), calls=%async_computation.1 | async-start | bytes 262144 | tf_op jit(solution)/shard_map/all_to_all | solution.py:886

commit v12 on v11

--- a/solution.py
+++ b/solution.py
@@ -191,9 +191,9 @@
             pltpu.make_async_copy(d.at[:, :, part], fields.at[side], sems.at[3 + side]),
             pltpu.make_async_copy(f.at[:, :, part], forces.at[side], sems.at[5 + side]),
         ]
-    for copy in copies:
-        copy.start()
-    for copy in copies[:2] + copies[4:5]:
+    layer_copies, field_copies, force_copies = copies[1::3], copies[2::3], copies[3::3]
+    start_all(copies[:1] + layer_copies + field_copies + force_copies)
+    for copy in copies[:1] + layer_copies:
         copy.wait()
     near_eta, far_eta = 2 * components, 2 * components + 1
     for side, near, far in ((0, 0, 1), (1, TILE - 1, TILE - 2)):
@@ -201,13 +201,18 @@
             eta = half_viscosity(layers[side, s], viscosity)
             rows_of[near_eta, side * shells + s] = eta[near]
             rows_of[far_eta, side * shells + s] = eta[far]
-    for copy in copies[2:4] + copies[5:]:
+    for copy in field_copies:
         copy.wait()
     for side, near, far in ((0, 0, 1), (1, TILE - 1, TILE - 2)):
         for s in range(shells):
             for c in range(components):
                 rows_of[c, side * shells + s] = fields[side, c, s, near]
                 rows_of[components + c, side * shells + s] = fields[side, c, s, far]
+    for copy in force_copies:
+        copy.wait()
+    for side, near in ((0, 0), (1, TILE - 1)):
+        for s in range(shells):
+            for c in range(components):
                 rows_of[far_eta + 1 + c, side * shells + s] = forces[side, c, s, near]
     radial = lax.axis_index("radial")
     place = row_number((2 * shells, count)) % shells

time: 46.3 us -> 46.2 us (level)
  no operation moved by 1% of the time
where the time goes in v12:
time: 46.2 us; the launch traced here: 45.7 us
  Pallas kernels  23.9 us (52%)
  starting transfers between devices  18.3 us (40%)
  waiting for transfers between devices  2.76 us (6%)
  between operations  0.76 us (2%)
    pallas_call x1, Pallas kernels, shards(): pl.pallas_call(second_kernel, in_specs=[HBM] * 6 + [ANY] + [HBM] * (3 + l...  7.87 us
    all_to_all x1, starting transfers between devices, shards(): lax.all_to_all(orders, both, split_axis=0, concat_axis=0, tiled=True)  7.25 us
    pallas_call x1, Pallas kernels, shards(): pl.pallas_call(first_kernel, in_specs=[HBM] * 3 + [ANY] * 6 + [HBM] * len...  5.2 us
    pallas_call x1, Pallas kernels, shards(): pl.pallas_call(viscosity_kernel, in_specs=[HBM] * 4 + [ANY, HBM], out_spe...  4.94 us
    ppermute x1, starting transfers between devices, shards(): lower_one = lax.ppermute(lower_one, both, lower_only(first))  4.89 us
    all_to_all x1, starting transfers between devices, shards(): load = lax.all_to_all(load, both, split_axis=0, concat_axis=0, tiled=True)  3.54 us
    all_to_all x1, waiting for transfers between devices, shards(): lax.all_to_all(orders, both, split_axis=0, concat_axis=0, tiled=True)  2.7 us
    pallas_call x1, Pallas kernels, shards(): pl.pallas_call(message_kernel, in_specs=[HBM] * 4, out_specs=[VMEM] * 2,...  2.33 us
  transfers between devices with their start and end apart: 7, of which 1 were waited for; matrix products, arithmetic and copies ran while one was open for 0% of the time, Pallas kernels for 44%

profile of v12, /device:TPU:0, one launch (start us, length us, event | category | flops | bytes accessed | tf_op | source)
XLA Modules:
  0.0 45.7 jit_solution(1303462066196592848)
XLA Ops:
  0.6 2.3 %shard_map.121 = (f32[32,2048]{1,0:T(8,128)S(1)}, f32[32,2048]{1,0:T(8,128)S(1)}) custom-call(f32[16]{0:T(128)} %viscosity_from.3, f32[3,4,32,2048]{3,2,1,0:T(8,128)} %start.1, f32[3,4,32,2048]{3,2,1,0:T(8,128)} %f.7, s32[4,32,2048]{2,1,0:T(8,128)} %index_from.1), custom_call_target="tpu_custom_call" | custom-call | bytes 60000000 | tf_op jit(solution)/shard_map/pallas_call | solution.py:775
  3.0 0.7 %collective-permute-start.1 = (f32[32,2048]{1,0:T(8,128)S(1)}, f32[32,2048]{1,0:T(8,128)S(1)}, u32[]{:S(2)}, u32[]{:S(2)}) collective-permute-start(f32[32,2048]{1,0:T(8,128)S(1)} %get-tuple-element.44.own_two.mine_two), channel_id=1, source_target_pairs={{3,1},{5,3},{7,5},{9,7},{11,9},{13,11},{15,13},{19,17},{21,19},{23... | collective-permute-start | bytes 786440 | tf_op jit(solution)/shard_map/ppermute | solution.py:791
  3.6 0.7 %collective-permute-start = (f32[32,2048]{1,0:T(8,128)S(1)}, f32[32,2048]{1,0:T(8,128)S(1)}, u32[]{:S(2)}, u32[]{:S(2)}) collective-permute-start(f32[32,2048]{1,0:T(8,128)S(1)} %get-tuple-element.43.token.own_one.mine_one), channel_id=1, source_target_pairs={{1,3},{3,5},{5,7},{7,9},{9,11},{11,13},{13,15},{17,19},{19,21},{21... | collective-permute-start | bytes 786440 | tf_op jit(solution)/shard_map/ppermute | solution.py:792
  4.3 4.9 %shard_map.122 = (f32[4,32,2048]{2,1,0:T(8,128)}, f32[3,2,32,2048]{3,2,1,0:T(8,128)}, f32[2,32,2048]{2,1,0:T(8,128)S(1)}, f32[2,32,2048]{2,1,0:T(8,128)S(1)}, f3...) custom-call(f32[16]{0:T(128)} %viscosity_from.3, f32[3,4,32,2048]{3,2,1,0:T(8,128)} %start.1, f32[3,4,32,2048]{3,2,1,0:T(8,128)} %f.7, ...), custom_call_target="tpu_custom_call" | custom-call | bytes 60000000 | tf_op jit(solution)/shard_map/pallas_call | solution.py:795
  9.3 4.9 %collective-permute-start.2 = (f32[32,2048]{1,0:T(8,128)S(1)}, f32[32,2048]{1,0:T(8,128)S(1)}, u32[]{:S(2)}, u32[]{:S(2)}) collective-permute-start(f32[32,2048]{1,0:T(8,128)S(1)} %get-tuple-element.43.token.own_one.mine_one), channel_id=1, source_target_pairs={{0,2},{2,4},{4,6},{6,8},{8,10},{10,12},{12,14},{16,18},{18,20},{20... | collective-permute-start | bytes 786440 | tf_op jit(solution)/shard_map/ppermute | solution.py:821
  14.2 1.3 %collective-permute-start.3 = (f32[32,2048]{1,0:T(8,128)S(1)}, f32[32,2048]{1,0:T(8,128)S(1)}, u32[]{:S(2)}, u32[]{:S(2)}) collective-permute-start(f32[32,2048]{1,0:T(8,128)S(1)} %get-tuple-element.44.own_two.mine_two), channel_id=1, source_target_pairs={{2,0},{4,2},{6,4},{8,6},{10,8},{12,10},{14,12},{18,16},{20,18},{22... | collective-permute-start | bytes 786440 | tf_op jit(solution)/shard_map/ppermute | solution.py:822
  15.5 0.0 collective-permute-done.1.two
  15.5 0.0 collective-permute-done.one
  15.5 0.7 %shard_map.123 = f32[16,16,128]{2,1,0:T(8,128)} custom-call(f32[2,32,2048]{2,1,0:T(8,128)S(1)} %get-tuple-element.38.surface_swept, f32[2,32,2048]{2,1,0:T(8,128)S(1)} %get-tuple-element.39.surface_eta, f32[32,2048]{1,0:T(8,128)S(1)} %get-tuple-element.40.force, f32[32,2048]{1,0:T(8,128)S(1)} %get-tuple-element.43.token.own_one.mine_one, ...), custom_call_target="tpu_custom_call" | custom-call | bytes 600000000 | tf_op jit(solution)/shard_map/pallas_call | solution.py:825
  16.2 7.2 %all-to-all-start = ((f32[16,16,128]{2,1,0:T(8,128)}), f32[16,16,128]{2,1,0:T(8,128)S(1)}, u32[]{:S(2)}, u32[]{:S(2)}) async-start(f32[16,16,128]{2,1,0:T(8,128)} %shard_map.123), calls=%async_computation | async-start | bytes 262144 | tf_op jit(solution)/shard_map/all_to_all | solution.py:841
  23.4 0.0 collective-permute-done.2.lower_one
  23.5 0.0 collective-permute-done.3.lower_two
  23.5 5.2 %shard_map.124 = (f32[3,2,32,2048]{3,2,1,0:T(8,128)}, f32[32,2048]{1,0:T(8,128)}, f32[264,2048]{1,0:T(8,128)}, f32[2,32,2048]{2,1,0:T(8,128)}, f32[2,32,2048]{2,...) custom-call(f32[3,4,32,2048]{3,2,1,0:T(8,128)} %start.1, ...), custom_call_target="tpu_custom_call" | custom-call | bytes 150000000 | tf_op jit(solution)/shard_map/pallas_call | solution.py:859
  28.7 2.7 %all-to-all-done.orders = f32[16,16,128]{2,1,0:T(8,128)S(1)} async-done(((f32[16,16,128]{2,1,0:T(8,128)}), f32[16,16,128]{2,1,0:T(8,128)S(1)}, u32[]{:S(2)}, u32[]{:S(2)}) %all-to-all-start) | async-done | bytes 131104 | tf_op jit(solution)/shard_map/all_to_all | solution.py:841
  31.4 0.0 collective-permute-start.4
  31.4 1.4 %shard_map.125 = (f32[64,512]{1,0:T(8,128)}, f32[16,16,128]{2,1,0:T(8,128)}) custom-call(f32[16,16,128]{2,1,0:T(8,128)S(1)} %all-to-all-done.orders, bf16[256,512]{1,0:T(8,128)(2,1)S(1)} %get-tuple-element.48.high, bf16[256,512]{1,0:T(8,128)(2,1)S(1)} %get-tuple-element.49.low, f32[512,128]{1,0:T(8,128)S(1)} %get-tuple-element.50.response), custom_call_target="tpu_custom_call" | custom-call | bytes 600000000 | tf_op jit(solution)/shard_map/pallas_call | solution.py:882
  32.8 3.5 %all-to-all-start.1 = ((f32[16,16,128]{2,1,0:T(8,128)}), f32[16,16,128]{2,1,0:T(8,128)S(1)}, u32[]{:S(2)}, u32[]{:S(2)}) async-start(f32[16,16,128]{2,1,0:T(8,128)} %get-tuple-element.59), calls=%async_computation.1 | async-start | bytes 262144 | tf_op jit(solution)/shard_map/all_to_all | solution.py:891
  36.3 0.0 collective-permute-done.4.ring
  36.4 7.9 %shard_map.126 = (f32[3,4,32,2048]{3,2,1,0:T(8,128)}, f32[8,128]{1,0:T(8,128)}, bf16[32,2048]{1,0:T(8,128)(2,1)S(1)}, bf16[256,1024]{1,0:T(8,128)(2,1)S(1)}, bf16[256,1024]{1,0:T(8,128)(2,1)S(1)}) custom-call(f32[3,2,32,2048]{3,2,1,0:T(8,128)} %get-tuple-element.34.early, f32[3,2,32,2048]{3,2,1,0:T(8,128)} %get-tuple-element.45.late, f32[3,4,32,2048]{3,2,1,0:T(8,128)} %f.7, ...), custom_call_target="tpu_custom_call" | custom-call | bytes 150000000 | tf_op jit(solution)/shard_map/pallas_call | solution.py:894
  44.2 0.0 all-to-all-done.1.load
  44.3 1.4 %shard_map.127 = f32[32,2048]{1,0:T(8,128)} custom-call(f32[16,16,128]{2,1,0:T(8,128)S(1)} %all-to-all-done.1.load, bf16[256,1024]{1,0:T(8,128)(2,1)S(1)} %get-tuple-element.60.high, bf16[256,1024]{1,0:T(8,128)(2,1)S(1)} %get-tuple-element.61.low, bf16[32,2048]{1,0:T(8,128)(2,1)S(1)} %get-tuple-element.62.mask), custom_call_target="tpu_custom_call" | custom-call | bytes 9000000 | tf_op jit(solution)/shard_map/pallas_call | solution.py:924
Async XLA Ops:
  3.0 12.5 %collective-permute-start.1 = (f32[32,2048]{1,0:T(8,128)S(1)}, f32[32,2048]{1,0:T(8,128)S(1)}, u32[]{:S(2)}, u32[]{:S(2)}) collective-permute-start(f32[32,2048]{1,0:T(8,128)S(1)} %get-tuple-element.44.own_two.mine_two), channel_id=1, source_target_pairs={{3,1},{5,3},{7,5},{9,7},{11,9},{13,11},{15,13},{19,17},{21,19},{23... | collective-permute-start | bytes 786440 | tf_op jit(solution)/shard_map/ppermute | solution.py:791
  3.6 11.8 %collective-permute-start = (f32[32,2048]{1,0:T(8,128)S(1)}, f32[32,2048]{1,0:T(8,128)S(1)}, u32[]{:S(2)}, u32[]{:S(2)}) collective-permute-start(f32[32,2048]{1,0:T(8,128)S(1)} %get-tuple-element.43.token.own_one.mine_one), channel_id=1, source_target_pairs={{1,3},{3,5},{5,7},{7,9},{9,11},{11,13},{13,15},{17,19},{19,21},{21... | collective-permute-start | bytes 786440 | tf_op jit(solution)/shard_map/ppermute | solution.py:792
  9.3 14.2 %collective-permute-start.2 = (f32[32,2048]{1,0:T(8,128)S(1)}, f32[32,2048]{1,0:T(8,128)S(1)}, u32[]{:S(2)}, u32[]{:S(2)}) collective-permute-start(f32[32,2048]{1,0:T(8,128)S(1)} %get-tuple-element.43.token.own_one.mine_one), channel_id=1, source_target_pairs={{0,2},{2,4},{4,6},{6,8},{8,10},{10,12},{12,14},{16,18},{18,20},{20... | collective-permute-start | bytes 786440 | tf_op jit(solution)/shard_map/ppermute | solution.py:821
  14.2 9.3 %collective-permute-start.3 = (f32[32,2048]{1,0:T(8,128)S(1)}, f32[32,2048]{1,0:T(8,128)S(1)}, u32[]{:S(2)}, u32[]{:S(2)}) collective-permute-start(f32[32,2048]{1,0:T(8,128)S(1)} %get-tuple-element.44.own_two.mine_two), channel_id=1, source_target_pairs={{2,0},{4,2},{6,4},{8,6},{10,8},{12,10},{14,12},{18,16},{20,18},{22... | collective-permute-start | bytes 786440 | tf_op jit(solution)/shard_map/ppermute | solution.py:822
  16.2 15.2 %all-to-all-start = ((f32[16,16,128]{2,1,0:T(8,128)}), f32[16,16,128]{2,1,0:T(8,128)S(1)}, u32[]{:S(2)}, u32[]{:S(2)}) async-start(f32[16,16,128]{2,1,0:T(8,128)} %shard_map.123), calls=%async_computation | async-start | bytes 262144 | tf_op jit(solution)/shard_map/all_to_all | solution.py:841
  31.4 5.0 %collective-permute-start.4 = (f32[264,2048]{1,0:T(8,128)}, f32[264,2048]{1,0:T(8,128)S(1)}, u32[]{:S(2)}, u32[]{:S(2)}) collective-permute-start(f32[264,2048]{1,0:T(8,128)} %get-tuple-element.54), channel_id=1, source_target_pairs={{0,1},{1,0},{2,3},{3,2},{4,5},{5,4},{6,7},{7,6},{8,9},{9,8},{10,11... | collective-permute-start | bytes 6488072 | tf_op jit(solution)/shard_map/ppermute | solution.py:881
  32.8 11.5 %all-to-all-start.1 = ((f32[16,16,128]{2,1,0:T(8,128)}), f32[16,16,128]{2,1,0:T(8,128)S(1)}, u32[]{:S(2)}, u32[]{:S(2)}) async-start(f32[16,16,128]{2,1,0:T(8,128)} %get-tuple-element.59), calls=%async_computation.1 | async-start | bytes 262144 | tf_op jit(solution)/shard_map/all_to_all | solution.py:891

commit v13 on v12

--- a/solution.py
+++ b/solution.py
@@ -675,7 +675,7 @@
                 )
             return 0
 
-        lax.fori_loop(0, rows // TILE, tile, 0)
+        lax.fori_loop(0, rows // TILE, tile, 0, unroll=2)
 
     def finish(s, first):
         part = pl.ds(first, TILE)
@@ -685,7 +685,7 @@
             result[c, s, part] = relax(weights, factor, middle, others, force[c, s, part])
 
     def after_shell(s, k):
-        if k == shells - 2:
+        if k == 0:
             copies.extend(
                 start_all(
                     [

time: 46.2 us -> 46.1 us (level)
  no operation moved by 1% of the time
where the time goes in v13:
time: 46.1 us; the launch traced here: 45.7 us
  Pallas kernels  23.9 us (52%)
  starting transfers between devices  18.3 us (40%)
  waiting for transfers between devices  2.76 us (6%)
  between operations  0.76 us (2%)
    pallas_call x1, Pallas kernels, shards(): pl.pallas_call(second_kernel, in_specs=[HBM] * 6 + [ANY] + [HBM] * (3 + l...  7.88 us
    all_to_all x1, starting transfers between devices, shards(): lax.all_to_all(orders, both, split_axis=0, concat_axis=0, tiled=True)  7.25 us
    pallas_call x1, Pallas kernels, shards(): pl.pallas_call(first_kernel, in_specs=[HBM] * 3 + [ANY] * 6 + [HBM] * len...  5.2 us
    pallas_call x1, Pallas kernels, shards(): pl.pallas_call(viscosity_kernel, in_specs=[HBM] * 4 + [ANY, HBM], out_spe...  4.94 us
    ppermute x1, starting transfers between devices, shards(): lower_one = lax.ppermute(lower_one, both, lower_only(first))  4.89 us
    all_to_all x1, starting transfers between devices, shards(): load = lax.all_to_all(load, both, split_axis=0, concat_axis=0, tiled=True)  3.54 us
    all_to_all x1, waiting for transfers between devices, shards(): lax.all_to_all(orders, both, split_axis=0, concat_axis=0, tiled=True)  2.7 us
    pallas_call x1, Pallas kernels, shards(): pl.pallas_call(message_kernel, in_specs=[HBM] * 4, out_specs=[VMEM] * 2,...  2.33 us
  transfers between devices with their start and end apart: 7, of which 1 were waited for; matrix products, arithmetic and copies ran while one was open for 0% of the time, Pallas kernels for 44%

profile of v13, /device:TPU:0, one launch (start us, length us, event | category | flops | bytes accessed | tf_op | source)
XLA Modules:
  0.0 45.7 jit_solution(15919465084355590586)
XLA Ops:
  0.6 2.3 %shard_map.121 = (f32[32,2048]{1,0:T(8,128)S(1)}, f32[32,2048]{1,0:T(8,128)S(1)}) custom-call(f32[16]{0:T(128)} %viscosity_from.3, f32[3,4,32,2048]{3,2,1,0:T(8,128)} %start.1, f32[3,4,32,2048]{3,2,1,0:T(8,128)} %f.7, s32[4,32,2048]{2,1,0:T(8,128)} %index_from.1), custom_call_target="tpu_custom_call" | custom-call | bytes 60000000 | tf_op jit(solution)/shard_map/pallas_call | solution.py:775
  3.0 0.7 %collective-permute-start.1 = (f32[32,2048]{1,0:T(8,128)S(1)}, f32[32,2048]{1,0:T(8,128)S(1)}, u32[]{:S(2)}, u32[]{:S(2)}) collective-permute-start(f32[32,2048]{1,0:T(8,128)S(1)} %get-tuple-element.44.own_two.mine_two), channel_id=1, source_target_pairs={{3,1},{5,3},{7,5},{9,7},{11,9},{13,11},{15,13},{19,17},{21,19},{23... | collective-permute-start | bytes 786440 | tf_op jit(solution)/shard_map/ppermute | solution.py:791
  3.6 0.7 %collective-permute-start = (f32[32,2048]{1,0:T(8,128)S(1)}, f32[32,2048]{1,0:T(8,128)S(1)}, u32[]{:S(2)}, u32[]{:S(2)}) collective-permute-start(f32[32,2048]{1,0:T(8,128)S(1)} %get-tuple-element.43.token.own_one.mine_one), channel_id=1, source_target_pairs={{1,3},{3,5},{5,7},{7,9},{9,11},{11,13},{13,15},{17,19},{19,21},{21... | collective-permute-start | bytes 786440 | tf_op jit(solution)/shard_map/ppermute | solution.py:792
  4.3 4.9 %shard_map.122 = (f32[4,32,2048]{2,1,0:T(8,128)}, f32[3,2,32,2048]{3,2,1,0:T(8,128)}, f32[2,32,2048]{2,1,0:T(8,128)S(1)}, f32[2,32,2048]{2,1,0:T(8,128)S(1)}, f3...) custom-call(f32[16]{0:T(128)} %viscosity_from.3, f32[3,4,32,2048]{3,2,1,0:T(8,128)} %start.1, f32[3,4,32,2048]{3,2,1,0:T(8,128)} %f.7, ...), custom_call_target="tpu_custom_call" | custom-call | bytes 60000000 | tf_op jit(solution)/shard_map/pallas_call | solution.py:795
  9.3 4.9 %collective-permute-start.2 = (f32[32,2048]{1,0:T(8,128)S(1)}, f32[32,2048]{1,0:T(8,128)S(1)}, u32[]{:S(2)}, u32[]{:S(2)}) collective-permute-start(f32[32,2048]{1,0:T(8,128)S(1)} %get-tuple-element.43.token.own_one.mine_one), channel_id=1, source_target_pairs={{0,2},{2,4},{4,6},{6,8},{8,10},{10,12},{12,14},{16,18},{18,20},{20... | collective-permute-start | bytes 786440 | tf_op jit(solution)/shard_map/ppermute | solution.py:821
  14.2 1.3 %collective-permute-start.3 = (f32[32,2048]{1,0:T(8,128)S(1)}, f32[32,2048]{1,0:T(8,128)S(1)}, u32[]{:S(2)}, u32[]{:S(2)}) collective-permute-start(f32[32,2048]{1,0:T(8,128)S(1)} %get-tuple-element.44.own_two.mine_two), channel_id=1, source_target_pairs={{2,0},{4,2},{6,4},{8,6},{10,8},{12,10},{14,12},{18,16},{20,18},{22... | collective-permute-start | bytes 786440 | tf_op jit(solution)/shard_map/ppermute | solution.py:822
  15.5 0.0 collective-permute-done.1.two
  15.5 0.0 collective-permute-done.one
  15.5 0.7 %shard_map.123 = f32[16,16,128]{2,1,0:T(8,128)} custom-call(f32[2,32,2048]{2,1,0:T(8,128)S(1)} %get-tuple-element.38.surface_swept, f32[2,32,2048]{2,1,0:T(8,128)S(1)} %get-tuple-element.39.surface_eta, f32[32,2048]{1,0:T(8,128)S(1)} %get-tuple-element.40.force, f32[32,2048]{1,0:T(8,128)S(1)} %get-tuple-element.43.token.own_one.mine_one, ...), custom_call_target="tpu_custom_call" | custom-call | bytes 600000000 | tf_op jit(solution)/shard_map/pallas_call | solution.py:825
  16.2 7.2 %all-to-all-start = ((f32[16,16,128]{2,1,0:T(8,128)}), f32[16,16,128]{2,1,0:T(8,128)S(1)}, u32[]{:S(2)}, u32[]{:S(2)}) async-start(f32[16,16,128]{2,1,0:T(8,128)} %shard_map.123), calls=%async_computation | async-start | bytes 262144 | tf_op jit(solution)/shard_map/all_to_all | solution.py:841
  23.4 0.0 collective-permute-done.2.lower_one
  23.5 0.0 collective-permute-done.3.lower_two
  23.5 5.2 %shard_map.124 = (f32[3,2,32,2048]{3,2,1,0:T(8,128)}, f32[32,2048]{1,0:T(8,128)}, f32[264,2048]{1,0:T(8,128)}, f32[2,32,2048]{2,1,0:T(8,128)}, f32[2,32,2048]{2,...) custom-call(f32[3,4,32,2048]{3,2,1,0:T(8,128)} %start.1, ...), custom_call_target="tpu_custom_call" | custom-call | bytes 150000000 | tf_op jit(solution)/shard_map/pallas_call | solution.py:859
  28.7 2.7 %all-to-all-done.orders = f32[16,16,128]{2,1,0:T(8,128)S(1)} async-done(((f32[16,16,128]{2,1,0:T(8,128)}), f32[16,16,128]{2,1,0:T(8,128)S(1)}, u32[]{:S(2)}, u32[]{:S(2)}) %all-to-all-start) | async-done | bytes 131104 | tf_op jit(solution)/shard_map/all_to_all | solution.py:841
  31.4 0.0 collective-permute-start.4
  31.4 1.4 %shard_map.125 = (f32[64,512]{1,0:T(8,128)}, f32[16,16,128]{2,1,0:T(8,128)}) custom-call(f32[16,16,128]{2,1,0:T(8,128)S(1)} %all-to-all-done.orders, bf16[256,512]{1,0:T(8,128)(2,1)S(1)} %get-tuple-element.48.high, bf16[256,512]{1,0:T(8,128)(2,1)S(1)} %get-tuple-element.49.low, f32[512,128]{1,0:T(8,128)S(1)} %get-tuple-element.50.response), custom_call_target="tpu_custom_call" | custom-call | bytes 600000000 | tf_op jit(solution)/shard_map/pallas_call | solution.py:882
  32.8 3.5 %all-to-all-start.1 = ((f32[16,16,128]{2,1,0:T(8,128)}), f32[16,16,128]{2,1,0:T(8,128)S(1)}, u32[]{:S(2)}, u32[]{:S(2)}) async-start(f32[16,16,128]{2,1,0:T(8,128)} %get-tuple-element.59), calls=%async_computation.1 | async-start | bytes 262144 | tf_op jit(solution)/shard_map/all_to_all | solution.py:891
  36.3 0.0 collective-permute-done.4.ring
  36.4 7.9 %shard_map.126 = (f32[3,4,32,2048]{3,2,1,0:T(8,128)}, f32[8,128]{1,0:T(8,128)}, bf16[32,2048]{1,0:T(8,128)(2,1)S(1)}, bf16[256,1024]{1,0:T(8,128)(2,1)S(1)}, bf16[256,1024]{1,0:T(8,128)(2,1)S(1)}) custom-call(f32[3,2,32,2048]{3,2,1,0:T(8,128)} %get-tuple-element.34.early, f32[3,2,32,2048]{3,2,1,0:T(8,128)} %get-tuple-element.45.late, f32[3,4,32,2048]{3,2,1,0:T(8,128)} %f.7, ...), custom_call_target="tpu_custom_call" | custom-call | bytes 150000000 | tf_op jit(solution)/shard_map/pallas_call | solution.py:894
  44.2 0.0 all-to-all-done.1.load
  44.3 1.4 %shard_map.127 = f32[32,2048]{1,0:T(8,128)} custom-call(f32[16,16,128]{2,1,0:T(8,128)S(1)} %all-to-all-done.1.load, bf16[256,1024]{1,0:T(8,128)(2,1)S(1)} %get-tuple-element.60.high, bf16[256,1024]{1,0:T(8,128)(2,1)S(1)} %get-tuple-element.61.low, bf16[32,2048]{1,0:T(8,128)(2,1)S(1)} %get-tuple-element.62.mask), custom_call_target="tpu_custom_call" | custom-call | bytes 9000000 | tf_op jit(solution)/shard_map/pallas_call | solution.py:924
Async XLA Ops:
  3.0 12.5 %collective-permute-start.1 = (f32[32,2048]{1,0:T(8,128)S(1)}, f32[32,2048]{1,0:T(8,128)S(1)}, u32[]{:S(2)}, u32[]{:S(2)}) collective-permute-start(f32[32,2048]{1,0:T(8,128)S(1)} %get-tuple-element.44.own_two.mine_two), channel_id=1, source_target_pairs={{3,1},{5,3},{7,5},{9,7},{11,9},{13,11},{15,13},{19,17},{21,19},{23... | collective-permute-start | bytes 786440 | tf_op jit(solution)/shard_map/ppermute | solution.py:791
  3.6 11.8 %collective-permute-start = (f32[32,2048]{1,0:T(8,128)S(1)}, f32[32,2048]{1,0:T(8,128)S(1)}, u32[]{:S(2)}, u32[]{:S(2)}) collective-permute-start(f32[32,2048]{1,0:T(8,128)S(1)} %get-tuple-element.43.token.own_one.mine_one), channel_id=1, source_target_pairs={{1,3},{3,5},{5,7},{7,9},{9,11},{11,13},{13,15},{17,19},{19,21},{21... | collective-permute-start | bytes 786440 | tf_op jit(solution)/shard_map/ppermute | solution.py:792
  9.3 14.2 %collective-permute-start.2 = (f32[32,2048]{1,0:T(8,128)S(1)}, f32[32,2048]{1,0:T(8,128)S(1)}, u32[]{:S(2)}, u32[]{:S(2)}) collective-permute-start(f32[32,2048]{1,0:T(8,128)S(1)} %get-tuple-element.43.token.own_one.mine_one), channel_id=1, source_target_pairs={{0,2},{2,4},{4,6},{6,8},{8,10},{10,12},{12,14},{16,18},{18,20},{20... | collective-permute-start | bytes 786440 | tf_op jit(solution)/shard_map/ppermute | solution.py:821
  14.2 9.3 %collective-permute-start.3 = (f32[32,2048]{1,0:T(8,128)S(1)}, f32[32,2048]{1,0:T(8,128)S(1)}, u32[]{:S(2)}, u32[]{:S(2)}) collective-permute-start(f32[32,2048]{1,0:T(8,128)S(1)} %get-tuple-element.44.own_two.mine_two), channel_id=1, source_target_pairs={{2,0},{4,2},{6,4},{8,6},{10,8},{12,10},{14,12},{18,16},{20,18},{22... | collective-permute-start | bytes 786440 | tf_op jit(solution)/shard_map/ppermute | solution.py:822
  16.2 15.2 %all-to-all-start = ((f32[16,16,128]{2,1,0:T(8,128)}), f32[16,16,128]{2,1,0:T(8,128)S(1)}, u32[]{:S(2)}, u32[]{:S(2)}) async-start(f32[16,16,128]{2,1,0:T(8,128)} %shard_map.123), calls=%async_computation | async-start | bytes 262144 | tf_op jit(solution)/shard_map/all_to_all | solution.py:841
  31.4 5.0 %collective-permute-start.4 = (f32[264,2048]{1,0:T(8,128)}, f32[264,2048]{1,0:T(8,128)S(1)}, u32[]{:S(2)}, u32[]{:S(2)}) collective-permute-start(f32[264,2048]{1,0:T(8,128)} %get-tuple-element.54), channel_id=1, source_target_pairs={{0,1},{1,0},{2,3},{3,2},{4,5},{5,4},{6,7},{7,6},{8,9},{9,8},{10,11... | collective-permute-start | bytes 6488072 | tf_op jit(solution)/shard_map/ppermute | solution.py:881
  32.8 11.5 %all-to-all-start.1 = ((f32[16,16,128]{2,1,0:T(8,128)}), f32[16,16,128]{2,1,0:T(8,128)S(1)}, u32[]{:S(2)}, u32[]{:S(2)}) async-start(f32[16,16,128]{2,1,0:T(8,128)} %get-tuple-element.59), calls=%async_computation.1 | async-start | bytes 262144 | tf_op jit(solution)/shard_map/all_to_all | solution.py:891
